TPU v7x, 128 devices: a whole 4x4x4 slice. The times are simulated.
128 devices in a mesh: gx: 16 (over x, y), gy: 8 (over z, core).
Axes of the slice: x: 4, y: 4, z: 4, core: 2. Of those that a mesh axis runs over, the one named last changes fastest.
Arguments:
- features: bfloat16 [32, 32, 256, 128], P(None, 'gx', 'gy'), may hold values from -80 to 80
- kernel_one: bfloat16 [32, 32, 3, 3, 3], replicated, may hold values from -0.21875 to 0.21875
- gain_one: float32 [32], replicated, may hold values from 0.5 to 1.5
- bias_one: float32 [32], replicated, may hold values from -0.5 to 0.5
- kernel_two: bfloat16 [32, 32, 3, 3, 3], replicated, may hold values from -0.21875 to 0.21875
- gain_two: float32 [32], replicated, may hold values from 0.5 to 1.5
- bias_two: float32 [32], replicated, may hold values from -0.5 to 0.5
- cotangent: bfloat16 [32, 32, 256, 128], P(None, 'gx', 'gy'), may hold values from -80 to 80
Outputs:
- output: bfloat16 [32, 32, 256, 128], P(None, 'gx', 'gy')
- features_grad: bfloat16 [32, 32, 256, 128], P(None, 'gx', 'gy')
- kernel_one_grad: float32 [32, 32, 3, 3, 3], replicated
- kernel_two_grad: float32 [32, 32, 3, 3, 3], replicated
- norm_grads: float32 [4, 32], replicated
All inputs are finite; a program needn't handle non-finite values.
Results may differ from a plain program's by a relative error of at most 0.0078.
Values may be sent and summed in bfloat16 or wider, within the bound.
No kernel may reach another device: no remote copies, remote signals or barrier semaphores. Data moves between devices by JAX's collectives and lax.ppermute only.
A program may use at most 192 MiB of HBM per device.

v0:
```python
import jax
import jax.numpy as jnp
from jax import lax
from jax.experimental import pallas as pl
from jax.experimental.pallas import tpu as pltpu
from jax.sharding import Mesh
from jax.sharding import PartitionSpec as P

GX = ("gx_0", "gx_1")
GY = ("gy_0", "gy_1")
ALL = GX + GY

EPSILON = 1e-05
C = 32
ROWS = 32
F32 = jnp.float32
BF16 = jnp.bfloat16
LN2 = 0.6931471805599453
VM = pl.BlockSpec(memory_space=pltpu.VMEM)
SM = pl.BlockSpec(memory_space=pltpu.SMEM)


def sh(shape, kind):
    return jax.ShapeDtypeStruct(shape, kind)


def from_below(values, lane):
    return jnp.where(lane == 0, 0.0, pltpu.roll(values, 1, 1))


def from_above(values, lane):
    return jnp.where(lane == 127, 0.0, pltpu.roll(values, 127, 1))


def lanes(rows):
    return lax.broadcasted_iota(jnp.int32, (rows, 128), 1)


def conv_rows(v_ref, w_ref, rows, emit):
    lane = lanes(64)
    weights = w_ref[...]
    for y in range(0, rows, 2):
        first = v_ref[y : y + 3].reshape(384, 128)
        second = v_ref[y + 1 : y + 4].reshape(384, 128)
        product = jnp.dot(
            weights, jnp.concatenate([first, second], axis=1), preferred_element_type=F32
        )
        for k in range(2):
            part = product[:, k * 128 : (k + 1) * 128]
            emit(
                y + k,
                part[64:128] + from_below(part[0:64], lane) + from_above(part[128:192], lane),
            )


def fold(column):
    return column[0:C] + column[C : 2 * C]


def total(values):
    return jnp.sum(values, axis=1, keepdims=True)


def twice(column):
    return jnp.concatenate([column, column], axis=0)


def message(columns, msg_ref):
    count = msg_ref.shape[0]
    spare = jnp.zeros((128 - C * len(columns), 1), F32)
    column = jnp.concatenate([*columns, spare], axis=0)
    msg_ref[...] = jnp.transpose(jnp.broadcast_to(column, (128, count)))


def stats_out(h_ref, acc, start, low_ref, high_ref, msg_ref):
    center = fold(total(acc)) / (2 * ROWS * 128)
    both = twice(center)
    spread = jnp.zeros((64, 128), F32)
    for y in range(h_ref.shape[0]):
        off = h_ref[y] - both
        if start <= y < start + ROWS:
            spread = spread + off * off
        low_ref[y] = off[0:C].astype(BF16)
        high_ref[y] = off[C:].astype(BF16)
    message((center, fold(total(spread))), msg_ref)


def read_stats(r_ref, place_ref, cells):
    parts = jnp.transpose(r_ref[...])
    centers = parts[0:C]
    count = parts.shape[1]
    mean = total(centers) / count
    off = centers - mean
    spread = (total(parts[C : 2 * C]) + (2 * ROWS * 128) * total(off * off)) / cells
    at = lax.broadcasted_iota(jnp.int32, centers.shape, 1)
    low = total(jnp.where(at == place_ref[0], off, 0.0))
    high = total(jnp.where(at == place_ref[1], off, 0.0))
    return mean, lax.rsqrt(spread + EPSILON), low, high


def read_sums(r_ref):
    parts = jnp.transpose(r_ref[...])
    return total(parts[0:C]), total(parts[C : 2 * C])


def act(z):
    e = jnp.exp2(jnp.abs(z) * (-8.0 / LN2))
    soft = jnp.maximum(z, 0.0) * 0.99 + jnp.log2(1.0 + e) * (0.99 * LN2 / 8.0)
    return 0.01 * z + soft


def act_slope(z):
    return 0.505 + 0.495 * jnp.tanh(4.0 * z)


def kept(place_ref, y, rows, margin):
    low = place_ref[2].astype(F32)
    high = place_ref[3].astype(F32)
    if y < margin:
        edge = place_ref[4].astype(F32)
    elif y >= rows - margin:
        edge = place_ref[5].astype(F32)
    else:
        return low, None, high
    return low * edge, edge, high * edge


def masked(low, own, high, factors):
    f_low, f_own, f_high = factors
    own = own if f_own is None else own * f_own
    return jnp.concatenate([low * f_low, own, high * f_high], axis=0).astype(BF16)


def weight_sums(g_ref, v_ref, first, acc_ref, out_ref):
    step = 4
    for y in range(0, ROWS, step):
        right = jnp.concatenate(
            [v_ref[first + y + k : first + y + k + 3].reshape(384, 128) for k in range(step)], axis=1
        )
        left = g_ref[:, y * 128 : (y + step) * 128]
        product = lax.dot_general(
            left, right, (((1,), (1,)), ((), ())), preferred_element_type=F32
        )
        if y == 0:
            acc_ref[...] = product
        else:
            acc_ref[...] += product
    for dz in range(3):
        for dy in range(3):
            tile = acc_ref[dz * 64 : dz * 64 + 64, dy * 128 : dy * 128 + 128]
            out_ref[dz * 3 + dy] = tile[0:C] + pltpu.roll(tile[C:], 96, 1)


def put_shifted(g_ref, y, values, lane):
    at = slice(y * 128, (y + 1) * 128)
    g_ref[0:64, at] = from_above(values, lane).astype(BF16)
    g_ref[64:128, at] = values.astype(BF16)
    g_ref[128:192, at] = from_below(values, lane).astype(BF16)


def first_kernel(own, y_low, y_high, x_low, x_high, c_low, c_high, w, v, h, low, high, msg):
    for part, (rows, at) in (
        ((y_low, c_low, c_high, 0), (4, 0)),
        ((own, x_low, x_high, 0), (ROWS, 4)),
        ((y_high, c_low, c_high, 4), (4, ROWS + 4)),
    ):
        middle, left, right, offset = part
        for y in range(rows):
            v[at + y] = jnp.concatenate([left[offset + y], middle[y], right[offset + y]], axis=0)
    acc = [jnp.zeros((64, 128), F32)]

    def emit(y, values):
        h[y] = values
        if 3 <= y < 3 + ROWS:
            acc[0] = acc[0] + values

    conv_rows(v, w, ROWS + 6, emit)
    stats_out(h, acc[0], 3, low, high, msg)


def second_kernel(cells, place, h1, x_low, x_high, r1, gb, w, v, h, low, high, msg):
    mean, inverse, o_low, o_high = read_stats(r1, place, cells)
    scale = inverse * gb[:, 0:1]
    shift = gb[:, 1:2]
    mean2, scale2, shift2 = twice(mean), twice(scale), twice(shift)
    b_low, b_high = shift + o_low * scale, shift + o_high * scale
    rows = ROWS + 6
    for y in range(rows):
        a_low = act(x_low[y].astype(F32) * scale + b_low)
        a_own = act((h1[y] - mean2) * scale2 + shift2)
        a_high = act(x_high[y].astype(F32) * scale + b_high)
        v[y] = masked(a_low, a_own, a_high, kept(place, y, rows, 3))
    acc = [jnp.zeros((64, 128), F32)]

    def emit(y, values):
        h[y] = values
        if 2 <= y < 2 + ROWS:
            acc[0] = acc[0] + values

    conv_rows(v, w, ROWS + 4, emit)
    stats_out(h, acc[0], 2, low, high, msg)


def third_kernel(cells, place, h2, cot, r2, gb, out, msg):
    mean, inverse, _, _ = read_stats(r2, place, cells)
    mean2, inverse2 = twice(mean), twice(inverse)
    gain2, bias2 = twice(gb[:, 2:3]), twice(gb[:, 3:4])
    plain = jnp.zeros((64, 128), F32)
    both = jnp.zeros((64, 128), F32)
    for y in range(ROWS):
        normed = (h2[y + 2] - mean2) * inverse2
        z = normed * gain2 + bias2
        out[y] = act(z).astype(BF16)
        slope = cot[y + 2].astype(F32) * act_slope(z)
        plain = plain + slope
        both = both + slope * normed
    message((fold(total(both)), fold(total(plain))), msg)


def fourth_kernel(
    cells, place, h2, x_low, x_high, cot, t_low, t_high, r2, r3, h1, r1, gb, v2, w,
    slope1, low, high, msg, wg, v, g, acc,
):
    mean, inverse, o_low, o_high = read_stats(r2, place, cells)
    nsum, plain = read_sums(r3)
    gain, bias = gb[:, 2:3], gb[:, 3:4]
    lead = gain * inverse
    p_mean, n_mean = plain / cells, nsum / cells

    def grad(normed, c, gain, bias, lead, p_mean, n_mean):
        slope = c.astype(F32) * act_slope(normed * gain + bias)
        return lead * (slope - p_mean - normed * n_mean)

    one = (gain, bias, lead, p_mean, n_mean)
    two = tuple(twice(a) for a in one)
    mean2, inverse2 = twice(mean), twice(inverse)
    lane = lanes(64)
    rows = ROWS + 4
    for y in range(rows):
        g_low = grad((x_low[y].astype(F32) + o_low) * inverse, t_low[y], *one)
        g_own = grad((h2[y] - mean2) * inverse2, cot[y], *two)
        g_high = grad((x_high[y].astype(F32) + o_high) * inverse, t_high[y], *one)
        v[y] = masked(g_low, g_own, g_high, kept(place, y, rows, 2))
        if 2 <= y < 2 + ROWS:
            put_shifted(g, y - 2, g_own, lane)

    mean, inverse, _, _ = read_stats(r1, place, cells)
    mean2, inverse2 = twice(mean), twice(inverse)
    gain2, bias2 = twice(gb[:, 0:1]), twice(gb[:, 1:2])
    sums = [jnp.zeros((64, 128), F32), jnp.zeros((64, 128), F32)]

    def emit(y, values):
        normed = (h1[y + 2] - mean2) * inverse2
        slope = values * act_slope(normed * gain2 + bias2)
        slope1[y] = slope
        low[y] = slope[0:C].astype(BF16)
        high[y] = slope[C:].astype(BF16)
        if 1 <= y < 1 + ROWS:
            sums[0] = sums[0] + slope * normed
            sums[1] = sums[1] + slope

    conv_rows(v, w, ROWS + 2, emit)
    message((fold(total(sums[0])), fold(total(sums[1]))), msg)
    weight_sums(g, v2, 2, acc, wg)


def fifth_kernel(
    cells, place, slope1, s_low, s_high, h1, x_low, x_high, r1, r4, gb, v1, w, out, wg, v, g, acc
):
    mean, inverse, o_low, o_high = read_stats(r1, place, cells)
    nsum, plain = read_sums(r4)
    lead = gb[:, 0:1] * inverse
    p_mean, n_mean = plain / cells, nsum / cells
    mean2, inverse2, lead2 = twice(mean), twice(inverse), twice(lead)
    p_mean2, n_mean2 = twice(p_mean), twice(n_mean)
    lane = lanes(64)
    rows = ROWS + 2
    for y in range(rows):
        n_low = (x_low[y + 2].astype(F32) + o_low) * inverse
        n_own = (h1[y + 2] - mean2) * inverse2
        n_high = (x_high[y + 2].astype(F32) + o_high) * inverse
        g_low = lead * (s_low[y].astype(F32) - p_mean - n_low * n_mean)
        g_own = lead2 * (slope1[y] - p_mean2 - n_own * n_mean2)
        g_high = lead * (s_high[y].astype(F32) - p_mean - n_high * n_mean)
        v[y] = masked(g_low, g_own, g_high, kept(place, y, rows, 1))
        if 1 <= y < 1 + ROWS:
            put_shifted(g, y - 1, g_own, lane)

    def emit(y, values):
        out[y] = values.astype(BF16)

    conv_rows(v, w, ROWS, emit)
    weight_sums(g, v1, 3, acc, wg)


def call(kernel, ins, outs, name, scratch=(), smem_first=True):
    specs = [SM if (k == 0 and smem_first) else VM for k in range(len(ins))]
    return pl.pallas_call(
        kernel,
        out_shape=outs,
        in_specs=specs,
        out_specs=[VM] * len(outs),
        scratch_shapes=list(scratch),
        compiler_params=pltpu.CompilerParams(vmem_limit_bytes=40 * 1024 * 1024),
        cost_estimate=pl.CostEstimate(
            flops=2_000_000_000, bytes_accessed=6_000_000, transcendentals=0
        ),
        name=name,
    )(*ins)


def up(values, axes):
    count = lax.axis_size(axes)
    return lax.ppermute(values, axes, [(i, i + 1) for i in range(count - 1)])


def down(values, axes):
    count = lax.axis_size(axes)
    return lax.ppermute(values, axes, [(i + 1, i) for i in range(count - 1)])


def share(msg):
    return lax.all_to_all(msg, ALL, 0, 0, tiled=True)


def summed(pieces, count):
    rows = pieces.reshape(-1, 128)
    spare = -rows.shape[0] % count
    rows = jnp.pad(rows, ((0, spare), (0, 0))).reshape(count, -1, 128)
    own = share(rows).sum(axis=0)
    whole = share(jnp.broadcast_to(own[None], rows.shape))
    return whole.reshape(-1, 128)[: rows.shape[0] * rows.shape[1] - spare]


def kernel_matrix(kernel):
    first = jnp.pad(kernel, ((0, 0), (0, 0), (0, 1), (0, 0), (0, 0)))
    second = jnp.pad(kernel, ((0, 0), (0, 0), (1, 0), (0, 0), (0, 0)))
    both = jnp.stack([first, second])
    return jnp.transpose(both, (5, 0, 1, 4, 3, 2)).reshape(192, 384)


def flip_kernel(kernel):
    return jnp.transpose(kernel[:, :, ::-1, ::-1, ::-1], (1, 0, 2, 3, 4))


def unfolded(rows):
    tiles = rows.reshape(3, 3, C, 128)[..., :96].reshape(3, 3, C, 3, C)
    return jnp.transpose(tiles, (2, 4, 3, 1, 0))


def local(features, kernel_one, gain_one, bias_one, kernel_two, gain_two, bias_two, cotangent):
    count_x, count_y = lax.axis_size(GX), lax.axis_size(GY)
    count = count_x * count_y
    cells = float(count * 2 * ROWS * 128)
    gx, gy = lax.axis_index(GX), lax.axis_index(GY)
    at = gx * count_y + gy
    place = jnp.stack(
        [at - count_y, at + count_y, gx > 0, gx < count_x - 1, gy > 0, gy < count_y - 1]
    ).astype(jnp.int32)
    gb = jnp.stack([gain_one, bias_one, gain_two, bias_two], axis=1)

    own = jnp.transpose(features, (2, 1, 0, 3)).reshape(ROWS, 64, 128)
    cot = jnp.transpose(cotangent, (2, 1, 0, 3)).reshape(ROWS, 64, 128)
    x_low = up(own[:, C:], GX)
    x_high = down(own[:, :C], GX)
    y_low = up(jnp.concatenate([own[-4:], cot[-2:]]), GY)
    y_high = down(jnp.concatenate([own[:4], cot[:2]]), GY)
    corner = jnp.concatenate([y_low[:4], y_high[:4]])
    c_low = up(corner[:, C:], GX)
    c_high = down(corner[:, :C], GX)
    w1, w2 = kernel_matrix(kernel_one), kernel_matrix(kernel_two)
    b1, b2 = kernel_matrix(flip_kernel(kernel_one)), kernel_matrix(flip_kernel(kernel_two))

    def rims(rows):
        return [sh((rows, C, 128), BF16)] * 2

    msg = sh((count, 128), F32)
    work = (pltpu.VMEM((192, ROWS * 128), BF16), pltpu.VMEM((192, 384), F32))

    v1, h1, low, high, m1 = call(
        first_kernel,
        (own, y_low[:4], y_high[:4], x_low, x_high, c_low, c_high, w1),
        [sh((40, 128, 128), BF16), sh((38, 64, 128), F32), *rims(38), msg],
        "conv_one",
        smem_first=False,
    )
    h1_low, h1_high = up(high, GX), down(low, GX)
    cot = jnp.concatenate([y_low[4:], cot, y_high[4:]])
    t_low, t_high = up(cot[:, C:], GX), down(cot[:, :C], GX)
    r1 = share(m1)

    v2, h2, low, high, m2 = call(
        lambda *refs: second_kernel(cells, *refs),
        (place, h1, h1_low, h1_high, r1, gb, w2),
        [sh((38, 128, 128), BF16), sh((36, 64, 128), F32), *rims(36), msg],
        "conv_two",
    )
    h2_low, h2_high = up(high, GX), down(low, GX)
    r2 = share(m2)

    output, m3 = call(
        lambda *refs: third_kernel(cells, *refs),
        (place, h2, cot, r2, gb),
        [sh((ROWS, 64, 128), BF16), msg],
        "slope_two",
    )
    r3 = share(m3)

    slope1, low, high, m4, wg2 = call(
        lambda *refs: fourth_kernel(cells, *refs),
        (place, h2, h2_low, h2_high, cot, t_low, t_high, r2, r3, h1, r1, gb, v2, b2),
        [sh((34, 64, 128), F32), *rims(34), msg, sh((9, C, 128), F32)],
        "back_two",
        scratch=(pltpu.VMEM((36, 128, 128), BF16), *work),
    )
    s_low, s_high = up(high, GX), down(low, GX)
    r4 = share(m4)

    grad, wg1 = call(
        lambda *refs: fifth_kernel(cells, *refs),
        (place, slope1, s_low, s_high, h1, h1_low, h1_high, r1, r4, gb, v1, b1),
        [sh((ROWS, 64, 128), BF16), sh((9, C, 128), F32)],
        "back_one",
        scratch=(pltpu.VMEM((34, 128, 128), BF16), *work),
    )
    scale = 1.0 / jnp.sqrt(jnp.float32(cells))
    whole = summed(jnp.concatenate([wg1, wg2]), count) * scale
    half = whole.shape[0] // 2
    norm_grads = jnp.concatenate(
        [r4[:, : 2 * C].sum(axis=0).reshape(2, C), r3[:, : 2 * C].sum(axis=0).reshape(2, C)]
    )

    def back(rows):
        return jnp.transpose(rows.reshape(ROWS, 2, C, 128), (2, 1, 0, 3))

    return (
        back(output),
        back(grad),
        unfolded(whole[:half]),
        unfolded(whole[half:]),
        norm_grads * scale,
    )


def solution(mesh):
    nx, ny = mesh.devices.shape
    parts = (4, nx // 4, ny // 2, 2)
    split = Mesh(mesh.devices.reshape(parts), ALL)
    spec = P(None, GX, GY, None)
    in_specs = (spec, P(), P(), P(), P(), P(), P(), spec)
    out_specs = (spec, spec, P(), P(), P())
    return jax.shard_map(local, mesh=split, in_specs=in_specs, out_specs=out_specs, check_vma=False)
```

profile of v0, /device:TPU:1, one launch (start us, length us, event | category | flops | bytes accessed | tf_op | source)
XLA Modules:
  0.0 199.8 jit_solution(16880978187268158667)
XLA Ops:
  0.6 1.1 fusion.3
  1.7 1.0 fusion.4
  2.8 4.9 %collective-permute-start = (bf16[6,64,128]{2,1,0:T(8,128)(2,1)S(1)}, bf16[6,64,128]{2,1,0:T(8,128)(2,1)}, u32[]{:S(2)}, u32[]{:S(2)}) collective-permute-start(bf16[6,64,128]{2,1,0:T(8,128)(2,1)S(1)} %pad_maximum_fusion.2), channel_id=1, source_target_pairs={{0,1},{1,2},{2,3},{3,4},{4,5},{5,6},{6,7},{8,9},{9,10},{10,11},{11... | collective-permute-start | bytes 294920 | tf_op jit(solution)/shard_map/ppermute | solution.py:314
  8.5 2.0 %collective-permute-start.1 = (bf16[6,64,128]{2,1,0:T(8,128)(2,1)}, bf16[6,64,128]{2,1,0:T(8,128)(2,1)}, u32[]{:S(2)}, u32[]{:S(2)}) collective-permute-start(bf16[6,64,128]{2,1,0:T(8,128)(2,1)} %pad_maximum_fusion.3), channel_id=1, source_target_pairs={{1,0},{2,1},{3,2},{4,3},{5,4},{6,5},{7,6},{9,8},{10,9},{11,10},{12... | collective-permute-start | bytes 294920 | tf_op jit(solution)/shard_map/ppermute | solution.py:319
  10.9 0.8 fusion.2
  11.7 3.2 %collective-permute-start.2 = (bf16[32,32,128]{2,1,0:T(8,128)(2,1)}, bf16[32,32,128]{2,1,0:T(8,128)(2,1)S(1)}, u32[]{:S(2)}, u32[]{:S(2)}) collective-permute-start(bf16[32,32,128]{2,1,0:T(8,128)(2,1)} %get-tuple-element.56), channel_id=1, source_target_pairs={{0,8},{8,16},{16,24},{24,32},{32,40},{40,48},{48,56},{56,64},{64,7... | collective-permute-start | bytes 786440 | tf_op jit(solution)/shard_map/ppermute | solution.py:314
  14.9 1.3 collective-permute-start.3
  17.4 1.1 copy.56
  19.2 0.8 slice.104.y_low
  20.1 0.8 slice.107.y_high
  21.0 4.0 %collective-permute-start.4 = (bf16[8,32,128]{2,1,0:T(8,128)(2,1)S(1)}, bf16[8,32,128]{2,1,0:T(8,128)(2,1)S(1)}, u32[]{:S(2)}, u32[]{:S(2)}) collective-permute-start(bf16[8,32,128]{2,1,0:T(8,128)(2,1)S(1)} %get-tuple-element.72), channel_id=1, source_target_pairs={{0,8},{8,16},{16,24},{24,32},{32,40},{40,48},{48,56},{56,64},{64,7... | collective-permute-start | bytes 196616 | tf_op jit(solution)/shard_map/ppermute | solution.py:314
  25.0 1.3 collective-permute-start.5
  27.0 3.3 %collective-permute-done.5.c_high = bf16[8,32,128]{2,1,0:T(8,128)(2,1)S(1)} collective-permute-done((bf16[8,32,128]{2,1,0:T(8,128)(2,1)S(1)}, bf16[8,32,128]{2,1,0:T(8,128)(2,1)S(1)}, u32[]{:S(2)}, u32[]{:S(2)}) %collective-permute-start.5) | collective-permute-done | bytes 65568 | tf_op jit(solution)/shard_map/ppermute | solution.py:319
  30.3 2.4 %conv_one.1 = (bf16[40,128,128]{2,1,0:T(8,128)(2,1)S(1)}, f32[38,64,128]{2,1,0:T(8,128)S(1)}, bf16[38,32,128]{2,1,0:T(8,128)(2,1)S(1)}, bf16[38,32,128]{2,1,0:T(8,128)(2,1)S(1)}, f32[128,128]{1,0:T(8,128)}) custom-call(bf16[32,64,128]{2,1,0:T(8,128)(2,1)S(1)} %bitcast.80, bf16[4,64,128]{2,1,0:T(8,128)(2,1)S(1)} %slice.104.y_low, ...), custom_call_target="tpu_custom_call" | custom-call | flops 2000000000 | bytes 6000000 | tf_op jit(solution)/shard_map/conv_one/pallas_call | solution.py:298
  32.7 1.0 copy-done
  33.7 1.1 copy-done.11
  34.8 3.3 %collective-permute-start.6 = (bf16[38,32,128]{2,1,0:T(8,128)(2,1)S(1)}, bf16[38,32,128]{2,1,0:T(8,128)(2,1)S(1)}, u32[]{:S(2)}, u32[]{:S(2)}) collective-permute-start(bf16[38,32,128]{2,1,0:T(8,128)(2,1)S(1)} %get-tuple-element.25), channel_id=1, source_target_pairs={{0,8},{8,16},{16,24},{24,32},{32,40},{40,48},{48,56},{56,64},{64,7... | collective-permute-start | bytes 933896 | tf_op jit(solution)/shard_map/ppermute | solution.py:314
  38.2 1.3 collective-permute-start.7
  40.3 0.9 pad_bitcast_fusion.3
  42.8 16.5 %all-to-all-start = ((f32[128,1,128]{2,1,0:T(1,128)}), f32[128,1,128]{2,1,0:T(1,128)S(1)}, u32[]{:S(2)}, u32[]{:S(2)}) async-start(f32[128,1,128]{2,1,0:T(1,128)} %bitcast.17), calls=%async_computation | async-start | bytes 131072 | tf_op jit(solution)/shard_map/all_to_all | solution.py:323
  59.4 9.2 %all-to-all-done = f32[128,1,128]{2,1,0:T(1,128)S(1)} async-done(((f32[128,1,128]{2,1,0:T(1,128)}), f32[128,1,128]{2,1,0:T(1,128)S(1)}, u32[]{:S(2)}, u32[]{:S(2)}) %all-to-all-start) | async-done | bytes 65568 | tf_op jit(solution)/shard_map/all_to_all | solution.py:323
  68.6 1.3 copy-done.1
  69.9 4.0 %conv_two.1 = (bf16[38,128,128]{2,1,0:T(8,128)(2,1)S(1)}, f32[36,64,128]{2,1,0:T(8,128)S(1)}, bf16[36,32,128]{2,1,0:T(8,128)(2,1)S(1)}, bf16[36,32,128]{2,1,0:T(8,128)(2,1)S(1)}, f32[128,128]{1,0:T(8,128)}) custom-call(s32[6]{0:T(128)S(1)} %stack.94.refs_0_, f32[38,64,128]{2,1,0:T(8,128)S(1)} %copy-done.1, ...), custom_call_target="tpu_custom_call" | custom-call | flops 2000000000 | bytes 6000000 | tf_op jit(solution)/shard_map/conv_two/pallas_call | solution.py:298
  73.9 1.0 copy-done.4
  75.0 1.1 copy-done.6
  76.0 4.8 %all-to-all-start.1 = ((f32[128,1,128]{2,1,0:T(1,128)}), f32[128,1,128]{2,1,0:T(1,128)S(1)}, u32[]{:S(2)}, u32[]{:S(2)}) async-start(f32[128,1,128]{2,1,0:T(1,128)} %bitcast.28), calls=%async_computation.1 | async-start | bytes 131072 | tf_op jit(solution)/shard_map/all_to_all | solution.py:323
  80.8 0.9 fusion.1
  81.7 3.3 %collective-permute-start.10 = (bf16[36,32,128]{2,1,0:T(8,128)(2,1)}, bf16[36,32,128]{2,1,0:T(8,128)(2,1)S(1)}, u32[]{:S(2)}, u32[]{:S(2)}) collective-permute-start(bf16[36,32,128]{2,1,0:T(8,128)(2,1)} %get-tuple-element.54), channel_id=1, source_target_pairs={{0,8},{8,16},{16,24},{24,32},{32,40},{40,48},{48,56},{56,64},{64,7... | collective-permute-start | bytes 884744 | tf_op jit(solution)/shard_map/ppermute | solution.py:314
  85.0 1.3 collective-permute-start.11
  86.3 4.7 %collective-permute-start.8 = (bf16[36,32,128]{2,1,0:T(8,128)(2,1)S(1)}, bf16[36,32,128]{2,1,0:T(8,128)(2,1)}, u32[]{:S(2)}, u32[]{:S(2)}) collective-permute-start(bf16[36,32,128]{2,1,0:T(8,128)(2,1)S(1)} %get-tuple-element.31), channel_id=1, source_target_pairs={{0,8},{8,16},{16,24},{24,32},{32,40},{40,48},{48,56},{56,64},{64,7... | collective-permute-start | bytes 884744 | tf_op jit(solution)/shard_map/ppermute | solution.py:314
  91.0 1.3 collective-permute-start.9
  92.3 1.3 copy-done.7
  93.6 2.5 %slope_two.1 = (bf16[32,64,128]{2,1,0:T(8,128)(2,1)S(1)}, f32[128,128]{1,0:T(8,128)}) custom-call(s32[6]{0:T(128)S(1)} %stack.94.refs_0_, f32[36,64,128]{2,1,0:T(8,128)S(1)} %copy-done.7, bf16[36,64,128]{2,1,0:T(8,128)(2,1)S(1)} %pad_maximum_fusion.refs_2_.refs_4_, f32[128,128]{1,0:T(8,128)S(1)} %bitcast.90, f32[32,4]{1,0:T(8,128)S(1)} %copy.55.refs_5_.refs_4_.refs_11_.refs_9_), custom_call_target="tpu_custom_call" | custom-call | flops 2000000000 | bytes 6000000 | tf_op jit(solution)/shard_map/slope_two/pallas_call | solution.py:298
  96.1 12.5 %all-to-all-start.2 = ((f32[128,1,128]{2,1,0:T(1,128)}), f32[128,1,128]{2,1,0:T(1,128)S(1)}, u32[]{:S(2)}, u32[]{:S(2)}) async-start(f32[128,1,128]{2,1,0:T(1,128)} %bitcast.33), calls=%async_computation.2 | async-start | bytes 131072 | tf_op jit(solution)/shard_map/all_to_all | solution.py:323
  108.7 1.9 maximum_bitcast_fusion.2
  110.6 2.0 %copy.61 = bf16[3,2,32,3,4,32]{5,4,3,2,1,0:T(4,128)(2,1)} copy(bf16[3,2,32,3,4,32]{2,5,0,3,4,1:T(8,128)(2,1)} %maximum_bitcast_fusion.2) | data formatting | bytes 294912 | tf_op jit(solution)/shard_map/transpose | solution.py:339
  112.6 1.5 reshape.79.refs_13_
  114.2 3.8 %all-to-all-done.2 = f32[128,1,128]{2,1,0:T(1,128)S(1)} async-done(((f32[128,1,128]{2,1,0:T(1,128)}), f32[128,1,128]{2,1,0:T(1,128)S(1)}, u32[]{:S(2)}, u32[]{:S(2)}) %all-to-all-start.2) | async-done | bytes 65568 | tf_op jit(solution)/shard_map/all_to_all | solution.py:323
  118.0 1.3 copy-done.2
  119.2 1.3 copy-done.5
  120.5 1.3 copy-done.8
  121.8 5.5 %back_two.1 = (f32[34,64,128]{2,1,0:T(8,128)S(1)}, bf16[34,32,128]{2,1,0:T(8,128)(2,1)S(1)}, bf16[34,32,128]{2,1,0:T(8,128)(2,1)S(1)}, f32[128,128]{1,0:T(8,128)}, f32[9,32,128]{2,1,0:T(8,128)S(1)}) custom-call(s32[6]{0:T(128)S(1)} %stack.94.refs_0_, f32[36,64,128]{2,1,0:T(8,128)S(1)} %copy-done.8, bf16[36,32,128]{2,1,0:T(8,128)(2,1)} %collective-permute-done.8.refs_2_, ...), custom_call_target="tpu_custom_call" | custom-call | flops 2000000000 | bytes 6000000 | tf_op jit(solution)/shard_map/back_two/pallas_call | solution.py:298
  127.3 1.0 copy-done.9
  128.3 2.3 %collective-permute-start.12 = (bf16[34,32,128]{2,1,0:T(8,128)(2,1)S(1)}, bf16[34,32,128]{2,1,0:T(8,128)(2,1)S(1)}, u32[]{:S(2)}, u32[]{:S(2)}) collective-permute-start(bf16[34,32,128]{2,1,0:T(8,128)(2,1)S(1)} %get-tuple-element.36), channel_id=1, source_target_pairs={{0,8},{8,16},{16,24},{24,32},{32,40},{40,48},{48,56},{56,64},{64,7... | collective-permute-start | bytes 835592 | tf_op jit(solution)/shard_map/ppermute | solution.py:314
  130.5 1.3 collective-permute-start.13
  131.9 0.8 pad_bitcast_fusion.1
  132.7 8.4 %all-to-all-start.3 = ((f32[128,1,128]{2,1,0:T(1,128)}), f32[128,1,128]{2,1,0:T(1,128)S(1)}, u32[]{:S(2)}, u32[]{:S(2)}) async-start(f32[128,1,128]{2,1,0:T(1,128)} %bitcast.40), calls=%async_computation.3 | async-start | bytes 131072 | tf_op jit(solution)/shard_map/all_to_all | solution.py:323
  141.1 1.9 maximum_bitcast_fusion.3
  143.0 2.0 %copy.64 = bf16[3,2,32,3,4,32]{5,4,3,2,1,0:T(4,128)(2,1)} copy(bf16[3,2,32,3,4,32]{2,5,0,3,4,1:T(8,128)(2,1)} %maximum_bitcast_fusion.3) | data formatting | bytes 294912 | tf_op jit(solution)/shard_map/transpose | solution.py:339
  145.0 1.5 reshape.80.refs_11_
  146.6 3.8 %all-to-all-done.3 = f32[128,1,128]{2,1,0:T(1,128)S(1)} async-done(((f32[128,1,128]{2,1,0:T(1,128)}), f32[128,1,128]{2,1,0:T(1,128)S(1)}, u32[]{:S(2)}, u32[]{:S(2)}) %all-to-all-start.3) | async-done | bytes 65568 | tf_op jit(solution)/shard_map/all_to_all | solution.py:323
  150.4 1.3 copy-done.3
  151.6 1.2 copy-done.10
  152.9 1.3 copy-done.12
  154.2 3.5 %back_one.1 = (bf16[32,64,128]{2,1,0:T(8,128)(2,1)S(1)}, f32[9,32,128]{2,1,0:T(8,128)S(1)}) custom-call(s32[6]{0:T(128)S(1)} %stack.94.refs_0_, f32[34,64,128]{2,1,0:T(8,128)S(1)} %copy-done.10, bf16[34,32,128]{2,1,0:T(8,128)(2,1)S(1)} %collective-permute-done.12.refs_2_, bf16[34,32,128]{2,1,0:T(8,128)(2,1)S(1)} %collective-permute-done.13.refs_3_, ...), custom_call_target="tpu_custom_call" | custom-call | flops 2000000000 | bytes 6000000 | tf_op jit(solution)/shard_map/back_one/pallas_call | solution.py:298
  157.7 0.8 reshape.83
  158.6 6.0 %all-to-all-start.4 = ((f32[128,5,128]{2,1,0:T(8,128)}), f32[128,5,128]{2,1,0:T(8,128)S(1)}, u32[]{:S(2)}, u32[]{:S(2)}) async-start(f32[128,5,128]{2,1,0:T(8,128)} %reshape.83), calls=%async_computation.4 | async-start | bytes 1048576 | tf_op jit(solution)/shard_map/all_to_all | solution.py:323
  164.8 13.4 %all-to-all-done.4 = f32[128,5,128]{2,1,0:T(8,128)S(1)} async-done(((f32[128,5,128]{2,1,0:T(8,128)}), f32[128,5,128]{2,1,0:T(8,128)S(1)}, u32[]{:S(2)}, u32[]{:S(2)}) %all-to-all-start.4) | async-done | bytes 327712 | tf_op jit(solution)/shard_map/all_to_all | solution.py:323
  178.4 0.8 broadcast_in_dim.2
  179.2 4.6 %all-to-all-start.5 = ((f32[128,5,128]{2,1,0:T(8,128)}), f32[128,5,128]{2,1,0:T(8,128)S(1)}, u32[]{:S(2)}, u32[]{:S(2)}) async-start(f32[128,5,128]{2,1,0:T(8,128)} %broadcast_in_dim.2), calls=%async_computation.5 | async-start | bytes 1048576 | tf_op jit(solution)/shard_map/all_to_all | solution.py:323
  184.4 1.6 copy_bitcast_fusion
  186.1 11.5 %all-to-all-done.5 = f32[128,5,128]{2,1,0:T(8,128)S(1)} async-done(((f32[128,5,128]{2,1,0:T(8,128)}), f32[128,5,128]{2,1,0:T(8,128)S(1)}, u32[]{:S(2)}, u32[]{:S(2)}) %all-to-all-start.5) | async-done | bytes 327712 | tf_op jit(solution)/shard_map/all_to_all | solution.py:323
  198.0 0.8 copy.67
  199.0 0.8 copy.68
  (88 shorter events, 7.7 us)
Async XLA Ops:
  0.6 9.9 %copy-start.19 = (bf16[32,2,32,128]{3,2,1,0:T(8,128)(2,1)S(1)}, bf16[32,2,32,128]{3,2,1,0:T(8,128)(2,1)}, u32[]{:S(2)}) copy-start(bf16[32,2,32,128]{3,2,1,0:T(8,128)(2,1)} %param.8) | copy-start | bytes 1572868
  2.8 16.4 %collective-permute-start = (bf16[6,64,128]{2,1,0:T(8,128)(2,1)S(1)}, bf16[6,64,128]{2,1,0:T(8,128)(2,1)}, u32[]{:S(2)}, u32[]{:S(2)}) collective-permute-start(bf16[6,64,128]{2,1,0:T(8,128)(2,1)S(1)} %pad_maximum_fusion.2), channel_id=1, source_target_pairs={{0,1},{1,2},{2,3},{3,4},{4,5},{5,6},{6,7},{8,9},{9,10},{10,11},{11... | collective-permute-start | bytes 294920 | tf_op jit(solution)/shard_map/ppermute | solution.py:314
  7.8 8.5 %copy-start.16 = (bf16[32,32,3,3,3]{1,0,4,3,2:T(8,128)(2,1)S(1)}, bf16[32,32,3,3,3]{1,0,4,3,2:T(8,128)(2,1)}, u32[]{:S(2)}) copy-start(bf16[32,32,3,3,3]{1,0,4,3,2:T(8,128)(2,1)} %param.9) | copy-start | bytes 165892
  8.5 7.9 %copy-start.15 = (bf16[32,32,3,3,3]{1,0,4,3,2:T(8,128)(2,1)S(1)}, bf16[32,32,3,3,3]{1,0,4,3,2:T(8,128)(2,1)}, u32[]{:S(2)}) copy-start(bf16[32,32,3,3,3]{1,0,4,3,2:T(8,128)(2,1)} %param.12) | copy-start | bytes 165892
  8.5 11.6 %collective-permute-start.1 = (bf16[6,64,128]{2,1,0:T(8,128)(2,1)}, bf16[6,64,128]{2,1,0:T(8,128)(2,1)}, u32[]{:S(2)}, u32[]{:S(2)}) collective-permute-start(bf16[6,64,128]{2,1,0:T(8,128)(2,1)} %pad_maximum_fusion.3), channel_id=1, source_target_pairs={{1,0},{2,1},{3,2},{4,3},{5,4},{6,5},{7,6},{9,8},{10,9},{11,10},{12... | collective-permute-start | bytes 294920 | tf_op jit(solution)/shard_map/ppermute | solution.py:319
  11.7 18.6 %collective-permute-start.2 = (bf16[32,32,128]{2,1,0:T(8,128)(2,1)}, bf16[32,32,128]{2,1,0:T(8,128)(2,1)S(1)}, u32[]{:S(2)}, u32[]{:S(2)}) collective-permute-start(bf16[32,32,128]{2,1,0:T(8,128)(2,1)} %get-tuple-element.56), channel_id=1, source_target_pairs={{0,8},{8,16},{16,24},{24,32},{32,40},{40,48},{48,56},{56,64},{64,7... | collective-permute-start | bytes 786440 | tf_op jit(solution)/shard_map/ppermute | solution.py:314
  14.9 15.4 %collective-permute-start.3 = (bf16[32,32,128]{2,1,0:T(8,128)(2,1)}, bf16[32,32,128]{2,1,0:T(8,128)(2,1)S(1)}, u32[]{:S(2)}, u32[]{:S(2)}) collective-permute-start(bf16[32,32,128]{2,1,0:T(8,128)(2,1)} %get-tuple-element.55), channel_id=1, source_target_pairs={{8,0},{16,8},{24,16},{32,24},{40,32},{48,40},{56,48},{64,56},{72,6... | collective-permute-start | bytes 786440 | tf_op jit(solution)/shard_map/ppermute | solution.py:319
  16.4 1.0 copy-start.20
  21.0 6.0 %collective-permute-start.4 = (bf16[8,32,128]{2,1,0:T(8,128)(2,1)S(1)}, bf16[8,32,128]{2,1,0:T(8,128)(2,1)S(1)}, u32[]{:S(2)}, u32[]{:S(2)}) collective-permute-start(bf16[8,32,128]{2,1,0:T(8,128)(2,1)S(1)} %get-tuple-element.72), channel_id=1, source_target_pairs={{0,8},{8,16},{16,24},{24,32},{32,40},{40,48},{48,56},{56,64},{64,7... | collective-permute-start | bytes 196616 | tf_op jit(solution)/shard_map/ppermute | solution.py:314
  25.0 5.3 %collective-permute-start.5 = (bf16[8,32,128]{2,1,0:T(8,128)(2,1)S(1)}, bf16[8,32,128]{2,1,0:T(8,128)(2,1)S(1)}, u32[]{:S(2)}, u32[]{:S(2)}) collective-permute-start(bf16[8,32,128]{2,1,0:T(8,128)(2,1)S(1)} %get-tuple-element.71), channel_id=1, source_target_pairs={{8,0},{16,8},{24,16},{32,24},{40,32},{48,40},{56,48},{64,56},{72,6... | collective-permute-start | bytes 196616 | tf_op jit(solution)/shard_map/ppermute | solution.py:319
  27.0 12.5 %copy-start.21 = (f32[32]{0:T(128)S(1)}, f32[32]{0:T(128)}, u32[]{:S(2)}) copy-start(f32[32]{0:T(128)} %param.14) | copy-start | bytes 388
  27.0 12.5 %copy-start.22 = (f32[32]{0:T(128)S(1)}, f32[32]{0:T(128)}, u32[]{:S(2)}) copy-start(f32[32]{0:T(128)} %param.13) | copy-start | bytes 388
  27.0 12.5 %copy-start.23 = (f32[32]{0:T(128)S(1)}, f32[32]{0:T(128)}, u32[]{:S(2)}) copy-start(f32[32]{0:T(128)} %param.11) | copy-start | bytes 388
  27.0 12.5 %copy-start.24 = (f32[32]{0:T(128)S(1)}, f32[32]{0:T(128)}, u32[]{:S(2)}) copy-start(f32[32]{0:T(128)} %param.10) | copy-start | bytes 388
  32.7 1.0 copy-start
  33.7 1.1 copy-start.11
  34.8 5.5 %copy-start.18 = (bf16[32,32,3,3,3]{0,1,4,3,2:T(8,128)(2,1)S(1)}, bf16[32,32,3,3,3]{0,1,4,3,2:T(8,128)(2,1)}, u32[]{:S(2)}) copy-start(bf16[32,32,3,3,3]{0,1,4,3,2:T(8,128)(2,1)} %reverse_bitcast_fusion.1) | copy-start | bytes 165892
  34.8 33.8 %collective-permute-start.6 = (bf16[38,32,128]{2,1,0:T(8,128)(2,1)S(1)}, bf16[38,32,128]{2,1,0:T(8,128)(2,1)S(1)}, u32[]{:S(2)}, u32[]{:S(2)}) collective-permute-start(bf16[38,32,128]{2,1,0:T(8,128)(2,1)S(1)} %get-tuple-element.25), channel_id=1, source_target_pairs={{0,8},{8,16},{16,24},{24,32},{32,40},{40,48},{48,56},{56,64},{64,7... | collective-permute-start | bytes 933896 | tf_op jit(solution)/shard_map/ppermute | solution.py:314
  38.2 30.5 %collective-permute-start.7 = (bf16[38,32,128]{2,1,0:T(8,128)(2,1)S(1)}, bf16[38,32,128]{2,1,0:T(8,128)(2,1)S(1)}, u32[]{:S(2)}, u32[]{:S(2)}) collective-permute-start(bf16[38,32,128]{2,1,0:T(8,128)(2,1)S(1)} %get-tuple-element.26), channel_id=1, source_target_pairs={{8,0},{16,8},{24,16},{32,24},{40,32},{48,40},{56,48},{64,56},{72,6... | collective-permute-start | bytes 933896 | tf_op jit(solution)/shard_map/ppermute | solution.py:319
  39.6 19.7 %copy-start.13 = (bf16[32,2,32,128]{3,2,1,0:T(8,128)(2,1)S(1)}, bf16[32,2,32,128]{3,2,1,0:T(8,128)(2,1)}, u32[]{:S(2)}) copy-start(bf16[32,2,32,128]{3,2,1,0:T(8,128)(2,1)} %copy.56) | copy-start | bytes 1572868
  42.8 25.8 %all-to-all-start = ((f32[128,1,128]{2,1,0:T(1,128)}), f32[128,1,128]{2,1,0:T(1,128)S(1)}, u32[]{:S(2)}, u32[]{:S(2)}) async-start(f32[128,1,128]{2,1,0:T(1,128)} %bitcast.17), calls=%async_computation | async-start | bytes 131072 | tf_op jit(solution)/shard_map/all_to_all | solution.py:323
  68.6 1.3 copy-start.1
  73.9 1.0 copy-start.4
  75.0 1.1 copy-start.6
  76.0 16.2 %all-to-all-start.1 = ((f32[128,1,128]{2,1,0:T(1,128)}), f32[128,1,128]{2,1,0:T(1,128)S(1)}, u32[]{:S(2)}, u32[]{:S(2)}) async-start(f32[128,1,128]{2,1,0:T(1,128)} %bitcast.28), calls=%async_computation.1 | async-start | bytes 131072 | tf_op jit(solution)/shard_map/all_to_all | solution.py:323
  81.7 32.5 %collective-permute-start.10 = (bf16[36,32,128]{2,1,0:T(8,128)(2,1)}, bf16[36,32,128]{2,1,0:T(8,128)(2,1)S(1)}, u32[]{:S(2)}, u32[]{:S(2)}) collective-permute-start(bf16[36,32,128]{2,1,0:T(8,128)(2,1)} %get-tuple-element.54), channel_id=1, source_target_pairs={{0,8},{8,16},{16,24},{24,32},{32,40},{40,48},{48,56},{56,64},{64,7... | collective-permute-start | bytes 884744 | tf_op jit(solution)/shard_map/ppermute | solution.py:314
  85.0 29.2 %collective-permute-start.11 = (bf16[36,32,128]{2,1,0:T(8,128)(2,1)}, bf16[36,32,128]{2,1,0:T(8,128)(2,1)S(1)}, u32[]{:S(2)}, u32[]{:S(2)}) collective-permute-start(bf16[36,32,128]{2,1,0:T(8,128)(2,1)} %get-tuple-element.53), channel_id=1, source_target_pairs={{8,0},{16,8},{24,16},{32,24},{40,32},{48,40},{56,48},{64,56},{72,6... | collective-permute-start | bytes 884744 | tf_op jit(solution)/shard_map/ppermute | solution.py:319
  86.3 31.7 %collective-permute-start.8 = (bf16[36,32,128]{2,1,0:T(8,128)(2,1)S(1)}, bf16[36,32,128]{2,1,0:T(8,128)(2,1)}, u32[]{:S(2)}, u32[]{:S(2)}) collective-permute-start(bf16[36,32,128]{2,1,0:T(8,128)(2,1)S(1)} %get-tuple-element.31), channel_id=1, source_target_pairs={{0,8},{8,16},{16,24},{24,32},{32,40},{40,48},{48,56},{56,64},{64,7... | collective-permute-start | bytes 884744 | tf_op jit(solution)/shard_map/ppermute | solution.py:314
  91.0 27.0 %collective-permute-start.9 = (bf16[36,32,128]{2,1,0:T(8,128)(2,1)S(1)}, bf16[36,32,128]{2,1,0:T(8,128)(2,1)}, u32[]{:S(2)}, u32[]{:S(2)}) collective-permute-start(bf16[36,32,128]{2,1,0:T(8,128)(2,1)S(1)} %get-tuple-element.32), channel_id=1, source_target_pairs={{8,0},{16,8},{24,16},{32,24},{40,32},{48,40},{56,48},{64,56},{72,6... | collective-permute-start | bytes 884744 | tf_op jit(solution)/shard_map/ppermute | solution.py:319
  92.3 1.3 copy-start.7
  93.6 15.1 %copy-start.14 = (bf16[1,32,32,4,3,3]{1,2,5,4,3,0:T(8,128)(2,1)S(1)}, bf16[1,32,32,4,3,3]{1,2,5,4,3,0:T(8,128)(2,1)}, u32[]{:S(2)}) copy-start(bf16[1,32,32,4,3,3]{1,2,5,4,3,0:T(8,128)(2,1)} %get-tuple-element.65) | copy-start | bytes 221188
  96.1 21.8 %all-to-all-start.2 = ((f32[128,1,128]{2,1,0:T(1,128)}), f32[128,1,128]{2,1,0:T(1,128)S(1)}, u32[]{:S(2)}, u32[]{:S(2)}) async-start(f32[128,1,128]{2,1,0:T(1,128)} %bitcast.33), calls=%async_computation.2 | async-start | bytes 131072 | tf_op jit(solution)/shard_map/all_to_all | solution.py:323
  117.9 1.3 copy-start.2
  119.2 1.3 copy-start.5
  120.5 1.3 copy-start.8
  121.8 10.0 %copy-start.17 = (bf16[32,32,3,3,3]{1,0,4,3,2:T(8,128)(2,1)S(1)}, bf16[32,32,3,3,3]{1,0,4,3,2:T(8,128)(2,1)}, u32[]{:S(2)}) copy-start(bf16[32,32,3,3,3]{1,0,4,3,2:T(8,128)(2,1)} %param.9) | copy-start | bytes 165892
  127.3 1.0 copy-start.9
  128.3 22.1 %collective-permute-start.12 = (bf16[34,32,128]{2,1,0:T(8,128)(2,1)S(1)}, bf16[34,32,128]{2,1,0:T(8,128)(2,1)S(1)}, u32[]{:S(2)}, u32[]{:S(2)}) collective-permute-start(bf16[34,32,128]{2,1,0:T(8,128)(2,1)S(1)} %get-tuple-element.36), channel_id=1, source_target_pairs={{0,8},{8,16},{16,24},{24,32},{32,40},{40,48},{48,56},{56,64},{64,7... | collective-permute-start | bytes 835592 | tf_op jit(solution)/shard_map/ppermute | solution.py:314
  130.5 19.8 %collective-permute-start.13 = (bf16[34,32,128]{2,1,0:T(8,128)(2,1)S(1)}, bf16[34,32,128]{2,1,0:T(8,128)(2,1)S(1)}, u32[]{:S(2)}, u32[]{:S(2)}) collective-permute-start(bf16[34,32,128]{2,1,0:T(8,128)(2,1)S(1)} %get-tuple-element.37), channel_id=1, source_target_pairs={{8,0},{16,8},{24,16},{32,24},{40,32},{48,40},{56,48},{64,56},{72,6... | collective-permute-start | bytes 835592 | tf_op jit(solution)/shard_map/ppermute | solution.py:319
  132.7 17.7 %all-to-all-start.3 = ((f32[128,1,128]{2,1,0:T(1,128)}), f32[128,1,128]{2,1,0:T(1,128)S(1)}, u32[]{:S(2)}, u32[]{:S(2)}) async-start(f32[128,1,128]{2,1,0:T(1,128)} %bitcast.40), calls=%async_computation.3 | async-start | bytes 131072 | tf_op jit(solution)/shard_map/all_to_all | solution.py:323
  150.3 1.3 copy-start.3
  151.6 1.2 copy-start.10
  152.9 1.3 copy-start.12
  158.6 19.7 %all-to-all-start.4 = ((f32[128,5,128]{2,1,0:T(8,128)}), f32[128,5,128]{2,1,0:T(8,128)S(1)}, u32[]{:S(2)}, u32[]{:S(2)}) async-start(f32[128,5,128]{2,1,0:T(8,128)} %reshape.83), calls=%async_computation.4 | async-start | bytes 1048576 | tf_op jit(solution)/shard_map/all_to_all | solution.py:323
  179.2 18.4 %all-to-all-start.5 = ((f32[128,5,128]{2,1,0:T(8,128)}), f32[128,5,128]{2,1,0:T(8,128)S(1)}, u32[]{:S(2)}, u32[]{:S(2)}) async-start(f32[128,5,128]{2,1,0:T(8,128)} %broadcast_in_dim.2), calls=%async_computation.5 | async-start | bytes 1048576 | tf_op jit(solution)/shard_map/all_to_all | solution.py:323
where the time goes:
time: 201 us; the launch traced here: 200 us
  starting transfers between devices  88.3 us (44%)
  waiting for transfers between devices  45 us (22%)
  local copies, waits for them, and re-layouts  41.6 us (21%)
  Pallas kernels  17.9 us (9%)
  other arithmetic  5.73 us (3%)
    all_to_all x6, starting transfers between devices, share(): return lax.all_to_all(msg, ALL, 0, 0, tiled=True)  52.8 us
    all_to_all x6, waiting for transfers between devices, share(): return lax.all_to_all(msg, ALL, 0, 0, tiled=True)  41.7 us
    ppermute x7, starting transfers between devices, up(): return lax.ppermute(values, axes, [(i, i + 1) for i in range(count - 1)])  25.7 us
    unnamed x52, local copies, waits for them, and re-layouts  17.9 us
    pallas_call x5, Pallas kernels, call(): pl.pallas_call(kernel, out_shape=outs, in_specs=specs, out_specs=[VM] * l...  17.9 us
    ppermute x7, starting transfers between devices, down(): return lax.ppermute(values, axes, [(i + 1, i) for i in range(count - 1)])  9.78 us
    transpose x4, local copies, waits for them, and re-layouts, kernel_matrix(): return jnp.transpose(both, (5, 0, 1, 4, 3, 2)).reshape(192, 384)  4.7 us
    transpose x4, other arithmetic, kernel_matrix(): return jnp.transpose(both, (5, 0, 1, 4, 3, 2)).reshape(192, 384)  4.13 us
  transfers between devices with their start and end apart: 20, of which 6 were waited for; matrix products, arithmetic and copies ran while one was open for 12% of the time, Pallas kernels for 1%

commit v1 on v0

--- a/solution.py
+++ b/solution.py
@@ -72,6 +72,22 @@
     msg_ref[...] = jnp.transpose(jnp.broadcast_to(column, (128, count)))
 
 
+def as_row(column):
+    return jnp.transpose(jnp.broadcast_to(column, (128, 128)))[0:1]
+
+
+def rows_message(columns, groups, msg_ref):
+    spare = jnp.zeros((128 - C * len(columns), 1), F32)
+    row = as_row(jnp.concatenate([*columns, spare], axis=0))
+    at = lax.broadcasted_iota(jnp.int32, (8, 128), 0)
+    tile = jnp.where(at == 0, jnp.broadcast_to(row, (8, 128)), 0.0)
+    msg_ref[...] = jnp.broadcast_to(tile[None], msg_ref.shape)
+    for k, group in enumerate(groups):
+        for dz in range(3):
+            for dy in range(3):
+                msg_ref[dz * C : (dz + 1) * C, 1 + 3 * k + dy, :] = group(dz, dy)
+
+
 def stats_out(h_ref, acc, start, low_ref, high_ref, msg_ref):
     center = fold(total(acc)) / (2 * ROWS * 128)
     both = twice(center)
@@ -99,8 +115,8 @@
 
 
 def read_sums(r_ref):
-    parts = jnp.transpose(r_ref[...])
-    return total(parts[0:C]), total(parts[C : 2 * C])
+    parts = jnp.transpose(jnp.broadcast_to(jnp.sum(r_ref[...], axis=0)[0:1], (128, 128)))[:, 0:1]
+    return parts[0:C], parts[C : 2 * C]
 
 
 def act(z):
@@ -131,7 +147,7 @@
     return jnp.concatenate([low * f_low, own, high * f_high], axis=0).astype(BF16)
 
 
-def weight_sums(g_ref, v_ref, first, acc_ref, out_ref):
+def weight_sums(g_ref, v_ref, first, acc_ref):
     step = 4
     for y in range(0, ROWS, step):
         right = jnp.concatenate(
@@ -145,10 +161,14 @@
             acc_ref[...] = product
         else:
             acc_ref[...] += product
-    for dz in range(3):
-        for dy in range(3):
-            tile = acc_ref[dz * 64 : dz * 64 + 64, dy * 128 : dy * 128 + 128]
-            out_ref[dz * 3 + dy] = tile[0:C] + pltpu.roll(tile[C:], 96, 1)
+
+
+def folded(acc_ref):
+    def tile(dz, dy):
+        both = acc_ref[dz * 64 : dz * 64 + 64, dy * 128 : dy * 128 + 128]
+        return both[0:C] + pltpu.roll(both[C:], 96, 1)
+
+    return tile
 
 
 def put_shifted(g_ref, y, values, lane):
@@ -158,15 +178,57 @@
     g_ref[128:192, at] = from_below(values, lane).astype(BF16)
 
 
-def first_kernel(own, y_low, y_high, x_low, x_high, c_low, c_high, w, v, h, low, high, msg):
-    for part, (rows, at) in (
-        ((y_low, c_low, c_high, 0), (4, 0)),
-        ((own, x_low, x_high, 0), (ROWS, 4)),
-        ((y_high, c_low, c_high, 4), (4, ROWS + 4)),
-    ):
-        middle, left, right, offset = part
+def pack_kernel(own, cot, up_ref, down_ref):
+    up_ref[0:4] = own[ROWS - 4 : ROWS]
+    up_ref[4:6] = cot[ROWS - 2 : ROWS]
+    down_ref[0:4] = own[0:4]
+    down_ref[4:6] = cot[0:2]
+
+
+def planes_kernel(own, y_low, y_high, up_ref, down_ref):
+    for part, rows, at in ((y_low, 4, 0), (own, ROWS, 4), (y_high, 4, ROWS + 4)):
+        down_ref[at : at + rows] = part[0:rows, 0:C]
+        up_ref[at : at + rows] = part[0:rows, C : 2 * C]
+
+
+def weights_kernel(k1, k2, w1, w2, b1, b2):
+    row = lax.broadcasted_iota(jnp.int32, (C, 128), 0)
+    col = lax.broadcasted_iota(jnp.int32, (C, 128), 1)
+    eye = jnp.where(row == col, 1.0, 0.0)[:, 0:C].astype(BF16)
+    zero = jnp.zeros((C, C), BF16)
+    for k_ref, w_ref, b_ref in ((k1, w1, b1), (k2, w2, b2)):
+        lined = jnp.zeros((9 * C, 128), F32)
+        for dx in range(3):
+            spot = jnp.where(row + dx * C == col, 1.0, 0.0).astype(BF16)
+            lined = lined + jnp.dot(
+                k_ref[dx * 9 : dx * 9 + 9].reshape(9 * C, C), spot, preferred_element_type=F32
+            )
+        stack = []
+        for t in range(9):
+            stack += [k_ref[18 + t], k_ref[9 + t], k_ref[t], zero]
+        turned = lax.dot_general(
+            eye,
+            jnp.concatenate(stack, axis=0),
+            (((1,), (1,)), ((), ())),
+            preferred_element_type=F32,
+        )
+        for dy in range(3):
+            for dz in range(3):
+                here = slice(dy * 128, dy * 128 + 128)
+                t = dy * 3 + dz
+                tile = lined[t * C : t * C + C]
+                w_ref[dz * 64 : dz * 64 + C, here] = tile.astype(BF16)
+                w_ref[dz * 64 + C : dz * 64 + 64, here] = pltpu.roll(tile, C, 1).astype(BF16)
+                t = 8 - t
+                tile = turned[:, t * 128 : t * 128 + 128]
+                b_ref[dz * 64 : dz * 64 + C, here] = tile.astype(BF16)
+                b_ref[dz * 64 + C : dz * 64 + 64, here] = pltpu.roll(tile, C, 1).astype(BF16)
+
+
+def first_kernel(own, y_low, y_high, x_low, x_high, w, v, h, low, high, msg):
+    for middle, rows, at in ((y_low, 4, 0), (own, ROWS, 4), (y_high, 4, ROWS + 4)):
         for y in range(rows):
-            v[at + y] = jnp.concatenate([left[offset + y], middle[y], right[offset + y]], axis=0)
+            v[at + y] = jnp.concatenate([x_low[at + y], middle[y], x_high[at + y]], axis=0)
     acc = [jnp.zeros((64, 128), F32)]
 
     def emit(y, values):
@@ -201,7 +263,47 @@
     stats_out(h, acc[0], 2, low, high, msg)
 
 
-def third_kernel(cells, place, h2, cot, r2, gb, out, msg):
+def side_kernel(cells, place, h1, r1, v1, xn, x1, g, acc):
+    mean, inverse, _, _ = read_stats(r1, place, cells)
+    mean2, inverse2 = twice(mean), twice(inverse)
+    lane = lanes(64)
+    for y in range(ROWS):
+        put_shifted(g, y, (h1[y + 3] - mean2) * inverse2, lane)
+    weight_sums(g, v1, 3, acc)
+    tile = folded(acc)
+    for dz in range(3):
+        for dy in range(3):
+            xn[dz * 3 + dy] = tile(dz, dy)
+    lane = lanes(128)
+    inner = v1[5].astype(F32)
+    for y in range(6, 3 + ROWS):
+        inner = inner + v1[y].astype(F32)
+    ends = [v1[y].astype(F32) for y in (3, 4, 3 + ROWS, 4 + ROWS)]
+    windows = (inner + ends[0] + ends[1], inner + ends[1] + ends[2], inner + ends[2] + ends[3])
+    columns = []
+    for dz in range(3):
+        for dy in range(3):
+            values = windows[dy]
+            if dz == 0:
+                values = jnp.where(lane == 127, 0.0, values)
+            if dz == 2:
+                values = jnp.where(lane == 0, 0.0, values)
+            column = total(values)
+            column = column + jnp.concatenate([column[C:], column[:C]], axis=0)
+            columns.append(column)
+    wide = jnp.concatenate(columns + [jnp.zeros((128, 119), F32)], axis=1)
+    x1[...] = jnp.transpose(wide)[0:16]
+
+
+def cot_row(cot, y_low, y_high, y):
+    if y < 2:
+        return y_low[4 + y]
+    if y < 2 + ROWS:
+        return cot[y - 2]
+    return y_high[2 + y - ROWS]
+
+
+def third_kernel(cells, place, h2, cot, y_low, y_high, r2, gb, xn, x1, out, t_low, t_high, msg):
     mean, inverse, _, _ = read_stats(r2, place, cells)
     mean2, inverse2 = twice(mean), twice(inverse)
     gain2, bias2 = twice(gb[:, 2:3]), twice(gb[:, 3:4])
@@ -211,15 +313,25 @@
         normed = (h2[y + 2] - mean2) * inverse2
         z = normed * gain2 + bias2
         out[y] = act(z).astype(BF16)
-        slope = cot[y + 2].astype(F32) * act_slope(z)
+        slope = cot[y].astype(F32) * act_slope(z)
         plain = plain + slope
         both = both + slope * normed
-    message((fold(total(both)), fold(total(plain))), msg)
+    for y in range(ROWS + 4):
+        values = cot_row(cot, y_low, y_high, y)
+        t_low[y] = values[0:C]
+        t_high[y] = values[C:]
+
+    def ones(dz, dy):
+        return jnp.broadcast_to(x1[dz * 3 + dy : dz * 3 + dy + 1, :], (C, 128))
+
+    rows_message(
+        (fold(total(both)), fold(total(plain))), (lambda dz, dy: xn[dz * 3 + dy], ones), msg
+    )
 
 
 def fourth_kernel(
-    cells, place, h2, x_low, x_high, cot, t_low, t_high, r2, r3, h1, r1, gb, v2, w,
-    slope1, low, high, msg, wg, v, g, acc,
+    cells, place, h2, x_low, x_high, cot, y_low, y_high, t_low, t_high, r2, r3, h1, r1, gb,
+    v1, v2, w, slope1, low, high, msg, v, g, acc, acc1,
 ):
     mean, inverse, o_low, o_high = read_stats(r2, place, cells)
     nsum, plain = read_sums(r3)
@@ -238,11 +350,12 @@
     rows = ROWS + 4
     for y in range(rows):
         g_low = grad((x_low[y].astype(F32) + o_low) * inverse, t_low[y], *one)
-        g_own = grad((h2[y] - mean2) * inverse2, cot[y], *two)
+        g_own = grad((h2[y] - mean2) * inverse2, cot_row(cot, y_low, y_high, y), *two)
         g_high = grad((x_high[y].astype(F32) + o_high) * inverse, t_high[y], *one)
         v[y] = masked(g_low, g_own, g_high, kept(place, y, rows, 2))
         if 2 <= y < 2 + ROWS:
             put_shifted(g, y - 2, g_own, lane)
+    weight_sums(g, v2, 2, acc)
 
     mean, inverse, _, _ = read_stats(r1, place, cells)
     mean2, inverse2 = twice(mean), twice(inverse)
@@ -258,14 +371,47 @@
         if 1 <= y < 1 + ROWS:
             sums[0] = sums[0] + slope * normed
             sums[1] = sums[1] + slope
+            put_shifted(g, y - 1, slope, lane)
 
     conv_rows(v, w, ROWS + 2, emit)
-    message((fold(total(sums[0])), fold(total(sums[1]))), msg)
-    weight_sums(g, v2, 2, acc, wg)
+    weight_sums(g, v1, 3, acc1)
+    rows_message(
+        (fold(total(sums[0])), fold(total(sums[1]))), (folded(acc1), folded(acc)), msg
+    )
+
+
+def owner_kernel(cells, place, r1, r3, r4, gb, msg, norms):
+    _, inverse, _, _ = read_stats(r1, place, cells)
+    nsum, plain = read_sums(r4)
+    mine = lax.broadcasted_iota(jnp.int32, (C, 1), 0) == place[6]
+
+    def picked(column):
+        return jnp.sum(jnp.where(mine, column, 0.0), axis=0, keepdims=True)
+
+    scale = cells**-0.5
+    lead = picked(gb[:, 0:1] * inverse) * scale
+    third, fourth = jnp.sum(r3[...], axis=0), jnp.sum(r4[...], axis=0)
+    xn, x1 = third[1:4], third[4:7]
+    one = lead * (fourth[1:4] - picked(plain) * (x1 / cells) - picked(nsum) * (xn / cells))
+    two = fourth[4:7] * scale
+    tile = jnp.concatenate([one, two, jnp.zeros((2, 128), F32)], axis=0)
+    msg[...] = jnp.broadcast_to(tile[None], msg.shape)
+    for k, row in enumerate((fourth[0:1], third[0:1])):
+        norms[2 * k : 2 * k + 1] = row[:, 0:C] * scale
+        norms[2 * k + 1 : 2 * k + 2] = row[:, C : 2 * C] * scale
+
+
+def finish_kernel(parts, one, two):
+    for dz in range(3):
+        for dy in range(3):
+            for k, out in enumerate((one, two)):
+                tile = parts[dz * C : (dz + 1) * C, 3 * k + dy, :]
+                for dx in range(3):
+                    out[dx * 9 + dy * 3 + dz] = tile[:, dx * C : (dx + 1) * C]
 
 
 def fifth_kernel(
-    cells, place, slope1, s_low, s_high, h1, x_low, x_high, r1, r4, gb, v1, w, out, wg, v, g, acc
+    cells, place, slope1, s_low, s_high, h1, x_low, x_high, r1, r4, gb, w, out, v
 ):
     mean, inverse, o_low, o_high = read_stats(r1, place, cells)
     nsum, plain = read_sums(r4)
@@ -273,7 +419,6 @@
     p_mean, n_mean = plain / cells, nsum / cells
     mean2, inverse2, lead2 = twice(mean), twice(inverse), twice(lead)
     p_mean2, n_mean2 = twice(p_mean), twice(n_mean)
-    lane = lanes(64)
     rows = ROWS + 2
     for y in range(rows):
         n_low = (x_low[y + 2].astype(F32) + o_low) * inverse
@@ -283,14 +428,11 @@
         g_own = lead2 * (slope1[y] - p_mean2 - n_own * n_mean2)
         g_high = lead * (s_high[y].astype(F32) - p_mean - n_high * n_mean)
         v[y] = masked(g_low, g_own, g_high, kept(place, y, rows, 1))
-        if 1 <= y < 1 + ROWS:
-            put_shifted(g, y - 1, g_own, lane)
 
     def emit(y, values):
         out[y] = values.astype(BF16)
 
     conv_rows(v, w, ROWS, emit)
-    weight_sums(g, v1, 3, acc, wg)
 
 
 def call(kernel, ins, outs, name, scratch=(), smem_first=True):
@@ -301,7 +443,7 @@
         in_specs=specs,
         out_specs=[VM] * len(outs),
         scratch_shapes=list(scratch),
-        compiler_params=pltpu.CompilerParams(vmem_limit_bytes=40 * 1024 * 1024),
+        compiler_params=pltpu.CompilerParams(vmem_limit_bytes=24 * 1024 * 1024),
         cost_estimate=pl.CostEstimate(
             flops=2_000_000_000, bytes_accessed=6_000_000, transcendentals=0
         ),
@@ -321,31 +463,6 @@
 
 def share(msg):
     return lax.all_to_all(msg, ALL, 0, 0, tiled=True)
-
-
-def summed(pieces, count):
-    rows = pieces.reshape(-1, 128)
-    spare = -rows.shape[0] % count
-    rows = jnp.pad(rows, ((0, spare), (0, 0))).reshape(count, -1, 128)
-    own = share(rows).sum(axis=0)
-    whole = share(jnp.broadcast_to(own[None], rows.shape))
-    return whole.reshape(-1, 128)[: rows.shape[0] * rows.shape[1] - spare]
-
-
-def kernel_matrix(kernel):
-    first = jnp.pad(kernel, ((0, 0), (0, 0), (0, 1), (0, 0), (0, 0)))
-    second = jnp.pad(kernel, ((0, 0), (0, 0), (1, 0), (0, 0), (0, 0)))
-    both = jnp.stack([first, second])
-    return jnp.transpose(both, (5, 0, 1, 4, 3, 2)).reshape(192, 384)
-
-
-def flip_kernel(kernel):
-    return jnp.transpose(kernel[:, :, ::-1, ::-1, ::-1], (1, 0, 2, 3, 4))
-
-
-def unfolded(rows):
-    tiles = rows.reshape(3, 3, C, 128)[..., :96].reshape(3, 3, C, 3, C)
-    return jnp.transpose(tiles, (2, 4, 3, 1, 0))
 
 
 def local(features, kernel_one, gain_one, bias_one, kernel_two, gain_two, bias_two, cotangent):
@@ -355,38 +472,40 @@
     gx, gy = lax.axis_index(GX), lax.axis_index(GY)
     at = gx * count_y + gy
     place = jnp.stack(
-        [at - count_y, at + count_y, gx > 0, gx < count_x - 1, gy > 0, gy < count_y - 1]
+        [at - count_y, at + count_y, gx > 0, gx < count_x - 1, gy > 0, gy < count_y - 1, at % C]
     ).astype(jnp.int32)
     gb = jnp.stack([gain_one, bias_one, gain_two, bias_two], axis=1)
 
     own = jnp.transpose(features, (2, 1, 0, 3)).reshape(ROWS, 64, 128)
     cot = jnp.transpose(cotangent, (2, 1, 0, 3)).reshape(ROWS, 64, 128)
-    x_low = up(own[:, C:], GX)
-    x_high = down(own[:, :C], GX)
-    y_low = up(jnp.concatenate([own[-4:], cot[-2:]]), GY)
-    y_high = down(jnp.concatenate([own[:4], cot[:2]]), GY)
-    corner = jnp.concatenate([y_low[:4], y_high[:4]])
-    c_low = up(corner[:, C:], GX)
-    c_high = down(corner[:, :C], GX)
-    w1, w2 = kernel_matrix(kernel_one), kernel_matrix(kernel_two)
-    b1, b2 = kernel_matrix(flip_kernel(kernel_one)), kernel_matrix(flip_kernel(kernel_two))
 
     def rims(rows):
         return [sh((rows, C, 128), BF16)] * 2
 
-    msg = sh((count, 128), F32)
-    work = (pltpu.VMEM((192, ROWS * 128), BF16), pltpu.VMEM((192, 384), F32))
+    msg, wide = sh((count, 128), F32), sh((count, 8, 128), F32)
+    corr = (pltpu.VMEM((192, ROWS * 128), BF16), pltpu.VMEM((192, 384), F32))
+
+    y_up, y_down = call(
+        pack_kernel, (own, cot), [sh((6, 64, 128), BF16)] * 2, "pack", smem_first=False
+    )
+    y_low, y_high = up(y_up, GY), down(y_down, GY)
+    x_up, x_down = call(planes_kernel, (own, y_low, y_high), rims(40), "planes", smem_first=False)
+    x_low, x_high = up(x_up, GX), down(x_down, GX)
+    taps = [
+        jnp.transpose(k, (2, 3, 4, 0, 1)).reshape(27, C, C) for k in (kernel_one, kernel_two)
+    ]
+    w1, w2, b1, b2 = call(
+        weights_kernel, taps, [sh((192, 384), BF16)] * 4, "weights", smem_first=False
+    )
 
     v1, h1, low, high, m1 = call(
         first_kernel,
-        (own, y_low[:4], y_high[:4], x_low, x_high, c_low, c_high, w1),
+        (own, y_low, y_high, x_low, x_high, w1),
         [sh((40, 128, 128), BF16), sh((38, 64, 128), F32), *rims(38), msg],
         "conv_one",
         smem_first=False,
     )
     h1_low, h1_high = up(high, GX), down(low, GX)
-    cot = jnp.concatenate([y_low[4:], cot, y_high[4:]])
-    t_low, t_high = up(cot[:, C:], GX), down(cot[:, :C], GX)
     r1 = share(m1)
 
     v2, h2, low, high, m2 = call(
@@ -397,49 +516,57 @@
     )
     h2_low, h2_high = up(high, GX), down(low, GX)
     r2 = share(m2)
-
-    output, m3 = call(
+    xn, x1 = call(
+        lambda *refs: side_kernel(cells, *refs),
+        (place, h1, r1, v1),
+        [sh((9, C, 128), F32), sh((16, 128), F32)],
+        "normed_features",
+        scratch=corr,
+    )
+
+    output, low, high, m3 = call(
         lambda *refs: third_kernel(cells, *refs),
-        (place, h2, cot, r2, gb),
-        [sh((ROWS, 64, 128), BF16), msg],
+        (place, h2, cot, y_low, y_high, r2, gb, xn, x1),
+        [sh((ROWS, 64, 128), BF16), *rims(36), wide],
         "slope_two",
     )
+    t_low, t_high = up(high, GX), down(low, GX)
     r3 = share(m3)
 
-    slope1, low, high, m4, wg2 = call(
+    slope1, low, high, m4 = call(
         lambda *refs: fourth_kernel(cells, *refs),
-        (place, h2, h2_low, h2_high, cot, t_low, t_high, r2, r3, h1, r1, gb, v2, b2),
-        [sh((34, 64, 128), F32), *rims(34), msg, sh((9, C, 128), F32)],
+        (
+            place, h2, h2_low, h2_high, cot, y_low, y_high, t_low, t_high, r2, r3, h1, r1, gb,
+            v1, v2, b2,
+        ),
+        [sh((34, 64, 128), F32), *rims(34), wide],
         "back_two",
-        scratch=(pltpu.VMEM((36, 128, 128), BF16), *work),
+        scratch=(pltpu.VMEM((36, 128, 128), BF16), *corr, corr[1]),
     )
     s_low, s_high = up(high, GX), down(low, GX)
     r4 = share(m4)
 
-    grad, wg1 = call(
+    m5, norm_grads = call(
+        lambda *refs: owner_kernel(cells, *refs),
+        (place, r1, r3, r4, gb),
+        [wide, sh((4, C), F32)],
+        "own_rows",
+    )
+    r5 = share(m5)
+    (grad,) = call(
         lambda *refs: fifth_kernel(cells, *refs),
-        (place, slope1, s_low, s_high, h1, h1_low, h1_high, r1, r4, gb, v1, b1),
-        [sh((ROWS, 64, 128), BF16), sh((9, C, 128), F32)],
+        (place, slope1, s_low, s_high, h1, h1_low, h1_high, r1, r4, gb, b1),
+        [sh((ROWS, 64, 128), BF16)],
         "back_one",
-        scratch=(pltpu.VMEM((34, 128, 128), BF16), *work),
-    )
-    scale = 1.0 / jnp.sqrt(jnp.float32(cells))
-    whole = summed(jnp.concatenate([wg1, wg2]), count) * scale
-    half = whole.shape[0] // 2
-    norm_grads = jnp.concatenate(
-        [r4[:, : 2 * C].sum(axis=0).reshape(2, C), r3[:, : 2 * C].sum(axis=0).reshape(2, C)]
-    )
+        scratch=(pltpu.VMEM((34, 128, 128), BF16),),
+    )
+    grads = call(finish_kernel, (r5,), [sh((27, C, C), F32)] * 2, "finish", smem_first=False)
+    one, two = [jnp.transpose(k.reshape(3, 3, 3, C, C), (3, 4, 0, 1, 2)) for k in grads]
 
     def back(rows):
         return jnp.transpose(rows.reshape(ROWS, 2, C, 128), (2, 1, 0, 3))
 
-    return (
-        back(output),
-        back(grad),
-        unfolded(whole[:half]),
-        unfolded(whole[half:]),
-        norm_grads * scale,
-    )
+    return back(output), back(grad), one, two, norm_grads
 
 
 def solution(mesh):

time: 201 us -> 185 us (0.920)
  starting transfers between devices: 88.3 us -> 58.6 us
  blocking collectives: 0 us -> 25.2 us
  local copies, waits for them, and re-layouts: 41.6 us -> 34.7 us
  other arithmetic: 5.73 us -> 0.01 us
  Pallas kernels: 17.9 us -> 21.6 us
  waiting for transfers between devices: 45 us -> 42.5 us
    all_to_all x6 -> x4, waiting for transfers between devices: 41.7 us -> 14.8 us  [share(): return lax.all_to_all(msg, ALL, 0, 0, tiled=True)]
    all_to_all x0 -> x1, blocking collectives: none -> 25.2 us  [share(): return lax.all_to_all(msg, ALL, 0, 0, tiled=True)]
    all_to_all x6 -> x4, starting transfers between devices: 52.8 us -> 27.9 us  [share(): return lax.all_to_all(msg, ALL, 0, 0, tiled=True)]
    ppermute x7 -> x6, waiting for transfers between devices: 0.02 us -> 15.6 us  [up(): return lax.ppermute(values, axes, [(i, i + 1) for i in range(count - 1)])]
    unnamed x52 -> x110, local copies, waits for them, and re-layouts: 17.9 us -> 30.4 us
    ppermute x7 -> x6, waiting for transfers between devices: 3.3 us -> 12.2 us  [down(): return lax.ppermute(values, axes, [(i + 1, i) for i in range(count - 1)])]
    slice x13 -> x0, local copies, waits for them, and re-layouts: 7.07 us -> none  [the longest x4 2.13 us: local(): y_high = down(jnp.concatenate([own[:4], cot[:2]]), GY)]
    transpose x7 -> x0, local copies, waits for them, and re-layouts: 7.06 us -> none  [the longest x4 4.7 us: kernel_matrix(): return jnp.transpose(both, (5, 0, 1, 4, 3, 2)).reshape(192, 384)]
  transfers between devices with their start and end apart: 20 -> 16, of which waited for: 6 -> 11; matrix products, arithmetic and copies ran while one was open for 12% -> 1% of each run, Pallas kernels for 1% -> 3%
where the time goes in v1:
time: 185 us; the launch traced here: 184 us
  starting transfers between devices  58.6 us (32%)
  waiting for transfers between devices  42.5 us (23%)
  local copies, waits for them, and re-layouts  34.7 us (19%)
  blocking collectives  25.2 us (14%)
  Pallas kernels  21.6 us (12%)
    unnamed x110, local copies, waits for them, and re-layouts  30.4 us
    all_to_all x4, starting transfers between devices, share(): return lax.all_to_all(msg, ALL, 0, 0, tiled=True)  27.9 us
    all_to_all x1, blocking collectives, share(): return lax.all_to_all(msg, ALL, 0, 0, tiled=True)  25.2 us
    ppermute x6, starting transfers between devices, up(): return lax.ppermute(values, axes, [(i, i + 1) for i in range(count - 1)])  22 us
    pallas_call x11, Pallas kernels, call(): pl.pallas_call(kernel, out_shape=outs, in_specs=specs, out_specs=[VM] * l...  21.6 us
    ppermute x6, waiting for transfers between devices, up(): return lax.ppermute(values, axes, [(i, i + 1) for i in range(count - 1)])  15.6 us
    all_to_all x4, waiting for transfers between devices, share(): return lax.all_to_all(msg, ALL, 0, 0, tiled=True)  14.8 us
    ppermute x6, waiting for transfers between devices, down(): return lax.ppermute(values, axes, [(i + 1, i) for i in range(count - 1)])  12.2 us
  transfers between devices with their start and end apart: 16, of which 11 were waited for; matrix products, arithmetic and copies ran while one was open for 1% of the time, Pallas kernels for 3%

profile of v1, /device:TPU:1, one launch (start us, length us, event | category | flops | bytes accessed | tf_op | source)
XLA Modules:
  0.0 183.8 jit_solution(15277628411548126369)
XLA Ops:
  0.6 1.4 copy.21
  2.5 4.9 %collective-permute-start = (bf16[6,64,128]{2,1,0:T(8,128)(2,1)S(1)}, bf16[6,64,128]{2,1,0:T(8,128)(2,1)S(1)}, u32[]{:S(2)}, u32[]{:S(2)}) collective-permute-start(bf16[6,64,128]{2,1,0:T(8,128)(2,1)S(1)} %get-tuple-element.37), channel_id=1, source_target_pairs={{0,1},{1,2},{2,3},{3,4},{4,5},{5,6},{6,7},{8,9},{9,10},{10,11},{11... | collective-permute-start | bytes 294920 | tf_op jit(solution)/shard_map/ppermute | solution.py:456
  7.4 2.1 %collective-permute-start.1 = (bf16[6,64,128]{2,1,0:T(8,128)(2,1)S(1)}, bf16[6,64,128]{2,1,0:T(8,128)(2,1)S(1)}, u32[]{:S(2)}, u32[]{:S(2)}) collective-permute-start(bf16[6,64,128]{2,1,0:T(8,128)(2,1)S(1)} %get-tuple-element.38), channel_id=1, source_target_pairs={{1,0},{2,1},{3,2},{4,3},{5,4},{6,5},{7,6},{9,8},{10,9},{11,10},{12... | collective-permute-start | bytes 294920 | tf_op jit(solution)/shard_map/ppermute | solution.py:461
  9.5 4.0 %collective-permute-done.1.y_high.refs_4_.refs_6_ = bf16[6,64,128]{2,1,0:T(8,128)(2,1)S(1)} collective-permute-done((bf16[6,64,128]{2,1,0:T(8,128)(2,1)S(1)}, bf16[6,64,128]{2,1,0:T(8,128)(2,1)S(1)}, u32[]{:S(2)}, u32[]{:S(2)}) %collective-permute-start.1) | collective-permute-done | bytes 98336 | tf_op jit(solution)/shard_map/ppermute | solution.py:461
  13.6 3.2 %collective-permute-start.2 = (bf16[40,32,128]{2,1,0:T(8,128)(2,1)S(1)}, bf16[40,32,128]{2,1,0:T(8,128)(2,1)S(1)}, u32[]{:S(2)}, u32[]{:S(2)}) collective-permute-start(bf16[40,32,128]{2,1,0:T(8,128)(2,1)S(1)} %get-tuple-element.39), channel_id=1, source_target_pairs={{0,8},{8,16},{16,24},{24,32},{32,40},{40,48},{48,56},{56,64},{64,7... | collective-permute-start | bytes 983048 | tf_op jit(solution)/shard_map/ppermute | solution.py:456
  16.8 1.3 collective-permute-start.3
  20.0 2.0 %collective-permute-done.2.x_low = bf16[40,32,128]{2,1,0:T(8,128)(2,1)S(1)} collective-permute-done((bf16[40,32,128]{2,1,0:T(8,128)(2,1)S(1)}, bf16[40,32,128]{2,1,0:T(8,128)(2,1)S(1)}, u32[]{:S(2)}, u32[]{:S(2)}) %collective-permute-start.2) | collective-permute-done | bytes 327712 | tf_op jit(solution)/shard_map/ppermute | solution.py:456
  22.0 4.1 %collective-permute-done.3.x_high = bf16[40,32,128]{2,1,0:T(8,128)(2,1)S(1)} collective-permute-done((bf16[40,32,128]{2,1,0:T(8,128)(2,1)S(1)}, bf16[40,32,128]{2,1,0:T(8,128)(2,1)S(1)}, u32[]{:S(2)}, u32[]{:S(2)}) %collective-permute-start.3) | collective-permute-done | bytes 327712 | tf_op jit(solution)/shard_map/ppermute | solution.py:461
  26.1 2.4 %conv_one.1 = (bf16[40,128,128]{2,1,0:T(8,128)(2,1)S(1)}, f32[38,64,128]{2,1,0:T(8,128)S(1)}, bf16[38,32,128]{2,1,0:T(8,128)(2,1)S(1)}, bf16[38,32,128]{2,1,0:T(8,128)(2,1)}, f32[128,128]{1,0:T(8,128)}) custom-call(bf16[32,64,128]{2,1,0:T(8,128)(2,1)S(1)} %bitcast.49, bf16[6,64,128]{2,1,0:T(8,128)(2,1)S(1)} %collective-permute-done.y_low.refs_3_.refs_5_, ...), custom_call_target="tpu_custom_call" | custom-call | flops 2000000000 | bytes 6000000 | tf_op jit(solution)/shard_map/conv_one/pallas_call | solution.py:440
  28.6 1.1 copy-done
  29.6 3.2 %collective-permute-start.4 = (bf16[38,32,128]{2,1,0:T(8,128)(2,1)}, bf16[38,32,128]{2,1,0:T(8,128)(2,1)S(1)}, u32[]{:S(2)}, u32[]{:S(2)}) collective-permute-start(bf16[38,32,128]{2,1,0:T(8,128)(2,1)} %get-tuple-element.43), channel_id=1, source_target_pairs={{0,8},{8,16},{16,24},{24,32},{32,40},{40,48},{48,56},{56,64},{64,7... | collective-permute-start | bytes 933896 | tf_op jit(solution)/shard_map/ppermute | solution.py:456
  32.8 1.3 collective-permute-start.5
  34.1 13.7 %all-to-all-start = ((f32[128,1,128]{2,1,0:T(1,128)}), f32[128,1,128]{2,1,0:T(1,128)S(1)}, u32[]{:S(2)}, u32[]{:S(2)}) async-start(f32[128,1,128]{2,1,0:T(1,128)} %bitcast.16), calls=%async_computation | async-start | bytes 131072 | tf_op jit(solution)/shard_map/all_to_all | solution.py:465
  48.0 9.1 %all-to-all-done = f32[128,1,128]{2,1,0:T(1,128)S(1)} async-done(((f32[128,1,128]{2,1,0:T(1,128)}), f32[128,1,128]{2,1,0:T(1,128)S(1)}, u32[]{:S(2)}, u32[]{:S(2)}) %all-to-all-start) | async-done | bytes 65568 | tf_op jit(solution)/shard_map/all_to_all | solution.py:465
  57.1 0.7 copy-done.34
  58.6 1.3 copy-done.1
  59.9 1.0 copy-done.35
  60.8 1.0 copy-done.38
  61.8 4.1 %conv_two.1 = (bf16[38,128,128]{2,1,0:T(8,128)(2,1)S(1)}, f32[36,64,128]{2,1,0:T(8,128)S(1)}, bf16[36,32,128]{2,1,0:T(8,128)(2,1)S(1)}, bf16[36,32,128]{2,1,0:T(8,128)(2,1)S(1)}, f32[128,128]{1,0:T(8,128)}) custom-call(s32[7]{0:T(128)S(1)} %stack.62.refs_0_, f32[38,64,128]{2,1,0:T(8,128)S(1)} %copy-done.1, bf16[38,32,128]{2,1,0:T(8,128)(2,1)S(1)} %copy-done.35, ...), custom_call_target="tpu_custom_call" | custom-call | flops 2000000000 | bytes 6000000 | tf_op jit(solution)/shard_map/conv_two/pallas_call | solution.py:440
  65.8 1.1 copy-done.5
  67.6 0.7 copy-done.41
  68.4 4.8 %all-to-all-start.1 = ((f32[128,1,128]{2,1,0:T(1,128)}), f32[128,1,128]{2,1,0:T(1,128)S(1)}, u32[]{:S(2)}, u32[]{:S(2)}) async-start(f32[128,1,128]{2,1,0:T(1,128)} %bitcast.23), calls=%async_computation.1 | async-start | bytes 131072 | tf_op jit(solution)/shard_map/all_to_all | solution.py:465
  73.1 1.3 copy-done.2
  74.4 2.3 %normed_features.1 = (f32[9,32,128]{2,1,0:T(8,128)S(1)}, f32[16,128]{1,0:T(8,128)S(1)}) custom-call(s32[7]{0:T(128)S(1)} %stack.62.refs_0_, f32[38,64,128]{2,1,0:T(8,128)S(1)} %copy-done.2, f32[128,128]{1,0:T(8,128)S(1)} %bitcast.52, bf16[40,128,128]{2,1,0:T(8,128)(2,1)S(1)} %get-tuple-element.49.refs_3_.refs_14_), custom_call_target="tpu_custom_call" | custom-call | flops 2000000000 | bytes 6000000 | tf_op jit(solution)/shard_map/normed_features/pallas_call | solution.py:440
  76.7 5.7 %all-to-all-done.1 = f32[128,1,128]{2,1,0:T(1,128)S(1)} async-done(((f32[128,1,128]{2,1,0:T(1,128)}), f32[128,1,128]{2,1,0:T(1,128)S(1)}, u32[]{:S(2)}, u32[]{:S(2)}) %all-to-all-start.1) | async-done | bytes 65568 | tf_op jit(solution)/shard_map/all_to_all | solution.py:465
  82.4 2.1 %slope_two.1 = (bf16[32,64,128]{2,1,0:T(8,128)(2,1)S(1)}, bf16[36,32,128]{2,1,0:T(8,128)(2,1)S(1)}, bf16[36,32,128]{2,1,0:T(8,128)(2,1)S(1)}, f32[128,8,128]{2,1,0:T(8,128)S(1)}) custom-call(s32[7]{0:T(128)S(1)} %stack.62.refs_0_, f32[36,64,128]{2,1,0:T(8,128)S(1)} %get-tuple-element.47.refs_1_, bf16[32,64,128]{2,1,0:T(8,128)(2,1)S(1)} %bitcast.44, ...), custom_call_target="tpu_custom_call" | custom-call | flops 2000000000 | bytes 6000000 | tf_op jit(solution)/shard_map/slope_two/pallas_call | solution.py:440
  84.6 0.8 copy-done.7
  85.4 0.8 copy-done.9
  87.6 4.8 %all-to-all-start.2 = ((f32[128,8,128]{2,1,0:T(8,128)}), f32[128,8,128]{2,1,0:T(8,128)S(1)}, u32[]{:S(2)}, u32[]{:S(2)}) async-start(f32[128,8,128]{2,1,0:T(8,128)} %copy-done.9), calls=%async_computation.2 | async-start | bytes 1048576 | tf_op jit(solution)/shard_map/all_to_all | solution.py:465
  92.4 3.3 %collective-permute-start.6 = (bf16[36,32,128]{2,1,0:T(8,128)(2,1)}, bf16[36,32,128]{2,1,0:T(8,128)(2,1)S(1)}, u32[]{:S(2)}, u32[]{:S(2)}) collective-permute-start(bf16[36,32,128]{2,1,0:T(8,128)(2,1)} %copy-done.41), channel_id=1, source_target_pairs={{0,8},{8,16},{16,24},{24,32},{32,40},{40,48},{48,56},{56,64},{64,7... | collective-permute-start | bytes 884744 | tf_op jit(solution)/shard_map/ppermute | solution.py:456
  95.7 1.3 collective-permute-start.7
  97.0 4.0 %collective-permute-start.8 = (bf16[36,32,128]{2,1,0:T(8,128)(2,1)}, bf16[36,32,128]{2,1,0:T(8,128)(2,1)S(1)}, u32[]{:S(2)}, u32[]{:S(2)}) collective-permute-start(bf16[36,32,128]{2,1,0:T(8,128)(2,1)} %copy-done.43), channel_id=1, source_target_pairs={{0,8},{8,16},{16,24},{24,32},{32,40},{40,48},{48,56},{56,64},{64,7... | collective-permute-start | bytes 884744 | tf_op jit(solution)/shard_map/ppermute | solution.py:456
  101.0 1.5 collective-permute-start.9
  102.5 2.9 %collective-permute-done.6.refs_2_ = bf16[36,32,128]{2,1,0:T(8,128)(2,1)S(1)} collective-permute-done((bf16[36,32,128]{2,1,0:T(8,128)(2,1)}, bf16[36,32,128]{2,1,0:T(8,128)(2,1)S(1)}, u32[]{:S(2)}, u32[]{:S(2)}) %collective-permute-start.6) | collective-permute-done | bytes 294944 | tf_op jit(solution)/shard_map/ppermute | solution.py:456
  105.4 0.7 copy-done.10
  106.1 1.1 collective-permute-done.7.refs_3_
  107.9 3.8 %collective-permute-done.8.refs_7_ = bf16[36,32,128]{2,1,0:T(8,128)(2,1)S(1)} collective-permute-done((bf16[36,32,128]{2,1,0:T(8,128)(2,1)}, bf16[36,32,128]{2,1,0:T(8,128)(2,1)S(1)}, u32[]{:S(2)}, u32[]{:S(2)}) %collective-permute-start.8) | collective-permute-done | bytes 294944 | tf_op jit(solution)/shard_map/ppermute | solution.py:456
  111.7 0.7 copy-done.14
  112.4 1.1 collective-permute-done.9.refs_8_
  114.3 1.3 copy-done.3
  115.5 1.3 copy-done.6
  116.8 1.0 copy-done.11
  117.8 1.0 copy-done.13
  118.8 1.0 copy-done.15
  119.7 1.0 copy-done.17
  120.7 0.8 copy-done.19
  121.5 0.8 copy-done.22
  122.4 0.9 copy-done.24
  123.3 0.9 copy-done.26
  124.2 0.9 copy-done.28
  125.7 5.1 %back_two.1 = (f32[34,64,128]{2,1,0:T(8,128)S(1)}, bf16[34,32,128]{2,1,0:T(8,128)(2,1)S(1)}, bf16[34,32,128]{2,1,0:T(8,128)(2,1)S(1)}, f32[128,8,128]{2,1,0:T(8,128)S(1)}) custom-call(s32[7]{0:T(128)S(1)} %copy-done.30, f32[36,64,128]{2,1,0:T(8,128)S(1)} %get-tuple-element.47.refs_1_, bf16[36,32,128]{2,1,0:T(8,128)(2,1)S(1)} %copy-done.11, ...), custom_call_target="tpu_custom_call" | custom-call | flops 2000000000 | bytes 6000000 | tf_op jit(solution)/shard_map/back_two/pallas_call | solution.py:440
  130.9 25.2 %all_to_all.37.refs_8_.refs_3_ = f32[128,8,128]{2,1,0:T(8,128)S(1)} all-to-all(f32[128,8,128]{2,1,0:T(8,128)S(1)} %get-tuple-element.63), channel_id=1, replica_groups=mesh['gx_0'=4,'gx_1'=4,'gy_0'=4,'gy_1'=2] {'gx_0','gx_1','gy_0','gy_1'}, dimensions={0} | all-to-all | bytes 1048576 | tf_op jit(solution)/shard_map/all_to_all | solution.py:465
  156.0 1.7 own_rows.1
  157.8 4.7 %all-to-all-start.4 = ((f32[128,8,128]{2,1,0:T(8,128)}), f32[128,8,128]{2,1,0:T(8,128)S(1)}, u32[]{:S(2)}, u32[]{:S(2)}) async-start(f32[128,8,128]{2,1,0:T(8,128)} %get-tuple-element.65), calls=%async_computation.4 | async-start | bytes 1048576 | tf_op jit(solution)/shard_map/all_to_all | solution.py:465
  162.5 3.4 %collective-permute-start.10 = (bf16[34,32,128]{2,1,0:T(8,128)(2,1)}, bf16[34,32,128]{2,1,0:T(8,128)(2,1)S(1)}, u32[]{:S(2)}, u32[]{:S(2)}) collective-permute-start(bf16[34,32,128]{2,1,0:T(8,128)(2,1)} %copy-done.45), channel_id=1, source_target_pairs={{0,8},{8,16},{16,24},{24,32},{32,40},{40,48},{48,56},{56,64},{64,7... | collective-permute-start | bytes 835592 | tf_op jit(solution)/shard_map/ppermute | solution.py:456
  165.9 1.3 collective-permute-start.11
  167.2 1.1 copy.35
  168.3 6.9 %collective-permute-done.10.refs_2_ = bf16[34,32,128]{2,1,0:T(8,128)(2,1)S(1)} collective-permute-done((bf16[34,32,128]{2,1,0:T(8,128)(2,1)}, bf16[34,32,128]{2,1,0:T(8,128)(2,1)S(1)}, u32[]{:S(2)}, u32[]{:S(2)}) %collective-permute-start.10) | collective-permute-done | bytes 278560 | tf_op jit(solution)/shard_map/ppermute | solution.py:456
  175.2 1.9 %collective-permute-done.11.refs_3_ = bf16[34,32,128]{2,1,0:T(8,128)(2,1)S(1)} collective-permute-done((bf16[34,32,128]{2,1,0:T(8,128)(2,1)}, bf16[34,32,128]{2,1,0:T(8,128)(2,1)S(1)}, u32[]{:S(2)}, u32[]{:S(2)}) %collective-permute-start.11) | collective-permute-done | bytes 278560 | tf_op jit(solution)/shard_map/ppermute | solution.py:461
  177.2 1.2 copy-done.33
  178.4 0.9 copy-done.49
  179.3 2.2 %back_one.1 = bf16[32,64,128]{2,1,0:T(8,128)(2,1)S(1)} custom-call(s32[7]{0:T(128)S(1)} %copy-done.31, f32[34,64,128]{2,1,0:T(8,128)S(1)} %copy-done.33, bf16[34,32,128]{2,1,0:T(8,128)(2,1)S(1)} %collective-permute-done.10.refs_2_, bf16[34,32,128]{2,1,0:T(8,128)(2,1)S(1)} %collective-permute-done.11.refs_3_, f32[38,64,128]{2,1,0:T(8,128)S(1)} %copy-done.4, ...), custom_call_target="tpu_custom_call" | custom-call | flops 2000000000 | bytes 6000000 | tf_op jit(solution)/shard_map/back_one/pallas_call | solution.py:440
  181.5 1.1 copy.34
  182.6 1.1 finish.1
  (97 shorter events, 7.5 us)
Async XLA Ops:
  0.6 1.5 copy-start.50
  2.5 7.0 %collective-permute-start = (bf16[6,64,128]{2,1,0:T(8,128)(2,1)S(1)}, bf16[6,64,128]{2,1,0:T(8,128)(2,1)S(1)}, u32[]{:S(2)}, u32[]{:S(2)}) collective-permute-start(bf16[6,64,128]{2,1,0:T(8,128)(2,1)S(1)} %get-tuple-element.37), channel_id=1, source_target_pairs={{0,1},{1,2},{2,3},{3,4},{4,5},{5,6},{6,7},{8,9},{9,10},{10,11},{11... | collective-permute-start | bytes 294920 | tf_op jit(solution)/shard_map/ppermute | solution.py:456
  7.4 10.7 %copy-start.46 = (bf16[32,32,3,3,3]{1,0,4,3,2:T(8,128)(2,1)S(1)}, bf16[32,32,3,3,3]{1,0,4,3,2:T(8,128)(2,1)}, u32[]{:S(2)}) copy-start(bf16[32,32,3,3,3]{1,0,4,3,2:T(8,128)(2,1)} %param.9) | copy-start | bytes 165892
  7.4 10.7 %copy-start.47 = (bf16[32,32,3,3,3]{1,0,4,3,2:T(8,128)(2,1)S(1)}, bf16[32,32,3,3,3]{1,0,4,3,2:T(8,128)(2,1)}, u32[]{:S(2)}) copy-start(bf16[32,32,3,3,3]{1,0,4,3,2:T(8,128)(2,1)} %param.12) | copy-start | bytes 165892
  7.4 6.1 %collective-permute-start.1 = (bf16[6,64,128]{2,1,0:T(8,128)(2,1)S(1)}, bf16[6,64,128]{2,1,0:T(8,128)(2,1)S(1)}, u32[]{:S(2)}, u32[]{:S(2)}) collective-permute-start(bf16[6,64,128]{2,1,0:T(8,128)(2,1)S(1)} %get-tuple-element.38), channel_id=1, source_target_pairs={{1,0},{2,1},{3,2},{4,3},{5,4},{6,5},{7,6},{9,8},{10,9},{11,10},{12... | collective-permute-start | bytes 294920 | tf_op jit(solution)/shard_map/ppermute | solution.py:461
  9.5 72.9 %copy-start.25 = (bf16[6,64,128]{2,1,0:T(8,128)(2,1)}, bf16[6,64,128]{2,1,0:T(8,128)(2,1)S(1)}, u32[]{:S(2)}) copy-start(bf16[6,64,128]{2,1,0:T(8,128)(2,1)S(1)} %collective-permute-done.y_low.refs_3_.refs_5_) | copy-start | bytes 294916
  13.5 68.9 %copy-start.27 = (bf16[6,64,128]{2,1,0:T(8,128)(2,1)}, bf16[6,64,128]{2,1,0:T(8,128)(2,1)S(1)}, u32[]{:S(2)}) copy-start(bf16[6,64,128]{2,1,0:T(8,128)(2,1)S(1)} %collective-permute-done.1.y_high.refs_4_.refs_6_) | copy-start | bytes 294916
  13.6 8.5 %collective-permute-start.2 = (bf16[40,32,128]{2,1,0:T(8,128)(2,1)S(1)}, bf16[40,32,128]{2,1,0:T(8,128)(2,1)S(1)}, u32[]{:S(2)}, u32[]{:S(2)}) collective-permute-start(bf16[40,32,128]{2,1,0:T(8,128)(2,1)S(1)} %get-tuple-element.39), channel_id=1, source_target_pairs={{0,8},{8,16},{16,24},{24,32},{32,40},{40,48},{48,56},{56,64},{64,7... | collective-permute-start | bytes 983048 | tf_op jit(solution)/shard_map/ppermute | solution.py:456
  16.8 9.3 %collective-permute-start.3 = (bf16[40,32,128]{2,1,0:T(8,128)(2,1)S(1)}, bf16[40,32,128]{2,1,0:T(8,128)(2,1)S(1)}, u32[]{:S(2)}, u32[]{:S(2)}) collective-permute-start(bf16[40,32,128]{2,1,0:T(8,128)(2,1)S(1)} %get-tuple-element.40), channel_id=1, source_target_pairs={{8,0},{16,8},{24,16},{32,24},{40,32},{48,40},{56,48},{64,56},{72,6... | collective-permute-start | bytes 983048 | tf_op jit(solution)/shard_map/ppermute | solution.py:461
  26.1 21.7 %copy-start.51 = (f32[32]{0:T(128)S(1)}, f32[32]{0:T(128)}, u32[]{:S(2)}) copy-start(f32[32]{0:T(128)} %param.14) | copy-start | bytes 388
  26.1 21.7 %copy-start.52 = (f32[32]{0:T(128)S(1)}, f32[32]{0:T(128)}, u32[]{:S(2)}) copy-start(f32[32]{0:T(128)} %param.13) | copy-start | bytes 388
  26.1 21.7 %copy-start.53 = (f32[32]{0:T(128)S(1)}, f32[32]{0:T(128)}, u32[]{:S(2)}) copy-start(f32[32]{0:T(128)} %param.11) | copy-start | bytes 388
  26.1 21.7 %copy-start.54 = (f32[32]{0:T(128)S(1)}, f32[32]{0:T(128)}, u32[]{:S(2)}) copy-start(f32[32]{0:T(128)} %param.10) | copy-start | bytes 388
  28.6 1.1 copy-start
  29.6 27.5 %collective-permute-start.4 = (bf16[38,32,128]{2,1,0:T(8,128)(2,1)}, bf16[38,32,128]{2,1,0:T(8,128)(2,1)S(1)}, u32[]{:S(2)}, u32[]{:S(2)}) collective-permute-start(bf16[38,32,128]{2,1,0:T(8,128)(2,1)} %get-tuple-element.43), channel_id=1, source_target_pairs={{0,8},{8,16},{16,24},{24,32},{32,40},{40,48},{48,56},{56,64},{64,7... | collective-permute-start | bytes 933896 | tf_op jit(solution)/shard_map/ppermute | solution.py:456
  32.8 25.0 %collective-permute-start.5 = (bf16[38,32,128]{2,1,0:T(8,128)(2,1)S(1)}, bf16[38,32,128]{2,1,0:T(8,128)(2,1)S(1)}, u32[]{:S(2)}, u32[]{:S(2)}) collective-permute-start(bf16[38,32,128]{2,1,0:T(8,128)(2,1)S(1)} %get-tuple-element.44), channel_id=1, source_target_pairs={{8,0},{16,8},{24,16},{32,24},{40,32},{48,40},{56,48},{64,56},{72,6... | collective-permute-start | bytes 933896 | tf_op jit(solution)/shard_map/ppermute | solution.py:461
  34.1 23.0 %all-to-all-start = ((f32[128,1,128]{2,1,0:T(1,128)}), f32[128,1,128]{2,1,0:T(1,128)S(1)}, u32[]{:S(2)}, u32[]{:S(2)}) async-start(f32[128,1,128]{2,1,0:T(1,128)} %bitcast.16), calls=%async_computation | async-start | bytes 131072 | tf_op jit(solution)/shard_map/all_to_all | solution.py:465
  48.0 34.4 %copy-start.29 = (s32[7]{0:T(128)}, s32[7]{0:T(128)S(1)}, u32[]{:S(2)}) copy-start(s32[7]{0:T(128)S(1)} %stack.62.refs_0_) | copy-start | bytes 88
  57.1 16.0 %copy-start.18 = (f32[128,1,128]{2,1,0:T(1,128)}, f32[128,1,128]{2,1,0:T(1,128)S(1)}, u32[]{:S(2)}) copy-start(f32[128,1,128]{2,1,0:T(1,128)S(1)} %all-to-all-done) | copy-start | bytes 196612
  57.1 0.7 copy-start.34
  57.8 0.7 copy-start.37
  58.6 1.3 copy-start.1
  59.9 1.0 copy-start.35
  60.8 1.0 copy-start.38
  65.8 1.1 copy-start.5
  67.6 0.7 copy-start.41
  68.4 14.1 %all-to-all-start.1 = ((f32[128,1,128]{2,1,0:T(1,128)}), f32[128,1,128]{2,1,0:T(1,128)S(1)}, u32[]{:S(2)}, u32[]{:S(2)}) async-start(f32[128,1,128]{2,1,0:T(1,128)} %bitcast.23), calls=%async_computation.1 | async-start | bytes 131072 | tf_op jit(solution)/shard_map/all_to_all | solution.py:465
  73.1 1.3 copy-start.2
  82.4 2.2 %copy-start.21 = (f32[128,1,128]{2,1,0:T(1,128)}, f32[128,1,128]{2,1,0:T(1,128)S(1)}, u32[]{:S(2)}) copy-start(f32[128,1,128]{2,1,0:T(1,128)S(1)} %all-to-all-done.1) | copy-start | bytes 196612
  84.6 0.8 copy-start.7
  85.4 0.8 copy-start.9
  86.9 0.7 copy-start.43
  87.6 26.6 %all-to-all-start.2 = ((f32[128,8,128]{2,1,0:T(8,128)}), f32[128,8,128]{2,1,0:T(8,128)S(1)}, u32[]{:S(2)}, u32[]{:S(2)}) async-start(f32[128,8,128]{2,1,0:T(8,128)} %copy-done.9), calls=%async_computation.2 | async-start | bytes 1048576 | tf_op jit(solution)/shard_map/all_to_all | solution.py:465
  92.4 13.0 %collective-permute-start.6 = (bf16[36,32,128]{2,1,0:T(8,128)(2,1)}, bf16[36,32,128]{2,1,0:T(8,128)(2,1)S(1)}, u32[]{:S(2)}, u32[]{:S(2)}) collective-permute-start(bf16[36,32,128]{2,1,0:T(8,128)(2,1)} %copy-done.41), channel_id=1, source_target_pairs={{0,8},{8,16},{16,24},{24,32},{32,40},{40,48},{48,56},{56,64},{64,7... | collective-permute-start | bytes 884744 | tf_op jit(solution)/shard_map/ppermute | solution.py:456
  95.7 11.5 %collective-permute-start.7 = (bf16[36,32,128]{2,1,0:T(8,128)(2,1)}, bf16[36,32,128]{2,1,0:T(8,128)(2,1)S(1)}, u32[]{:S(2)}, u32[]{:S(2)}) collective-permute-start(bf16[36,32,128]{2,1,0:T(8,128)(2,1)} %copy-done.40), channel_id=1, source_target_pairs={{8,0},{16,8},{24,16},{32,24},{40,32},{48,40},{56,48},{64,56},{72,6... | collective-permute-start | bytes 884744 | tf_op jit(solution)/shard_map/ppermute | solution.py:461
  97.0 14.7 %collective-permute-start.8 = (bf16[36,32,128]{2,1,0:T(8,128)(2,1)}, bf16[36,32,128]{2,1,0:T(8,128)(2,1)S(1)}, u32[]{:S(2)}, u32[]{:S(2)}) collective-permute-start(bf16[36,32,128]{2,1,0:T(8,128)(2,1)} %copy-done.43), channel_id=1, source_target_pairs={{0,8},{8,16},{16,24},{24,32},{32,40},{40,48},{48,56},{56,64},{64,7... | collective-permute-start | bytes 884744 | tf_op jit(solution)/shard_map/ppermute | solution.py:456
  101.0 12.5 %collective-permute-start.9 = (bf16[36,32,128]{2,1,0:T(8,128)(2,1)}, bf16[36,32,128]{2,1,0:T(8,128)(2,1)S(1)}, u32[]{:S(2)}, u32[]{:S(2)}) collective-permute-start(bf16[36,32,128]{2,1,0:T(8,128)(2,1)} %copy-done.42), channel_id=1, source_target_pairs={{8,0},{16,8},{24,16},{32,24},{40,32},{48,40},{56,48},{64,56},{72,6... | collective-permute-start | bytes 884744 | tf_op jit(solution)/shard_map/ppermute | solution.py:461
  105.4 0.7 copy-start.10
  111.7 0.7 copy-start.14
  114.3 1.3 copy-start.3
  115.5 1.3 copy-start.6
  116.8 1.0 copy-start.11
  117.8 1.0 copy-start.13
  118.8 1.0 copy-start.15
  119.7 1.0 copy-start.17
  120.7 0.8 copy-start.19
  121.5 0.8 copy-start.22
  122.4 0.9 copy-start.24
  123.3 0.9 copy-start.26
  124.2 0.9 copy-start.28
  130.8 26.9 %copy-start.32 = (f32[34,64,128]{2,1,0:T(8,128)}, f32[34,64,128]{2,1,0:T(8,128)S(1)}, u32[]{:S(2)}) copy-start(f32[34,64,128]{2,1,0:T(8,128)S(1)} %get-tuple-element.60.refs_1_) | copy-start | bytes 3342340
  130.8 26.9 %copy-start.44 = (bf16[34,32,128]{2,1,0:T(8,128)(2,1)}, bf16[34,32,128]{2,1,0:T(8,128)(2,1)S(1)}, u32[]{:S(2)}) copy-start(bf16[34,32,128]{2,1,0:T(8,128)(2,1)S(1)} %get-tuple-element.62) | copy-start | bytes 835588
  130.8 26.9 %copy-start.45 = (bf16[34,32,128]{2,1,0:T(8,128)(2,1)}, bf16[34,32,128]{2,1,0:T(8,128)(2,1)S(1)}, u32[]{:S(2)}) copy-start(bf16[34,32,128]{2,1,0:T(8,128)(2,1)S(1)} %get-tuple-element.61) | copy-start | bytes 835588
  156.0 11.2 %copy-start.8 = (bf16[32,64,128]{2,1,0:T(8,128)(2,1)S(1)}, bf16[32,64,128]{2,1,0:T(8,128)(2,1)}, u32[]{:S(2)}) copy-start(bf16[32,64,128]{2,1,0:T(8,128)(2,1)} %copy-done.7) | copy-start | bytes 1572868
  157.8 19.4 %copy-start.4 = (f32[38,64,128]{2,1,0:T(8,128)S(1)}, f32[38,64,128]{2,1,0:T(8,128)}, u32[]{:S(2)}) copy-start(f32[38,64,128]{2,1,0:T(8,128)} %copy-done) | copy-start | bytes 3735556
  157.8 19.4 %copy-start.20 = (f32[128,1,128]{2,1,0:T(1,128)S(1)}, f32[128,1,128]{2,1,0:T(1,128)}, u32[]{:S(2)}) copy-start(f32[128,1,128]{2,1,0:T(1,128)} %copy-done.18) | copy-start | bytes 196612
  157.8 19.4 %copy-start.31 = (s32[7]{0:T(128)S(1)}, s32[7]{0:T(128)}, u32[]{:S(2)}) copy-start(s32[7]{0:T(128)} %copy-done.29) | copy-start | bytes 88
  157.8 19.4 %copy-start.36 = (bf16[38,32,128]{2,1,0:T(8,128)(2,1)S(1)}, bf16[38,32,128]{2,1,0:T(8,128)(2,1)}, u32[]{:S(2)}) copy-start(bf16[38,32,128]{2,1,0:T(8,128)(2,1)} %copy-done.34) | copy-start | bytes 933892
  157.8 19.3 %copy-start.39 = (bf16[38,32,128]{2,1,0:T(8,128)(2,1)S(1)}, bf16[38,32,128]{2,1,0:T(8,128)(2,1)}, u32[]{:S(2)}) copy-start(bf16[38,32,128]{2,1,0:T(8,128)(2,1)} %copy-done.37) | copy-start | bytes 933892
  157.8 24.8 %all-to-all-start.4 = ((f32[128,8,128]{2,1,0:T(8,128)}), f32[128,8,128]{2,1,0:T(8,128)S(1)}, u32[]{:S(2)}, u32[]{:S(2)}) async-start(f32[128,8,128]{2,1,0:T(8,128)} %get-tuple-element.65), calls=%async_computation.4 | async-start | bytes 1048576 | tf_op jit(solution)/shard_map/all_to_all | solution.py:465
  162.5 12.7 %collective-permute-start.10 = (bf16[34,32,128]{2,1,0:T(8,128)(2,1)}, bf16[34,32,128]{2,1,0:T(8,128)(2,1)S(1)}, u32[]{:S(2)}, u32[]{:S(2)}) collective-permute-start(bf16[34,32,128]{2,1,0:T(8,128)(2,1)} %copy-done.45), channel_id=1, source_target_pairs={{0,8},{8,16},{16,24},{24,32},{32,40},{40,48},{48,56},{56,64},{64,7... | collective-permute-start | bytes 835592 | tf_op jit(solution)/shard_map/ppermute | solution.py:456
  165.9 11.2 %collective-permute-start.11 = (bf16[34,32,128]{2,1,0:T(8,128)(2,1)}, bf16[34,32,128]{2,1,0:T(8,128)(2,1)S(1)}, u32[]{:S(2)}, u32[]{:S(2)}) collective-permute-start(bf16[34,32,128]{2,1,0:T(8,128)(2,1)} %copy-done.44), channel_id=1, source_target_pairs={{8,0},{16,8},{24,16},{32,24},{40,32},{48,40},{56,48},{64,56},{72,6... | collective-permute-start | bytes 835592 | tf_op jit(solution)/shard_map/ppermute | solution.py:461
  177.2 1.2 copy-start.33
  178.4 0.9 copy-start.49
  (7 other events, 4.8 us)

commit v2 on v1

--- a/solution.py
+++ b/solution.py
@@ -16,7 +16,6 @@
 F32 = jnp.float32
 BF16 = jnp.bfloat16
 LN2 = 0.6931471805599453
-VM = pl.BlockSpec(memory_space=pltpu.VMEM)
 SM = pl.BlockSpec(memory_space=pltpu.SMEM)
 
 
@@ -88,7 +87,7 @@
                 msg_ref[dz * C : (dz + 1) * C, 1 + 3 * k + dy, :] = group(dz, dy)
 
 
-def stats_out(h_ref, acc, start, low_ref, high_ref, msg_ref):
+def stats_out(send, h_ref, acc, start, low_ref, high_ref, msg_ref):
     center = fold(total(acc)) / (2 * ROWS * 128)
     both = twice(center)
     spread = jnp.zeros((64, 128), F32)
@@ -98,6 +97,7 @@
             spread = spread + off * off
         low_ref[y] = off[0:C].astype(BF16)
         high_ref[y] = off[C:].astype(BF16)
+    send(low_ref, high_ref)
     message((center, fold(total(spread))), msg_ref)
 
 
@@ -178,20 +178,23 @@
     g_ref[128:192, at] = from_below(values, lane).astype(BF16)
 
 
-def pack_kernel(own, cot, up_ref, down_ref):
+def pack_kernel(need, send, own, cot, up_ref, down_ref):
+    need(own, cot)
     up_ref[0:4] = own[ROWS - 4 : ROWS]
     up_ref[4:6] = cot[ROWS - 2 : ROWS]
     down_ref[0:4] = own[0:4]
     down_ref[4:6] = cot[0:2]
 
 
-def planes_kernel(own, y_low, y_high, up_ref, down_ref):
+def planes_kernel(need, send, own, y_low, y_high, up_ref, down_ref):
+    need(own, y_low, y_high)
     for part, rows, at in ((y_low, 4, 0), (own, ROWS, 4), (y_high, 4, ROWS + 4)):
         down_ref[at : at + rows] = part[0:rows, 0:C]
         up_ref[at : at + rows] = part[0:rows, C : 2 * C]
 
 
-def weights_kernel(k1, k2, w1, w2, b1, b2):
+def weights_kernel(need, send, k1, k2, w1, w2, b1, b2):
+    need(k1, k2)
     row = lax.broadcasted_iota(jnp.int32, (C, 128), 0)
     col = lax.broadcasted_iota(jnp.int32, (C, 128), 1)
     eye = jnp.where(row == col, 1.0, 0.0)[:, 0:C].astype(BF16)
@@ -225,10 +228,13 @@
                 b_ref[dz * 64 + C : dz * 64 + 64, here] = pltpu.roll(tile, C, 1).astype(BF16)
 
 
-def first_kernel(own, y_low, y_high, x_low, x_high, w, v, h, low, high, msg):
+def first_kernel(need, send, own, y_low, y_high, x_low, x_high, w, v, h, low, high, msg):
+    need(own, y_low, y_high, x_low, x_high)
     for middle, rows, at in ((y_low, 4, 0), (own, ROWS, 4), (y_high, 4, ROWS + 4)):
         for y in range(rows):
             v[at + y] = jnp.concatenate([x_low[at + y], middle[y], x_high[at + y]], axis=0)
+    send(v)
+    need(w)
     acc = [jnp.zeros((64, 128), F32)]
 
     def emit(y, values):
@@ -237,11 +243,14 @@
             acc[0] = acc[0] + values
 
     conv_rows(v, w, ROWS + 6, emit)
-    stats_out(h, acc[0], 3, low, high, msg)
-
-
-def second_kernel(cells, place, h1, x_low, x_high, r1, gb, w, v, h, low, high, msg):
+    send(h)
+    stats_out(send, h, acc[0], 3, low, high, msg)
+
+
+def second_kernel(cells, need, send, place, h1, x_low, x_high, r1, gb, w, v, h, low, high, msg):
+    need(r1, gb)
     mean, inverse, o_low, o_high = read_stats(r1, place, cells)
+    need(h1, x_low, x_high)
     scale = inverse * gb[:, 0:1]
     shift = gb[:, 1:2]
     mean2, scale2, shift2 = twice(mean), twice(scale), twice(shift)
@@ -252,6 +261,8 @@
         a_own = act((h1[y] - mean2) * scale2 + shift2)
         a_high = act(x_high[y].astype(F32) * scale + b_high)
         v[y] = masked(a_low, a_own, a_high, kept(place, y, rows, 3))
+    send(v)
+    need(w)
     acc = [jnp.zeros((64, 128), F32)]
 
     def emit(y, values):
@@ -260,10 +271,12 @@
             acc[0] = acc[0] + values
 
     conv_rows(v, w, ROWS + 4, emit)
-    stats_out(h, acc[0], 2, low, high, msg)
-
-
-def side_kernel(cells, place, h1, r1, v1, xn, x1, g, acc):
+    send(h)
+    stats_out(send, h, acc[0], 2, low, high, msg)
+
+
+def side_kernel(cells, need, send, place, h1, r1, v1, xn, x1, g, acc):
+    need(h1, r1, v1)
     mean, inverse, _, _ = read_stats(r1, place, cells)
     mean2, inverse2 = twice(mean), twice(inverse)
     lane = lanes(64)
@@ -303,8 +316,10 @@
     return y_high[2 + y - ROWS]
 
 
-def third_kernel(cells, place, h2, cot, y_low, y_high, r2, gb, xn, x1, out, t_low, t_high, msg):
+def third_kernel(cells, need, send, place, h2, cot, y_low, y_high, r2, gb, xn, x1, out, t_low, t_high, msg):
+    need(r2, gb)
     mean, inverse, _, _ = read_stats(r2, place, cells)
+    need(h2, cot, y_low, y_high)
     mean2, inverse2 = twice(mean), twice(inverse)
     gain2, bias2 = twice(gb[:, 2:3]), twice(gb[:, 3:4])
     plain = jnp.zeros((64, 128), F32)
@@ -316,10 +331,13 @@
         slope = cot[y].astype(F32) * act_slope(z)
         plain = plain + slope
         both = both + slope * normed
+    send(out)
     for y in range(ROWS + 4):
         values = cot_row(cot, y_low, y_high, y)
         t_low[y] = values[0:C]
         t_high[y] = values[C:]
+    send(t_low, t_high)
+    need(xn, x1)
 
     def ones(dz, dy):
         return jnp.broadcast_to(x1[dz * 3 + dy : dz * 3 + dy + 1, :], (C, 128))
@@ -330,11 +348,13 @@
 
 
 def fourth_kernel(
-    cells, place, h2, x_low, x_high, cot, y_low, y_high, t_low, t_high, r2, r3, h1, r1, gb,
+    cells, need, send, place, h2, x_low, x_high, cot, y_low, y_high, t_low, t_high, r2, r3, h1, r1, gb,
     v1, v2, w, slope1, low, high, msg, v, g, acc, acc1,
 ):
+    need(r2, r3, gb)
     mean, inverse, o_low, o_high = read_stats(r2, place, cells)
     nsum, plain = read_sums(r3)
+    need(h2, x_low, x_high, cot, y_low, y_high, t_low, t_high)
     gain, bias = gb[:, 2:3], gb[:, 3:4]
     lead = gain * inverse
     p_mean, n_mean = plain / cells, nsum / cells
@@ -355,8 +375,10 @@
         v[y] = masked(g_low, g_own, g_high, kept(place, y, rows, 2))
         if 2 <= y < 2 + ROWS:
             put_shifted(g, y - 2, g_own, lane)
+    need(v2)
     weight_sums(g, v2, 2, acc)
 
+    need(h1, r1, w)
     mean, inverse, _, _ = read_stats(r1, place, cells)
     mean2, inverse2 = twice(mean), twice(inverse)
     gain2, bias2 = twice(gb[:, 0:1]), twice(gb[:, 1:2])
@@ -374,13 +396,16 @@
             put_shifted(g, y - 1, slope, lane)
 
     conv_rows(v, w, ROWS + 2, emit)
+    send(slope1, low, high)
+    need(v1)
     weight_sums(g, v1, 3, acc1)
     rows_message(
         (fold(total(sums[0])), fold(total(sums[1]))), (folded(acc1), folded(acc)), msg
     )
 
 
-def owner_kernel(cells, place, r1, r3, r4, gb, msg, norms):
+def owner_kernel(cells, need, send, place, r1, r3, r4, gb, msg, norms):
+    need(r1, r3, r4, gb)
     _, inverse, _, _ = read_stats(r1, place, cells)
     nsum, plain = read_sums(r4)
     mine = lax.broadcasted_iota(jnp.int32, (C, 1), 0) == place[6]
@@ -401,7 +426,8 @@
         norms[2 * k + 1 : 2 * k + 2] = row[:, C : 2 * C] * scale
 
 
-def finish_kernel(parts, one, two):
+def finish_kernel(need, send, parts, one, two):
+    need(parts)
     for dz in range(3):
         for dy in range(3):
             for k, out in enumerate((one, two)):
@@ -411,10 +437,12 @@
 
 
 def fifth_kernel(
-    cells, place, slope1, s_low, s_high, h1, x_low, x_high, r1, r4, gb, w, out, v
+    cells, need, send, place, slope1, s_low, s_high, h1, x_low, x_high, r1, r4, gb, w, out, v
 ):
+    need(r1, r4, gb)
     mean, inverse, o_low, o_high = read_stats(r1, place, cells)
     nsum, plain = read_sums(r4)
+    need(slope1, s_low, s_high, h1, x_low, x_high)
     lead = gb[:, 0:1] * inverse
     p_mean, n_mean = plain / cells, nsum / cells
     mean2, inverse2, lead2 = twice(mean), twice(inverse), twice(lead)
@@ -429,6 +457,8 @@
         g_high = lead * (s_high[y].astype(F32) - p_mean - n_high * n_mean)
         v[y] = masked(g_low, g_own, g_high, kept(place, y, rows, 1))
 
+    need(w)
+
     def emit(y, values):
         out[y] = values.astype(BF16)
 
@@ -436,14 +466,60 @@
 
 
 def call(kernel, ins, outs, name, scratch=(), smem_first=True):
-    specs = [SM if (k == 0 and smem_first) else VM for k in range(len(ins))]
+    lead = 1 if smem_first else 0
+    count_in, count_out = len(ins) - lead, len(outs)
+
+    def body(*refs):
+        first, rest = refs[:lead], refs[lead:]
+        parts = []
+        for size in (count_in, count_out, count_in, count_out, 2):
+            parts.append(rest[:size])
+            rest = rest[size:]
+        sources, targets, in_bufs, out_bufs, (in_sems, out_sems) = parts
+        arriving = [
+            pltpu.make_async_copy(a, b, in_sems.at[k])
+            for k, (a, b) in enumerate(zip(sources, in_bufs))
+        ]
+        leaving = [
+            pltpu.make_async_copy(a, b, out_sems.at[k])
+            for k, (a, b) in enumerate(zip(out_bufs, targets))
+        ]
+        waiting, held = list(range(count_in)), list(range(count_out))
+        for copy in arriving:
+            copy.start()
+
+        def need(*wanted):
+            for k in list(waiting):
+                if any(in_bufs[k] is ref for ref in wanted):
+                    arriving[k].wait()
+                    waiting.remove(k)
+
+        def send(*ready):
+            for k in list(held):
+                if any(out_bufs[k] is ref for ref in ready):
+                    leaving[k].start()
+                    held.remove(k)
+
+        kernel(need, send, *first, *in_bufs, *out_bufs, *rest)
+        send(*out_bufs)
+        need(*in_bufs)
+        for copy in leaving:
+            copy.wait()
+
+    far = pl.BlockSpec(memory_space=pltpu.HBM)
     return pl.pallas_call(
-        kernel,
+        body,
         out_shape=outs,
-        in_specs=specs,
-        out_specs=[VM] * len(outs),
-        scratch_shapes=list(scratch),
-        compiler_params=pltpu.CompilerParams(vmem_limit_bytes=24 * 1024 * 1024),
+        in_specs=[SM] * lead + [far] * count_in,
+        out_specs=[far] * count_out,
+        scratch_shapes=[
+            *[pltpu.VMEM(a.shape, a.dtype) for a in ins[lead:]],
+            *[pltpu.VMEM(a.shape, a.dtype) for a in outs],
+            pltpu.SemaphoreType.DMA((count_in,)),
+            pltpu.SemaphoreType.DMA((count_out,)),
+            *scratch,
+        ],
+        compiler_params=pltpu.CompilerParams(vmem_limit_bytes=56 * 1024 * 1024),
         cost_estimate=pl.CostEstimate(
             flops=2_000_000_000, bytes_accessed=6_000_000, transcendentals=0
         ),

time: 185 us -> 191 us (1.032)
  Pallas kernels: 21.6 us -> 48.3 us
  local copies, waits for them, and re-layouts: 34.7 us -> 13.2 us
    pallas_call x11, Pallas kernels: 21.6 us -> 48.3 us  [call(): pl.pallas_call(body, out_shape=outs, in_specs=[SM] * lead + [far] * count...]
    unnamed x110 -> x52, local copies, waits for them, and re-layouts: 30.4 us -> 5.23 us
    ppermute x6, waiting for transfers between devices: 12.2 us -> 14.8 us  [down(): return lax.ppermute(values, axes, [(i + 1, i) for i in range(count - 1)])]
    all_to_all x4, waiting for transfers between devices: 14.8 us -> 12.5 us  [share(): return lax.all_to_all(msg, ALL, 0, 0, tiled=True)]
  transfers between devices with their start and end apart: 16 -> 16, of which waited for: 11 -> 11; matrix products, arithmetic and copies ran while one was open for 1% -> 2% of each run, Pallas kernels for 3% -> 7%
where the time goes in v2:
time: 191 us; the launch traced here: 190 us
  starting transfers between devices  59.2 us (31%)
  Pallas kernels  48.3 us (25%)
  waiting for transfers between devices  42.6 us (22%)
  blocking collectives  25.4 us (13%)
  local copies, waits for them, and re-layouts  13.2 us (7%)
    pallas_call x11, Pallas kernels, call(): pl.pallas_call(body, out_shape=outs, in_specs=[SM] * lead + [far] * count...  48.3 us
    all_to_all x4, starting transfers between devices, share(): return lax.all_to_all(msg, ALL, 0, 0, tiled=True)  28.6 us
    all_to_all x1, blocking collectives, share(): return lax.all_to_all(msg, ALL, 0, 0, tiled=True)  25.4 us
    ppermute x6, starting transfers between devices, up(): return lax.ppermute(values, axes, [(i, i + 1) for i in range(count - 1)])  22 us
    ppermute x6, waiting for transfers between devices, up(): return lax.ppermute(values, axes, [(i, i + 1) for i in range(count - 1)])  15.3 us
    ppermute x6, waiting for transfers between devices, down(): return lax.ppermute(values, axes, [(i + 1, i) for i in range(count - 1)])  14.8 us
    all_to_all x4, waiting for transfers between devices, share(): return lax.all_to_all(msg, ALL, 0, 0, tiled=True)  12.5 us
    ppermute x6, starting transfers between devices, down(): return lax.ppermute(values, axes, [(i + 1, i) for i in range(count - 1)])  8.56 us
  transfers between devices with their start and end apart: 16, of which 11 were waited for; matrix products, arithmetic and copies ran while one was open for 2% of the time, Pallas kernels for 7%

profile of v2, /device:TPU:1, one launch (start us, length us, event | category | flops | bytes accessed | tf_op | source)
XLA Modules:
  0.0 189.9 jit_solution(3368221734195277004)
XLA Ops:
  0.6 2.2 %copy.21 = bf16[32,2,32,128]{3,2,1,0:T(8,128)(2,1)} copy(bf16[32,2,32,128]{3,0,1,2:T(8,128)(2,1)} %bitcast.46) | data formatting | bytes 1048576 | tf_op jit(solution)/shard_map/transpose | solution.py:555
  2.9 1.1 copy.22
  4.0 1.9 %pack.1 = (bf16[6,64,128]{2,1,0:T(8,128)(2,1)}, bf16[6,64,128]{2,1,0:T(8,128)(2,1)}) custom-call(bf16[32,64,128]{2,1,0:T(8,128)(2,1)} %bitcast.49, bf16[32,64,128]{2,1,0:T(8,128)(2,1)} %bitcast.43), custom_call_target="tpu_custom_call" | custom-call | flops 2000000000 | bytes 6000000 | tf_op jit(solution)/shard_map/pack/pallas_call | solution.py:510
  5.9 4.9 %collective-permute-start = (bf16[6,64,128]{2,1,0:T(8,128)(2,1)}, bf16[6,64,128]{2,1,0:T(8,128)(2,1)S(1)}, u32[]{:S(2)}, u32[]{:S(2)}) collective-permute-start(bf16[6,64,128]{2,1,0:T(8,128)(2,1)} %get-tuple-element.37), channel_id=1, source_target_pairs={{0,1},{1,2},{2,3},{3,4},{4,5},{5,6},{6,7},{8,9},{9,10},{10,11},{11... | collective-permute-start | bytes 294920 | tf_op jit(solution)/shard_map/ppermute | solution.py:532
  10.9 1.9 %collective-permute-start.1 = (bf16[6,64,128]{2,1,0:T(8,128)(2,1)}, bf16[6,64,128]{2,1,0:T(8,128)(2,1)S(1)}, u32[]{:S(2)}, u32[]{:S(2)}) collective-permute-start(bf16[6,64,128]{2,1,0:T(8,128)(2,1)} %get-tuple-element.38), channel_id=1, source_target_pairs={{1,0},{2,1},{3,2},{4,3},{5,4},{6,5},{7,6},{9,8},{10,9},{11,10},{12... | collective-permute-start | bytes 294920 | tf_op jit(solution)/shard_map/ppermute | solution.py:537
  12.8 0.0 collective-permute-done.refs_1_.refs_3_.refs_5_
  12.8 4.2 %collective-permute-done.1.refs_2_.refs_4_.refs_6_ = bf16[6,64,128]{2,1,0:T(8,128)(2,1)S(1)} collective-permute-done((bf16[6,64,128]{2,1,0:T(8,128)(2,1)}, bf16[6,64,128]{2,1,0:T(8,128)(2,1)S(1)}, u32[]{:S(2)}, u32[]{:S(2)}) %collective-permute-start.1) | collective-permute-done | bytes 98336 | tf_op jit(solution)/shard_map/ppermute | solution.py:537
  17.0 0.0 copy-done.10
  17.0 0.6 copy-done.11
  17.7 2.0 %planes.1 = (bf16[40,32,128]{2,1,0:T(8,128)(2,1)}, bf16[40,32,128]{2,1,0:T(8,128)(2,1)}) custom-call(bf16[32,64,128]{2,1,0:T(8,128)(2,1)} %bitcast.50, bf16[6,64,128]{2,1,0:T(8,128)(2,1)} %copy-done.10, bf16[6,64,128]{2,1,0:T(8,128)(2,1)} %copy-done.11), custom_call_target="tpu_custom_call" | custom-call | flops 2000000000 | bytes 6000000 | tf_op jit(solution)/shard_map/planes/pallas_call | solution.py:510
  19.6 3.2 %collective-permute-start.2 = (bf16[40,32,128]{2,1,0:T(8,128)(2,1)}, bf16[40,32,128]{2,1,0:T(8,128)(2,1)S(1)}, u32[]{:S(2)}, u32[]{:S(2)}) collective-permute-start(bf16[40,32,128]{2,1,0:T(8,128)(2,1)} %get-tuple-element.39), channel_id=1, source_target_pairs={{0,8},{8,16},{16,24},{24,32},{32,40},{40,48},{48,56},{56,64},{64,7... | collective-permute-start | bytes 983048 | tf_op jit(solution)/shard_map/ppermute | solution.py:532
  22.9 1.3 collective-permute-start.3
  24.2 2.4 %weights.1 = (bf16[192,384]{1,0:T(8,128)(2,1)}, bf16[192,384]{1,0:T(8,128)(2,1)}, bf16[192,384]{1,0:T(8,128)(2,1)}, bf16[192,384]{1,0:T(8,128)(2,1)}) custom-call(bf16[27,32,32]{2,1,0:T(8,128)(2,1)} %bitcast.68, bf16[27,32,32]{2,1,0:T(8,128)(2,1)} %bitcast.69), custom_call_target="tpu_custom_call" | custom-call | flops 2000000000 | bytes 6000000 | tf_op jit(solution)/shard_map/weights/pallas_call | solution.py:510
  26.6 1.9 collective-permute-done.2.refs_3_
  28.4 4.0 %collective-permute-done.3.refs_4_ = bf16[40,32,128]{2,1,0:T(8,128)(2,1)S(1)} collective-permute-done((bf16[40,32,128]{2,1,0:T(8,128)(2,1)}, bf16[40,32,128]{2,1,0:T(8,128)(2,1)S(1)}, u32[]{:S(2)}, u32[]{:S(2)}) %collective-permute-start.3) | collective-permute-done | bytes 327712 | tf_op jit(solution)/shard_map/ppermute | solution.py:537
  32.4 0.7 copy-done.17
  33.2 4.6 %conv_one.1 = (bf16[40,128,128]{2,1,0:T(8,128)(2,1)}, f32[38,64,128]{2,1,0:T(8,128)}, bf16[38,32,128]{2,1,0:T(8,128)(2,1)}, bf16[38,32,128]{2,1,0:T(8,128)(2,1)}, f32[128,128]{1,0:T(8,128)}) custom-call(bf16[32,64,128]{2,1,0:T(8,128)(2,1)} %bitcast.51, bf16[6,64,128]{2,1,0:T(8,128)(2,1)} %copy-done.10, bf16[6,64,128]{2,1,0:T(8,128)(2,1)} %copy-done.11, ...), custom_call_target="tpu_custom_call" | custom-call | flops 2000000000 | bytes 6000000 | tf_op jit(solution)/shard_map/conv_one/pallas_call | solution.py:510
  37.7 3.2 %collective-permute-start.4 = (bf16[38,32,128]{2,1,0:T(8,128)(2,1)}, bf16[38,32,128]{2,1,0:T(8,128)(2,1)S(1)}, u32[]{:S(2)}, u32[]{:S(2)}) collective-permute-start(bf16[38,32,128]{2,1,0:T(8,128)(2,1)} %get-tuple-element.43), channel_id=1, source_target_pairs={{0,8},{8,16},{16,24},{24,32},{32,40},{40,48},{48,56},{56,64},{64,7... | collective-permute-start | bytes 933896 | tf_op jit(solution)/shard_map/ppermute | solution.py:532
  41.0 1.3 collective-permute-start.5
  42.3 13.9 %all-to-all-start = ((f32[128,1,128]{2,1,0:T(1,128)}), f32[128,1,128]{2,1,0:T(1,128)S(1)}, u32[]{:S(2)}, u32[]{:S(2)}) async-start(f32[128,1,128]{2,1,0:T(1,128)} %bitcast.62), calls=%async_computation | async-start | bytes 131072 | tf_op jit(solution)/shard_map/all_to_all | solution.py:541
  56.2 0.7 copy.24.refs_5_.refs_6_.refs_13_.refs_9_.refs_4_
  56.9 0.6 stack.62.refs_0_
  57.5 8.0 %all-to-all-done = f32[128,1,128]{2,1,0:T(1,128)S(1)} async-done(((f32[128,1,128]{2,1,0:T(1,128)}), f32[128,1,128]{2,1,0:T(1,128)S(1)}, u32[]{:S(2)}, u32[]{:S(2)}) %all-to-all-start) | async-done | bytes 65568 | tf_op jit(solution)/shard_map/all_to_all | solution.py:541
  65.5 0.0 collective-permute-done.4.refs_2_.refs_5_
  65.5 0.0 collective-permute-done.5.refs_3_.refs_6_
  65.6 0.0 copy-start.19
  65.6 0.6 copy-done.8
  66.2 0.1 copy-done.18
  66.3 0.1 copy-done.19
  66.4 6.6 %conv_two.1 = (bf16[38,128,128]{2,1,0:T(8,128)(2,1)}, f32[36,64,128]{2,1,0:T(8,128)}, bf16[36,32,128]{2,1,0:T(8,128)(2,1)}, bf16[36,32,128]{2,1,0:T(8,128)(2,1)}, f32[128,128]{1,0:T(8,128)}) custom-call(s32[7]{0:T(128)} %stack.62.refs_0_, f32[38,64,128]{2,1,0:T(8,128)} %get-tuple-element.42.refs_1_.refs_11_.refs_4_, bf16[38,32,128]{2,1,0:T(8,128)(2,1)} %copy-done.18, ...), custom_call_target="tpu_custom_call" | custom-call | flops 2000000000 | bytes 6000000 | tf_op jit(solution)/shard_map/conv_two/pallas_call | solution.py:510
  73.0 4.8 %all-to-all-start.1 = ((f32[128,1,128]{2,1,0:T(1,128)}), f32[128,1,128]{2,1,0:T(1,128)S(1)}, u32[]{:S(2)}, u32[]{:S(2)}) async-start(f32[128,1,128]{2,1,0:T(1,128)} %bitcast.63), calls=%async_computation.1 | async-start | bytes 131072 | tf_op jit(solution)/shard_map/all_to_all | solution.py:541
  77.8 4.7 %normed_features.1 = (f32[9,32,128]{2,1,0:T(8,128)}, f32[16,128]{1,0:T(8,128)}) custom-call(s32[7]{0:T(128)} %stack.62.refs_0_, f32[38,64,128]{2,1,0:T(8,128)} %get-tuple-element.42.refs_1_.refs_11_.refs_4_, f32[128,128]{1,0:T(8,128)} %bitcast.56, bf16[40,128,128]{2,1,0:T(8,128)(2,1)} %get-tuple-element.49.refs_3_.refs_14_), custom_call_target="tpu_custom_call" | custom-call | flops 2000000000 | bytes 6000000 | tf_op jit(solution)/shard_map/normed_features/pallas_call | solution.py:510
  82.5 4.5 %all-to-all-done.1 = f32[128,1,128]{2,1,0:T(1,128)S(1)} async-done(((f32[128,1,128]{2,1,0:T(1,128)}), f32[128,1,128]{2,1,0:T(1,128)S(1)}, u32[]{:S(2)}, u32[]{:S(2)}) %all-to-all-start.1) | async-done | bytes 65568 | tf_op jit(solution)/shard_map/all_to_all | solution.py:541
  87.1 0.6 copy-done.9
  87.7 4.8 %slope_two.1 = (bf16[32,64,128]{2,1,0:T(8,128)(2,1)}, bf16[36,32,128]{2,1,0:T(8,128)(2,1)}, bf16[36,32,128]{2,1,0:T(8,128)(2,1)}, f32[128,8,128]{2,1,0:T(8,128)}) custom-call(s32[7]{0:T(128)} %stack.62.refs_0_, f32[36,64,128]{2,1,0:T(8,128)} %get-tuple-element.47.refs_1_, bf16[32,64,128]{2,1,0:T(8,128)(2,1)} %bitcast.44, bf16[6,64,128]{2,1,0:T(8,128)(2,1)} %copy-done.10, ...), custom_call_target="tpu_custom_call" | custom-call | flops 2000000000 | bytes 6000000 | tf_op jit(solution)/shard_map/slope_two/pallas_call | solution.py:510
  92.5 5.2 %all-to-all-start.2 = ((f32[128,8,128]{2,1,0:T(8,128)}), f32[128,8,128]{2,1,0:T(8,128)S(1)}, u32[]{:S(2)}, u32[]{:S(2)}) async-start(f32[128,8,128]{2,1,0:T(8,128)} %get-tuple-element.57), calls=%async_computation.2 | async-start | bytes 1048576 | tf_op jit(solution)/shard_map/all_to_all | solution.py:541
  97.8 3.3 %collective-permute-start.6 = (bf16[36,32,128]{2,1,0:T(8,128)(2,1)S(1)}, bf16[36,32,128]{2,1,0:T(8,128)(2,1)S(1)}, u32[]{:S(2)}, u32[]{:S(2)}) collective-permute-start(bf16[36,32,128]{2,1,0:T(8,128)(2,1)S(1)} %copy-done.21), channel_id=1, source_target_pairs={{0,8},{8,16},{16,24},{24,32},{32,40},{40,48},{48,56},{56,64},{64,7... | collective-permute-start | bytes 884744 | tf_op jit(solution)/shard_map/ppermute | solution.py:532
  101.1 0.0 copy-done.20
  101.1 1.3 collective-permute-start.7
  102.4 4.0 %collective-permute-start.8 = (bf16[36,32,128]{2,1,0:T(8,128)(2,1)}, bf16[36,32,128]{2,1,0:T(8,128)(2,1)S(1)}, u32[]{:S(2)}, u32[]{:S(2)}) collective-permute-start(bf16[36,32,128]{2,1,0:T(8,128)(2,1)} %get-tuple-element.55), channel_id=1, source_target_pairs={{0,8},{8,16},{16,24},{24,32},{32,40},{40,48},{48,56},{56,64},{64,7... | collective-permute-start | bytes 884744 | tf_op jit(solution)/shard_map/ppermute | solution.py:532
  106.4 1.5 collective-permute-start.9
  107.9 2.6 %collective-permute-done.6.refs_2_ = bf16[36,32,128]{2,1,0:T(8,128)(2,1)S(1)} collective-permute-done((bf16[36,32,128]{2,1,0:T(8,128)(2,1)S(1)}, bf16[36,32,128]{2,1,0:T(8,128)(2,1)S(1)}, u32[]{:S(2)}, u32[]{:S(2)}) %collective-permute-start.6) | collective-permute-done | bytes 294944 | tf_op jit(solution)/shard_map/ppermute | solution.py:532
  110.5 2.2 %collective-permute-done.7.refs_3_ = bf16[36,32,128]{2,1,0:T(8,128)(2,1)S(1)} collective-permute-done((bf16[36,32,128]{2,1,0:T(8,128)(2,1)S(1)}, bf16[36,32,128]{2,1,0:T(8,128)(2,1)S(1)}, u32[]{:S(2)}, u32[]{:S(2)}) %collective-permute-start.7) | collective-permute-done | bytes 294944 | tf_op jit(solution)/shard_map/ppermute | solution.py:537
  112.7 4.2 %collective-permute-done.8.refs_7_ = bf16[36,32,128]{2,1,0:T(8,128)(2,1)S(1)} collective-permute-done((bf16[36,32,128]{2,1,0:T(8,128)(2,1)}, bf16[36,32,128]{2,1,0:T(8,128)(2,1)S(1)}, u32[]{:S(2)}, u32[]{:S(2)}) %collective-permute-start.8) | collective-permute-done | bytes 294944 | tf_op jit(solution)/shard_map/ppermute | solution.py:532
  116.9 2.1 %collective-permute-done.9.refs_8_ = bf16[36,32,128]{2,1,0:T(8,128)(2,1)S(1)} collective-permute-done((bf16[36,32,128]{2,1,0:T(8,128)(2,1)}, bf16[36,32,128]{2,1,0:T(8,128)(2,1)S(1)}, u32[]{:S(2)}, u32[]{:S(2)}) %collective-permute-start.9) | collective-permute-done | bytes 294944 | tf_op jit(solution)/shard_map/ppermute | solution.py:537
  119.0 0.0 all-to-all-done.2.refs_10_.refs_2_
  119.0 0.7 copy-done.7
  119.7 0.2 copy-done
  119.9 10.2 %back_two.1 = (f32[34,64,128]{2,1,0:T(8,128)}, bf16[34,32,128]{2,1,0:T(8,128)(2,1)}, bf16[34,32,128]{2,1,0:T(8,128)(2,1)}, f32[128,8,128]{2,1,0:T(8,128)}) custom-call(s32[7]{0:T(128)} %stack.62.refs_0_, f32[36,64,128]{2,1,0:T(8,128)} %get-tuple-element.47.refs_1_, bf16[36,32,128]{2,1,0:T(8,128)(2,1)} %copy-done.4, bf16[36,32,128]{2,1,0:T(8,128)(2,1)} %copy-done.5, ...), custom_call_target="tpu_custom_call" | custom-call | flops 2000000000 | bytes 6000000 | tf_op jit(solution)/shard_map/back_two/pallas_call | solution.py:510
  130.1 25.4 %all_to_all.37.refs_8_.refs_3_ = f32[128,8,128]{2,1,0:T(8,128)} all-to-all(f32[128,8,128]{2,1,0:T(8,128)} %get-tuple-element.63), channel_id=1, replica_groups=mesh['gx_0'=4,'gx_1'=4,'gy_0'=4,'gy_1'=2] {'gx_0','gx_1','gy_0','gy_1'}, dimensions={0} | all-to-all | bytes 1048576 | tf_op jit(solution)/shard_map/all_to_all | solution.py:541
  155.5 3.3 %own_rows.1 = (f32[128,8,128]{2,1,0:T(8,128)}, f32[4,32]{1,0:T(4,128)}) custom-call(s32[7]{0:T(128)} %stack.62.refs_0_, f32[128,128]{1,0:T(8,128)} %bitcast.58, f32[128,8,128]{2,1,0:T(8,128)} %copy-done, f32[128,8,128]{2,1,0:T(8,128)} %all_to_all.37.refs_8_.refs_3_, f32[32,4]{1,0:T(8,128)} %copy.24.refs_5_.refs_6_.refs_13_.refs_9_.refs_4_), custom_call_target="tpu_custom_call" | custom-call | flops 2000000000 | bytes 6000000 | tf_op jit(solution)/shard_map/own_rows/pallas_call | solution.py:510
  158.8 0.0 copy-start.2
  158.8 4.7 %all-to-all-start.4 = ((f32[128,8,128]{2,1,0:T(8,128)}), f32[128,8,128]{2,1,0:T(8,128)S(1)}, u32[]{:S(2)}, u32[]{:S(2)}) async-start(f32[128,8,128]{2,1,0:T(8,128)} %get-tuple-element.65), calls=%async_computation.4 | async-start | bytes 1048576 | tf_op jit(solution)/shard_map/all_to_all | solution.py:541
  163.5 3.4 %collective-permute-start.10 = (bf16[34,32,128]{2,1,0:T(8,128)(2,1)S(1)}, bf16[34,32,128]{2,1,0:T(8,128)(2,1)S(1)}, u32[]{:S(2)}, u32[]{:S(2)}) collective-permute-start(bf16[34,32,128]{2,1,0:T(8,128)(2,1)S(1)} %copy-done.23), channel_id=1, source_target_pairs={{0,8},{8,16},{16,24},{24,32},{32,40},{40,48},{48,56},{56,64},{64,7... | collective-permute-start | bytes 835592 | tf_op jit(solution)/shard_map/ppermute | solution.py:532
  166.9 1.3 collective-permute-start.11
  168.2 1.1 copy.35
  169.3 6.6 %collective-permute-done.10.refs_2_ = bf16[34,32,128]{2,1,0:T(8,128)(2,1)S(1)} collective-permute-done((bf16[34,32,128]{2,1,0:T(8,128)(2,1)S(1)}, bf16[34,32,128]{2,1,0:T(8,128)(2,1)S(1)}, u32[]{:S(2)}, u32[]{:S(2)}) %collective-permute-start.10) | collective-permute-done | bytes 278560 | tf_op jit(solution)/shard_map/ppermute | solution.py:532
  175.9 2.3 %collective-permute-done.11.refs_3_ = bf16[34,32,128]{2,1,0:T(8,128)(2,1)S(1)} collective-permute-done((bf16[34,32,128]{2,1,0:T(8,128)(2,1)S(1)}, bf16[34,32,128]{2,1,0:T(8,128)(2,1)S(1)}, u32[]{:S(2)}, u32[]{:S(2)}) %collective-permute-start.11) | collective-permute-done | bytes 278560 | tf_op jit(solution)/shard_map/ppermute | solution.py:537
  178.2 0.7 copy-done.25
  178.9 5.7 %back_one.1 = bf16[32,64,128]{2,1,0:T(8,128)(2,1)} custom-call(s32[7]{0:T(128)} %stack.62.refs_0_, f32[34,64,128]{2,1,0:T(8,128)} %get-tuple-element.60.refs_1_, bf16[34,32,128]{2,1,0:T(8,128)(2,1)} %copy-done.24, bf16[34,32,128]{2,1,0:T(8,128)(2,1)} %copy-done.25, f32[38,64,128]{2,1,0:T(8,128)} %get-tuple-element.42.refs_1_.refs_11_.refs_4_, ...), custom_call_target="tpu_custom_call" | custom-call | flops 2000000000 | bytes 6000000 | tf_op jit(solution)/shard_map/back_one/pallas_call | solution.py:510
  184.6 2.2 %copy.34 = bf16[32,2,32,128]{3,0,1,2:T(8,128)(2,1)} copy(bf16[32,2,32,128]{3,2,1,0:T(8,128)(2,1)} %bitcast.54) | data formatting | bytes 1048576 | tf_op jit(solution)/shard_map/reshape | solution.py:643
  186.8 0.0 all-to-all-done.4.refs_0_
  186.8 0.8 copy-done.3
  187.6 2.2 %finish.1 = (f32[27,32,32]{2,1,0:T(8,128)}, f32[27,32,32]{2,1,0:T(8,128)}) custom-call(f32[128,8,128]{2,1,0:T(8,128)} %copy-done.3), custom_call_target="tpu_custom_call" | custom-call | flops 2000000000 | bytes 6000000 | tf_op jit(solution)/shard_map/finish/pallas_call | solution.py:510
  (39 shorter events, 0.1 us)
Async XLA Ops:
  0.6 2.2 %copy-start.1 = (bf16[32,2,32,128]{3,2,1,0:T(8,128)(2,1)S(1)}, bf16[32,2,32,128]{3,2,1,0:T(8,128)(2,1)}, u32[]{:S(2)}) copy-start(bf16[32,2,32,128]{3,2,1,0:T(8,128)(2,1)} %param.15) | copy-start | bytes 1572868
  5.9 6.9 %collective-permute-start = (bf16[6,64,128]{2,1,0:T(8,128)(2,1)}, bf16[6,64,128]{2,1,0:T(8,128)(2,1)S(1)}, u32[]{:S(2)}, u32[]{:S(2)}) collective-permute-start(bf16[6,64,128]{2,1,0:T(8,128)(2,1)} %get-tuple-element.37), channel_id=1, source_target_pairs={{0,1},{1,2},{2,3},{3,4},{4,5},{5,6},{6,7},{8,9},{9,10},{10,11},{11... | collective-permute-start | bytes 294920 | tf_op jit(solution)/shard_map/ppermute | solution.py:532
  10.9 6.1 %collective-permute-start.1 = (bf16[6,64,128]{2,1,0:T(8,128)(2,1)}, bf16[6,64,128]{2,1,0:T(8,128)(2,1)S(1)}, u32[]{:S(2)}, u32[]{:S(2)}) collective-permute-start(bf16[6,64,128]{2,1,0:T(8,128)(2,1)} %get-tuple-element.38), channel_id=1, source_target_pairs={{1,0},{2,1},{3,2},{4,3},{5,4},{6,5},{7,6},{9,8},{10,9},{11,10},{12... | collective-permute-start | bytes 294920 | tf_op jit(solution)/shard_map/ppermute | solution.py:537
  12.8 4.2 %copy-start.10 = (bf16[6,64,128]{2,1,0:T(8,128)(2,1)}, bf16[6,64,128]{2,1,0:T(8,128)(2,1)S(1)}, u32[]{:S(2)}) copy-start(bf16[6,64,128]{2,1,0:T(8,128)(2,1)S(1)} %collective-permute-done.refs_1_.refs_3_.refs_5_) | copy-start | bytes 294916
  17.0 0.6 copy-start.11
  19.6 8.8 %collective-permute-start.2 = (bf16[40,32,128]{2,1,0:T(8,128)(2,1)}, bf16[40,32,128]{2,1,0:T(8,128)(2,1)S(1)}, u32[]{:S(2)}, u32[]{:S(2)}) collective-permute-start(bf16[40,32,128]{2,1,0:T(8,128)(2,1)} %get-tuple-element.39), channel_id=1, source_target_pairs={{0,8},{8,16},{16,24},{24,32},{32,40},{40,48},{48,56},{56,64},{64,7... | collective-permute-start | bytes 983048 | tf_op jit(solution)/shard_map/ppermute | solution.py:532
  22.9 9.6 %collective-permute-start.3 = (bf16[40,32,128]{2,1,0:T(8,128)(2,1)}, bf16[40,32,128]{2,1,0:T(8,128)(2,1)S(1)}, u32[]{:S(2)}, u32[]{:S(2)}) collective-permute-start(bf16[40,32,128]{2,1,0:T(8,128)(2,1)} %get-tuple-element.40), channel_id=1, source_target_pairs={{8,0},{16,8},{24,16},{32,24},{40,32},{48,40},{56,48},{64,56},{72,6... | collective-permute-start | bytes 983048 | tf_op jit(solution)/shard_map/ppermute | solution.py:537
  28.4 4.0 %copy-start.16 = (bf16[40,32,128]{2,1,0:T(8,128)(2,1)}, bf16[40,32,128]{2,1,0:T(8,128)(2,1)S(1)}, u32[]{:S(2)}) copy-start(bf16[40,32,128]{2,1,0:T(8,128)(2,1)S(1)} %collective-permute-done.2.refs_3_) | copy-start | bytes 983044
  32.4 0.7 copy-start.17
  33.1 23.1 %copy-start.12 = (f32[32]{0:T(128)S(1)}, f32[32]{0:T(128)}, u32[]{:S(2)}) copy-start(f32[32]{0:T(128)} %param.14) | copy-start | bytes 388
  33.1 23.1 %copy-start.13 = (f32[32]{0:T(128)S(1)}, f32[32]{0:T(128)}, u32[]{:S(2)}) copy-start(f32[32]{0:T(128)} %param.13) | copy-start | bytes 388
  33.1 23.1 %copy-start.14 = (f32[32]{0:T(128)S(1)}, f32[32]{0:T(128)}, u32[]{:S(2)}) copy-start(f32[32]{0:T(128)} %param.11) | copy-start | bytes 388
  33.1 23.1 %copy-start.15 = (f32[32]{0:T(128)S(1)}, f32[32]{0:T(128)}, u32[]{:S(2)}) copy-start(f32[32]{0:T(128)} %param.10) | copy-start | bytes 388
  37.7 27.8 %collective-permute-start.4 = (bf16[38,32,128]{2,1,0:T(8,128)(2,1)}, bf16[38,32,128]{2,1,0:T(8,128)(2,1)S(1)}, u32[]{:S(2)}, u32[]{:S(2)}) collective-permute-start(bf16[38,32,128]{2,1,0:T(8,128)(2,1)} %get-tuple-element.43), channel_id=1, source_target_pairs={{0,8},{8,16},{16,24},{24,32},{32,40},{40,48},{48,56},{56,64},{64,7... | collective-permute-start | bytes 933896 | tf_op jit(solution)/shard_map/ppermute | solution.py:532
  41.0 24.6 %collective-permute-start.5 = (bf16[38,32,128]{2,1,0:T(8,128)(2,1)}, bf16[38,32,128]{2,1,0:T(8,128)(2,1)S(1)}, u32[]{:S(2)}, u32[]{:S(2)}) collective-permute-start(bf16[38,32,128]{2,1,0:T(8,128)(2,1)} %get-tuple-element.44), channel_id=1, source_target_pairs={{8,0},{16,8},{24,16},{32,24},{40,32},{48,40},{56,48},{64,56},{72,6... | collective-permute-start | bytes 933896 | tf_op jit(solution)/shard_map/ppermute | solution.py:537
  42.3 23.3 %all-to-all-start = ((f32[128,1,128]{2,1,0:T(1,128)}), f32[128,1,128]{2,1,0:T(1,128)S(1)}, u32[]{:S(2)}, u32[]{:S(2)}) async-start(f32[128,1,128]{2,1,0:T(1,128)} %bitcast.62), calls=%async_computation | async-start | bytes 131072 | tf_op jit(solution)/shard_map/all_to_all | solution.py:541
  65.5 0.6 copy-start.8
  65.5 0.7 copy-start.18
  65.6 0.8 copy-start.19
  73.0 14.1 %all-to-all-start.1 = ((f32[128,1,128]{2,1,0:T(1,128)}), f32[128,1,128]{2,1,0:T(1,128)S(1)}, u32[]{:S(2)}, u32[]{:S(2)}) async-start(f32[128,1,128]{2,1,0:T(1,128)} %bitcast.63), calls=%async_computation.1 | async-start | bytes 131072 | tf_op jit(solution)/shard_map/all_to_all | solution.py:541
  87.1 0.6 copy-start.9
  87.7 10.1 %copy-start.21 = (bf16[36,32,128]{2,1,0:T(8,128)(2,1)S(1)}, bf16[36,32,128]{2,1,0:T(8,128)(2,1)}, u32[]{:S(2)}) copy-start(bf16[36,32,128]{2,1,0:T(8,128)(2,1)} %get-tuple-element.53) | copy-start | bytes 884740
  87.7 13.4 %copy-start.20 = (bf16[36,32,128]{2,1,0:T(8,128)(2,1)S(1)}, bf16[36,32,128]{2,1,0:T(8,128)(2,1)}, u32[]{:S(2)}) copy-start(bf16[36,32,128]{2,1,0:T(8,128)(2,1)} %get-tuple-element.54) | copy-start | bytes 884740
  92.5 26.5 %all-to-all-start.2 = ((f32[128,8,128]{2,1,0:T(8,128)}), f32[128,8,128]{2,1,0:T(8,128)S(1)}, u32[]{:S(2)}, u32[]{:S(2)}) async-start(f32[128,8,128]{2,1,0:T(8,128)} %get-tuple-element.57), calls=%async_computation.2 | async-start | bytes 1048576 | tf_op jit(solution)/shard_map/all_to_all | solution.py:541
  97.8 12.7 %collective-permute-start.6 = (bf16[36,32,128]{2,1,0:T(8,128)(2,1)S(1)}, bf16[36,32,128]{2,1,0:T(8,128)(2,1)S(1)}, u32[]{:S(2)}, u32[]{:S(2)}) collective-permute-start(bf16[36,32,128]{2,1,0:T(8,128)(2,1)S(1)} %copy-done.21), channel_id=1, source_target_pairs={{0,8},{8,16},{16,24},{24,32},{32,40},{40,48},{48,56},{56,64},{64,7... | collective-permute-start | bytes 884744 | tf_op jit(solution)/shard_map/ppermute | solution.py:532
  101.1 11.6 %collective-permute-start.7 = (bf16[36,32,128]{2,1,0:T(8,128)(2,1)S(1)}, bf16[36,32,128]{2,1,0:T(8,128)(2,1)S(1)}, u32[]{:S(2)}, u32[]{:S(2)}) collective-permute-start(bf16[36,32,128]{2,1,0:T(8,128)(2,1)S(1)} %copy-done.20), channel_id=1, source_target_pairs={{8,0},{16,8},{24,16},{32,24},{40,32},{48,40},{56,48},{64,56},{72,6... | collective-permute-start | bytes 884744 | tf_op jit(solution)/shard_map/ppermute | solution.py:537
  102.4 14.5 %collective-permute-start.8 = (bf16[36,32,128]{2,1,0:T(8,128)(2,1)}, bf16[36,32,128]{2,1,0:T(8,128)(2,1)S(1)}, u32[]{:S(2)}, u32[]{:S(2)}) collective-permute-start(bf16[36,32,128]{2,1,0:T(8,128)(2,1)} %get-tuple-element.55), channel_id=1, source_target_pairs={{0,8},{8,16},{16,24},{24,32},{32,40},{40,48},{48,56},{56,64},{64,7... | collective-permute-start | bytes 884744 | tf_op jit(solution)/shard_map/ppermute | solution.py:532
  106.4 12.6 %collective-permute-start.9 = (bf16[36,32,128]{2,1,0:T(8,128)(2,1)}, bf16[36,32,128]{2,1,0:T(8,128)(2,1)S(1)}, u32[]{:S(2)}, u32[]{:S(2)}) collective-permute-start(bf16[36,32,128]{2,1,0:T(8,128)(2,1)} %get-tuple-element.56), channel_id=1, source_target_pairs={{8,0},{16,8},{24,16},{32,24},{40,32},{48,40},{56,48},{64,56},{72,6... | collective-permute-start | bytes 884744 | tf_op jit(solution)/shard_map/ppermute | solution.py:537
  110.5 8.5 %copy-start.4 = (bf16[36,32,128]{2,1,0:T(8,128)(2,1)}, bf16[36,32,128]{2,1,0:T(8,128)(2,1)S(1)}, u32[]{:S(2)}) copy-start(bf16[36,32,128]{2,1,0:T(8,128)(2,1)S(1)} %collective-permute-done.6.refs_2_) | copy-start | bytes 884740
  112.7 6.3 %copy-start.5 = (bf16[36,32,128]{2,1,0:T(8,128)(2,1)}, bf16[36,32,128]{2,1,0:T(8,128)(2,1)S(1)}, u32[]{:S(2)}) copy-start(bf16[36,32,128]{2,1,0:T(8,128)(2,1)S(1)} %collective-permute-done.7.refs_3_) | copy-start | bytes 884740
  116.9 2.1 %copy-start.6 = (bf16[36,32,128]{2,1,0:T(8,128)(2,1)}, bf16[36,32,128]{2,1,0:T(8,128)(2,1)S(1)}, u32[]{:S(2)}) copy-start(bf16[36,32,128]{2,1,0:T(8,128)(2,1)S(1)} %collective-permute-done.8.refs_7_) | copy-start | bytes 884740
  119.0 0.7 copy-start.7
  119.0 0.9 copy-start
  155.5 8.0 %copy-start.23 = (bf16[34,32,128]{2,1,0:T(8,128)(2,1)S(1)}, bf16[34,32,128]{2,1,0:T(8,128)(2,1)}, u32[]{:S(2)}) copy-start(bf16[34,32,128]{2,1,0:T(8,128)(2,1)} %get-tuple-element.61) | copy-start | bytes 835588
  155.5 11.4 %copy-start.22 = (bf16[34,32,128]{2,1,0:T(8,128)(2,1)S(1)}, bf16[34,32,128]{2,1,0:T(8,128)(2,1)}, u32[]{:S(2)}) copy-start(bf16[34,32,128]{2,1,0:T(8,128)(2,1)} %get-tuple-element.62) | copy-start | bytes 835588
  158.8 9.4 %copy-start.2 = (bf16[32,64,128]{2,1,0:T(8,128)(2,1)S(1)}, bf16[32,64,128]{2,1,0:T(8,128)(2,1)}, u32[]{:S(2)}) copy-start(bf16[32,64,128]{2,1,0:T(8,128)(2,1)} %get-tuple-element.52) | copy-start | bytes 1572868
  158.8 28.0 %all-to-all-start.4 = ((f32[128,8,128]{2,1,0:T(8,128)}), f32[128,8,128]{2,1,0:T(8,128)S(1)}, u32[]{:S(2)}, u32[]{:S(2)}) async-start(f32[128,8,128]{2,1,0:T(8,128)} %get-tuple-element.65), calls=%async_computation.4 | async-start | bytes 1048576 | tf_op jit(solution)/shard_map/all_to_all | solution.py:541
  163.5 12.4 %collective-permute-start.10 = (bf16[34,32,128]{2,1,0:T(8,128)(2,1)S(1)}, bf16[34,32,128]{2,1,0:T(8,128)(2,1)S(1)}, u32[]{:S(2)}, u32[]{:S(2)}) collective-permute-start(bf16[34,32,128]{2,1,0:T(8,128)(2,1)S(1)} %copy-done.23), channel_id=1, source_target_pairs={{0,8},{8,16},{16,24},{24,32},{32,40},{40,48},{48,56},{56,64},{64,7... | collective-permute-start | bytes 835592 | tf_op jit(solution)/shard_map/ppermute | solution.py:532
  166.9 11.3 %collective-permute-start.11 = (bf16[34,32,128]{2,1,0:T(8,128)(2,1)S(1)}, bf16[34,32,128]{2,1,0:T(8,128)(2,1)S(1)}, u32[]{:S(2)}, u32[]{:S(2)}) collective-permute-start(bf16[34,32,128]{2,1,0:T(8,128)(2,1)S(1)} %copy-done.22), channel_id=1, source_target_pairs={{8,0},{16,8},{24,16},{32,24},{40,32},{48,40},{56,48},{64,56},{72,6... | collective-permute-start | bytes 835592 | tf_op jit(solution)/shard_map/ppermute | solution.py:537
  175.9 2.3 %copy-start.24 = (bf16[34,32,128]{2,1,0:T(8,128)(2,1)}, bf16[34,32,128]{2,1,0:T(8,128)(2,1)S(1)}, u32[]{:S(2)}) copy-start(bf16[34,32,128]{2,1,0:T(8,128)(2,1)S(1)} %collective-permute-done.10.refs_2_) | copy-start | bytes 835588
  178.2 0.7 copy-start.25
  186.8 0.8 copy-start.3

commit v3 on v2

--- a/solution.py
+++ b/solution.py
@@ -78,8 +78,9 @@
 def rows_message(columns, groups, msg_ref):
     spare = jnp.zeros((128 - C * len(columns), 1), F32)
     row = as_row(jnp.concatenate([*columns, spare], axis=0))
-    at = lax.broadcasted_iota(jnp.int32, (8, 128), 0)
-    tile = jnp.where(at == 0, jnp.broadcast_to(row, (8, 128)), 0.0)
+    height = msg_ref.shape[1]
+    at = lax.broadcasted_iota(jnp.int32, (height, 128), 0)
+    tile = jnp.where(at == 0, jnp.broadcast_to(row, (height, 128)), 0.0)
     msg_ref[...] = jnp.broadcast_to(tile[None], msg_ref.shape)
     for k, group in enumerate(groups):
         for dz in range(3):
@@ -87,7 +88,7 @@
                 msg_ref[dz * C : (dz + 1) * C, 1 + 3 * k + dy, :] = group(dz, dy)
 
 
-def stats_out(send, h_ref, acc, start, low_ref, high_ref, msg_ref):
+def stats_out(send, h_ref, acc, start, low_ref, high_ref):
     center = fold(total(acc)) / (2 * ROWS * 128)
     both = twice(center)
     spread = jnp.zeros((64, 128), F32)
@@ -98,11 +99,11 @@
         low_ref[y] = off[0:C].astype(BF16)
         high_ref[y] = off[C:].astype(BF16)
     send(low_ref, high_ref)
-    message((center, fold(total(spread))), msg_ref)
-
-
-def read_stats(r_ref, place_ref, cells):
-    parts = jnp.transpose(r_ref[...])
+    return center, fold(total(spread))
+
+
+def stats_of(rows, place_ref, cells, st_ref):
+    parts = jnp.transpose(rows)
     centers = parts[0:C]
     count = parts.shape[1]
     mean = total(centers) / count
@@ -111,12 +112,39 @@
     at = lax.broadcasted_iota(jnp.int32, centers.shape, 1)
     low = total(jnp.where(at == place_ref[0], off, 0.0))
     high = total(jnp.where(at == place_ref[1], off, 0.0))
-    return mean, lax.rsqrt(spread + EPSILON), low, high
-
-
-def read_sums(r_ref):
-    parts = jnp.transpose(jnp.broadcast_to(jnp.sum(r_ref[...], axis=0)[0:1], (128, 128)))[:, 0:1]
+    found = (mean, lax.rsqrt(spread + EPSILON), low, high)
+    st_ref[...] = jnp.concatenate([*found, jnp.zeros((C, 124), F32)], axis=1)
+    return found
+
+
+def kept_stats(st_ref):
+    return tuple(st_ref[:, k : k + 1] for k in range(4))
+
+
+def sums_of(row):
+    parts = jnp.transpose(jnp.broadcast_to(row, (128, 128)))[:, 0:1]
     return parts[0:C], parts[C : 2 * C]
+
+
+def feature_sums(v):
+    lane = lanes(128)
+    inner = v[5].astype(F32)
+    for y in range(6, 3 + ROWS):
+        inner = inner + v[y].astype(F32)
+    ends = [v[y].astype(F32) for y in (3, 4, 3 + ROWS, 4 + ROWS)]
+    windows = (inner + ends[0] + ends[1], inner + ends[1] + ends[2], inner + ends[2] + ends[3])
+    columns = []
+    for dz in range(3):
+        for dy in range(3):
+            values = windows[dy]
+            if dz == 0:
+                values = jnp.where(lane == 127, 0.0, values)
+            if dz == 2:
+                values = jnp.where(lane == 0, 0.0, values)
+            column = total(values)
+            columns.append(column + jnp.concatenate([column[C:], column[:C]], axis=0))
+    rows = jnp.transpose(jnp.concatenate(columns + [jnp.zeros((128, 119), F32)], axis=1))
+    return lambda dz, dy: jnp.broadcast_to(rows[dz * 3 + dy : dz * 3 + dy + 1], (C, 128))
 
 
 def act(z):
@@ -186,11 +214,15 @@
     down_ref[4:6] = cot[0:2]
 
 
-def planes_kernel(need, send, own, y_low, y_high, up_ref, down_ref):
-    need(own, y_low, y_high)
+def planes_kernel(need, send, own, cot, y_low, y_high, up_ref, down_ref, t_up, t_down):
+    need(own, cot, y_low, y_high)
     for part, rows, at in ((y_low, 4, 0), (own, ROWS, 4), (y_high, 4, ROWS + 4)):
         down_ref[at : at + rows] = part[0:rows, 0:C]
         up_ref[at : at + rows] = part[0:rows, C : 2 * C]
+    send(up_ref, down_ref)
+    for part, first, rows, at in ((y_low, 4, 2, 0), (cot, 0, ROWS, 2), (y_high, 4, 2, ROWS + 2)):
+        t_down[at : at + rows] = part[first : first + rows, 0:C]
+        t_up[at : at + rows] = part[first : first + rows, C : 2 * C]
 
 
 def weights_kernel(need, send, k1, k2, w1, w2, b1, b2):
@@ -244,12 +276,15 @@
 
     conv_rows(v, w, ROWS + 6, emit)
     send(h)
-    stats_out(send, h, acc[0], 3, low, high, msg)
-
-
-def second_kernel(cells, need, send, place, h1, x_low, x_high, r1, gb, w, v, h, low, high, msg):
+    columns = stats_out(send, h, acc[0], 3, low, high)
+    rows_message(columns, (feature_sums(v),), msg)
+
+
+def second_kernel(cells, need, send, place, r1, gb, h1, x_low, x_high, w, v, h, low, high, msg, st1, x1):
     need(r1, gb)
-    mean, inverse, o_low, o_high = read_stats(r1, place, cells)
+    mean, inverse, o_low, o_high = stats_of(r1[:, 0, :], place, cells, st1)
+    x1[...] = jnp.sum(r1[...], axis=0)
+    send(st1, x1)
     need(h1, x_low, x_high)
     scale = inverse * gb[:, 0:1]
     shift = gb[:, 1:2]
@@ -272,40 +307,22 @@
 
     conv_rows(v, w, ROWS + 4, emit)
     send(h)
-    stats_out(send, h, acc[0], 2, low, high, msg)
-
-
-def side_kernel(cells, need, send, place, h1, r1, v1, xn, x1, g, acc):
-    need(h1, r1, v1)
-    mean, inverse, _, _ = read_stats(r1, place, cells)
+    message(stats_out(send, h, acc[0], 2, low, high), msg)
+
+
+def side_kernel(need, send, st1, h1, v1, xn, g, acc):
+    need(st1, h1)
+    mean, inverse, _, _ = kept_stats(st1)
     mean2, inverse2 = twice(mean), twice(inverse)
     lane = lanes(64)
     for y in range(ROWS):
         put_shifted(g, y, (h1[y + 3] - mean2) * inverse2, lane)
+    need(v1)
     weight_sums(g, v1, 3, acc)
     tile = folded(acc)
     for dz in range(3):
         for dy in range(3):
             xn[dz * 3 + dy] = tile(dz, dy)
-    lane = lanes(128)
-    inner = v1[5].astype(F32)
-    for y in range(6, 3 + ROWS):
-        inner = inner + v1[y].astype(F32)
-    ends = [v1[y].astype(F32) for y in (3, 4, 3 + ROWS, 4 + ROWS)]
-    windows = (inner + ends[0] + ends[1], inner + ends[1] + ends[2], inner + ends[2] + ends[3])
-    columns = []
-    for dz in range(3):
-        for dy in range(3):
-            values = windows[dy]
-            if dz == 0:
-                values = jnp.where(lane == 127, 0.0, values)
-            if dz == 2:
-                values = jnp.where(lane == 0, 0.0, values)
-            column = total(values)
-            column = column + jnp.concatenate([column[C:], column[:C]], axis=0)
-            columns.append(column)
-    wide = jnp.concatenate(columns + [jnp.zeros((128, 119), F32)], axis=1)
-    x1[...] = jnp.transpose(wide)[0:16]
 
 
 def cot_row(cot, y_low, y_high, y):
@@ -316,10 +333,10 @@
     return y_high[2 + y - ROWS]
 
 
-def third_kernel(cells, need, send, place, h2, cot, y_low, y_high, r2, gb, xn, x1, out, t_low, t_high, msg):
+def third_kernel(cells, need, send, place, r2, gb, cot, h2, xn, out, msg, st2):
     need(r2, gb)
-    mean, inverse, _, _ = read_stats(r2, place, cells)
-    need(h2, cot, y_low, y_high)
+    mean, inverse, _, _ = stats_of(r2[...], place, cells, st2)
+    need(h2, cot)
     mean2, inverse2 = twice(mean), twice(inverse)
     gain2, bias2 = twice(gb[:, 2:3]), twice(gb[:, 3:4])
     plain = jnp.zeros((64, 128), F32)
@@ -332,28 +349,20 @@
         plain = plain + slope
         both = both + slope * normed
     send(out)
-    for y in range(ROWS + 4):
-        values = cot_row(cot, y_low, y_high, y)
-        t_low[y] = values[0:C]
-        t_high[y] = values[C:]
-    send(t_low, t_high)
-    need(xn, x1)
-
-    def ones(dz, dy):
-        return jnp.broadcast_to(x1[dz * 3 + dy : dz * 3 + dy + 1, :], (C, 128))
-
-    rows_message(
-        (fold(total(both)), fold(total(plain))), (lambda dz, dy: xn[dz * 3 + dy], ones), msg
-    )
+    need(xn)
+
+    rows_message((fold(total(both)), fold(total(plain))), (lambda dz, dy: xn[dz * 3 + dy],), msg)
 
 
 def fourth_kernel(
-    cells, need, send, place, h2, x_low, x_high, cot, y_low, y_high, t_low, t_high, r2, r3, h1, r1, gb,
-    v1, v2, w, slope1, low, high, msg, v, g, acc, acc1,
+    cells, need, send, place, r3, st2, gb, h2, x_low, x_high, cot, y_low, y_high, t_low, t_high,
+    w, st1, h1, v2, v1, slope1, low, high, msg, t3, v, g, acc, acc1,
 ):
-    need(r2, r3, gb)
-    mean, inverse, o_low, o_high = read_stats(r2, place, cells)
-    nsum, plain = read_sums(r3)
+    need(r3, st2, gb)
+    mean, inverse, o_low, o_high = kept_stats(st2)
+    t3[...] = jnp.sum(r3[...], axis=0)
+    send(t3)
+    nsum, plain = sums_of(t3[0:1])
     need(h2, x_low, x_high, cot, y_low, y_high, t_low, t_high)
     gain, bias = gb[:, 2:3], gb[:, 3:4]
     lead = gain * inverse
@@ -378,8 +387,8 @@
     need(v2)
     weight_sums(g, v2, 2, acc)
 
-    need(h1, r1, w)
-    mean, inverse, _, _ = read_stats(r1, place, cells)
+    need(h1, st1, w)
+    mean, inverse, _, _ = kept_stats(st1)
     mean2, inverse2 = twice(mean), twice(inverse)
     gain2, bias2 = twice(gb[:, 0:1]), twice(gb[:, 1:2])
     sums = [jnp.zeros((64, 128), F32), jnp.zeros((64, 128), F32)]
@@ -404,10 +413,11 @@
     )
 
 
-def owner_kernel(cells, need, send, place, r1, r3, r4, gb, msg, norms):
-    need(r1, r3, r4, gb)
-    _, inverse, _, _ = read_stats(r1, place, cells)
-    nsum, plain = read_sums(r4)
+def owner_kernel(cells, need, send, place, r4, st1, gb, t3, x1, msg, norms, t4):
+    need(r4, st1, gb, t3, x1)
+    _, inverse, _, _ = kept_stats(st1)
+    t4[...] = jnp.sum(r4[...], axis=0)
+    nsum, plain = sums_of(t4[0:1])
     mine = lax.broadcasted_iota(jnp.int32, (C, 1), 0) == place[6]
 
     def picked(column):
@@ -415,9 +425,9 @@
 
     scale = cells**-0.5
     lead = picked(gb[:, 0:1] * inverse) * scale
-    third, fourth = jnp.sum(r3[...], axis=0), jnp.sum(r4[...], axis=0)
-    xn, x1 = third[1:4], third[4:7]
-    one = lead * (fourth[1:4] - picked(plain) * (x1 / cells) - picked(nsum) * (xn / cells))
+    third, fourth = t3[...], t4[...]
+    one = fourth[1:4] - picked(plain) * (x1[1:4] / cells) - picked(nsum) * (third[1:4] / cells)
+    one = lead * one
     two = fourth[4:7] * scale
     tile = jnp.concatenate([one, two, jnp.zeros((2, 128), F32)], axis=0)
     msg[...] = jnp.broadcast_to(tile[None], msg.shape)
@@ -437,11 +447,11 @@
 
 
 def fifth_kernel(
-    cells, need, send, place, slope1, s_low, s_high, h1, x_low, x_high, r1, r4, gb, w, out, v
+    cells, need, send, place, t4, st1, gb, slope1, s_low, s_high, h1, x_low, x_high, w, out, v
 ):
-    need(r1, r4, gb)
-    mean, inverse, o_low, o_high = read_stats(r1, place, cells)
-    nsum, plain = read_sums(r4)
+    need(t4, st1, gb)
+    mean, inverse, o_low, o_high = kept_stats(st1)
+    nsum, plain = sums_of(t4[0:1])
     need(slope1, s_low, s_high, h1, x_low, x_high)
     lead = gb[:, 0:1] * inverse
     p_mean, n_mean = plain / cells, nsum / cells
@@ -465,17 +475,17 @@
     conv_rows(v, w, ROWS, emit)
 
 
-def call(kernel, ins, outs, name, scratch=(), smem_first=True):
+def call(kernel, ins, outs, name, scratch=(), smem_first=True, after=()):
     lead = 1 if smem_first else 0
     count_in, count_out = len(ins) - lead, len(outs)
 
     def body(*refs):
         first, rest = refs[:lead], refs[lead:]
         parts = []
-        for size in (count_in, count_out, count_in, count_out, 2):
+        for size in (count_in, len(after), count_out, count_in, count_out, 2):
             parts.append(rest[:size])
             rest = rest[size:]
-        sources, targets, in_bufs, out_bufs, (in_sems, out_sems) = parts
+        sources, _, targets, in_bufs, out_bufs, (in_sems, out_sems) = parts
         arriving = [
             pltpu.make_async_copy(a, b, in_sems.at[k])
             for k, (a, b) in enumerate(zip(sources, in_bufs))
@@ -510,7 +520,7 @@
     return pl.pallas_call(
         body,
         out_shape=outs,
-        in_specs=[SM] * lead + [far] * count_in,
+        in_specs=[SM] * lead + [far] * (count_in + len(after)),
         out_specs=[far] * count_out,
         scratch_shapes=[
             *[pltpu.VMEM(a.shape, a.dtype) for a in ins[lead:]],
@@ -524,7 +534,7 @@
             flops=2_000_000_000, bytes_accessed=6_000_000, transcendentals=0
         ),
         name=name,
-    )(*ins)
+    )(*ins, *after)
 
 
 def up(values, axes):
@@ -558,14 +568,19 @@
     def rims(rows):
         return [sh((rows, C, 128), BF16)] * 2
 
-    msg, wide = sh((count, 128), F32), sh((count, 8, 128), F32)
+    msg, four, five, wide = (
+        sh((count, *tile), F32) for tile in ((128,), (4, 128), (5, 128), (8, 128))
+    )
+    stats = sh((C, 128), F32)
     corr = (pltpu.VMEM((192, ROWS * 128), BF16), pltpu.VMEM((192, 384), F32))
 
     y_up, y_down = call(
         pack_kernel, (own, cot), [sh((6, 64, 128), BF16)] * 2, "pack", smem_first=False
     )
     y_low, y_high = up(y_up, GY), down(y_down, GY)
-    x_up, x_down = call(planes_kernel, (own, y_low, y_high), rims(40), "planes", smem_first=False)
+    x_up, x_down, t_up, t_down = call(
+        planes_kernel, (own, cot, y_low, y_high), rims(40) + rims(36), "planes", smem_first=False
+    )
     x_low, x_high = up(x_up, GX), down(x_down, GX)
     taps = [
         jnp.transpose(k, (2, 3, 4, 0, 1)).reshape(27, C, C) for k in (kernel_one, kernel_two)
@@ -577,61 +592,66 @@
     v1, h1, low, high, m1 = call(
         first_kernel,
         (own, y_low, y_high, x_low, x_high, w1),
-        [sh((40, 128, 128), BF16), sh((38, 64, 128), F32), *rims(38), msg],
+        [sh((40, 128, 128), BF16), sh((38, 64, 128), F32), *rims(38), five],
         "conv_one",
         smem_first=False,
     )
     h1_low, h1_high = up(high, GX), down(low, GX)
     r1 = share(m1)
 
-    v2, h2, low, high, m2 = call(
+    v2, h2, low, high, m2, st1, x1 = call(
         lambda *refs: second_kernel(cells, *refs),
-        (place, h1, h1_low, h1_high, r1, gb, w2),
-        [sh((38, 128, 128), BF16), sh((36, 64, 128), F32), *rims(36), msg],
+        (place, r1, gb, h1, h1_low, h1_high, w2),
+        [
+            sh((38, 128, 128), BF16), sh((36, 64, 128), F32), *rims(36), msg, stats,
+            sh((5, 128), F32),
+        ],
         "conv_two",
     )
     h2_low, h2_high = up(high, GX), down(low, GX)
+    t_low, t_high = up(t_up, GX), down(t_down, GX)
     r2 = share(m2)
-    xn, x1 = call(
-        lambda *refs: side_kernel(cells, *refs),
-        (place, h1, r1, v1),
-        [sh((9, C, 128), F32), sh((16, 128), F32)],
+    (xn,) = call(
+        side_kernel,
+        (st1, h1, v1),
+        [sh((9, C, 128), F32)],
         "normed_features",
         scratch=corr,
-    )
-
-    output, low, high, m3 = call(
+        smem_first=False,
+    )
+
+    output, m3, st2 = call(
         lambda *refs: third_kernel(cells, *refs),
-        (place, h2, cot, y_low, y_high, r2, gb, xn, x1),
-        [sh((ROWS, 64, 128), BF16), *rims(36), wide],
+        (place, r2, gb, cot, h2, xn),
+        [sh((ROWS, 64, 128), BF16), four, stats],
         "slope_two",
     )
-    t_low, t_high = up(high, GX), down(low, GX)
     r3 = share(m3)
 
-    slope1, low, high, m4 = call(
+    slope1, low, high, m4, t3 = call(
         lambda *refs: fourth_kernel(cells, *refs),
         (
-            place, h2, h2_low, h2_high, cot, y_low, y_high, t_low, t_high, r2, r3, h1, r1, gb,
-            v1, v2, b2,
+            place, r3, st2, gb, h2, h2_low, h2_high, cot, y_low, y_high, t_low, t_high,
+            b2, st1, h1, v2, v1,
         ),
-        [sh((34, 64, 128), F32), *rims(34), wide],
+        [sh((34, 64, 128), F32), *rims(34), wide, sh((4, 128), F32)],
         "back_two",
         scratch=(pltpu.VMEM((36, 128, 128), BF16), *corr, corr[1]),
     )
     s_low, s_high = up(high, GX), down(low, GX)
     r4 = share(m4)
 
-    m5, norm_grads = call(
+    m5, norm_grads, t4 = call(
         lambda *refs: owner_kernel(cells, *refs),
-        (place, r1, r3, r4, gb),
-        [wide, sh((4, C), F32)],
+        (place, r4, st1, gb, t3, x1),
+        [wide, sh((4, C), F32), sh((8, 128), F32)],
         "own_rows",
+        after=(s_low, s_high),
     )
     r5 = share(m5)
     (grad,) = call(
         lambda *refs: fifth_kernel(cells, *refs),
-        (place, slope1, s_low, s_high, h1, h1_low, h1_high, r1, r4, gb, b1),
+        (place, t4, st1, gb, slope1, s_low, s_high, h1, h1_low, h1_high, b1),
         [sh((ROWS, 64, 128), BF16)],
         "back_one",
         scratch=(pltpu.VMEM((34, 128, 128), BF16),),

time: 191 us -> 184 us (0.963)
  blocking collectives: 25.4 us -> 0 us
  starting transfers between devices: 59.2 us -> 81.8 us
  Pallas kernels: 48.3 us -> 45.4 us
    all_to_all x1 -> x0, blocking collectives: 25.4 us -> none  [share(): return lax.all_to_all(msg, ALL, 0, 0, tiled=True)]
    all_to_all x4 -> x5, starting transfers between devices: 28.6 us -> 51.4 us  [share(): return lax.all_to_all(msg, ALL, 0, 0, tiled=True)]
    all_to_all x4 -> x5, waiting for transfers between devices: 12.5 us -> 16.9 us  [share(): return lax.all_to_all(msg, ALL, 0, 0, tiled=True)]
    ppermute x6, waiting for transfers between devices: 15.3 us -> 12 us  [up(): return lax.ppermute(values, axes, [(i, i + 1) for i in range(count - 1)])]
    pallas_call x11, Pallas kernels: 48.3 us -> 45.4 us  [call(): pl.pallas_call(body, out_shape=outs, in_specs=[SM] * lead + [far] * (coun...]
    ppermute x6, waiting for transfers between devices: 14.8 us -> 11.9 us  [down(): return lax.ppermute(values, axes, [(i + 1, i) for i in range(count - 1)])]
    unnamed x52 -> x50, local copies, waits for them, and re-layouts: 5.23 us -> 5.31 us
  transfers between devices with their start and end apart: 16 -> 17, of which waited for: 11 -> 10; matrix products, arithmetic and copies ran while one was open for 2% -> 3% of each run, Pallas kernels for 7% -> 12%
where the time goes in v3:
time: 184 us; the launch traced here: 183 us
  starting transfers between devices  81.8 us (44%)
  Pallas kernels  45.4 us (25%)
  waiting for transfers between devices  40.8 us (22%)
  local copies, waits for them, and re-layouts  13.3 us (7%)
    all_to_all x5, starting transfers between devices, share(): return lax.all_to_all(msg, ALL, 0, 0, tiled=True)  51.4 us
    pallas_call x11, Pallas kernels, call(): pl.pallas_call(body, out_shape=outs, in_specs=[SM] * lead + [far] * (coun...  45.4 us
    ppermute x6, starting transfers between devices, up(): return lax.ppermute(values, axes, [(i, i + 1) for i in range(count - 1)])  22.1 us
    all_to_all x5, waiting for transfers between devices, share(): return lax.all_to_all(msg, ALL, 0, 0, tiled=True)  16.9 us
    ppermute x6, waiting for transfers between devices, up(): return lax.ppermute(values, axes, [(i, i + 1) for i in range(count - 1)])  12 us
    ppermute x6, waiting for transfers between devices, down(): return lax.ppermute(values, axes, [(i + 1, i) for i in range(count - 1)])  11.9 us
    ppermute x6, starting transfers between devices, down(): return lax.ppermute(values, axes, [(i + 1, i) for i in range(count - 1)])  8.38 us
    unnamed x50, local copies, waits for them, and re-layouts  5.31 us
  transfers between devices with their start and end apart: 17, of which 10 were waited for; matrix products, arithmetic and copies ran while one was open for 3% of the time, Pallas kernels for 12%

profile of v3, /device:TPU:1, one launch (start us, length us, event | category | flops | bytes accessed | tf_op | source)
XLA Modules:
  0.0 182.5 jit_solution(8504888730295844405)
XLA Ops:
  0.6 2.2 %copy.21 = bf16[32,2,32,128]{3,2,1,0:T(8,128)(2,1)} copy(bf16[32,2,32,128]{3,0,1,2:T(8,128)(2,1)} %bitcast.39) | data formatting | bytes 1048576 | tf_op jit(solution)/shard_map/transpose | solution.py:565
  2.9 0.0 copy-done
  2.9 1.1 copy.22
  4.0 1.9 %pack.1 = (bf16[6,64,128]{2,1,0:T(8,128)(2,1)}, bf16[6,64,128]{2,1,0:T(8,128)(2,1)}) custom-call(bf16[32,64,128]{2,1,0:T(8,128)(2,1)} %bitcast.46, bf16[32,64,128]{2,1,0:T(8,128)(2,1)} %bitcast.41), custom_call_target="tpu_custom_call" | custom-call | flops 2000000000 | bytes 6000000 | tf_op jit(solution)/shard_map/pack/pallas_call | solution.py:520
  5.9 4.9 %collective-permute-start = (bf16[6,64,128]{2,1,0:T(8,128)(2,1)}, bf16[6,64,128]{2,1,0:T(8,128)(2,1)S(1)}, u32[]{:S(2)}, u32[]{:S(2)}) collective-permute-start(bf16[6,64,128]{2,1,0:T(8,128)(2,1)} %get-tuple-element.40), channel_id=1, source_target_pairs={{0,1},{1,2},{2,3},{3,4},{4,5},{5,6},{6,7},{8,9},{9,10},{10,11},{11... | collective-permute-start | bytes 294920 | tf_op jit(solution)/shard_map/ppermute | solution.py:542
  10.9 1.9 %collective-permute-start.1 = (bf16[6,64,128]{2,1,0:T(8,128)(2,1)}, bf16[6,64,128]{2,1,0:T(8,128)(2,1)S(1)}, u32[]{:S(2)}, u32[]{:S(2)}) collective-permute-start(bf16[6,64,128]{2,1,0:T(8,128)(2,1)} %get-tuple-element.41), channel_id=1, source_target_pairs={{1,0},{2,1},{3,2},{4,3},{5,4},{6,5},{7,6},{9,8},{10,9},{11,10},{12... | collective-permute-start | bytes 294920 | tf_op jit(solution)/shard_map/ppermute | solution.py:547
  12.8 0.0 collective-permute-done.refs_2_.refs_1_.refs_8_
  12.8 4.2 %collective-permute-done.1.refs_3_.refs_2_.refs_9_ = bf16[6,64,128]{2,1,0:T(8,128)(2,1)S(1)} collective-permute-done((bf16[6,64,128]{2,1,0:T(8,128)(2,1)}, bf16[6,64,128]{2,1,0:T(8,128)(2,1)S(1)}, u32[]{:S(2)}, u32[]{:S(2)}) %collective-permute-start.1) | collective-permute-done | bytes 98336 | tf_op jit(solution)/shard_map/ppermute | solution.py:547
  17.0 0.6 copy-done.24
  17.7 2.4 %planes.1 = (bf16[40,32,128]{2,1,0:T(8,128)(2,1)}, bf16[40,32,128]{2,1,0:T(8,128)(2,1)}, bf16[36,32,128]{2,1,0:T(8,128)(2,1)}, bf16[36,32,128]{2,1,0:T(8,128)(2,1)}) custom-call(bf16[32,64,128]{2,1,0:T(8,128)(2,1)} %bitcast.47, bf16[32,64,128]{2,1,0:T(8,128)(2,1)} %bitcast.42, bf16[6,64,128]{2,1,0:T(8,128)(2,1)} %copy-done.23, bf16[6,64,128]{2,1,0:T(8,128)(2,1)} %copy-done.24), custom_call_target="tpu_custom_call" | custom-call | flops 2000000000 | bytes 6000000 | tf_op jit(solution)/shard_map/planes/pallas_call | solution.py:520
  20.0 3.2 %collective-permute-start.2 = (bf16[40,32,128]{2,1,0:T(8,128)(2,1)}, bf16[40,32,128]{2,1,0:T(8,128)(2,1)S(1)}, u32[]{:S(2)}, u32[]{:S(2)}) collective-permute-start(bf16[40,32,128]{2,1,0:T(8,128)(2,1)} %get-tuple-element.42), channel_id=1, source_target_pairs={{0,8},{8,16},{16,24},{24,32},{32,40},{40,48},{48,56},{56,64},{64,7... | collective-permute-start | bytes 983048 | tf_op jit(solution)/shard_map/ppermute | solution.py:542
  23.3 1.3 collective-permute-start.3
  24.6 2.4 %weights.1 = (bf16[192,384]{1,0:T(8,128)(2,1)}, bf16[192,384]{1,0:T(8,128)(2,1)}, bf16[192,384]{1,0:T(8,128)(2,1)}, bf16[192,384]{1,0:T(8,128)(2,1)}) custom-call(bf16[27,32,32]{2,1,0:T(8,128)(2,1)} %bitcast.58, bf16[27,32,32]{2,1,0:T(8,128)(2,1)} %bitcast.59), custom_call_target="tpu_custom_call" | custom-call | flops 2000000000 | bytes 6000000 | tf_op jit(solution)/shard_map/weights/pallas_call | solution.py:520
  26.9 1.9 %collective-permute-done.2.refs_3_ = bf16[40,32,128]{2,1,0:T(8,128)(2,1)S(1)} collective-permute-done((bf16[40,32,128]{2,1,0:T(8,128)(2,1)}, bf16[40,32,128]{2,1,0:T(8,128)(2,1)S(1)}, u32[]{:S(2)}, u32[]{:S(2)}) %collective-permute-start.2) | collective-permute-done | bytes 327712 | tf_op jit(solution)/shard_map/ppermute | solution.py:542
  28.8 4.0 %collective-permute-done.3.refs_4_ = bf16[40,32,128]{2,1,0:T(8,128)(2,1)S(1)} collective-permute-done((bf16[40,32,128]{2,1,0:T(8,128)(2,1)}, bf16[40,32,128]{2,1,0:T(8,128)(2,1)S(1)}, u32[]{:S(2)}, u32[]{:S(2)}) %collective-permute-start.3) | collective-permute-done | bytes 327712 | tf_op jit(solution)/shard_map/ppermute | solution.py:547
  32.8 0.7 copy-done.12
  33.6 4.4 %conv_one.1 = (bf16[40,128,128]{2,1,0:T(8,128)(2,1)}, f32[38,64,128]{2,1,0:T(8,128)}, bf16[38,32,128]{2,1,0:T(8,128)(2,1)}, bf16[38,32,128]{2,1,0:T(8,128)(2,1)}, f32[128,5,128]{2,1,0:T(8,128)}) custom-call(bf16[32,64,128]{2,1,0:T(8,128)(2,1)} %bitcast.48, bf16[6,64,128]{2,1,0:T(8,128)(2,1)} %copy-done.23, bf16[6,64,128]{2,1,0:T(8,128)(2,1)} %copy-done.24, ...), custom_call_target="tpu_custom_call" | custom-call | flops 2000000000 | bytes 6000000 | tf_op jit(solution)/shard_map/conv_one/pallas_call | solution.py:520
  37.9 12.5 %all-to-all-start = ((f32[128,5,128]{2,1,0:T(8,128)}), f32[128,5,128]{2,1,0:T(8,128)S(1)}, u32[]{:S(2)}, u32[]{:S(2)}) async-start(f32[128,5,128]{2,1,0:T(8,128)} %get-tuple-element.45), calls=%async_computation | async-start | bytes 1048576 | tf_op jit(solution)/shard_map/all_to_all | solution.py:551
  50.5 3.3 %collective-permute-start.4 = (bf16[38,32,128]{2,1,0:T(8,128)(2,1)}, bf16[38,32,128]{2,1,0:T(8,128)(2,1)S(1)}, u32[]{:S(2)}, u32[]{:S(2)}) collective-permute-start(bf16[38,32,128]{2,1,0:T(8,128)(2,1)} %get-tuple-element.47), channel_id=1, source_target_pairs={{0,8},{8,16},{16,24},{24,32},{32,40},{40,48},{48,56},{56,64},{64,7... | collective-permute-start | bytes 933896 | tf_op jit(solution)/shard_map/ppermute | solution.py:542
  53.8 1.3 collective-permute-start.5
  55.2 0.7 copy.23.refs_2_.refs_3_
  55.9 0.6 stack.62.refs_0_
  56.5 4.0 %collective-permute-start.8 = (bf16[36,32,128]{2,1,0:T(8,128)(2,1)S(1)}, bf16[36,32,128]{2,1,0:T(8,128)(2,1)S(1)}, u32[]{:S(2)}, u32[]{:S(2)}) collective-permute-start(bf16[36,32,128]{2,1,0:T(8,128)(2,1)S(1)} %copy-done.16), channel_id=1, source_target_pairs={{0,8},{8,16},{16,24},{24,32},{32,40},{40,48},{48,56},{56,64},{64,7... | collective-permute-start | bytes 884744 | tf_op jit(solution)/shard_map/ppermute | solution.py:542
  60.5 1.3 collective-permute-start.9
  61.8 2.0 %collective-permute-done.4.refs_4_.refs_8_ = bf16[38,32,128]{2,1,0:T(8,128)(2,1)S(1)} collective-permute-done((bf16[38,32,128]{2,1,0:T(8,128)(2,1)}, bf16[38,32,128]{2,1,0:T(8,128)(2,1)S(1)}, u32[]{:S(2)}, u32[]{:S(2)}) %collective-permute-start.4) | collective-permute-done | bytes 311328 | tf_op jit(solution)/shard_map/ppermute | solution.py:542
  63.8 1.8 %collective-permute-done.5.refs_5_.refs_9_ = bf16[38,32,128]{2,1,0:T(8,128)(2,1)S(1)} collective-permute-done((bf16[38,32,128]{2,1,0:T(8,128)(2,1)}, bf16[38,32,128]{2,1,0:T(8,128)(2,1)S(1)}, u32[]{:S(2)}, u32[]{:S(2)}) %collective-permute-start.5) | collective-permute-done | bytes 311328 | tf_op jit(solution)/shard_map/ppermute | solution.py:547
  65.7 0.0 all-to-all-done.refs_1_
  65.7 0.7 copy-done.14
  66.4 0.2 copy-done.1
  66.6 6.5 %conv_two.1 = (bf16[38,128,128]{2,1,0:T(8,128)(2,1)}, f32[36,64,128]{2,1,0:T(8,128)}, bf16[36,32,128]{2,1,0:T(8,128)(2,1)}, bf16[36,32,128]{2,1,0:T(8,128)(2,1)}...) custom-call(s32[7]{0:T(128)} %stack.62.refs_0_, f32[128,5,128]{2,1,0:T(8,128)} %copy-done.1, ...), custom_call_target="tpu_custom_call" | custom-call | flops 2000000000 | bytes 6000000 | tf_op jit(solution)/shard_map/conv_two/pallas_call | solution.py:520
  73.1 13.6 %all-to-all-start.1 = ((f32[128,1,128]{2,1,0:T(1,128)}), f32[128,1,128]{2,1,0:T(1,128)S(1)}, u32[]{:S(2)}, u32[]{:S(2)}) async-start(f32[128,1,128]{2,1,0:T(1,128)} %bitcast.52), calls=%async_computation.1 | async-start | bytes 131072 | tf_op jit(solution)/shard_map/all_to_all | solution.py:551
  86.7 3.3 %collective-permute-start.6 = (bf16[36,32,128]{2,1,0:T(8,128)(2,1)}, bf16[36,32,128]{2,1,0:T(8,128)(2,1)S(1)}, u32[]{:S(2)}, u32[]{:S(2)}) collective-permute-start(bf16[36,32,128]{2,1,0:T(8,128)(2,1)} %get-tuple-element.57), channel_id=1, source_target_pairs={{0,8},{8,16},{16,24},{24,32},{32,40},{40,48},{48,56},{56,64},{64,7... | collective-permute-start | bytes 884744 | tf_op jit(solution)/shard_map/ppermute | solution.py:542
  90.0 1.3 collective-permute-start.7
  91.3 3.7 %normed_features.1.refs_5_ = f32[9,32,128]{2,1,0:T(8,128)} custom-call(f32[32,128]{1,0:T(8,128)} %get-tuple-element.52.refs_0_.refs_13_.refs_2_, f32[38,64,128]{2,1,0:T(8,128)} %get-tuple-element.46.refs_3_.refs_1_.refs_14_.refs_7_, bf16[40,128,128]{2,1,0:T(8,128)(2,1)} %get-tuple-element.53.refs_2_.refs_16_), custom_call_target="tpu_custom_call" | custom-call | flops 2000000000 | bytes 6000000 | tf_op jit(solution)/shard_map/normed_features/pallas_call | solution.py:520
  95.0 1.0 all-to-all-done.1
  96.1 0.6 copy-done.6
  96.7 4.2 %slope_two.1 = (bf16[32,64,128]{2,1,0:T(8,128)(2,1)}, f32[128,4,128]{2,1,0:T(4,128)}, f32[32,128]{1,0:T(8,128)}) custom-call(s32[7]{0:T(128)} %stack.62.refs_0_, f32[128,128]{1,0:T(8,128)} %bitcast.53, f32[32,4]{1,0:T(8,128)} %copy.23.refs_2_.refs_3_, bf16[32,64,128]{2,1,0:T(8,128)(2,1)} %bitcast.43, f32[36,64,128]{2,1,0:T(8,128)} %get-tuple-element.51.refs_4_, ...), custom_call_target="tpu_custom_call" | custom-call | flops 2000000000 | bytes 6000000 | tf_op jit(solution)/shard_map/slope_two/pallas_call | solution.py:520
  100.9 10.0 %all-to-all-start.2 = ((f32[128,4,128]{2,1,0:T(4,128)}), f32[128,4,128]{2,1,0:T(4,128)S(1)}, u32[]{:S(2)}, u32[]{:S(2)}) async-start(f32[128,4,128]{2,1,0:T(4,128)} %get-tuple-element.55), calls=%async_computation.2 | async-start | bytes 524288 | tf_op jit(solution)/shard_map/all_to_all | solution.py:551
  110.9 0.0 collective-permute-done.8.refs_10_
  111.0 0.0 collective-permute-done.9.refs_11_
  111.0 0.0 copy-start.18
  111.0 0.0 collective-permute-done.6.refs_5_
  111.0 0.0 collective-permute-done.7.refs_6_
  111.0 10.8 %all-to-all-done.2.refs_1_ = f32[128,4,128]{2,1,0:T(4,128)S(1)} async-done(((f32[128,4,128]{2,1,0:T(4,128)}), f32[128,4,128]{2,1,0:T(4,128)S(1)}, u32[]{:S(2)}, u32[]{:S(2)}) %all-to-all-start.2) | async-done | bytes 262176 | tf_op jit(solution)/shard_map/all_to_all | solution.py:551
  121.9 0.0 copy-done.20
  121.9 0.7 copy-done.5
  122.6 9.6 %back_two.1 = (f32[34,64,128]{2,1,0:T(8,128)}, bf16[34,32,128]{2,1,0:T(8,128)(2,1)}, bf16[34,32,128]{2,1,0:T(8,128)(2,1)}, f32[128,8,128]{2,1,0:T(8,128)}, f32[4,128]{1,0:T(4,128)}) custom-call(s32[7]{0:T(128)} %stack.62.refs_0_, f32[128,4,128]{2,1,0:T(4,128)} %copy-done.5, f32[32,128]{1,0:T(8,128)} %get-tuple-element.56.refs_2_, ...), custom_call_target="tpu_custom_call" | custom-call | flops 2000000000 | bytes 6000000 | tf_op jit(solution)/shard_map/back_two/pallas_call | solution.py:520
  132.2 4.6 %all-to-all-start.3 = ((f32[128,8,128]{2,1,0:T(8,128)}), f32[128,8,128]{2,1,0:T(8,128)S(1)}, u32[]{:S(2)}, u32[]{:S(2)}) async-start(f32[128,8,128]{2,1,0:T(8,128)} %get-tuple-element.63), calls=%async_computation.3 | async-start | bytes 1048576 | tf_op jit(solution)/shard_map/all_to_all | solution.py:551
  136.8 3.3 %collective-permute-start.10 = (bf16[34,32,128]{2,1,0:T(8,128)(2,1)}, bf16[34,32,128]{2,1,0:T(8,128)(2,1)S(1)}, u32[]{:S(2)}, u32[]{:S(2)}) collective-permute-start(bf16[34,32,128]{2,1,0:T(8,128)(2,1)} %get-tuple-element.66), channel_id=1, source_target_pairs={{0,8},{8,16},{16,24},{24,32},{32,40},{40,48},{48,56},{56,64},{64,7... | collective-permute-start | bytes 835592 | tf_op jit(solution)/shard_map/ppermute | solution.py:542
  140.1 1.3 collective-permute-start.11
  141.4 8.0 %collective-permute-done.10.refs_6_.refs_5_ = bf16[34,32,128]{2,1,0:T(8,128)(2,1)S(1)} collective-permute-done((bf16[34,32,128]{2,1,0:T(8,128)(2,1)}, bf16[34,32,128]{2,1,0:T(8,128)(2,1)S(1)}, u32[]{:S(2)}, u32[]{:S(2)}) %collective-permute-start.10) | collective-permute-done | bytes 278560 | tf_op jit(solution)/shard_map/ppermute | solution.py:542
  149.4 1.8 %collective-permute-done.11.refs_7_.refs_6_ = bf16[34,32,128]{2,1,0:T(8,128)(2,1)S(1)} collective-permute-done((bf16[34,32,128]{2,1,0:T(8,128)(2,1)}, bf16[34,32,128]{2,1,0:T(8,128)(2,1)S(1)}, u32[]{:S(2)}, u32[]{:S(2)}) %collective-permute-start.11) | collective-permute-done | bytes 278560 | tf_op jit(solution)/shard_map/ppermute | solution.py:547
  151.3 0.0 all-to-all-done.3.refs_1_
  151.3 0.7 copy-done.22
  152.0 0.2 copy-done.3
  152.2 2.9 %own_rows.1 = (f32[128,8,128]{2,1,0:T(8,128)}, f32[4,32]{1,0:T(4,128)}, f32[8,128]{1,0:T(8,128)}) custom-call(s32[7]{0:T(128)} %stack.62.refs_0_, f32[128,8,128]{2,1,0:T(8,128)} %copy-done.3, f32[32,128]{1,0:T(8,128)} %get-tuple-element.52.refs_0_.refs_13_.refs_2_, f32[32,4]{1,0:T(8,128)} %copy.23.refs_2_.refs_3_, f32[4,128]{1,0:T(4,128)} %get-tuple-element.64.refs_4_, ...), custom_call_target="tpu_custom_call" | custom-call | flops 2000000000 | bytes 6000000 | tf_op jit(solution)/shard_map/own_rows/pallas_call | solution.py:520
  155.1 0.0 copy-start.2
  155.1 10.6 %all-to-all-start.4 = ((f32[128,8,128]{2,1,0:T(8,128)}), f32[128,8,128]{2,1,0:T(8,128)S(1)}, u32[]{:S(2)}, u32[]{:S(2)}) async-start(f32[128,8,128]{2,1,0:T(8,128)} %get-tuple-element.71), calls=%async_computation.4 | async-start | bytes 1048576 | tf_op jit(solution)/shard_map/all_to_all | solution.py:551
  165.7 1.1 copy.34
  166.9 5.3 %back_one.1 = bf16[32,64,128]{2,1,0:T(8,128)(2,1)} custom-call(s32[7]{0:T(128)} %stack.62.refs_0_, f32[8,128]{1,0:T(8,128)} %get-tuple-element.68.refs_1_, f32[32,128]{1,0:T(8,128)} %get-tuple-element.52.refs_0_.refs_13_.refs_2_, f32[32,4]{1,0:T(8,128)} %copy.23.refs_2_.refs_3_, f32[34,64,128]{2,1,0:T(8,128)} %get-tuple-element.69.refs_4_, ...), custom_call_target="tpu_custom_call" | custom-call | flops 2000000000 | bytes 6000000 | tf_op jit(solution)/shard_map/back_one/pallas_call | solution.py:520
  172.1 2.2 %copy.33 = bf16[32,2,32,128]{3,0,1,2:T(8,128)(2,1)} copy(bf16[32,2,32,128]{3,2,1,0:T(8,128)(2,1)} %bitcast.51) | data formatting | bytes 1048576 | tf_op jit(solution)/shard_map/reshape | solution.py:663
  174.3 5.1 %all-to-all-done.4.refs_0_ = f32[128,8,128]{2,1,0:T(8,128)S(1)} async-done(((f32[128,8,128]{2,1,0:T(8,128)}), f32[128,8,128]{2,1,0:T(8,128)S(1)}, u32[]{:S(2)}, u32[]{:S(2)}) %all-to-all-start.4) | async-done | bytes 524320 | tf_op jit(solution)/shard_map/all_to_all | solution.py:551
  179.4 0.8 copy-done.4
  180.2 2.2 %finish.1 = (f32[27,32,32]{2,1,0:T(8,128)}, f32[27,32,32]{2,1,0:T(8,128)}) custom-call(f32[128,8,128]{2,1,0:T(8,128)} %copy-done.4), custom_call_target="tpu_custom_call" | custom-call | flops 2000000000 | bytes 6000000 | tf_op jit(solution)/shard_map/finish/pallas_call | solution.py:520
  (38 shorter events, 0.1 us)
Async XLA Ops:
  0.6 2.2 %copy-start = (bf16[32,2,32,128]{3,2,1,0:T(8,128)(2,1)S(1)}, bf16[32,2,32,128]{3,2,1,0:T(8,128)(2,1)}, u32[]{:S(2)}) copy-start(bf16[32,2,32,128]{3,2,1,0:T(8,128)(2,1)} %param.15) | copy-start | bytes 1572868
  5.9 6.9 %collective-permute-start = (bf16[6,64,128]{2,1,0:T(8,128)(2,1)}, bf16[6,64,128]{2,1,0:T(8,128)(2,1)S(1)}, u32[]{:S(2)}, u32[]{:S(2)}) collective-permute-start(bf16[6,64,128]{2,1,0:T(8,128)(2,1)} %get-tuple-element.40), channel_id=1, source_target_pairs={{0,1},{1,2},{2,3},{3,4},{4,5},{5,6},{6,7},{8,9},{9,10},{10,11},{11... | collective-permute-start | bytes 294920 | tf_op jit(solution)/shard_map/ppermute | solution.py:542
  10.9 6.1 %collective-permute-start.1 = (bf16[6,64,128]{2,1,0:T(8,128)(2,1)}, bf16[6,64,128]{2,1,0:T(8,128)(2,1)S(1)}, u32[]{:S(2)}, u32[]{:S(2)}) collective-permute-start(bf16[6,64,128]{2,1,0:T(8,128)(2,1)} %get-tuple-element.41), channel_id=1, source_target_pairs={{1,0},{2,1},{3,2},{4,3},{5,4},{6,5},{7,6},{9,8},{10,9},{11,10},{12... | collective-permute-start | bytes 294920 | tf_op jit(solution)/shard_map/ppermute | solution.py:547
  12.8 4.2 %copy-start.23 = (bf16[6,64,128]{2,1,0:T(8,128)(2,1)}, bf16[6,64,128]{2,1,0:T(8,128)(2,1)S(1)}, u32[]{:S(2)}) copy-start(bf16[6,64,128]{2,1,0:T(8,128)(2,1)S(1)} %collective-permute-done.refs_2_.refs_1_.refs_8_) | copy-start | bytes 294916
  17.0 0.6 copy-start.24
  20.0 8.8 %collective-permute-start.2 = (bf16[40,32,128]{2,1,0:T(8,128)(2,1)}, bf16[40,32,128]{2,1,0:T(8,128)(2,1)S(1)}, u32[]{:S(2)}, u32[]{:S(2)}) collective-permute-start(bf16[40,32,128]{2,1,0:T(8,128)(2,1)} %get-tuple-element.42), channel_id=1, source_target_pairs={{0,8},{8,16},{16,24},{24,32},{32,40},{40,48},{48,56},{56,64},{64,7... | collective-permute-start | bytes 983048 | tf_op jit(solution)/shard_map/ppermute | solution.py:542
  23.3 9.6 %collective-permute-start.3 = (bf16[40,32,128]{2,1,0:T(8,128)(2,1)}, bf16[40,32,128]{2,1,0:T(8,128)(2,1)S(1)}, u32[]{:S(2)}, u32[]{:S(2)}) collective-permute-start(bf16[40,32,128]{2,1,0:T(8,128)(2,1)} %get-tuple-element.43), channel_id=1, source_target_pairs={{8,0},{16,8},{24,16},{32,24},{40,32},{48,40},{56,48},{64,56},{72,6... | collective-permute-start | bytes 983048 | tf_op jit(solution)/shard_map/ppermute | solution.py:547
  28.8 4.0 %copy-start.11 = (bf16[40,32,128]{2,1,0:T(8,128)(2,1)}, bf16[40,32,128]{2,1,0:T(8,128)(2,1)S(1)}, u32[]{:S(2)}) copy-start(bf16[40,32,128]{2,1,0:T(8,128)(2,1)S(1)} %collective-permute-done.2.refs_3_) | copy-start | bytes 983044
  32.8 0.7 copy-start.12
  33.5 21.6 %copy-start.7 = (f32[32]{0:T(128)S(1)}, f32[32]{0:T(128)}, u32[]{:S(2)}) copy-start(f32[32]{0:T(128)} %param.14) | copy-start | bytes 388
  33.5 21.6 %copy-start.8 = (f32[32]{0:T(128)S(1)}, f32[32]{0:T(128)}, u32[]{:S(2)}) copy-start(f32[32]{0:T(128)} %param.13) | copy-start | bytes 388
  33.5 21.6 %copy-start.9 = (f32[32]{0:T(128)S(1)}, f32[32]{0:T(128)}, u32[]{:S(2)}) copy-start(f32[32]{0:T(128)} %param.11) | copy-start | bytes 388
  33.5 21.6 %copy-start.10 = (f32[32]{0:T(128)S(1)}, f32[32]{0:T(128)}, u32[]{:S(2)}) copy-start(f32[32]{0:T(128)} %param.10) | copy-start | bytes 388
  33.5 22.9 %copy-start.16 = (bf16[36,32,128]{2,1,0:T(8,128)(2,1)S(1)}, bf16[36,32,128]{2,1,0:T(8,128)(2,1)}, u32[]{:S(2)}) copy-start(bf16[36,32,128]{2,1,0:T(8,128)(2,1)} %get-tuple-element.59) | copy-start | bytes 884740
  33.6 26.9 %copy-start.15 = (bf16[36,32,128]{2,1,0:T(8,128)(2,1)S(1)}, bf16[36,32,128]{2,1,0:T(8,128)(2,1)}, u32[]{:S(2)}) copy-start(bf16[36,32,128]{2,1,0:T(8,128)(2,1)} %get-tuple-element.60) | copy-start | bytes 884740
  37.9 27.8 %all-to-all-start = ((f32[128,5,128]{2,1,0:T(8,128)}), f32[128,5,128]{2,1,0:T(8,128)S(1)}, u32[]{:S(2)}, u32[]{:S(2)}) async-start(f32[128,5,128]{2,1,0:T(8,128)} %get-tuple-element.45), calls=%async_computation | async-start | bytes 1048576 | tf_op jit(solution)/shard_map/all_to_all | solution.py:551
  50.5 13.3 %collective-permute-start.4 = (bf16[38,32,128]{2,1,0:T(8,128)(2,1)}, bf16[38,32,128]{2,1,0:T(8,128)(2,1)S(1)}, u32[]{:S(2)}, u32[]{:S(2)}) collective-permute-start(bf16[38,32,128]{2,1,0:T(8,128)(2,1)} %get-tuple-element.47), channel_id=1, source_target_pairs={{0,8},{8,16},{16,24},{24,32},{32,40},{40,48},{48,56},{56,64},{64,7... | collective-permute-start | bytes 933896 | tf_op jit(solution)/shard_map/ppermute | solution.py:542
  53.8 11.9 %collective-permute-start.5 = (bf16[38,32,128]{2,1,0:T(8,128)(2,1)}, bf16[38,32,128]{2,1,0:T(8,128)(2,1)S(1)}, u32[]{:S(2)}, u32[]{:S(2)}) collective-permute-start(bf16[38,32,128]{2,1,0:T(8,128)(2,1)} %get-tuple-element.48), channel_id=1, source_target_pairs={{8,0},{16,8},{24,16},{32,24},{40,32},{48,40},{56,48},{64,56},{72,6... | collective-permute-start | bytes 933896 | tf_op jit(solution)/shard_map/ppermute | solution.py:547
  56.5 54.5 %collective-permute-start.8 = (bf16[36,32,128]{2,1,0:T(8,128)(2,1)S(1)}, bf16[36,32,128]{2,1,0:T(8,128)(2,1)S(1)}, u32[]{:S(2)}, u32[]{:S(2)}) collective-permute-start(bf16[36,32,128]{2,1,0:T(8,128)(2,1)S(1)} %copy-done.16), channel_id=1, source_target_pairs={{0,8},{8,16},{16,24},{24,32},{32,40},{40,48},{48,56},{56,64},{64,7... | collective-permute-start | bytes 884744 | tf_op jit(solution)/shard_map/ppermute | solution.py:542
  60.5 50.5 %collective-permute-start.9 = (bf16[36,32,128]{2,1,0:T(8,128)(2,1)S(1)}, bf16[36,32,128]{2,1,0:T(8,128)(2,1)S(1)}, u32[]{:S(2)}, u32[]{:S(2)}) collective-permute-start(bf16[36,32,128]{2,1,0:T(8,128)(2,1)S(1)} %copy-done.15), channel_id=1, source_target_pairs={{8,0},{16,8},{24,16},{32,24},{40,32},{48,40},{56,48},{64,56},{72,6... | collective-permute-start | bytes 884744 | tf_op jit(solution)/shard_map/ppermute | solution.py:547
  63.8 1.9 %copy-start.13 = (bf16[38,32,128]{2,1,0:T(8,128)(2,1)}, bf16[38,32,128]{2,1,0:T(8,128)(2,1)S(1)}, u32[]{:S(2)}) copy-start(bf16[38,32,128]{2,1,0:T(8,128)(2,1)S(1)} %collective-permute-done.4.refs_4_.refs_8_) | copy-start | bytes 933892
  65.7 0.7 copy-start.14
  65.7 0.9 copy-start.1
  73.1 23.0 %all-to-all-start.1 = ((f32[128,1,128]{2,1,0:T(1,128)}), f32[128,1,128]{2,1,0:T(1,128)S(1)}, u32[]{:S(2)}, u32[]{:S(2)}) async-start(f32[128,1,128]{2,1,0:T(1,128)} %bitcast.52), calls=%async_computation.1 | async-start | bytes 131072 | tf_op jit(solution)/shard_map/all_to_all | solution.py:551
  86.7 24.3 %collective-permute-start.6 = (bf16[36,32,128]{2,1,0:T(8,128)(2,1)}, bf16[36,32,128]{2,1,0:T(8,128)(2,1)S(1)}, u32[]{:S(2)}, u32[]{:S(2)}) collective-permute-start(bf16[36,32,128]{2,1,0:T(8,128)(2,1)} %get-tuple-element.57), channel_id=1, source_target_pairs={{0,8},{8,16},{16,24},{24,32},{32,40},{40,48},{48,56},{56,64},{64,7... | collective-permute-start | bytes 884744 | tf_op jit(solution)/shard_map/ppermute | solution.py:542
  90.0 21.0 %collective-permute-start.7 = (bf16[36,32,128]{2,1,0:T(8,128)(2,1)}, bf16[36,32,128]{2,1,0:T(8,128)(2,1)S(1)}, u32[]{:S(2)}, u32[]{:S(2)}) collective-permute-start(bf16[36,32,128]{2,1,0:T(8,128)(2,1)} %get-tuple-element.58), channel_id=1, source_target_pairs={{8,0},{16,8},{24,16},{32,24},{40,32},{48,40},{56,48},{64,56},{72,6... | collective-permute-start | bytes 884744 | tf_op jit(solution)/shard_map/ppermute | solution.py:547
  96.1 0.6 copy-start.6
  100.9 20.9 %all-to-all-start.2 = ((f32[128,4,128]{2,1,0:T(4,128)}), f32[128,4,128]{2,1,0:T(4,128)S(1)}, u32[]{:S(2)}, u32[]{:S(2)}) async-start(f32[128,4,128]{2,1,0:T(4,128)} %get-tuple-element.55), calls=%async_computation.2 | async-start | bytes 524288 | tf_op jit(solution)/shard_map/all_to_all | solution.py:551
  110.9 10.9 %copy-start.17 = (bf16[36,32,128]{2,1,0:T(8,128)(2,1)}, bf16[36,32,128]{2,1,0:T(8,128)(2,1)S(1)}, u32[]{:S(2)}) copy-start(bf16[36,32,128]{2,1,0:T(8,128)(2,1)S(1)} %collective-permute-done.8.refs_10_) | copy-start | bytes 884740
  111.0 10.9 %copy-start.18 = (bf16[36,32,128]{2,1,0:T(8,128)(2,1)}, bf16[36,32,128]{2,1,0:T(8,128)(2,1)S(1)}, u32[]{:S(2)}) copy-start(bf16[36,32,128]{2,1,0:T(8,128)(2,1)S(1)} %collective-permute-done.9.refs_11_) | copy-start | bytes 884740
  111.0 10.9 %copy-start.19 = (bf16[36,32,128]{2,1,0:T(8,128)(2,1)}, bf16[36,32,128]{2,1,0:T(8,128)(2,1)S(1)}, u32[]{:S(2)}) copy-start(bf16[36,32,128]{2,1,0:T(8,128)(2,1)S(1)} %collective-permute-done.6.refs_5_) | copy-start | bytes 884740
  111.0 10.9 %copy-start.20 = (bf16[36,32,128]{2,1,0:T(8,128)(2,1)}, bf16[36,32,128]{2,1,0:T(8,128)(2,1)S(1)}, u32[]{:S(2)}) copy-start(bf16[36,32,128]{2,1,0:T(8,128)(2,1)S(1)} %collective-permute-done.7.refs_6_) | copy-start | bytes 884740
  121.9 0.7 copy-start.5
  132.2 19.1 %all-to-all-start.3 = ((f32[128,8,128]{2,1,0:T(8,128)}), f32[128,8,128]{2,1,0:T(8,128)S(1)}, u32[]{:S(2)}, u32[]{:S(2)}) async-start(f32[128,8,128]{2,1,0:T(8,128)} %get-tuple-element.63), calls=%async_computation.3 | async-start | bytes 1048576 | tf_op jit(solution)/shard_map/all_to_all | solution.py:551
  136.8 12.6 %collective-permute-start.10 = (bf16[34,32,128]{2,1,0:T(8,128)(2,1)}, bf16[34,32,128]{2,1,0:T(8,128)(2,1)S(1)}, u32[]{:S(2)}, u32[]{:S(2)}) collective-permute-start(bf16[34,32,128]{2,1,0:T(8,128)(2,1)} %get-tuple-element.66), channel_id=1, source_target_pairs={{0,8},{8,16},{16,24},{24,32},{32,40},{40,48},{48,56},{56,64},{64,7... | collective-permute-start | bytes 835592 | tf_op jit(solution)/shard_map/ppermute | solution.py:542
  140.1 11.2 %collective-permute-start.11 = (bf16[34,32,128]{2,1,0:T(8,128)(2,1)}, bf16[34,32,128]{2,1,0:T(8,128)(2,1)S(1)}, u32[]{:S(2)}, u32[]{:S(2)}) collective-permute-start(bf16[34,32,128]{2,1,0:T(8,128)(2,1)} %get-tuple-element.67), channel_id=1, source_target_pairs={{8,0},{16,8},{24,16},{32,24},{40,32},{48,40},{56,48},{64,56},{72,6... | collective-permute-start | bytes 835592 | tf_op jit(solution)/shard_map/ppermute | solution.py:547
  149.4 1.9 %copy-start.21 = (bf16[34,32,128]{2,1,0:T(8,128)(2,1)}, bf16[34,32,128]{2,1,0:T(8,128)(2,1)S(1)}, u32[]{:S(2)}) copy-start(bf16[34,32,128]{2,1,0:T(8,128)(2,1)S(1)} %collective-permute-done.10.refs_6_.refs_5_) | copy-start | bytes 835588
  151.3 0.7 copy-start.22
  151.3 0.9 copy-start.3
  155.1 10.6 %copy-start.2 = (bf16[32,64,128]{2,1,0:T(8,128)(2,1)S(1)}, bf16[32,64,128]{2,1,0:T(8,128)(2,1)}, u32[]{:S(2)}) copy-start(bf16[32,64,128]{2,1,0:T(8,128)(2,1)} %get-tuple-element.54) | copy-start | bytes 1572868
  155.1 24.3 %all-to-all-start.4 = ((f32[128,8,128]{2,1,0:T(8,128)}), f32[128,8,128]{2,1,0:T(8,128)S(1)}, u32[]{:S(2)}, u32[]{:S(2)}) async-start(f32[128,8,128]{2,1,0:T(8,128)} %get-tuple-element.71), calls=%async_computation.4 | async-start | bytes 1048576 | tf_op jit(solution)/shard_map/all_to_all | solution.py:551
  179.4 0.8 copy-start.4

commit v4 on v3

--- a/solution.py
+++ b/solution.py
@@ -35,15 +35,18 @@
     return lax.broadcasted_iota(jnp.int32, (rows, 128), 1)
 
 
-def conv_rows(v_ref, w_ref, rows, emit):
+def windows_of(*refs):
+    if len(refs) == 1:
+        return lambda y: refs[0][y : y + 3].reshape(384, 128)
+    return lambda y: jnp.concatenate([ref[y + k] for k in range(3) for ref in refs], axis=0)
+
+
+def conv_rows(window, w_ref, rows, emit):
     lane = lanes(64)
     weights = w_ref[...]
     for y in range(0, rows, 2):
-        first = v_ref[y : y + 3].reshape(384, 128)
-        second = v_ref[y + 1 : y + 4].reshape(384, 128)
-        product = jnp.dot(
-            weights, jnp.concatenate([first, second], axis=1), preferred_element_type=F32
-        )
+        both = jnp.concatenate([window(y), window(y + 1)], axis=1)
+        product = jnp.dot(weights, both, preferred_element_type=F32)
         for k in range(2):
             part = product[:, k * 128 : (k + 1) * 128]
             emit(
@@ -62,6 +65,10 @@
 
 def twice(column):
     return jnp.concatenate([column, column], axis=0)
+
+
+def fourfold(column):
+    return twice(twice(column))
 
 
 def message(columns, msg_ref):
@@ -88,18 +95,8 @@
                 msg_ref[dz * C : (dz + 1) * C, 1 + 3 * k + dy, :] = group(dz, dy)
 
 
-def stats_out(send, h_ref, acc, start, low_ref, high_ref):
-    center = fold(total(acc)) / (2 * ROWS * 128)
-    both = twice(center)
-    spread = jnp.zeros((64, 128), F32)
-    for y in range(h_ref.shape[0]):
-        off = h_ref[y] - both
-        if start <= y < start + ROWS:
-            spread = spread + off * off
-        low_ref[y] = off[0:C].astype(BF16)
-        high_ref[y] = off[C:].astype(BF16)
-    send(low_ref, high_ref)
-    return center, fold(total(spread))
+def center_of(acc):
+    return fold(total(acc)) / (2 * ROWS * 128)
 
 
 def stats_of(rows, place_ref, cells, st_ref):
@@ -169,10 +166,13 @@
     return low * edge, edge, high * edge
 
 
-def masked(low, own, high, factors):
+def masked(values, factors):
     f_low, f_own, f_high = factors
+    own = values[C : 3 * C]
     own = own if f_own is None else own * f_own
-    return jnp.concatenate([low * f_low, own, high * f_high], axis=0).astype(BF16)
+    return jnp.concatenate([values[0:C] * f_low, own, values[3 * C :] * f_high], axis=0).astype(
+        BF16
+    )
 
 
 def weight_sums(g_ref, v_ref, first, acc_ref):
@@ -214,15 +214,11 @@
     down_ref[4:6] = cot[0:2]
 
 
-def planes_kernel(need, send, own, cot, y_low, y_high, up_ref, down_ref, t_up, t_down):
-    need(own, cot, y_low, y_high)
-    for part, rows, at in ((y_low, 4, 0), (own, ROWS, 4), (y_high, 4, ROWS + 4)):
-        down_ref[at : at + rows] = part[0:rows, 0:C]
-        up_ref[at : at + rows] = part[0:rows, C : 2 * C]
-    send(up_ref, down_ref)
-    for part, first, rows, at in ((y_low, 4, 2, 0), (cot, 0, ROWS, 2), (y_high, 4, 2, ROWS + 2)):
-        t_down[at : at + rows] = part[first : first + rows, 0:C]
-        t_up[at : at + rows] = part[first : first + rows, C : 2 * C]
+def planes_kernel(need, send, own, y_low, y_high, ext):
+    need(own, y_low, y_high)
+    ext[0:4] = y_low[0:4]
+    ext[4 : 4 + ROWS] = own[...]
+    ext[4 + ROWS : 8 + ROWS] = y_high[0:4]
 
 
 def weights_kernel(need, send, k1, k2, w1, w2, b1, b2):
@@ -260,44 +256,45 @@
                 b_ref[dz * 64 + C : dz * 64 + 64, here] = pltpu.roll(tile, C, 1).astype(BF16)
 
 
-def first_kernel(need, send, own, y_low, y_high, x_low, x_high, w, v, h, low, high, msg):
-    need(own, y_low, y_high, x_low, x_high)
-    for middle, rows, at in ((y_low, 4, 0), (own, ROWS, 4), (y_high, 4, ROWS + 4)):
-        for y in range(rows):
-            v[at + y] = jnp.concatenate([x_low[at + y], middle[y], x_high[at + y]], axis=0)
+def first_kernel(need, send, low, high, own, w, v, h, msg):
+    need(own, w)
+    acc = [jnp.zeros((64, 128), F32), jnp.zeros((64, 128), F32)]
+    for k, pair in enumerate(((low, own), (own, high))):
+
+        def emit(y, values, k=k):
+            h[y, 64 * k : 64 * k + 64] = values
+            if 3 <= y < 3 + ROWS:
+                acc[k] = acc[k] + values
+
+        conv_rows(windows_of(*pair), w, ROWS + 6, emit)
+    send(h)
+    for y in range(ROWS + 8):
+        v[y] = jnp.concatenate([low[y][C:], own[y], high[y][0:C]], axis=0)
     send(v)
-    need(w)
-    acc = [jnp.zeros((64, 128), F32)]
-
-    def emit(y, values):
-        h[y] = values
-        if 3 <= y < 3 + ROWS:
-            acc[0] = acc[0] + values
-
-    conv_rows(v, w, ROWS + 6, emit)
-    send(h)
-    columns = stats_out(send, h, acc[0], 3, low, high)
-    rows_message(columns, (feature_sums(v),), msg)
-
-
-def second_kernel(cells, need, send, place, r1, gb, h1, x_low, x_high, w, v, h, low, high, msg, st1, x1):
-    need(r1, gb)
-    mean, inverse, o_low, o_high = stats_of(r1[:, 0, :], place, cells, st1)
+    center = center_of(jnp.concatenate([acc[0][C:], acc[1][0:C]], axis=0))
+    both = twice(center)
+    spread = jnp.zeros((64, 128), F32)
+    for y in range(3, 3 + ROWS):
+        off = h[y, C : 3 * C] - both
+        spread = spread + off * off
+    rows_message((center, fold(total(spread))), (feature_sums(v),), msg)
+
+
+def second_kernel(
+    cells, need, send, place, r1, gb, h1, cot, y_low, y_high, w, v, h, low, high, msg, st1, x1
+):
+    need(gb)
+    mean, inverse, _, _ = stats_of(r1[:, 0, :], place, cells, st1)
     x1[...] = jnp.sum(r1[...], axis=0)
     send(st1, x1)
-    need(h1, x_low, x_high)
-    scale = inverse * gb[:, 0:1]
-    shift = gb[:, 1:2]
-    mean2, scale2, shift2 = twice(mean), twice(scale), twice(shift)
-    b_low, b_high = shift + o_low * scale, shift + o_high * scale
+    mean4, scale4 = fourfold(mean), fourfold(inverse * gb[:, 0:1])
+    shift4 = fourfold(gb[:, 1:2])
     rows = ROWS + 6
+    need(h1)
     for y in range(rows):
-        a_low = act(x_low[y].astype(F32) * scale + b_low)
-        a_own = act((h1[y] - mean2) * scale2 + shift2)
-        a_high = act(x_high[y].astype(F32) * scale + b_high)
-        v[y] = masked(a_low, a_own, a_high, kept(place, y, rows, 3))
+        v[y] = masked(act((h1[y] - mean4) * scale4 + shift4), kept(place, y, rows, 3))
     send(v)
-    need(w)
+    need(w, cot, y_low, y_high)
     acc = [jnp.zeros((64, 128), F32)]
 
     def emit(y, values):
@@ -305,9 +302,23 @@
         if 2 <= y < 2 + ROWS:
             acc[0] = acc[0] + values
 
-    conv_rows(v, w, ROWS + 4, emit)
+    rows = ROWS + 4
+    conv_rows(windows_of(v), w, rows, emit)
     send(h)
-    message(stats_out(send, h, acc[0], 2, low, high), msg)
+    center = center_of(acc[0])
+    both = twice(center)
+    spread = jnp.zeros((64, 128), F32)
+    for y in range(rows):
+        off = h[y] - both
+        if 2 <= y < 2 + ROWS:
+            spread = spread + off * off
+        low[y] = off[0:C].astype(BF16)
+        high[y] = off[C:].astype(BF16)
+        values = cot_row(cot, y_low, y_high, y)
+        low[rows + y] = values[0:C]
+        high[rows + y] = values[C:]
+    send(low, high)
+    message((center, fold(total(spread))), msg)
 
 
 def side_kernel(need, send, st1, h1, v1, xn, g, acc):
@@ -334,7 +345,7 @@
 
 
 def third_kernel(cells, need, send, place, r2, gb, cot, h2, xn, out, msg, st2):
-    need(r2, gb)
+    need(gb)
     mean, inverse, _, _ = stats_of(r2[...], place, cells, st2)
     need(h2, cot)
     mean2, inverse2 = twice(mean), twice(inverse)
@@ -355,15 +366,14 @@
 
 
 def fourth_kernel(
-    cells, need, send, place, r3, st2, gb, h2, x_low, x_high, cot, y_low, y_high, t_low, t_high,
-    w, st1, h1, v2, v1, slope1, low, high, msg, t3, v, g, acc, acc1,
+    cells, need, send, place, r3, st2, gb, h2, x_low, x_high, cot, y_low, y_high, w, st1, h1, v2, v1, slope1, low, high, msg, t3, v, g, acc, acc1,
 ):
-    need(r3, st2, gb)
+    need(st2, gb)
     mean, inverse, o_low, o_high = kept_stats(st2)
     t3[...] = jnp.sum(r3[...], axis=0)
     send(t3)
     nsum, plain = sums_of(t3[0:1])
-    need(h2, x_low, x_high, cot, y_low, y_high, t_low, t_high)
+    need(h2, x_low, x_high, cot, y_low, y_high)
     gain, bias = gb[:, 2:3], gb[:, 3:4]
     lead = gain * inverse
     p_mean, n_mean = plain / cells, nsum / cells
@@ -378,10 +388,11 @@
     lane = lanes(64)
     rows = ROWS + 4
     for y in range(rows):
-        g_low = grad((x_low[y].astype(F32) + o_low) * inverse, t_low[y], *one)
+        g_low = grad((x_low[y].astype(F32) + o_low) * inverse, x_low[rows + y], *one)
         g_own = grad((h2[y] - mean2) * inverse2, cot_row(cot, y_low, y_high, y), *two)
-        g_high = grad((x_high[y].astype(F32) + o_high) * inverse, t_high[y], *one)
-        v[y] = masked(g_low, g_own, g_high, kept(place, y, rows, 2))
+        g_high = grad((x_high[y].astype(F32) + o_high) * inverse, x_high[rows + y], *one)
+        both = jnp.concatenate([g_low, g_own, g_high], axis=0)
+        v[y] = masked(both, kept(place, y, rows, 2))
         if 2 <= y < 2 + ROWS:
             put_shifted(g, y - 2, g_own, lane)
     need(v2)
@@ -404,7 +415,7 @@
             sums[1] = sums[1] + slope
             put_shifted(g, y - 1, slope, lane)
 
-    conv_rows(v, w, ROWS + 2, emit)
+    conv_rows(windows_of(v), w, ROWS + 2, emit)
     send(slope1, low, high)
     need(v1)
     weight_sums(g, v1, 3, acc1)
@@ -414,7 +425,7 @@
 
 
 def owner_kernel(cells, need, send, place, r4, st1, gb, t3, x1, msg, norms, t4):
-    need(r4, st1, gb, t3, x1)
+    need(st1, gb, t3, x1)
     _, inverse, _, _ = kept_stats(st1)
     t4[...] = jnp.sum(r4[...], axis=0)
     nsum, plain = sums_of(t4[0:1])
@@ -437,7 +448,6 @@
 
 
 def finish_kernel(need, send, parts, one, two):
-    need(parts)
     for dz in range(3):
         for dy in range(3):
             for k, out in enumerate((one, two)):
@@ -446,49 +456,46 @@
                     out[dx * 9 + dy * 3 + dz] = tile[:, dx * C : (dx + 1) * C]
 
 
-def fifth_kernel(
-    cells, need, send, place, t4, st1, gb, slope1, s_low, s_high, h1, x_low, x_high, w, out, v
-):
+def fifth_kernel(cells, need, send, place, t4, st1, gb, h1, slope1, s_low, s_high, w, out, v):
     need(t4, st1, gb)
-    mean, inverse, o_low, o_high = kept_stats(st1)
+    mean, inverse, _, _ = kept_stats(st1)
     nsum, plain = sums_of(t4[0:1])
-    need(slope1, s_low, s_high, h1, x_low, x_high)
-    lead = gb[:, 0:1] * inverse
-    p_mean, n_mean = plain / cells, nsum / cells
-    mean2, inverse2, lead2 = twice(mean), twice(inverse), twice(lead)
-    p_mean2, n_mean2 = twice(p_mean), twice(n_mean)
+    mean4, inverse4 = fourfold(mean), fourfold(inverse)
+    lead4 = fourfold(gb[:, 0:1] * inverse)
+    p_mean4, n_mean4 = fourfold(plain / cells), fourfold(nsum / cells)
     rows = ROWS + 2
+    need(slope1, s_low, s_high, h1)
     for y in range(rows):
-        n_low = (x_low[y + 2].astype(F32) + o_low) * inverse
-        n_own = (h1[y + 2] - mean2) * inverse2
-        n_high = (x_high[y + 2].astype(F32) + o_high) * inverse
-        g_low = lead * (s_low[y].astype(F32) - p_mean - n_low * n_mean)
-        g_own = lead2 * (slope1[y] - p_mean2 - n_own * n_mean2)
-        g_high = lead * (s_high[y].astype(F32) - p_mean - n_high * n_mean)
-        v[y] = masked(g_low, g_own, g_high, kept(place, y, rows, 1))
-
+        slope = jnp.concatenate(
+            [s_low[y].astype(F32), slope1[y], s_high[y].astype(F32)], axis=0
+        )
+        normed = (h1[y + 2] - mean4) * inverse4
+        v[y] = masked(lead4 * (slope - p_mean4 - normed * n_mean4), kept(place, y, rows, 1))
     need(w)
 
     def emit(y, values):
         out[y] = values.astype(BF16)
 
-    conv_rows(v, w, ROWS, emit)
-
-
-def call(kernel, ins, outs, name, scratch=(), smem_first=True, after=()):
+    conv_rows(windows_of(v), w, ROWS, emit)
+
+
+def call(kernel, ins, outs, name, scratch=(), smem_first=True, after=(), near=0, cut=()):
     lead = 1 if smem_first else 0
-    count_in, count_out = len(ins) - lead, len(outs)
+    count_in, count_out = len(ins) - lead - near, len(outs)
+    far_ins = ins[lead + near :]
+    own = [any(a is b for b in cut) for a in far_ins]
+    shapes = [(a.shape[0], 2 * C, 128) if c else a.shape for a, c in zip(far_ins, own)]
 
     def body(*refs):
-        first, rest = refs[:lead], refs[lead:]
+        first, rest = refs[: lead + near], refs[lead + near :]
         parts = []
         for size in (count_in, len(after), count_out, count_in, count_out, 2):
             parts.append(rest[:size])
             rest = rest[size:]
         sources, _, targets, in_bufs, out_bufs, (in_sems, out_sems) = parts
         arriving = [
-            pltpu.make_async_copy(a, b, in_sems.at[k])
-            for k, (a, b) in enumerate(zip(sources, in_bufs))
+            pltpu.make_async_copy(a.at[:, C : 3 * C] if c else a, b, in_sems.at[k])
+            for k, (a, b, c) in enumerate(zip(sources, in_bufs, own))
         ]
         leaving = [
             pltpu.make_async_copy(a, b, out_sems.at[k])
@@ -520,12 +527,14 @@
     return pl.pallas_call(
         body,
         out_shape=outs,
-        in_specs=[SM] * lead + [far] * (count_in + len(after)),
+        in_specs=[SM] * lead
+        + [pl.BlockSpec(memory_space=pltpu.VMEM)] * near
+        + [far] * (count_in + len(after)),
         out_specs=[far] * count_out,
         scratch_shapes=[
-            *[pltpu.VMEM(a.shape, a.dtype) for a in ins[lead:]],
+            *[pltpu.VMEM(shape, a.dtype) for shape, a in zip(shapes, far_ins)],
             *[pltpu.VMEM(a.shape, a.dtype) for a in outs],
-            pltpu.SemaphoreType.DMA((count_in,)),
+            pltpu.SemaphoreType.DMA((max(count_in, 1),)),
             pltpu.SemaphoreType.DMA((count_out,)),
             *scratch,
         ],
@@ -568,9 +577,7 @@
     def rims(rows):
         return [sh((rows, C, 128), BF16)] * 2
 
-    msg, four, five, wide = (
-        sh((count, *tile), F32) for tile in ((128,), (4, 128), (5, 128), (8, 128))
-    )
+    msg, four, wide = (sh((count, *tile), F32) for tile in ((128,), (4, 128), (8, 128)))
     stats = sh((C, 128), F32)
     corr = (pltpu.VMEM((192, ROWS * 128), BF16), pltpu.VMEM((192, 384), F32))
 
@@ -578,10 +585,10 @@
         pack_kernel, (own, cot), [sh((6, 64, 128), BF16)] * 2, "pack", smem_first=False
     )
     y_low, y_high = up(y_up, GY), down(y_down, GY)
-    x_up, x_down, t_up, t_down = call(
-        planes_kernel, (own, cot, y_low, y_high), rims(40) + rims(36), "planes", smem_first=False
-    )
-    x_low, x_high = up(x_up, GX), down(x_down, GX)
+    (ext,) = call(
+        planes_kernel, (own, y_low, y_high), [sh((40, 64, 128), BF16)], "planes", smem_first=False
+    )
+    x_low, x_high = up(ext, GX), down(ext, GX)
     taps = [
         jnp.transpose(k, (2, 3, 4, 0, 1)).reshape(27, C, C) for k in (kernel_one, kernel_two)
     ]
@@ -589,27 +596,27 @@
         weights_kernel, taps, [sh((192, 384), BF16)] * 4, "weights", smem_first=False
     )
 
-    v1, h1, low, high, m1 = call(
+    v1, h1, m1 = call(
         first_kernel,
-        (own, y_low, y_high, x_low, x_high, w1),
-        [sh((40, 128, 128), BF16), sh((38, 64, 128), F32), *rims(38), five],
+        (x_low, x_high, ext, w1),
+        [sh((40, 128, 128), BF16), sh((38, 128, 128), F32), four],
         "conv_one",
         smem_first=False,
-    )
-    h1_low, h1_high = up(high, GX), down(low, GX)
+        near=2,
+    )
     r1 = share(m1)
 
     v2, h2, low, high, m2, st1, x1 = call(
         lambda *refs: second_kernel(cells, *refs),
-        (place, r1, gb, h1, h1_low, h1_high, w2),
+        (place, r1, gb, h1, cot, y_low, y_high, w2),
         [
-            sh((38, 128, 128), BF16), sh((36, 64, 128), F32), *rims(36), msg, stats,
-            sh((5, 128), F32),
+            sh((38, 128, 128), BF16), sh((36, 64, 128), F32), *rims(72), msg, stats,
+            sh((4, 128), F32),
         ],
         "conv_two",
+        near=1,
     )
     h2_low, h2_high = up(high, GX), down(low, GX)
-    t_low, t_high = up(t_up, GX), down(t_down, GX)
     r2 = share(m2)
     (xn,) = call(
         side_kernel,
@@ -618,6 +625,7 @@
         "normed_features",
         scratch=corr,
         smem_first=False,
+        cut=(h1,),
     )
 
     output, m3, st2 = call(
@@ -625,17 +633,20 @@
         (place, r2, gb, cot, h2, xn),
         [sh((ROWS, 64, 128), BF16), four, stats],
         "slope_two",
+        near=1,
     )
     r3 = share(m3)
 
     slope1, low, high, m4, t3 = call(
         lambda *refs: fourth_kernel(cells, *refs),
         (
-            place, r3, st2, gb, h2, h2_low, h2_high, cot, y_low, y_high, t_low, t_high,
+            place, r3, st2, gb, h2, h2_low, h2_high, cot, y_low, y_high,
             b2, st1, h1, v2, v1,
         ),
         [sh((34, 64, 128), F32), *rims(34), wide, sh((4, 128), F32)],
         "back_two",
+        near=1,
+        cut=(h1,),
         scratch=(pltpu.VMEM((36, 128, 128), BF16), *corr, corr[1]),
     )
     s_low, s_high = up(high, GX), down(low, GX)
@@ -646,17 +657,18 @@
         (place, r4, st1, gb, t3, x1),
         [wide, sh((4, C), F32), sh((8, 128), F32)],
         "own_rows",
+        near=1,
         after=(s_low, s_high),
     )
     r5 = share(m5)
     (grad,) = call(
         lambda *refs: fifth_kernel(cells, *refs),
-        (place, t4, st1, gb, slope1, s_low, s_high, h1, h1_low, h1_high, b1),
+        (place, t4, st1, gb, h1, slope1, s_low, s_high, b1),
         [sh((ROWS, 64, 128), BF16)],
         "back_one",
         scratch=(pltpu.VMEM((34, 128, 128), BF16),),
     )
-    grads = call(finish_kernel, (r5,), [sh((27, C, C), F32)] * 2, "finish", smem_first=False)
+    grads = call(finish_kernel, (r5,), [sh((27, C, C), F32)] * 2, "finish", smem_first=False, near=1)
     one, two = [jnp.transpose(k.reshape(3, 3, 3, C, C), (3, 4, 0, 1, 2)) for k in grads]
 
     def back(rows):

time: 184 us -> 181 us (0.984)
  starting transfers between devices: 81.8 us -> 55.2 us
  blocking collectives: 0 us -> 21.1 us
  Pallas kernels: 45.4 us -> 48.7 us
    all_to_all x0 -> x1, blocking collectives: none -> 21.1 us  [share(): return lax.all_to_all(msg, ALL, 0, 0, tiled=True)]
    all_to_all x5 -> x4, starting transfers between devices: 51.4 us -> 33.8 us  [share(): return lax.all_to_all(msg, ALL, 0, 0, tiled=True)]
    ppermute x6 -> x4, starting transfers between devices: 22.1 us -> 15.6 us  [up(): return lax.ppermute(values, axes, [(i, i + 1) for i in range(count - 1)])]
    pallas_call x11, Pallas kernels: 45.4 us -> 48.7 us  [call(): pl.pallas_call(body, out_shape=outs, in_specs=[SM] * lead + [pl.BlockSpec...]
    ppermute x6 -> x4, waiting for transfers between devices: 11.9 us -> 14.6 us  [down(): return lax.ppermute(values, axes, [(i + 1, i) for i in range(count - 1)])]
    ppermute x6 -> x4, starting transfers between devices: 8.38 us -> 5.8 us  [down(): return lax.ppermute(values, axes, [(i + 1, i) for i in range(count - 1)])]
    ppermute x6 -> x4, waiting for transfers between devices: 12 us -> 9.9 us  [up(): return lax.ppermute(values, axes, [(i, i + 1) for i in range(count - 1)])]
    all_to_all x5 -> x4, waiting for transfers between devices: 16.9 us -> 15.5 us  [share(): return lax.all_to_all(msg, ALL, 0, 0, tiled=True)]
  transfers between devices with their start and end apart: 17 -> 12, of which waited for: 10 -> 8; matrix products, arithmetic and copies ran while one was open for 3% -> 3% of each run, Pallas kernels for 12% -> 9%
where the time goes in v4:
time: 181 us; the launch traced here: 180 us
  starting transfers between devices  55.2 us (30%)
  Pallas kernels  48.7 us (27%)
  waiting for transfers between devices  40 us (22%)
  blocking collectives  21.1 us (12%)
  local copies, waits for them, and re-layouts  13.5 us (7%)
    pallas_call x11, Pallas kernels, call(): pl.pallas_call(body, out_shape=outs, in_specs=[SM] * lead + [pl.BlockSpec...  48.7 us
    all_to_all x4, starting transfers between devices, share(): return lax.all_to_all(msg, ALL, 0, 0, tiled=True)  33.8 us
    all_to_all x1, blocking collectives, share(): return lax.all_to_all(msg, ALL, 0, 0, tiled=True)  21.1 us
    ppermute x4, starting transfers between devices, up(): return lax.ppermute(values, axes, [(i, i + 1) for i in range(count - 1)])  15.6 us
    all_to_all x4, waiting for transfers between devices, share(): return lax.all_to_all(msg, ALL, 0, 0, tiled=True)  15.5 us
    ppermute x4, waiting for transfers between devices, down(): return lax.ppermute(values, axes, [(i + 1, i) for i in range(count - 1)])  14.6 us
    ppermute x4, waiting for transfers between devices, up(): return lax.ppermute(values, axes, [(i, i + 1) for i in range(count - 1)])  9.9 us
    ppermute x4, starting transfers between devices, down(): return lax.ppermute(values, axes, [(i + 1, i) for i in range(count - 1)])  5.8 us
  transfers between devices with their start and end apart: 12, of which 8 were waited for; matrix products, arithmetic and copies ran while one was open for 3% of the time, Pallas kernels for 9%

profile of v4, /device:TPU:1, one launch (start us, length us, event | category | flops | bytes accessed | tf_op | source)
XLA Modules:
  0.0 179.6 jit_solution(11877739717340553810)
XLA Ops:
  0.6 0.0 copy-start.2
  0.6 2.2 %copy.21 = bf16[32,2,32,128]{3,2,1,0:T(8,128)(2,1)} copy(bf16[32,2,32,128]{3,0,1,2:T(8,128)(2,1)} %bitcast.43) | data formatting | bytes 1048576 | tf_op jit(solution)/shard_map/transpose | solution.py:574
  2.9 0.0 copy-done.2
  2.9 1.1 copy.22
  4.0 1.9 %pack.1 = (bf16[6,64,128]{2,1,0:T(8,128)(2,1)}, bf16[6,64,128]{2,1,0:T(8,128)(2,1)}) custom-call(bf16[32,64,128]{2,1,0:T(8,128)(2,1)} %bitcast.48, bf16[32,64,128]{2,1,0:T(8,128)(2,1)} %bitcast.39), custom_call_target="tpu_custom_call" | custom-call | flops 2000000000 | bytes 6000000 | tf_op jit(solution)/shard_map/pack/pallas_call | solution.py:527
  5.9 4.9 %collective-permute-start = (bf16[6,64,128]{2,1,0:T(8,128)(2,1)}, bf16[6,64,128]{2,1,0:T(8,128)(2,1)S(1)}, u32[]{:S(2)}, u32[]{:S(2)}) collective-permute-start(bf16[6,64,128]{2,1,0:T(8,128)(2,1)} %get-tuple-element.34), channel_id=1, source_target_pairs={{0,1},{1,2},{2,3},{3,4},{4,5},{5,6},{6,7},{8,9},{9,10},{10,11},{11... | collective-permute-start | bytes 294920 | tf_op jit(solution)/shard_map/ppermute | solution.py:551
  10.9 1.9 %collective-permute-start.1 = (bf16[6,64,128]{2,1,0:T(8,128)(2,1)}, bf16[6,64,128]{2,1,0:T(8,128)(2,1)S(1)}, u32[]{:S(2)}, u32[]{:S(2)}) collective-permute-start(bf16[6,64,128]{2,1,0:T(8,128)(2,1)} %get-tuple-element.35), channel_id=1, source_target_pairs={{1,0},{2,1},{3,2},{4,3},{5,4},{6,5},{7,6},{9,8},{10,9},{11,10},{12... | collective-permute-start | bytes 294920 | tf_op jit(solution)/shard_map/ppermute | solution.py:556
  12.8 0.0 collective-permute-done.refs_1_.refs_5_.refs_8_
  12.8 0.0 copy-start.7
  12.8 4.2 %collective-permute-done.1.refs_2_.refs_6_.refs_9_ = bf16[6,64,128]{2,1,0:T(8,128)(2,1)S(1)} collective-permute-done((bf16[6,64,128]{2,1,0:T(8,128)(2,1)}, bf16[6,64,128]{2,1,0:T(8,128)(2,1)S(1)}, u32[]{:S(2)}, u32[]{:S(2)}) %collective-permute-start.1) | collective-permute-done | bytes 98336 | tf_op jit(solution)/shard_map/ppermute | solution.py:556
  17.0 0.0 copy-done.7
  17.0 0.6 copy-done.8
  17.7 2.0 %planes.1.refs_2_ = bf16[40,64,128]{2,1,0:T(8,128)(2,1)} custom-call(bf16[32,64,128]{2,1,0:T(8,128)(2,1)} %bitcast.49, bf16[6,64,128]{2,1,0:T(8,128)(2,1)} %copy-done.7, bf16[6,64,128]{2,1,0:T(8,128)(2,1)} %copy-done.8), custom_call_target="tpu_custom_call" | custom-call | flops 2000000000 | bytes 6000000 | tf_op jit(solution)/shard_map/planes/pallas_call | solution.py:527
  19.7 1.3 collective-permute-start.3
  21.0 4.0 %collective-permute-start.2 = (bf16[40,64,128]{2,1,0:T(8,128)(2,1)}, bf16[40,64,128]{2,1,0:T(8,128)(2,1)S(1)}, u32[]{:S(2)}, u32[]{:S(2)}) collective-permute-start(bf16[40,64,128]{2,1,0:T(8,128)(2,1)} %planes.1.refs_2_), channel_id=1, source_target_pairs={{0,8},{8,16},{16,24},{24,32},{32,40},{40,48},{48,56},{56,64},{64,7... | collective-permute-start | bytes 1966088 | tf_op jit(solution)/shard_map/ppermute | solution.py:551
  25.0 2.4 %weights.1 = (bf16[192,384]{1,0:T(8,128)(2,1)}, bf16[192,384]{1,0:T(8,128)(2,1)}, bf16[192,384]{1,0:T(8,128)(2,1)}, bf16[192,384]{1,0:T(8,128)(2,1)}) custom-call(bf16[27,32,32]{2,1,0:T(8,128)(2,1)} %bitcast.57, bf16[27,32,32]{2,1,0:T(8,128)(2,1)} %bitcast.58), custom_call_target="tpu_custom_call" | custom-call | flops 2000000000 | bytes 6000000 | tf_op jit(solution)/shard_map/weights/pallas_call | solution.py:527
  27.4 8.6 %collective-permute-done.3.refs_1_ = bf16[40,64,128]{2,1,0:T(8,128)(2,1)S(1)} collective-permute-done((bf16[40,64,128]{2,1,0:T(8,128)(2,1)}, bf16[40,64,128]{2,1,0:T(8,128)(2,1)S(1)}, u32[]{:S(2)}, u32[]{:S(2)}) %collective-permute-start.3) | collective-permute-done | bytes 655392 | tf_op jit(solution)/shard_map/ppermute | solution.py:556
  36.0 1.9 %collective-permute-done.2.refs_0_ = bf16[40,64,128]{2,1,0:T(8,128)(2,1)S(1)} collective-permute-done((bf16[40,64,128]{2,1,0:T(8,128)(2,1)}, bf16[40,64,128]{2,1,0:T(8,128)(2,1)S(1)}, u32[]{:S(2)}, u32[]{:S(2)}) %collective-permute-start.2) | collective-permute-done | bytes 655392 | tf_op jit(solution)/shard_map/ppermute | solution.py:551
  37.8 0.0 copy-done.14
  37.8 0.8 copy-done.15
  38.7 6.8 %conv_one.1 = (bf16[40,128,128]{2,1,0:T(8,128)(2,1)}, f32[38,128,128]{2,1,0:T(8,128)}, f32[128,4,128]{2,1,0:T(4,128)}) custom-call(bf16[40,64,128]{2,1,0:T(8,128)(2,1)} %copy-done.15, bf16[40,64,128]{2,1,0:T(8,128)(2,1)} %copy-done.14, bf16[40,64,128]{2,1,0:T(8,128)(2,1)} %planes.1.refs_2_, bf16[192,384]{1,0:T(8,128)(2,1)} %get-tuple-element.36.refs_3_), custom_call_target="tpu_custom_call" | custom-call | flops 2000000000 | bytes 6000000 | tf_op jit(solution)/shard_map/conv_one/pallas_call | solution.py:527
  45.5 13.9 %all-to-all-start = ((f32[128,4,128]{2,1,0:T(4,128)}), f32[128,4,128]{2,1,0:T(4,128)S(1)}, u32[]{:S(2)}, u32[]{:S(2)}) async-start(f32[128,4,128]{2,1,0:T(4,128)} %get-tuple-element.37), calls=%async_computation | async-start | bytes 524288 | tf_op jit(solution)/shard_map/all_to_all | solution.py:560
  59.5 0.0 copy-done.10
  59.5 0.0 copy-done.11
  59.5 0.0 copy-done.12
  59.5 0.0 copy-done.13
  59.5 0.7 copy.23.refs_2_.refs_3_
  60.2 0.6 stack.62.refs_0_
  60.8 9.6 %all-to-all-done.refs_1_ = f32[128,4,128]{2,1,0:T(4,128)S(1)} async-done(((f32[128,4,128]{2,1,0:T(4,128)}), f32[128,4,128]{2,1,0:T(4,128)S(1)}, u32[]{:S(2)}, u32[]{:S(2)}) %all-to-all-start) | async-done | bytes 262176 | tf_op jit(solution)/shard_map/all_to_all | solution.py:560
  70.4 0.7 copy-done.6
  71.1 7.1 %conv_two.1 = (bf16[38,128,128]{2,1,0:T(8,128)(2,1)}, f32[36,64,128]{2,1,0:T(8,128)}, bf16[72,32,128]{2,1,0:T(8,128)(2,1)}, bf16[72,32,128]{2,1,0:T(8,128)(2,1)}...) custom-call(s32[7]{0:T(128)} %stack.62.refs_0_, f32[128,4,128]{2,1,0:T(4,128)} %copy-done.6, ...), custom_call_target="tpu_custom_call" | custom-call | flops 2000000000 | bytes 6000000 | tf_op jit(solution)/shard_map/conv_two/pallas_call | solution.py:527
  78.2 4.6 %all-to-all-start.1 = ((f32[128,1,128]{2,1,0:T(1,128)}), f32[128,1,128]{2,1,0:T(1,128)S(1)}, u32[]{:S(2)}, u32[]{:S(2)}) async-start(f32[128,1,128]{2,1,0:T(1,128)} %bitcast.51), calls=%async_computation.1 | async-start | bytes 131072 | tf_op jit(solution)/shard_map/all_to_all | solution.py:560
  82.8 3.3 %collective-permute-start.4 = (bf16[72,32,128]{2,1,0:T(8,128)(2,1)}, bf16[72,32,128]{2,1,0:T(8,128)(2,1)S(1)}, u32[]{:S(2)}, u32[]{:S(2)}) collective-permute-start(bf16[72,32,128]{2,1,0:T(8,128)(2,1)} %get-tuple-element.47), channel_id=1, source_target_pairs={{0,8},{8,16},{16,24},{24,32},{32,40},{40,48},{48,56},{56,64},{64,7... | collective-permute-start | bytes 1769480 | tf_op jit(solution)/shard_map/ppermute | solution.py:551
  86.2 1.3 collective-permute-start.5
  87.5 3.7 %normed_features.1.refs_5_ = f32[9,32,128]{2,1,0:T(8,128)} custom-call(f32[32,128]{1,0:T(8,128)} %get-tuple-element.42.refs_0_.refs_11_.refs_2_, f32[38,128,128]{2,1,0:T(8,128)} %get-tuple-element.38.refs_3_.refs_1_.refs_12_.refs_4_, bf16[40,128,128]{2,1,0:T(8,128)(2,1)} %get-tuple-element.43.refs_2_.refs_14_), custom_call_target="tpu_custom_call" | custom-call | flops 2000000000 | bytes 6000000 | tf_op jit(solution)/shard_map/normed_features/pallas_call | solution.py:527
  91.2 1.0 all-to-all-done.1
  92.2 0.6 copy-done.9
  92.8 4.4 %slope_two.1 = (bf16[32,64,128]{2,1,0:T(8,128)(2,1)}, f32[128,4,128]{2,1,0:T(4,128)}, f32[32,128]{1,0:T(8,128)}) custom-call(s32[7]{0:T(128)} %stack.62.refs_0_, f32[128,128]{1,0:T(8,128)} %bitcast.52, f32[32,4]{1,0:T(8,128)} %copy.23.refs_2_.refs_3_, bf16[32,64,128]{2,1,0:T(8,128)(2,1)} %bitcast.41, f32[36,64,128]{2,1,0:T(8,128)} %get-tuple-element.41.refs_4_, ...), custom_call_target="tpu_custom_call" | custom-call | flops 2000000000 | bytes 6000000 | tf_op jit(solution)/shard_map/slope_two/pallas_call | solution.py:527
  97.2 21.1 %all_to_all.31.refs_1_ = f32[128,4,128]{2,1,0:T(4,128)} all-to-all(f32[128,4,128]{2,1,0:T(4,128)} %get-tuple-element.45), channel_id=1, replica_groups=mesh['gx_0'=4,'gx_1'=4,'gy_0'=4,'gy_1'=2] {'gx_0','gx_1','gy_0','gy_1'}, dimensions={0} | all-to-all | bytes 524288 | tf_op jit(solution)/shard_map/all_to_all | solution.py:560
  118.3 0.0 collective-permute-done.4.refs_5_
  118.3 0.0 collective-permute-done.5.refs_6_
  118.3 0.0 copy-start.1
  118.3 0.8 copy-done
  119.1 0.2 copy-done.1
  119.4 9.8 %back_two.1 = (f32[34,64,128]{2,1,0:T(8,128)}, bf16[34,32,128]{2,1,0:T(8,128)(2,1)}, bf16[34,32,128]{2,1,0:T(8,128)(2,1)}, f32[128,8,128]{2,1,0:T(8,128)}, f32[4,128]{1,0:T(4,128)}) custom-call(s32[7]{0:T(128)} %stack.62.refs_0_, f32[128,4,128]{2,1,0:T(4,128)} %all_to_all.31.refs_1_, f32[32,128]{1,0:T(8,128)} %get-tuple-element.46.refs_2_, ...), custom_call_target="tpu_custom_call" | custom-call | flops 2000000000 | bytes 6000000 | tf_op jit(solution)/shard_map/back_two/pallas_call | solution.py:527
  129.1 4.6 %all-to-all-start.3 = ((f32[128,8,128]{2,1,0:T(8,128)}), f32[128,8,128]{2,1,0:T(8,128)S(1)}, u32[]{:S(2)}, u32[]{:S(2)}) async-start(f32[128,8,128]{2,1,0:T(8,128)} %get-tuple-element.51), calls=%async_computation.3 | async-start | bytes 1048576 | tf_op jit(solution)/shard_map/all_to_all | solution.py:560
  133.8 3.3 %collective-permute-start.6 = (bf16[34,32,128]{2,1,0:T(8,128)(2,1)}, bf16[34,32,128]{2,1,0:T(8,128)(2,1)S(1)}, u32[]{:S(2)}, u32[]{:S(2)}) collective-permute-start(bf16[34,32,128]{2,1,0:T(8,128)(2,1)} %get-tuple-element.54), channel_id=1, source_target_pairs={{0,8},{8,16},{16,24},{24,32},{32,40},{40,48},{48,56},{56,64},{64,7... | collective-permute-start | bytes 835592 | tf_op jit(solution)/shard_map/ppermute | solution.py:551
  137.1 1.3 collective-permute-start.7
  138.4 8.0 %collective-permute-done.6.refs_6_ = bf16[34,32,128]{2,1,0:T(8,128)(2,1)S(1)} collective-permute-done((bf16[34,32,128]{2,1,0:T(8,128)(2,1)}, bf16[34,32,128]{2,1,0:T(8,128)(2,1)S(1)}, u32[]{:S(2)}, u32[]{:S(2)}) %collective-permute-start.6) | collective-permute-done | bytes 278560 | tf_op jit(solution)/shard_map/ppermute | solution.py:551
  146.4 1.8 %collective-permute-done.7.refs_7_ = bf16[34,32,128]{2,1,0:T(8,128)(2,1)S(1)} collective-permute-done((bf16[34,32,128]{2,1,0:T(8,128)(2,1)}, bf16[34,32,128]{2,1,0:T(8,128)(2,1)S(1)}, u32[]{:S(2)}, u32[]{:S(2)}) %collective-permute-start.7) | collective-permute-done | bytes 278560 | tf_op jit(solution)/shard_map/ppermute | solution.py:556
  148.3 0.0 all-to-all-done.3.refs_1_
  148.3 0.0 copy-done.16
  148.3 0.7 copy-done.17
  149.0 0.2 copy-done.4
  149.1 3.0 %own_rows.1 = (f32[128,8,128]{2,1,0:T(8,128)}, f32[4,32]{1,0:T(4,128)}, f32[8,128]{1,0:T(8,128)}) custom-call(s32[7]{0:T(128)} %stack.62.refs_0_, f32[128,8,128]{2,1,0:T(8,128)} %copy-done.4, f32[32,128]{1,0:T(8,128)} %get-tuple-element.42.refs_0_.refs_11_.refs_2_, f32[32,4]{1,0:T(8,128)} %copy.23.refs_2_.refs_3_, f32[4,128]{1,0:T(4,128)} %get-tuple-element.52.refs_4_, ...), custom_call_target="tpu_custom_call" | custom-call | flops 2000000000 | bytes 6000000 | tf_op jit(solution)/shard_map/own_rows/pallas_call | solution.py:527
  152.1 0.0 copy-start.3
  152.1 10.6 %all-to-all-start.4 = ((f32[128,8,128]{2,1,0:T(8,128)}), f32[128,8,128]{2,1,0:T(8,128)S(1)}, u32[]{:S(2)}, u32[]{:S(2)}) async-start(f32[128,8,128]{2,1,0:T(8,128)} %get-tuple-element.59), calls=%async_computation.4 | async-start | bytes 1048576 | tf_op jit(solution)/shard_map/all_to_all | solution.py:560
  162.8 0.0 copy-done.3
  162.8 1.1 copy.34
  163.9 5.4 %back_one.1 = bf16[32,64,128]{2,1,0:T(8,128)(2,1)} custom-call(s32[7]{0:T(128)} %stack.62.refs_0_, f32[8,128]{1,0:T(8,128)} %get-tuple-element.56.refs_1_, f32[32,128]{1,0:T(8,128)} %get-tuple-element.42.refs_0_.refs_11_.refs_2_, f32[32,4]{1,0:T(8,128)} %copy.23.refs_2_.refs_3_, f32[38,128,128]{2,1,0:T(8,128)} %get-tuple-element.38.refs_3_.refs_1_.refs_12_.refs_4_, ...), custom_call_target="tpu_custom_call" | custom-call | flops 2000000000 | bytes 6000000 | tf_op jit(solution)/shard_map/back_one/pallas_call | solution.py:527
  169.3 2.2 %copy.33 = bf16[32,2,32,128]{3,0,1,2:T(8,128)(2,1)} copy(bf16[32,2,32,128]{3,2,1,0:T(8,128)(2,1)} %bitcast.50) | data formatting | bytes 1048576 | tf_op jit(solution)/shard_map/reshape | solution.py:675
  171.5 5.0 %all-to-all-done.4.refs_0_ = f32[128,8,128]{2,1,0:T(8,128)S(1)} async-done(((f32[128,8,128]{2,1,0:T(8,128)}), f32[128,8,128]{2,1,0:T(8,128)S(1)}, u32[]{:S(2)}, u32[]{:S(2)}) %all-to-all-start.4) | async-done | bytes 524320 | tf_op jit(solution)/shard_map/all_to_all | solution.py:560
  176.4 0.8 copy-done.5
  177.2 2.2 %finish.1 = (f32[27,32,32]{2,1,0:T(8,128)}, f32[27,32,32]{2,1,0:T(8,128)}) custom-call(f32[128,8,128]{2,1,0:T(8,128)} %copy-done.5), custom_call_target="tpu_custom_call" | custom-call | flops 2000000000 | bytes 6000000 | tf_op jit(solution)/shard_map/finish/pallas_call | solution.py:527
  (15 shorter events, 0.0 us)
Async XLA Ops:
  0.6 2.2 %copy-start.2 = (bf16[32,2,32,128]{3,2,1,0:T(8,128)(2,1)S(1)}, bf16[32,2,32,128]{3,2,1,0:T(8,128)(2,1)}, u32[]{:S(2)}) copy-start(bf16[32,2,32,128]{3,2,1,0:T(8,128)(2,1)} %param.15) | copy-start | bytes 1572868
  5.9 6.9 %collective-permute-start = (bf16[6,64,128]{2,1,0:T(8,128)(2,1)}, bf16[6,64,128]{2,1,0:T(8,128)(2,1)S(1)}, u32[]{:S(2)}, u32[]{:S(2)}) collective-permute-start(bf16[6,64,128]{2,1,0:T(8,128)(2,1)} %get-tuple-element.34), channel_id=1, source_target_pairs={{0,1},{1,2},{2,3},{3,4},{4,5},{5,6},{6,7},{8,9},{9,10},{10,11},{11... | collective-permute-start | bytes 294920 | tf_op jit(solution)/shard_map/ppermute | solution.py:551
  10.9 6.1 %collective-permute-start.1 = (bf16[6,64,128]{2,1,0:T(8,128)(2,1)}, bf16[6,64,128]{2,1,0:T(8,128)(2,1)S(1)}, u32[]{:S(2)}, u32[]{:S(2)}) collective-permute-start(bf16[6,64,128]{2,1,0:T(8,128)(2,1)} %get-tuple-element.35), channel_id=1, source_target_pairs={{1,0},{2,1},{3,2},{4,3},{5,4},{6,5},{7,6},{9,8},{10,9},{11,10},{12... | collective-permute-start | bytes 294920 | tf_op jit(solution)/shard_map/ppermute | solution.py:556
  12.8 4.2 %copy-start.7 = (bf16[6,64,128]{2,1,0:T(8,128)(2,1)}, bf16[6,64,128]{2,1,0:T(8,128)(2,1)S(1)}, u32[]{:S(2)}) copy-start(bf16[6,64,128]{2,1,0:T(8,128)(2,1)S(1)} %collective-permute-done.refs_1_.refs_5_.refs_8_) | copy-start | bytes 294916
  17.0 0.6 copy-start.8
  19.7 16.3 %collective-permute-start.3 = (bf16[40,64,128]{2,1,0:T(8,128)(2,1)}, bf16[40,64,128]{2,1,0:T(8,128)(2,1)S(1)}, u32[]{:S(2)}, u32[]{:S(2)}) collective-permute-start(bf16[40,64,128]{2,1,0:T(8,128)(2,1)} %planes.1.refs_2_), channel_id=1, source_target_pairs={{8,0},{16,8},{24,16},{32,24},{40,32},{48,40},{56,48},{64,56},{72,6... | collective-permute-start | bytes 1966088 | tf_op jit(solution)/shard_map/ppermute | solution.py:556
  21.0 16.9 %collective-permute-start.2 = (bf16[40,64,128]{2,1,0:T(8,128)(2,1)}, bf16[40,64,128]{2,1,0:T(8,128)(2,1)S(1)}, u32[]{:S(2)}, u32[]{:S(2)}) collective-permute-start(bf16[40,64,128]{2,1,0:T(8,128)(2,1)} %planes.1.refs_2_), channel_id=1, source_target_pairs={{0,8},{8,16},{16,24},{24,32},{32,40},{40,48},{48,56},{56,64},{64,7... | collective-permute-start | bytes 1966088 | tf_op jit(solution)/shard_map/ppermute | solution.py:551
  36.0 1.9 %copy-start.14 = (bf16[40,64,128]{2,1,0:T(8,128)(2,1)}, bf16[40,64,128]{2,1,0:T(8,128)(2,1)S(1)}, u32[]{:S(2)}) copy-start(bf16[40,64,128]{2,1,0:T(8,128)(2,1)S(1)} %collective-permute-done.3.refs_1_) | copy-start | bytes 1966084
  37.8 0.9 copy-start.15
  38.7 20.8 %copy-start.10 = (f32[32]{0:T(128)S(1)}, f32[32]{0:T(128)}, u32[]{:S(2)}) copy-start(f32[32]{0:T(128)} %param.14) | copy-start | bytes 388
  38.7 20.8 %copy-start.11 = (f32[32]{0:T(128)S(1)}, f32[32]{0:T(128)}, u32[]{:S(2)}) copy-start(f32[32]{0:T(128)} %param.13) | copy-start | bytes 388
  38.7 20.8 %copy-start.12 = (f32[32]{0:T(128)S(1)}, f32[32]{0:T(128)}, u32[]{:S(2)}) copy-start(f32[32]{0:T(128)} %param.11) | copy-start | bytes 388
  38.7 20.8 %copy-start.13 = (f32[32]{0:T(128)S(1)}, f32[32]{0:T(128)}, u32[]{:S(2)}) copy-start(f32[32]{0:T(128)} %param.10) | copy-start | bytes 388
  45.5 24.8 %all-to-all-start = ((f32[128,4,128]{2,1,0:T(4,128)}), f32[128,4,128]{2,1,0:T(4,128)S(1)}, u32[]{:S(2)}, u32[]{:S(2)}) async-start(f32[128,4,128]{2,1,0:T(4,128)} %get-tuple-element.37), calls=%async_computation | async-start | bytes 524288 | tf_op jit(solution)/shard_map/all_to_all | solution.py:560
  70.4 0.7 copy-start.6
  78.2 14.0 %all-to-all-start.1 = ((f32[128,1,128]{2,1,0:T(1,128)}), f32[128,1,128]{2,1,0:T(1,128)S(1)}, u32[]{:S(2)}, u32[]{:S(2)}) async-start(f32[128,1,128]{2,1,0:T(1,128)} %bitcast.51), calls=%async_computation.1 | async-start | bytes 131072 | tf_op jit(solution)/shard_map/all_to_all | solution.py:560
  82.8 35.4 %collective-permute-start.4 = (bf16[72,32,128]{2,1,0:T(8,128)(2,1)}, bf16[72,32,128]{2,1,0:T(8,128)(2,1)S(1)}, u32[]{:S(2)}, u32[]{:S(2)}) collective-permute-start(bf16[72,32,128]{2,1,0:T(8,128)(2,1)} %get-tuple-element.47), channel_id=1, source_target_pairs={{0,8},{8,16},{16,24},{24,32},{32,40},{40,48},{48,56},{56,64},{64,7... | collective-permute-start | bytes 1769480 | tf_op jit(solution)/shard_map/ppermute | solution.py:551
  86.2 32.1 %collective-permute-start.5 = (bf16[72,32,128]{2,1,0:T(8,128)(2,1)}, bf16[72,32,128]{2,1,0:T(8,128)(2,1)S(1)}, u32[]{:S(2)}, u32[]{:S(2)}) collective-permute-start(bf16[72,32,128]{2,1,0:T(8,128)(2,1)} %get-tuple-element.48), channel_id=1, source_target_pairs={{8,0},{16,8},{24,16},{32,24},{40,32},{48,40},{56,48},{64,56},{72,6... | collective-permute-start | bytes 1769480 | tf_op jit(solution)/shard_map/ppermute | solution.py:556
  92.2 0.6 copy-start.9
  118.3 0.9 copy-start
  118.3 1.1 copy-start.1
  129.1 19.1 %all-to-all-start.3 = ((f32[128,8,128]{2,1,0:T(8,128)}), f32[128,8,128]{2,1,0:T(8,128)S(1)}, u32[]{:S(2)}, u32[]{:S(2)}) async-start(f32[128,8,128]{2,1,0:T(8,128)} %get-tuple-element.51), calls=%async_computation.3 | async-start | bytes 1048576 | tf_op jit(solution)/shard_map/all_to_all | solution.py:560
  133.8 12.6 %collective-permute-start.6 = (bf16[34,32,128]{2,1,0:T(8,128)(2,1)}, bf16[34,32,128]{2,1,0:T(8,128)(2,1)S(1)}, u32[]{:S(2)}, u32[]{:S(2)}) collective-permute-start(bf16[34,32,128]{2,1,0:T(8,128)(2,1)} %get-tuple-element.54), channel_id=1, source_target_pairs={{0,8},{8,16},{16,24},{24,32},{32,40},{40,48},{48,56},{56,64},{64,7... | collective-permute-start | bytes 835592 | tf_op jit(solution)/shard_map/ppermute | solution.py:551
  137.1 11.2 %collective-permute-start.7 = (bf16[34,32,128]{2,1,0:T(8,128)(2,1)}, bf16[34,32,128]{2,1,0:T(8,128)(2,1)S(1)}, u32[]{:S(2)}, u32[]{:S(2)}) collective-permute-start(bf16[34,32,128]{2,1,0:T(8,128)(2,1)} %get-tuple-element.55), channel_id=1, source_target_pairs={{8,0},{16,8},{24,16},{32,24},{40,32},{48,40},{56,48},{64,56},{72,6... | collective-permute-start | bytes 835592 | tf_op jit(solution)/shard_map/ppermute | solution.py:556
  146.4 1.9 %copy-start.16 = (bf16[34,32,128]{2,1,0:T(8,128)(2,1)}, bf16[34,32,128]{2,1,0:T(8,128)(2,1)S(1)}, u32[]{:S(2)}) copy-start(bf16[34,32,128]{2,1,0:T(8,128)(2,1)S(1)} %collective-permute-done.6.refs_6_) | copy-start | bytes 835588
  148.3 0.7 copy-start.17
  148.3 0.9 copy-start.4
  152.1 10.6 %copy-start.3 = (bf16[32,64,128]{2,1,0:T(8,128)(2,1)S(1)}, bf16[32,64,128]{2,1,0:T(8,128)(2,1)}, u32[]{:S(2)}) copy-start(bf16[32,64,128]{2,1,0:T(8,128)(2,1)} %get-tuple-element.44) | copy-start | bytes 1572868
  152.1 24.3 %all-to-all-start.4 = ((f32[128,8,128]{2,1,0:T(8,128)}), f32[128,8,128]{2,1,0:T(8,128)S(1)}, u32[]{:S(2)}, u32[]{:S(2)}) async-start(f32[128,8,128]{2,1,0:T(8,128)} %get-tuple-element.59), calls=%async_computation.4 | async-start | bytes 1048576 | tf_op jit(solution)/shard_map/all_to_all | solution.py:560
  176.4 0.8 copy-start.5

commit v5 on v4

--- a/solution.py
+++ b/solution.py
@@ -38,7 +38,18 @@
 def windows_of(*refs):
     if len(refs) == 1:
         return lambda y: refs[0][y : y + 3].reshape(384, 128)
-    return lambda y: jnp.concatenate([ref[y + k] for k in range(3) for ref in refs], axis=0)
+    return lambda y: jnp.concatenate([rows(y + k) for k in range(3) for rows in refs], axis=0)
+
+
+def joined(margin, middle, below, above, first):
+    def row(y):
+        if y < margin:
+            return below[y]
+        if y < margin + ROWS:
+            return middle[y - margin]
+        return above[first + y - margin - ROWS]
+
+    return row
 
 
 def conv_rows(window, w_ref, rows, emit):
@@ -109,8 +120,9 @@
     at = lax.broadcasted_iota(jnp.int32, centers.shape, 1)
     low = total(jnp.where(at == place_ref[0], off, 0.0))
     high = total(jnp.where(at == place_ref[1], off, 0.0))
+    own = total(jnp.where(at == place_ref[7], off, 0.0))
     found = (mean, lax.rsqrt(spread + EPSILON), low, high)
-    st_ref[...] = jnp.concatenate([*found, jnp.zeros((C, 124), F32)], axis=1)
+    st_ref[...] = jnp.concatenate([*found, own, jnp.zeros((C, 123), F32)], axis=1)
     return found
 
 
@@ -140,8 +152,11 @@
                 values = jnp.where(lane == 0, 0.0, values)
             column = total(values)
             columns.append(column + jnp.concatenate([column[C:], column[:C]], axis=0))
-    rows = jnp.transpose(jnp.concatenate(columns + [jnp.zeros((128, 119), F32)], axis=1))
-    return lambda dz, dy: jnp.broadcast_to(rows[dz * 3 + dy : dz * 3 + dy + 1], (C, 128))
+    return jnp.transpose(jnp.concatenate(columns + [jnp.zeros((128, 119), F32)], axis=1))[0:16]
+
+
+def ones_of(x1):
+    return lambda dz, dy: jnp.broadcast_to(x1[dz * 3 + dy : dz * 3 + dy + 1], (C, 128))
 
 
 def act(z):
@@ -214,11 +229,10 @@
     down_ref[4:6] = cot[0:2]
 
 
-def planes_kernel(need, send, own, y_low, y_high, ext):
-    need(own, y_low, y_high)
-    ext[0:4] = y_low[0:4]
-    ext[4 : 4 + ROWS] = own[...]
-    ext[4 + ROWS : 8 + ROWS] = y_high[0:4]
+def corner_kernel(need, send, y_low, y_high, rows):
+    need(y_low, y_high)
+    rows[0:4] = y_low[0:4]
+    rows[4:8] = y_high[0:4]
 
 
 def weights_kernel(need, send, k1, k2, w1, w2, b1, b2):
@@ -256,8 +270,13 @@
                 b_ref[dz * 64 + C : dz * 64 + 64, here] = pltpu.roll(tile, C, 1).astype(BF16)
 
 
-def first_kernel(need, send, low, high, own, w, v, h, msg):
-    need(own, w)
+def first_kernel(
+    need, send, own, x_low, x_high, y_low, y_high, c_low, c_high, w, v, h, msg, x1, center_out
+):
+    need(own, x_low, x_high, y_low, y_high, c_low, c_high, w)
+    low = joined(4, x_low, c_low, c_low, 4)
+    high = joined(4, x_high, c_high, c_high, 4)
+    own = joined(4, own, y_low, y_high, 0)
     acc = [jnp.zeros((64, 128), F32), jnp.zeros((64, 128), F32)]
     for k, pair in enumerate(((low, own), (own, high))):
 
@@ -269,7 +288,7 @@
         conv_rows(windows_of(*pair), w, ROWS + 6, emit)
     send(h)
     for y in range(ROWS + 8):
-        v[y] = jnp.concatenate([low[y][C:], own[y], high[y][0:C]], axis=0)
+        v[y] = jnp.concatenate([low(y)[C:], own(y), high(y)[0:C]], axis=0)
     send(v)
     center = center_of(jnp.concatenate([acc[0][C:], acc[1][0:C]], axis=0))
     both = twice(center)
@@ -277,7 +296,10 @@
     for y in range(3, 3 + ROWS):
         off = h[y, C : 3 * C] - both
         spread = spread + off * off
-    rows_message((center, fold(total(spread))), (feature_sums(v),), msg)
+    center_out[...] = jnp.broadcast_to(center, (C, 128))
+    x1[...] = feature_sums(v)
+    send(center_out, x1)
+    rows_message((center, fold(total(spread))), (ones_of(x1),), msg)
 
 
 def second_kernel(
@@ -321,19 +343,18 @@
     message((center, fold(total(spread))), msg)
 
 
-def side_kernel(need, send, st1, h1, v1, xn, g, acc):
-    need(st1, h1)
-    mean, inverse, _, _ = kept_stats(st1)
-    mean2, inverse2 = twice(mean), twice(inverse)
+def side_kernel(need, send, center, h1, v1, xh, g, acc):
+    need(center, h1)
+    both = twice(center[...])
     lane = lanes(64)
     for y in range(ROWS):
-        put_shifted(g, y, (h1[y + 3] - mean2) * inverse2, lane)
+        put_shifted(g, y, h1[y + 3] - both, lane)
     need(v1)
     weight_sums(g, v1, 3, acc)
     tile = folded(acc)
     for dz in range(3):
         for dy in range(3):
-            xn[dz * 3 + dy] = tile(dz, dy)
+            xh[dz * 3 + dy] = tile(dz, dy)
 
 
 def cot_row(cot, y_low, y_high, y):
@@ -344,7 +365,7 @@
     return y_high[2 + y - ROWS]
 
 
-def third_kernel(cells, need, send, place, r2, gb, cot, h2, xn, out, msg, st2):
+def third_kernel(cells, need, send, place, r2, gb, cot, h2, st1, x1, xh, out, msg, st2):
     need(gb)
     mean, inverse, _, _ = stats_of(r2[...], place, cells, st2)
     need(h2, cot)
@@ -360,9 +381,15 @@
         plain = plain + slope
         both = both + slope * normed
     send(out)
-    need(xn)
-
-    rows_message((fold(total(both)), fold(total(plain))), (lambda dz, dy: xn[dz * 3 + dy],), msg)
+    need(st1, x1, xh)
+    inverse1, own1 = st1[:, 1:2], st1[:, 4:5]
+    ones = ones_of(x1)
+
+    def xn(dz, dy):
+        return inverse1 * (xh[dz * 3 + dy] + own1 * ones(dz, dy))
+
+
+    rows_message((fold(total(both)), fold(total(plain))), (xn,), msg)
 
 
 def fourth_kernel(
@@ -567,7 +594,7 @@
     gx, gy = lax.axis_index(GX), lax.axis_index(GY)
     at = gx * count_y + gy
     place = jnp.stack(
-        [at - count_y, at + count_y, gx > 0, gx < count_x - 1, gy > 0, gy < count_y - 1, at % C]
+        [at - count_y, at + count_y, gx > 0, gx < count_x - 1, gy > 0, gy < count_y - 1, at % C, at]
     ).astype(jnp.int32)
     gb = jnp.stack([gain_one, bias_one, gain_two, bias_two], axis=1)
 
@@ -581,14 +608,15 @@
     stats = sh((C, 128), F32)
     corr = (pltpu.VMEM((192, ROWS * 128), BF16), pltpu.VMEM((192, 384), F32))
 
+    x_low, x_high = up(own, GX), down(own, GX)
     y_up, y_down = call(
         pack_kernel, (own, cot), [sh((6, 64, 128), BF16)] * 2, "pack", smem_first=False
     )
     y_low, y_high = up(y_up, GY), down(y_down, GY)
-    (ext,) = call(
-        planes_kernel, (own, y_low, y_high), [sh((40, 64, 128), BF16)], "planes", smem_first=False
-    )
-    x_low, x_high = up(ext, GX), down(ext, GX)
+    (corner,) = call(
+        corner_kernel, (y_low, y_high), [sh((8, 64, 128), BF16)], "corner", smem_first=False
+    )
+    c_low, c_high = up(corner, GX), down(corner, GX)
     taps = [
         jnp.transpose(k, (2, 3, 4, 0, 1)).reshape(27, C, C) for k in (kernel_one, kernel_two)
     ]
@@ -596,15 +624,24 @@
         weights_kernel, taps, [sh((192, 384), BF16)] * 4, "weights", smem_first=False
     )
 
-    v1, h1, m1 = call(
+    v1, h1, m1, x1_own, center = call(
         first_kernel,
-        (x_low, x_high, ext, w1),
-        [sh((40, 128, 128), BF16), sh((38, 128, 128), F32), four],
+        (own, x_low, x_high, y_low, y_high, c_low, c_high, w1),
+        [sh((40, 128, 128), BF16), sh((38, 128, 128), F32), four, sh((16, 128), F32), stats],
         "conv_one",
         smem_first=False,
-        near=2,
     )
     r1 = share(m1)
+
+    (xh,) = call(
+        side_kernel,
+        (center, h1, v1),
+        [sh((9, C, 128), F32)],
+        "hidden_features",
+        scratch=corr,
+        smem_first=False,
+        cut=(h1,),
+    )
 
     v2, h2, low, high, m2, st1, x1 = call(
         lambda *refs: second_kernel(cells, *refs),
@@ -615,27 +652,23 @@
         ],
         "conv_two",
         near=1,
+        after=(xh,),
     )
     h2_low, h2_high = up(high, GX), down(low, GX)
     r2 = share(m2)
-    (xn,) = call(
-        side_kernel,
-        (st1, h1, v1),
-        [sh((9, C, 128), F32)],
-        "normed_features",
-        scratch=corr,
-        smem_first=False,
-        cut=(h1,),
-    )
-
     output, m3, st2 = call(
         lambda *refs: third_kernel(cells, *refs),
-        (place, r2, gb, cot, h2, xn),
+        (place, r2, gb, cot, h2, st1, x1_own, xh),
         [sh((ROWS, 64, 128), BF16), four, stats],
         "slope_two",
         near=1,
     )
     r3 = share(m3)
+
+    def back(rows):
+        return jnp.transpose(rows.reshape(ROWS, 2, C, 128), (2, 1, 0, 3))
+
+    output = back(output)
 
     slope1, low, high, m4, t3 = call(
         lambda *refs: fourth_kernel(cells, *refs),
@@ -658,7 +691,7 @@
         [wide, sh((4, C), F32), sh((8, 128), F32)],
         "own_rows",
         near=1,
-        after=(s_low, s_high),
+        after=(s_low, s_high, output),
     )
     r5 = share(m5)
     (grad,) = call(
@@ -671,10 +704,7 @@
     grads = call(finish_kernel, (r5,), [sh((27, C, C), F32)] * 2, "finish", smem_first=False, near=1)
     one, two = [jnp.transpose(k.reshape(3, 3, 3, C, C), (3, 4, 0, 1, 2)) for k in grads]
 
-    def back(rows):
-        return jnp.transpose(rows.reshape(ROWS, 2, C, 128), (2, 1, 0, 3))
-
-    return back(output), back(grad), one, two, norm_grads
+    return output, back(grad), one, two, norm_grads
 
 
 def solution(mesh):

time: 181 us -> 183 us (1.011)
  blocking collectives: 21.1 us -> 39.1 us
  waiting for transfers between devices: 40 us -> 25 us
    all_to_all x1 -> x2, blocking collectives: 21.1 us -> 39.1 us  [share(): return lax.all_to_all(msg, ALL, 0, 0, tiled=True)]
    ppermute x4 -> x5, waiting for transfers between devices: 14.6 us -> 6.06 us  [down(): return lax.ppermute(values, axes, [(i + 1, i) for i in range(count - 1)])]
    ppermute x4 -> x5, starting transfers between devices: 15.6 us -> 19.1 us  [up(): return lax.ppermute(values, axes, [(i, i + 1) for i in range(count - 1)])]
    all_to_all x4 -> x3, waiting for transfers between devices: 15.5 us -> 12 us  [share(): return lax.all_to_all(msg, ALL, 0, 0, tiled=True)]
    all_to_all x4 -> x3, starting transfers between devices: 33.8 us -> 30.5 us  [share(): return lax.all_to_all(msg, ALL, 0, 0, tiled=True)]
    ppermute x4 -> x5, waiting for transfers between devices: 9.9 us -> 6.91 us  [up(): return lax.ppermute(values, axes, [(i, i + 1) for i in range(count - 1)])]
    ppermute x4 -> x5, starting transfers between devices: 5.8 us -> 7.09 us  [down(): return lax.ppermute(values, axes, [(i + 1, i) for i in range(count - 1)])]
    unnamed x36 -> x40, local copies, waits for them, and re-layouts: 5.59 us -> 5.09 us
  transfers between devices with their start and end apart: 12 -> 13, of which waited for: 8 -> 5; matrix products, arithmetic and copies ran while one was open for 3% -> 3% of each run, Pallas kernels for 9% -> 11%
where the time goes in v5:
time: 183 us; the launch traced here: 182 us
  starting transfers between devices  56.7 us (31%)
  Pallas kernels  47.5 us (26%)
  blocking collectives  39.1 us (21%)
  waiting for transfers between devices  25 us (14%)
  local copies, waits for them, and re-layouts  12.3 us (7%)
    pallas_call x11, Pallas kernels, call(): pl.pallas_call(body, out_shape=outs, in_specs=[SM] * lead + [pl.BlockSpec...  47.5 us
    all_to_all x2, blocking collectives, share(): return lax.all_to_all(msg, ALL, 0, 0, tiled=True)  39.1 us
    all_to_all x3, starting transfers between devices, share(): return lax.all_to_all(msg, ALL, 0, 0, tiled=True)  30.5 us
    ppermute x5, starting transfers between devices, up(): return lax.ppermute(values, axes, [(i, i + 1) for i in range(count - 1)])  19.1 us
    all_to_all x3, waiting for transfers between devices, share(): return lax.all_to_all(msg, ALL, 0, 0, tiled=True)  12 us
    ppermute x5, starting transfers between devices, down(): return lax.ppermute(values, axes, [(i + 1, i) for i in range(count - 1)])  7.09 us
    ppermute x5, waiting for transfers between devices, up(): return lax.ppermute(values, axes, [(i, i + 1) for i in range(count - 1)])  6.91 us
    ppermute x5, waiting for transfers between devices, down(): return lax.ppermute(values, axes, [(i + 1, i) for i in range(count - 1)])  6.06 us
  transfers between devices with their start and end apart: 13, of which 5 were waited for; matrix products, arithmetic and copies ran while one was open for 3% of the time, Pallas kernels for 11%

profile of v5, /device:TPU:1, one launch (start us, length us, event | category | flops | bytes accessed | tf_op | source)
XLA Modules:
  0.0 181.7 jit_solution(16200053179540325674)
XLA Ops:
  0.6 0.0 copy-start.2
  0.6 1.4 copy.28
  2.1 0.0 copy-start.3
  2.1 1.3 collective-permute-start.1
  3.4 4.7 %collective-permute-start = (bf16[32,64,128]{2,1,0:T(8,128)(2,1)S(1)}, bf16[32,64,128]{2,1,0:T(8,128)(2,1)S(1)}, u32[]{:S(2)}, u32[]{:S(2)}) collective-permute-start(bf16[32,64,128]{2,1,0:T(8,128)(2,1)S(1)} %bitcast.47), channel_id=1, source_target_pairs={{0,8},{8,16},{16,24},{24,32},{32,40},{40,48},{48,56},{56,64},{64,7... | collective-permute-start | bytes 1572872 | tf_op jit(solution)/shard_map/ppermute | solution.py:578
  8.1 0.0 copy-done.2
  8.1 1.2 copy.29
  9.3 0.0 copy-done.3
  9.3 1.9 %pack.1 = (bf16[6,64,128]{2,1,0:T(8,128)(2,1)}, bf16[6,64,128]{2,1,0:T(8,128)(2,1)}) custom-call(bf16[32,64,128]{2,1,0:T(8,128)(2,1)} %bitcast.48, bf16[32,64,128]{2,1,0:T(8,128)(2,1)} %bitcast.40), custom_call_target="tpu_custom_call" | custom-call | flops 2000000000 | bytes 6000000 | tf_op jit(solution)/shard_map/pack/pallas_call | solution.py:554
  11.2 4.8 %collective-permute-start.2 = (bf16[6,64,128]{2,1,0:T(8,128)(2,1)}, bf16[6,64,128]{2,1,0:T(8,128)(2,1)S(1)}, u32[]{:S(2)}, u32[]{:S(2)}) collective-permute-start(bf16[6,64,128]{2,1,0:T(8,128)(2,1)} %get-tuple-element.36), channel_id=1, source_target_pairs={{0,1},{1,2},{2,3},{3,4},{4,5},{5,6},{6,7},{8,9},{9,10},{10,11},{11... | collective-permute-start | bytes 294920 | tf_op jit(solution)/shard_map/ppermute | solution.py:578
  16.0 1.9 %collective-permute-start.3 = (bf16[6,64,128]{2,1,0:T(8,128)(2,1)}, bf16[6,64,128]{2,1,0:T(8,128)(2,1)S(1)}, u32[]{:S(2)}, u32[]{:S(2)}) collective-permute-start(bf16[6,64,128]{2,1,0:T(8,128)(2,1)} %get-tuple-element.37), channel_id=1, source_target_pairs={{1,0},{2,1},{3,2},{4,3},{5,4},{6,5},{7,6},{9,8},{10,9},{11,10},{12... | collective-permute-start | bytes 294920 | tf_op jit(solution)/shard_map/ppermute | solution.py:583
  18.0 0.0 collective-permute-done.2.refs_0_.refs_3_.refs_5_.refs_8_
  18.0 0.0 copy-start.8
  18.0 4.2 %collective-permute-done.3.refs_1_.refs_4_.refs_6_.refs_9_ = bf16[6,64,128]{2,1,0:T(8,128)(2,1)S(1)} collective-permute-done((bf16[6,64,128]{2,1,0:T(8,128)(2,1)}, bf16[6,64,128]{2,1,0:T(8,128)(2,1)S(1)}, u32[]{:S(2)}, u32[]{:S(2)}) %collective-permute-start.3) | collective-permute-done | bytes 98336 | tf_op jit(solution)/shard_map/ppermute | solution.py:583
  22.2 0.6 copy-done.9
  22.8 1.6 corner.1
  24.4 1.3 collective-permute-start.5
  25.7 4.0 %collective-permute-start.4 = (bf16[8,64,128]{2,1,0:T(8,128)(2,1)}, bf16[8,64,128]{2,1,0:T(8,128)(2,1)S(1)}, u32[]{:S(2)}, u32[]{:S(2)}) collective-permute-start(bf16[8,64,128]{2,1,0:T(8,128)(2,1)} %corner.1), channel_id=1, source_target_pairs={{0,8},{8,16},{16,24},{24,32},{32,40},{40,48},{48,56},{56,64},{64,7... | collective-permute-start | bytes 393224 | tf_op jit(solution)/shard_map/ppermute | solution.py:578
  29.7 2.3 %weights.1 = (bf16[192,384]{1,0:T(8,128)(2,1)}, bf16[192,384]{1,0:T(8,128)(2,1)}, bf16[192,384]{1,0:T(8,128)(2,1)}, bf16[192,384]{1,0:T(8,128)(2,1)}) custom-call(bf16[27,32,32]{2,1,0:T(8,128)(2,1)} %bitcast.61, bf16[27,32,32]{2,1,0:T(8,128)(2,1)} %bitcast.62), custom_call_target="tpu_custom_call" | custom-call | flops 2000000000 | bytes 6000000 | tf_op jit(solution)/shard_map/weights/pallas_call | solution.py:554
  32.1 0.0 collective-permute-done.5.refs_6_
  32.1 0.0 collective-permute-done.4.refs_5_
  32.1 0.0 copy-start.19
  32.1 0.0 collective-permute-done.1.refs_2_
  32.2 0.0 collective-permute-done.refs_1_
  32.2 0.0 copy-start.15
  32.2 0.6 copy-done.18
  32.8 0.1 copy-done.19
  32.8 0.2 copy-done.14
  33.0 0.2 copy-done.15
  33.2 6.1 %conv_one.1 = (bf16[40,128,128]{2,1,0:T(8,128)(2,1)}, f32[38,128,128]{2,1,0:T(8,128)}, f32[128,4,128]{2,1,0:T(4,128)}, f32[16,128]{1,0:T(8,128)}, f32[32,128]{1,0:T(8,128)}) custom-call(bf16[32,64,128]{2,1,0:T(8,128)(2,1)} %bitcast.49, bf16[32,64,128]{2,1,0:T(8,128)(2,1)} %copy-done.15, bf16[32,64,128]{2,1,0:T(8,128)(2,1)} %copy-done.14, ...), custom_call_target="tpu_custom_call" | custom-call | flops 2000000000 | bytes 6000000 | tf_op jit(solution)/shard_map/conv_one/pallas_call | solution.py:554
  39.3 15.2 %all-to-all-start = ((f32[128,4,128]{2,1,0:T(4,128)}), f32[128,4,128]{2,1,0:T(4,128)S(1)}, u32[]{:S(2)}, u32[]{:S(2)}) async-start(f32[128,4,128]{2,1,0:T(4,128)} %get-tuple-element.39), calls=%async_computation | async-start | bytes 524288 | tf_op jit(solution)/shard_map/all_to_all | solution.py:587
  54.5 0.7 copy.30.refs_2_.refs_3_
  55.2 0.6 stack.66.refs_0_
  55.8 3.6 %hidden_features.1.refs_8_.refs_7_ = f32[9,32,128]{2,1,0:T(8,128)} custom-call(f32[32,128]{1,0:T(8,128)} %get-tuple-element.42.refs_0_, f32[38,128,128]{2,1,0:T(8,128)} %get-tuple-element.40.refs_1_.refs_3_.refs_12_.refs_4_, bf16[40,128,128]{2,1,0:T(8,128)(2,1)} %get-tuple-element.43.refs_2_.refs_14_), custom_call_target="tpu_custom_call" | custom-call | flops 2000000000 | bytes 6000000 | tf_op jit(solution)/shard_map/hidden_features/pallas_call | solution.py:554
  59.5 5.9 %all-to-all-done.refs_1_ = f32[128,4,128]{2,1,0:T(4,128)S(1)} async-done(((f32[128,4,128]{2,1,0:T(4,128)}), f32[128,4,128]{2,1,0:T(4,128)S(1)}, u32[]{:S(2)}, u32[]{:S(2)}) %all-to-all-start) | async-done | bytes 262176 | tf_op jit(solution)/shard_map/all_to_all | solution.py:587
  65.4 0.7 copy-done.7
  66.1 7.1 %conv_two.1 = (bf16[38,128,128]{2,1,0:T(8,128)(2,1)}, f32[36,64,128]{2,1,0:T(8,128)}, bf16[72,32,128]{2,1,0:T(8,128)(2,1)}, bf16[72,32,128]{2,1,0:T(8,128)(2,1)}...) custom-call(s32[8]{0:T(128)} %stack.66.refs_0_, f32[128,4,128]{2,1,0:T(4,128)} %copy-done.7, ...), custom_call_target="tpu_custom_call" | custom-call | flops 2000000000 | bytes 6000000 | tf_op jit(solution)/shard_map/conv_two/pallas_call | solution.py:554
  73.3 2.3 %collective-permute-start.6 = (bf16[72,32,128]{2,1,0:T(8,128)(2,1)}, bf16[72,32,128]{2,1,0:T(8,128)(2,1)S(1)}, u32[]{:S(2)}, u32[]{:S(2)}) collective-permute-start(bf16[72,32,128]{2,1,0:T(8,128)(2,1)} %get-tuple-element.51), channel_id=1, source_target_pairs={{0,8},{8,16},{16,24},{24,32},{32,40},{40,48},{48,56},{56,64},{64,7... | collective-permute-start | bytes 1769480 | tf_op jit(solution)/shard_map/ppermute | solution.py:578
  75.5 1.3 collective-permute-start.7
  76.8 19.8 %all_to_all.31 = f32[128,1,128]{2,1,0:T(1,128)} all-to-all(f32[128,1,128]{2,1,0:T(1,128)} %bitcast.55), channel_id=1, replica_groups=mesh['gx_0'=4,'gx_1'=4,'gy_0'=4,'gy_1'=2] {'gx_0','gx_1','gy_0','gy_1'}, dimensions={0} | all-to-all | bytes 131072 | tf_op jit(solution)/shard_map/all_to_all | solution.py:587
  96.6 4.4 %slope_two.1 = (bf16[32,64,128]{2,1,0:T(8,128)(2,1)}, f32[128,4,128]{2,1,0:T(4,128)}, f32[32,128]{1,0:T(8,128)}) custom-call(s32[8]{0:T(128)} %stack.66.refs_0_, f32[128,128]{1,0:T(8,128)} %bitcast.56, f32[32,4]{1,0:T(8,128)} %copy.30.refs_2_.refs_3_, bf16[32,64,128]{2,1,0:T(8,128)(2,1)} %bitcast.42, f32[36,64,128]{2,1,0:T(8,128)} %get-tuple-element.45.refs_4_, ...), custom_call_target="tpu_custom_call" | custom-call | flops 2000000000 | bytes 6000000 | tf_op jit(solution)/shard_map/slope_two/pallas_call | solution.py:554
  101.0 19.3 %all_to_all.32.refs_1_ = f32[128,4,128]{2,1,0:T(4,128)} all-to-all(f32[128,4,128]{2,1,0:T(4,128)} %get-tuple-element.49), channel_id=1, replica_groups=mesh['gx_0'=4,'gx_1'=4,'gy_0'=4,'gy_1'=2] {'gx_0','gx_1','gy_0','gy_1'}, dimensions={0} | all-to-all | bytes 524288 | tf_op jit(solution)/shard_map/all_to_all | solution.py:587
  120.3 0.0 collective-permute-done.6.refs_5_
  120.3 0.0 collective-permute-done.7.refs_6_
  120.3 0.9 copy-done
  121.2 0.2 copy-done.1
  121.4 9.7 %back_two.1 = (f32[34,64,128]{2,1,0:T(8,128)}, bf16[34,32,128]{2,1,0:T(8,128)(2,1)}, bf16[34,32,128]{2,1,0:T(8,128)(2,1)}, f32[128,8,128]{2,1,0:T(8,128)}, f32[4,128]{1,0:T(4,128)}) custom-call(s32[8]{0:T(128)} %stack.66.refs_0_, f32[128,4,128]{2,1,0:T(4,128)} %all_to_all.32.refs_1_, f32[32,128]{1,0:T(8,128)} %get-tuple-element.50.refs_2_, ...), custom_call_target="tpu_custom_call" | custom-call | flops 2000000000 | bytes 6000000 | tf_op jit(solution)/shard_map/back_two/pallas_call | solution.py:554
  131.1 0.0 copy-start.4
  131.1 4.6 %all-to-all-start.3 = ((f32[128,8,128]{2,1,0:T(8,128)}), f32[128,8,128]{2,1,0:T(8,128)S(1)}, u32[]{:S(2)}, u32[]{:S(2)}) async-start(f32[128,8,128]{2,1,0:T(8,128)} %get-tuple-element.55), calls=%async_computation.3 | async-start | bytes 1048576 | tf_op jit(solution)/shard_map/all_to_all | solution.py:587
  135.8 3.4 %collective-permute-start.8 = (bf16[34,32,128]{2,1,0:T(8,128)(2,1)}, bf16[34,32,128]{2,1,0:T(8,128)(2,1)S(1)}, u32[]{:S(2)}, u32[]{:S(2)}) collective-permute-start(bf16[34,32,128]{2,1,0:T(8,128)(2,1)} %get-tuple-element.58), channel_id=1, source_target_pairs={{0,8},{8,16},{16,24},{24,32},{32,40},{40,48},{48,56},{56,64},{64,7... | collective-permute-start | bytes 835592 | tf_op jit(solution)/shard_map/ppermute | solution.py:578
  139.2 1.3 collective-permute-start.9
  140.5 1.1 copy.41
  141.6 6.9 %collective-permute-done.8.refs_6_ = bf16[34,32,128]{2,1,0:T(8,128)(2,1)S(1)} collective-permute-done((bf16[34,32,128]{2,1,0:T(8,128)(2,1)}, bf16[34,32,128]{2,1,0:T(8,128)(2,1)S(1)}, u32[]{:S(2)}, u32[]{:S(2)}) %collective-permute-start.8) | collective-permute-done | bytes 278560 | tf_op jit(solution)/shard_map/ppermute | solution.py:578
  148.5 1.9 %collective-permute-done.9.refs_7_ = bf16[34,32,128]{2,1,0:T(8,128)(2,1)S(1)} collective-permute-done((bf16[34,32,128]{2,1,0:T(8,128)(2,1)}, bf16[34,32,128]{2,1,0:T(8,128)(2,1)S(1)}, u32[]{:S(2)}, u32[]{:S(2)}) %collective-permute-start.9) | collective-permute-done | bytes 278560 | tf_op jit(solution)/shard_map/ppermute | solution.py:583
  150.4 0.0 all-to-all-done.3.refs_1_
  150.4 0.7 copy-done.17
  151.1 0.2 copy-done.5
  151.3 3.0 %own_rows.1 = (f32[128,8,128]{2,1,0:T(8,128)}, f32[4,32]{1,0:T(4,128)}, f32[8,128]{1,0:T(8,128)}) custom-call(s32[8]{0:T(128)} %stack.66.refs_0_, f32[128,8,128]{2,1,0:T(8,128)} %copy-done.5, f32[32,128]{1,0:T(8,128)} %get-tuple-element.46.refs_5_.refs_11_.refs_2_, f32[32,4]{1,0:T(8,128)} %copy.30.refs_2_.refs_3_, f32[4,128]{1,0:T(4,128)} %get-tuple-element.56.refs_4_, ...), custom_call_target="tpu_custom_call" | custom-call | flops 2000000000 | bytes 6000000 | tf_op jit(solution)/shard_map/own_rows/pallas_call | solution.py:554
  154.3 10.6 %all-to-all-start.4 = ((f32[128,8,128]{2,1,0:T(8,128)}), f32[128,8,128]{2,1,0:T(8,128)S(1)}, u32[]{:S(2)}, u32[]{:S(2)}) async-start(f32[128,8,128]{2,1,0:T(8,128)} %get-tuple-element.63), calls=%async_computation.4 | async-start | bytes 1048576 | tf_op jit(solution)/shard_map/all_to_all | solution.py:587
  164.9 5.4 %back_one.1 = bf16[32,64,128]{2,1,0:T(8,128)(2,1)} custom-call(s32[8]{0:T(128)} %stack.66.refs_0_, f32[8,128]{1,0:T(8,128)} %get-tuple-element.60.refs_1_, f32[32,128]{1,0:T(8,128)} %get-tuple-element.46.refs_5_.refs_11_.refs_2_, f32[32,4]{1,0:T(8,128)} %copy.30.refs_2_.refs_3_, f32[38,128,128]{2,1,0:T(8,128)} %get-tuple-element.40.refs_1_.refs_3_.refs_12_.refs_4_, ...), custom_call_target="tpu_custom_call" | custom-call | flops 2000000000 | bytes 6000000 | tf_op jit(solution)/shard_map/back_one/pallas_call | solution.py:554
  170.3 2.2 %copy.40 = bf16[32,2,32,128]{3,0,1,2:T(8,128)(2,1)} copy(bf16[32,2,32,128]{3,2,1,0:T(8,128)(2,1)} %bitcast.54) | data formatting | bytes 1048576 | tf_op jit(solution)/shard_map/reshape | solution.py:669
  172.5 6.1 %all-to-all-done.4.refs_0_ = f32[128,8,128]{2,1,0:T(8,128)S(1)} async-done(((f32[128,8,128]{2,1,0:T(8,128)}), f32[128,8,128]{2,1,0:T(8,128)S(1)}, u32[]{:S(2)}, u32[]{:S(2)}) %all-to-all-start.4) | async-done | bytes 524320 | tf_op jit(solution)/shard_map/all_to_all | solution.py:587
  178.6 0.8 copy-done.6
  179.3 2.2 %finish.1 = (f32[27,32,32]{2,1,0:T(8,128)}, f32[27,32,32]{2,1,0:T(8,128)}) custom-call(f32[128,8,128]{2,1,0:T(8,128)} %copy-done.6), custom_call_target="tpu_custom_call" | custom-call | flops 2000000000 | bytes 6000000 | tf_op jit(solution)/shard_map/finish/pallas_call | solution.py:554
  (22 shorter events, 0.1 us)
Async XLA Ops:
  0.6 7.5 %copy-start.2 = (bf16[32,2,32,128]{3,2,1,0:T(8,128)(2,1)S(1)}, bf16[32,2,32,128]{3,2,1,0:T(8,128)(2,1)}, u32[]{:S(2)}) copy-start(bf16[32,2,32,128]{3,2,1,0:T(8,128)(2,1)} %param.15) | copy-start | bytes 1572868
  2.1 7.2 %copy-start.3 = (bf16[32,2,32,128]{3,2,1,0:T(8,128)(2,1)}, bf16[32,2,32,128]{3,2,1,0:T(8,128)(2,1)S(1)}, u32[]{:S(2)}) copy-start(bf16[32,2,32,128]{3,2,1,0:T(8,128)(2,1)S(1)} %copy.28) | copy-start | bytes 1572868
  2.1 30.0 %collective-permute-start.1 = (bf16[32,64,128]{2,1,0:T(8,128)(2,1)S(1)}, bf16[32,64,128]{2,1,0:T(8,128)(2,1)S(1)}, u32[]{:S(2)}, u32[]{:S(2)}) collective-permute-start(bf16[32,64,128]{2,1,0:T(8,128)(2,1)S(1)} %bitcast.46), channel_id=1, source_target_pairs={{8,0},{16,8},{24,16},{32,24},{40,32},{48,40},{56,48},{64,56},{72,6... | collective-permute-start | bytes 1572872 | tf_op jit(solution)/shard_map/ppermute | solution.py:583
  3.4 28.8 %collective-permute-start = (bf16[32,64,128]{2,1,0:T(8,128)(2,1)S(1)}, bf16[32,64,128]{2,1,0:T(8,128)(2,1)S(1)}, u32[]{:S(2)}, u32[]{:S(2)}) collective-permute-start(bf16[32,64,128]{2,1,0:T(8,128)(2,1)S(1)} %bitcast.47), channel_id=1, source_target_pairs={{0,8},{8,16},{16,24},{24,32},{32,40},{40,48},{48,56},{56,64},{64,7... | collective-permute-start | bytes 1572872 | tf_op jit(solution)/shard_map/ppermute | solution.py:578
  11.2 6.8 %collective-permute-start.2 = (bf16[6,64,128]{2,1,0:T(8,128)(2,1)}, bf16[6,64,128]{2,1,0:T(8,128)(2,1)S(1)}, u32[]{:S(2)}, u32[]{:S(2)}) collective-permute-start(bf16[6,64,128]{2,1,0:T(8,128)(2,1)} %get-tuple-element.36), channel_id=1, source_target_pairs={{0,1},{1,2},{2,3},{3,4},{4,5},{5,6},{6,7},{8,9},{9,10},{10,11},{11... | collective-permute-start | bytes 294920 | tf_op jit(solution)/shard_map/ppermute | solution.py:578
  16.0 6.1 %collective-permute-start.3 = (bf16[6,64,128]{2,1,0:T(8,128)(2,1)}, bf16[6,64,128]{2,1,0:T(8,128)(2,1)S(1)}, u32[]{:S(2)}, u32[]{:S(2)}) collective-permute-start(bf16[6,64,128]{2,1,0:T(8,128)(2,1)} %get-tuple-element.37), channel_id=1, source_target_pairs={{1,0},{2,1},{3,2},{4,3},{5,4},{6,5},{7,6},{9,8},{10,9},{11,10},{12... | collective-permute-start | bytes 294920 | tf_op jit(solution)/shard_map/ppermute | solution.py:583
  18.0 4.2 %copy-start.8 = (bf16[6,64,128]{2,1,0:T(8,128)(2,1)}, bf16[6,64,128]{2,1,0:T(8,128)(2,1)S(1)}, u32[]{:S(2)}) copy-start(bf16[6,64,128]{2,1,0:T(8,128)(2,1)S(1)} %collective-permute-done.2.refs_0_.refs_3_.refs_5_.refs_8_) | copy-start | bytes 294916
  22.2 0.6 copy-start.9
  24.4 7.7 %collective-permute-start.5 = (bf16[8,64,128]{2,1,0:T(8,128)(2,1)}, bf16[8,64,128]{2,1,0:T(8,128)(2,1)S(1)}, u32[]{:S(2)}, u32[]{:S(2)}) collective-permute-start(bf16[8,64,128]{2,1,0:T(8,128)(2,1)} %corner.1), channel_id=1, source_target_pairs={{8,0},{16,8},{24,16},{32,24},{40,32},{48,40},{56,48},{64,56},{72,6... | collective-permute-start | bytes 393224 | tf_op jit(solution)/shard_map/ppermute | solution.py:583
  25.7 6.4 %collective-permute-start.4 = (bf16[8,64,128]{2,1,0:T(8,128)(2,1)}, bf16[8,64,128]{2,1,0:T(8,128)(2,1)S(1)}, u32[]{:S(2)}, u32[]{:S(2)}) collective-permute-start(bf16[8,64,128]{2,1,0:T(8,128)(2,1)} %corner.1), channel_id=1, source_target_pairs={{0,8},{8,16},{16,24},{24,32},{32,40},{40,48},{48,56},{56,64},{64,7... | collective-permute-start | bytes 393224 | tf_op jit(solution)/shard_map/ppermute | solution.py:578
  32.1 0.7 copy-start.18
  32.1 0.7 copy-start.19
  32.1 0.9 copy-start.14
  32.2 1.0 copy-start.15
  33.2 21.3 %copy-start.10 = (f32[32]{0:T(128)S(1)}, f32[32]{0:T(128)}, u32[]{:S(2)}) copy-start(f32[32]{0:T(128)} %param.14) | copy-start | bytes 388
  33.2 21.3 %copy-start.11 = (f32[32]{0:T(128)S(1)}, f32[32]{0:T(128)}, u32[]{:S(2)}) copy-start(f32[32]{0:T(128)} %param.13) | copy-start | bytes 388
  33.2 21.3 %copy-start.12 = (f32[32]{0:T(128)S(1)}, f32[32]{0:T(128)}, u32[]{:S(2)}) copy-start(f32[32]{0:T(128)} %param.11) | copy-start | bytes 388
  33.2 21.3 %copy-start.13 = (f32[32]{0:T(128)S(1)}, f32[32]{0:T(128)}, u32[]{:S(2)}) copy-start(f32[32]{0:T(128)} %param.10) | copy-start | bytes 388
  39.3 26.1 %all-to-all-start = ((f32[128,4,128]{2,1,0:T(4,128)}), f32[128,4,128]{2,1,0:T(4,128)S(1)}, u32[]{:S(2)}, u32[]{:S(2)}) async-start(f32[128,4,128]{2,1,0:T(4,128)} %get-tuple-element.39), calls=%async_computation | async-start | bytes 524288 | tf_op jit(solution)/shard_map/all_to_all | solution.py:587
  65.4 0.7 copy-start.7
  73.3 47.0 %collective-permute-start.6 = (bf16[72,32,128]{2,1,0:T(8,128)(2,1)}, bf16[72,32,128]{2,1,0:T(8,128)(2,1)S(1)}, u32[]{:S(2)}, u32[]{:S(2)}) collective-permute-start(bf16[72,32,128]{2,1,0:T(8,128)(2,1)} %get-tuple-element.51), channel_id=1, source_target_pairs={{0,8},{8,16},{16,24},{24,32},{32,40},{40,48},{48,56},{56,64},{64,7... | collective-permute-start | bytes 1769480 | tf_op jit(solution)/shard_map/ppermute | solution.py:578
  75.5 44.8 %collective-permute-start.7 = (bf16[72,32,128]{2,1,0:T(8,128)(2,1)}, bf16[72,32,128]{2,1,0:T(8,128)(2,1)S(1)}, u32[]{:S(2)}, u32[]{:S(2)}) collective-permute-start(bf16[72,32,128]{2,1,0:T(8,128)(2,1)} %get-tuple-element.52), channel_id=1, source_target_pairs={{8,0},{16,8},{24,16},{32,24},{40,32},{48,40},{56,48},{64,56},{72,6... | collective-permute-start | bytes 1769480 | tf_op jit(solution)/shard_map/ppermute | solution.py:583
  120.3 0.9 copy-start
  120.3 1.1 copy-start.1
  131.1 9.3 %copy-start.4 = (bf16[32,64,128]{2,1,0:T(8,128)(2,1)S(1)}, bf16[32,64,128]{2,1,0:T(8,128)(2,1)}, u32[]{:S(2)}) copy-start(bf16[32,64,128]{2,1,0:T(8,128)(2,1)} %get-tuple-element.48) | copy-start | bytes 1572868
  131.1 19.3 %all-to-all-start.3 = ((f32[128,8,128]{2,1,0:T(8,128)}), f32[128,8,128]{2,1,0:T(8,128)S(1)}, u32[]{:S(2)}, u32[]{:S(2)}) async-start(f32[128,8,128]{2,1,0:T(8,128)} %get-tuple-element.55), calls=%async_computation.3 | async-start | bytes 1048576 | tf_op jit(solution)/shard_map/all_to_all | solution.py:587
  135.8 12.7 %collective-permute-start.8 = (bf16[34,32,128]{2,1,0:T(8,128)(2,1)}, bf16[34,32,128]{2,1,0:T(8,128)(2,1)S(1)}, u32[]{:S(2)}, u32[]{:S(2)}) collective-permute-start(bf16[34,32,128]{2,1,0:T(8,128)(2,1)} %get-tuple-element.58), channel_id=1, source_target_pairs={{0,8},{8,16},{16,24},{24,32},{32,40},{40,48},{48,56},{56,64},{64,7... | collective-permute-start | bytes 835592 | tf_op jit(solution)/shard_map/ppermute | solution.py:578
  139.2 11.2 %collective-permute-start.9 = (bf16[34,32,128]{2,1,0:T(8,128)(2,1)}, bf16[34,32,128]{2,1,0:T(8,128)(2,1)S(1)}, u32[]{:S(2)}, u32[]{:S(2)}) collective-permute-start(bf16[34,32,128]{2,1,0:T(8,128)(2,1)} %get-tuple-element.59), channel_id=1, source_target_pairs={{8,0},{16,8},{24,16},{32,24},{40,32},{48,40},{56,48},{64,56},{72,6... | collective-permute-start | bytes 835592 | tf_op jit(solution)/shard_map/ppermute | solution.py:583
  148.5 1.9 %copy-start.16 = (bf16[34,32,128]{2,1,0:T(8,128)(2,1)}, bf16[34,32,128]{2,1,0:T(8,128)(2,1)S(1)}, u32[]{:S(2)}) copy-start(bf16[34,32,128]{2,1,0:T(8,128)(2,1)S(1)} %collective-permute-done.8.refs_6_) | copy-start | bytes 835588
  150.4 0.7 copy-start.17
  150.4 0.9 copy-start.5
  154.3 24.3 %all-to-all-start.4 = ((f32[128,8,128]{2,1,0:T(8,128)}), f32[128,8,128]{2,1,0:T(8,128)S(1)}, u32[]{:S(2)}, u32[]{:S(2)}) async-start(f32[128,8,128]{2,1,0:T(8,128)} %get-tuple-element.63), calls=%async_computation.4 | async-start | bytes 1048576 | tf_op jit(solution)/shard_map/all_to_all | solution.py:587
  178.6 0.8 copy-start.6

commit v6 on v5

--- a/solution.py
+++ b/solution.py
@@ -235,19 +235,30 @@
     rows[4:8] = y_high[0:4]
 
 
-def weights_kernel(need, send, k1, k2, w1, w2, b1, b2):
+def weights_kernel(need, send, k1, k2, w1, w2):
     need(k1, k2)
     row = lax.broadcasted_iota(jnp.int32, (C, 128), 0)
     col = lax.broadcasted_iota(jnp.int32, (C, 128), 1)
-    eye = jnp.where(row == col, 1.0, 0.0)[:, 0:C].astype(BF16)
-    zero = jnp.zeros((C, C), BF16)
-    for k_ref, w_ref, b_ref in ((k1, w1, b1), (k2, w2, b2)):
+    for k_ref, w_ref in ((k1, w1), (k2, w2)):
         lined = jnp.zeros((9 * C, 128), F32)
         for dx in range(3):
             spot = jnp.where(row + dx * C == col, 1.0, 0.0).astype(BF16)
             lined = lined + jnp.dot(
                 k_ref[dx * 9 : dx * 9 + 9].reshape(9 * C, C), spot, preferred_element_type=F32
             )
+        for dy in range(3):
+            for dz in range(3):
+                t = dy * 3 + dz
+                put_tile(w_ref, dz, dy, lined[t * C : t * C + C])
+
+
+def flipped_kernel(need, send, k1, k2, b1, b2):
+    need(k1, k2)
+    row = lax.broadcasted_iota(jnp.int32, (C, 128), 0)
+    col = lax.broadcasted_iota(jnp.int32, (C, 128), 1)
+    eye = jnp.where(row == col, 1.0, 0.0)[:, 0:C].astype(BF16)
+    zero = jnp.zeros((C, C), BF16)
+    for k_ref, b_ref in ((k1, b1), (k2, b2)):
         stack = []
         for t in range(9):
             stack += [k_ref[18 + t], k_ref[9 + t], k_ref[t], zero]
@@ -259,15 +270,14 @@
         )
         for dy in range(3):
             for dz in range(3):
-                here = slice(dy * 128, dy * 128 + 128)
-                t = dy * 3 + dz
-                tile = lined[t * C : t * C + C]
-                w_ref[dz * 64 : dz * 64 + C, here] = tile.astype(BF16)
-                w_ref[dz * 64 + C : dz * 64 + 64, here] = pltpu.roll(tile, C, 1).astype(BF16)
-                t = 8 - t
-                tile = turned[:, t * 128 : t * 128 + 128]
-                b_ref[dz * 64 : dz * 64 + C, here] = tile.astype(BF16)
-                b_ref[dz * 64 + C : dz * 64 + 64, here] = pltpu.roll(tile, C, 1).astype(BF16)
+                t = 8 - dy * 3 - dz
+                put_tile(b_ref, dz, dy, turned[:, t * 128 : t * 128 + 128])
+
+
+def put_tile(ref, dz, dy, tile):
+    here = slice(dy * 128, dy * 128 + 128)
+    ref[dz * 64 : dz * 64 + C, here] = tile.astype(BF16)
+    ref[dz * 64 + C : dz * 64 + 64, here] = pltpu.roll(tile, C, 1).astype(BF16)
 
 
 def first_kernel(
@@ -282,6 +292,8 @@
 
         def emit(y, values, k=k):
             h[y, 64 * k : 64 * k + 64] = values
+            if k == 1:
+                send(h, row=y)
             if 3 <= y < 3 + ROWS:
                 acc[k] = acc[k] + values
 
@@ -289,6 +301,7 @@
     send(h)
     for y in range(ROWS + 8):
         v[y] = jnp.concatenate([low(y)[C:], own(y), high(y)[0:C]], axis=0)
+        send(v, row=y)
     send(v)
     center = center_of(jnp.concatenate([acc[0][C:], acc[1][0:C]], axis=0))
     both = twice(center)
@@ -312,15 +325,16 @@
     mean4, scale4 = fourfold(mean), fourfold(inverse * gb[:, 0:1])
     shift4 = fourfold(gb[:, 1:2])
     rows = ROWS + 6
-    need(h1)
     for y in range(rows):
+        need(h1, row=y)
         v[y] = masked(act((h1[y] - mean4) * scale4 + shift4), kept(place, y, rows, 3))
-    send(v)
+        send(v, row=y)
     need(w, cot, y_low, y_high)
     acc = [jnp.zeros((64, 128), F32)]
 
     def emit(y, values):
         h[y] = values
+        send(h, row=y)
         if 2 <= y < 2 + ROWS:
             acc[0] = acc[0] + values
 
@@ -334,20 +348,21 @@
         off = h[y] - both
         if 2 <= y < 2 + ROWS:
             spread = spread + off * off
-        low[y] = off[0:C].astype(BF16)
-        high[y] = off[C:].astype(BF16)
+        low[2 * y] = off[0:C].astype(BF16)
+        high[2 * y] = off[C:].astype(BF16)
         values = cot_row(cot, y_low, y_high, y)
-        low[rows + y] = values[0:C]
-        high[rows + y] = values[C:]
-    send(low, high)
+        low[2 * y + 1] = values[0:C]
+        high[2 * y + 1] = values[C:]
+        send(low, high, row=2 * y + 1)
     message((center, fold(total(spread))), msg)
 
 
 def side_kernel(need, send, center, h1, v1, xh, g, acc):
-    need(center, h1)
+    need(center)
     both = twice(center[...])
     lane = lanes(64)
     for y in range(ROWS):
+        need(h1, row=y + 3)
         put_shifted(g, y, h1[y + 3] - both, lane)
     need(v1)
     weight_sums(g, v1, 3, acc)
@@ -368,15 +383,17 @@
 def third_kernel(cells, need, send, place, r2, gb, cot, h2, st1, x1, xh, out, msg, st2):
     need(gb)
     mean, inverse, _, _ = stats_of(r2[...], place, cells, st2)
-    need(h2, cot)
     mean2, inverse2 = twice(mean), twice(inverse)
     gain2, bias2 = twice(gb[:, 2:3]), twice(gb[:, 3:4])
     plain = jnp.zeros((64, 128), F32)
     both = jnp.zeros((64, 128), F32)
     for y in range(ROWS):
+        need(h2, row=y + 2)
+        need(cot, row=y)
         normed = (h2[y + 2] - mean2) * inverse2
         z = normed * gain2 + bias2
         out[y] = act(z).astype(BF16)
+        send(out, row=y)
         slope = cot[y].astype(F32) * act_slope(z)
         plain = plain + slope
         both = both + slope * normed
@@ -400,7 +417,7 @@
     t3[...] = jnp.sum(r3[...], axis=0)
     send(t3)
     nsum, plain = sums_of(t3[0:1])
-    need(h2, x_low, x_high, cot, y_low, y_high)
+    need(y_low, y_high)
     gain, bias = gb[:, 2:3], gb[:, 3:4]
     lead = gain * inverse
     p_mean, n_mean = plain / cells, nsum / cells
@@ -415,9 +432,12 @@
     lane = lanes(64)
     rows = ROWS + 4
     for y in range(rows):
-        g_low = grad((x_low[y].astype(F32) + o_low) * inverse, x_low[rows + y], *one)
+        need(h2, row=y)
+        need(x_low, x_high, row=2 * y + 1)
+        need(cot, row=min(max(y - 2, 0), ROWS - 1))
+        g_low = grad((x_low[2 * y].astype(F32) + o_low) * inverse, x_low[2 * y + 1], *one)
         g_own = grad((h2[y] - mean2) * inverse2, cot_row(cot, y_low, y_high, y), *two)
-        g_high = grad((x_high[y].astype(F32) + o_high) * inverse, x_high[rows + y], *one)
+        g_high = grad((x_high[2 * y].astype(F32) + o_high) * inverse, x_high[2 * y + 1], *one)
         both = jnp.concatenate([g_low, g_own, g_high], axis=0)
         v[y] = masked(both, kept(place, y, rows, 2))
         if 2 <= y < 2 + ROWS:
@@ -437,6 +457,7 @@
         slope1[y] = slope
         low[y] = slope[0:C].astype(BF16)
         high[y] = slope[C:].astype(BF16)
+        send(slope1, low, high, row=y)
         if 1 <= y < 1 + ROWS:
             sums[0] = sums[0] + slope * normed
             sums[1] = sums[1] + slope
@@ -491,8 +512,9 @@
     lead4 = fourfold(gb[:, 0:1] * inverse)
     p_mean4, n_mean4 = fourfold(plain / cells), fourfold(nsum / cells)
     rows = ROWS + 2
-    need(slope1, s_low, s_high, h1)
     for y in range(rows):
+        need(slope1, s_low, s_high, row=y)
+        need(h1, row=y + 2)
         slope = jnp.concatenate(
             [s_low[y].astype(F32), slope1[y], s_high[y].astype(F32)], axis=0
         )
@@ -502,11 +524,22 @@
 
     def emit(y, values):
         out[y] = values.astype(BF16)
+        send(out, row=y)
 
     conv_rows(windows_of(v), w, ROWS, emit)
 
 
-def call(kernel, ins, outs, name, scratch=(), smem_first=True, after=(), near=0, cut=()):
+def pieces_of(shape):
+    rows = shape[0]
+    if len(shape) < 3 or rows < 32 or rows > 100:
+        return [(0, rows)]
+    cuts = [rows * c // 4 for c in range(5)]
+    return list(zip(cuts, cuts[1:]))
+
+
+def call(
+    kernel, ins, outs, name, scratch=(), smem_first=True, after=(), near=0, cut=(), late=0, grant=56
+):
     lead = 1 if smem_first else 0
     count_in, count_out = len(ins) - lead - near, len(outs)
     far_ins = ins[lead + near :]
@@ -520,35 +553,50 @@
             parts.append(rest[:size])
             rest = rest[size:]
         sources, _, targets, in_bufs, out_bufs, (in_sems, out_sems) = parts
+
+        def source(k, a, b):
+            return sources[k].at[a:b, C : 3 * C] if own[k] else sources[k].at[a:b]
+
         arriving = [
-            pltpu.make_async_copy(a.at[:, C : 3 * C] if c else a, b, in_sems.at[k])
-            for k, (a, b, c) in enumerate(zip(sources, in_bufs, own))
+            [
+                (a, b, pltpu.make_async_copy(source(k, a, b), buf.at[a:b], in_sems.at[k, c]))
+                for c, (a, b) in enumerate(pieces_of(buf.shape))
+            ]
+            for k, buf in enumerate(in_bufs)
         ]
         leaving = [
-            pltpu.make_async_copy(a, b, out_sems.at[k])
-            for k, (a, b) in enumerate(zip(out_bufs, targets))
+            [
+                (a, b, pltpu.make_async_copy(buf.at[a:b], targets[k].at[a:b], out_sems.at[k, c]))
+                for c, (a, b) in enumerate(pieces_of(buf.shape))
+            ]
+            for k, buf in enumerate(out_bufs)
         ]
-        waiting, held = list(range(count_in)), list(range(count_out))
-        for copy in arriving:
-            copy.start()
-
-        def need(*wanted):
-            for k in list(waiting):
-                if any(in_bufs[k] is ref for ref in wanted):
-                    arriving[k].wait()
-                    waiting.remove(k)
-
-        def send(*ready):
-            for k in list(held):
-                if any(out_bufs[k] is ref for ref in ready):
-                    leaving[k].start()
-                    held.remove(k)
+        early, later = arriving[: count_in - late], arriving[count_in - late :]
+        for group in (early, later):
+            for c in range(4):
+                for pieces in group:
+                    if c < len(pieces):
+                        pieces[c][2].start()
+        waiting, held = [list(pieces) for pieces in arriving], [list(pieces) for pieces in leaving]
+
+        def need(*wanted, row=None):
+            for ref in wanted:
+                for k, buf in enumerate(in_bufs):
+                    while buf is ref and waiting[k] and (row is None or waiting[k][0][0] <= row):
+                        waiting[k].pop(0)[2].wait()
+
+        def send(*ready, row=None):
+            for ref in ready:
+                for k, buf in enumerate(out_bufs):
+                    while buf is ref and held[k] and (row is None or held[k][0][1] <= row + 1):
+                        held[k].pop(0)[2].start()
 
         kernel(need, send, *first, *in_bufs, *out_bufs, *rest)
         send(*out_bufs)
         need(*in_bufs)
-        for copy in leaving:
-            copy.wait()
+        for pieces in leaving:
+            for piece in pieces:
+                piece[2].wait()
 
     far = pl.BlockSpec(memory_space=pltpu.HBM)
     return pl.pallas_call(
@@ -561,11 +609,11 @@
         scratch_shapes=[
             *[pltpu.VMEM(shape, a.dtype) for shape, a in zip(shapes, far_ins)],
             *[pltpu.VMEM(a.shape, a.dtype) for a in outs],
-            pltpu.SemaphoreType.DMA((max(count_in, 1),)),
-            pltpu.SemaphoreType.DMA((count_out,)),
+            pltpu.SemaphoreType.DMA((max(count_in, 1), 4)),
+            pltpu.SemaphoreType.DMA((count_out, 4)),
             *scratch,
         ],
-        compiler_params=pltpu.CompilerParams(vmem_limit_bytes=56 * 1024 * 1024),
+        compiler_params=pltpu.CompilerParams(vmem_limit_bytes=grant * 1024 * 1024),
         cost_estimate=pl.CostEstimate(
             flops=2_000_000_000, bytes_accessed=6_000_000, transcendentals=0
         ),
@@ -620,9 +668,8 @@
     taps = [
         jnp.transpose(k, (2, 3, 4, 0, 1)).reshape(27, C, C) for k in (kernel_one, kernel_two)
     ]
-    w1, w2, b1, b2 = call(
-        weights_kernel, taps, [sh((192, 384), BF16)] * 4, "weights", smem_first=False
-    )
+    matrices = [sh((192, 384), BF16)] * 2
+    w1, w2 = call(weights_kernel, taps, matrices, "weights", smem_first=False)
 
     v1, h1, m1, x1_own, center = call(
         first_kernel,
@@ -656,12 +703,14 @@
     )
     h2_low, h2_high = up(high, GX), down(low, GX)
     r2 = share(m2)
+    b1, b2 = call(flipped_kernel, taps, matrices, "flipped", smem_first=False, after=(h2,))
     output, m3, st2 = call(
         lambda *refs: third_kernel(cells, *refs),
         (place, r2, gb, cot, h2, st1, x1_own, xh),
         [sh((ROWS, 64, 128), BF16), four, stats],
         "slope_two",
         near=1,
+        after=(b1,),
     )
     r3 = share(m3)
 
@@ -679,6 +728,7 @@
         [sh((34, 64, 128), F32), *rims(34), wide, sh((4, 128), F32)],
         "back_two",
         near=1,
+        late=5,
         cut=(h1,),
         scratch=(pltpu.VMEM((36, 128, 128), BF16), *corr, corr[1]),
     )
@@ -701,7 +751,7 @@
         "back_one",
         scratch=(pltpu.VMEM((34, 128, 128), BF16),),
     )
-    grads = call(finish_kernel, (r5,), [sh((27, C, C), F32)] * 2, "finish", smem_first=False, near=1)
+    grads = call(finish_kernel, (r5,), [sh((27, C, C), F32)] * 2, "finish", smem_first=False, near=1, grant=16)
     one, two = [jnp.transpose(k.reshape(3, 3, 3, C, C), (3, 4, 0, 1, 2)) for k in grads]
 
     return output, back(grad), one, two, norm_grads

time: 183 us -> 173 us (0.945)
  blocking collectives: 39.1 us -> 19.9 us
  starting transfers between devices: 56.7 us -> 62.6 us
  waiting for transfers between devices: 25 us -> 27.3 us
    all_to_all x2 -> x1, blocking collectives: 39.1 us -> 19.9 us  [share(): return lax.all_to_all(msg, ALL, 0, 0, tiled=True)]
    all_to_all x3 -> x4, starting transfers between devices: 30.5 us -> 35.2 us  [share(): return lax.all_to_all(msg, ALL, 0, 0, tiled=True)]
    all_to_all x3 -> x4, waiting for transfers between devices: 12 us -> 14.4 us  [share(): return lax.all_to_all(msg, ALL, 0, 0, tiled=True)]
    pallas_call x11 -> x12, Pallas kernels: 47.5 us -> 48.4 us  [call(): pl.pallas_call(body, out_shape=outs, in_specs=[SM] * lead + [pl.BlockSpec...]
  transfers between devices with their start and end apart: 13 -> 14, of which waited for: 5 -> 6; matrix products, arithmetic and copies ran while one was open for 3% -> 3% of each run, Pallas kernels for 11% -> 12%
where the time goes in v6:
time: 173 us; the launch traced here: 172 us
  starting transfers between devices  62.6 us (36%)
  Pallas kernels  48.4 us (28%)
  waiting for transfers between devices  27.3 us (16%)
  blocking collectives  19.9 us (12%)
  local copies, waits for them, and re-layouts  12.1 us (7%)
    pallas_call x12, Pallas kernels, call(): pl.pallas_call(body, out_shape=outs, in_specs=[SM] * lead + [pl.BlockSpec...  48.4 us
    all_to_all x4, starting transfers between devices, share(): return lax.all_to_all(msg, ALL, 0, 0, tiled=True)  35.2 us
    ppermute x5, starting transfers between devices, up(): return lax.ppermute(values, axes, [(i, i + 1) for i in range(count - 1)])  20.1 us
    all_to_all x1, blocking collectives, share(): return lax.all_to_all(msg, ALL, 0, 0, tiled=True)  19.9 us
    all_to_all x4, waiting for transfers between devices, share(): return lax.all_to_all(msg, ALL, 0, 0, tiled=True)  14.4 us
    ppermute x5, starting transfers between devices, down(): return lax.ppermute(values, axes, [(i + 1, i) for i in range(count - 1)])  7.27 us
    ppermute x5, waiting for transfers between devices, up(): return lax.ppermute(values, axes, [(i, i + 1) for i in range(count - 1)])  6.9 us
    ppermute x5, waiting for transfers between devices, down(): return lax.ppermute(values, axes, [(i + 1, i) for i in range(count - 1)])  6.03 us
  transfers between devices with their start and end apart: 14, of which 6 were waited for; matrix products, arithmetic and copies ran while one was open for 3% of the time, Pallas kernels for 12%

profile of v6, /device:TPU:1, one launch (start us, length us, event | category | flops | bytes accessed | tf_op | source)
XLA Modules:
  0.0 171.5 jit_solution(14158266904859213881)
XLA Ops:
  0.6 1.4 copy.28
  2.1 0.0 copy-start.3
  2.1 1.3 collective-permute-start.1
  3.4 4.7 %collective-permute-start = (bf16[32,64,128]{2,1,0:T(8,128)(2,1)S(1)}, bf16[32,64,128]{2,1,0:T(8,128)(2,1)S(1)}, u32[]{:S(2)}, u32[]{:S(2)}) collective-permute-start(bf16[32,64,128]{2,1,0:T(8,128)(2,1)S(1)} %bitcast.47), channel_id=1, source_target_pairs={{0,8},{8,16},{16,24},{24,32},{32,40},{40,48},{48,56},{56,64},{64,7... | collective-permute-start | bytes 1572872 | tf_op jit(solution)/shard_map/ppermute | solution.py:626
  8.1 1.1 copy.29
  9.3 2.1 %pack.1 = (bf16[6,64,128]{2,1,0:T(8,128)(2,1)}, bf16[6,64,128]{2,1,0:T(8,128)(2,1)}) custom-call(bf16[32,64,128]{2,1,0:T(8,128)(2,1)} %bitcast.48, bf16[32,64,128]{2,1,0:T(8,128)(2,1)} %bitcast.40), custom_call_target="tpu_custom_call" | custom-call | flops 2000000000 | bytes 6000000 | tf_op jit(solution)/shard_map/pack/pallas_call | solution.py:602
  11.4 4.8 %collective-permute-start.2 = (bf16[6,64,128]{2,1,0:T(8,128)(2,1)}, bf16[6,64,128]{2,1,0:T(8,128)(2,1)S(1)}, u32[]{:S(2)}, u32[]{:S(2)}) collective-permute-start(bf16[6,64,128]{2,1,0:T(8,128)(2,1)} %get-tuple-element.36), channel_id=1, source_target_pairs={{0,1},{1,2},{2,3},{3,4},{4,5},{5,6},{6,7},{8,9},{9,10},{10,11},{11... | collective-permute-start | bytes 294920 | tf_op jit(solution)/shard_map/ppermute | solution.py:626
  16.2 1.9 %collective-permute-start.3 = (bf16[6,64,128]{2,1,0:T(8,128)(2,1)}, bf16[6,64,128]{2,1,0:T(8,128)(2,1)S(1)}, u32[]{:S(2)}, u32[]{:S(2)}) collective-permute-start(bf16[6,64,128]{2,1,0:T(8,128)(2,1)} %get-tuple-element.37), channel_id=1, source_target_pairs={{1,0},{2,1},{3,2},{4,3},{5,4},{6,5},{7,6},{9,8},{10,9},{11,10},{12... | collective-permute-start | bytes 294920 | tf_op jit(solution)/shard_map/ppermute | solution.py:631
  18.1 0.0 collective-permute-done.2.refs_0_.refs_3_.refs_5_.refs_8_
  18.2 0.0 copy-start.7
  18.2 4.2 %collective-permute-done.3.refs_1_.refs_4_.refs_6_.refs_9_ = bf16[6,64,128]{2,1,0:T(8,128)(2,1)S(1)} collective-permute-done((bf16[6,64,128]{2,1,0:T(8,128)(2,1)}, bf16[6,64,128]{2,1,0:T(8,128)(2,1)S(1)}, u32[]{:S(2)}, u32[]{:S(2)}) %collective-permute-start.3) | collective-permute-done | bytes 98336 | tf_op jit(solution)/shard_map/ppermute | solution.py:631
  22.3 0.6 copy-done.8
  23.0 1.7 corner.1
  24.7 1.3 collective-permute-start.5
  26.0 4.0 %collective-permute-start.4 = (bf16[8,64,128]{2,1,0:T(8,128)(2,1)}, bf16[8,64,128]{2,1,0:T(8,128)(2,1)S(1)}, u32[]{:S(2)}, u32[]{:S(2)}) collective-permute-start(bf16[8,64,128]{2,1,0:T(8,128)(2,1)} %corner.1), channel_id=1, source_target_pairs={{0,8},{8,16},{16,24},{24,32},{32,40},{40,48},{48,56},{56,64},{64,7... | collective-permute-start | bytes 393224 | tf_op jit(solution)/shard_map/ppermute | solution.py:626
  30.0 2.2 %weights.1 = (bf16[192,384]{1,0:T(8,128)(2,1)}, bf16[192,384]{1,0:T(8,128)(2,1)}) custom-call(bf16[27,32,32]{2,1,0:T(8,128)(2,1)} %bitcast.61, bf16[27,32,32]{2,1,0:T(8,128)(2,1)} %bitcast.63), custom_call_target="tpu_custom_call" | custom-call | flops 2000000000 | bytes 6000000 | tf_op jit(solution)/shard_map/weights/pallas_call | solution.py:602
  32.2 0.0 collective-permute-done.5.refs_6_
  32.2 0.0 collective-permute-done.4.refs_5_
  32.3 0.0 collective-permute-done.1.refs_2_
  32.3 0.0 copy-start.14
  32.3 0.0 collective-permute-done.refs_1_
  32.3 0.0 copy-start.15
  32.3 0.6 copy-done.18
  32.9 0.1 copy-done.19
  33.0 0.2 copy-done.14
  33.2 0.1 copy-done.15
  33.3 6.0 %conv_one.1 = (bf16[40,128,128]{2,1,0:T(8,128)(2,1)}, f32[38,128,128]{2,1,0:T(8,128)}, f32[128,4,128]{2,1,0:T(4,128)}, f32[16,128]{1,0:T(8,128)}, f32[32,128]{1,0:T(8,128)}) custom-call(bf16[32,64,128]{2,1,0:T(8,128)(2,1)} %bitcast.49, bf16[32,64,128]{2,1,0:T(8,128)(2,1)} %copy-done.15, bf16[32,64,128]{2,1,0:T(8,128)(2,1)} %copy-done.14, ...), custom_call_target="tpu_custom_call" | custom-call | flops 2000000000 | bytes 6000000 | tf_op jit(solution)/shard_map/conv_one/pallas_call | solution.py:602
  39.3 15.3 %all-to-all-start = ((f32[128,4,128]{2,1,0:T(4,128)}), f32[128,4,128]{2,1,0:T(4,128)S(1)}, u32[]{:S(2)}, u32[]{:S(2)}) async-start(f32[128,4,128]{2,1,0:T(4,128)} %get-tuple-element.39), calls=%async_computation | async-start | bytes 524288 | tf_op jit(solution)/shard_map/all_to_all | solution.py:635
  54.7 0.7 copy.30.refs_2_.refs_3_
  55.4 0.6 stack.66.refs_0_
  56.0 3.7 %hidden_features.1.refs_8_.refs_7_ = f32[9,32,128]{2,1,0:T(8,128)} custom-call(f32[32,128]{1,0:T(8,128)} %get-tuple-element.42.refs_0_, f32[38,128,128]{2,1,0:T(8,128)} %get-tuple-element.40.refs_1_.refs_3_.refs_12_.refs_4_, bf16[40,128,128]{2,1,0:T(8,128)(2,1)} %get-tuple-element.43.refs_2_.refs_14_), custom_call_target="tpu_custom_call" | custom-call | flops 2000000000 | bytes 6000000 | tf_op jit(solution)/shard_map/hidden_features/pallas_call | solution.py:602
  59.7 5.8 %all-to-all-done.refs_1_ = f32[128,4,128]{2,1,0:T(4,128)S(1)} async-done(((f32[128,4,128]{2,1,0:T(4,128)}), f32[128,4,128]{2,1,0:T(4,128)S(1)}, u32[]{:S(2)}, u32[]{:S(2)}) %all-to-all-start) | async-done | bytes 262176 | tf_op jit(solution)/shard_map/all_to_all | solution.py:635
  65.5 0.7 copy-done.6
  66.2 6.6 %conv_two.1 = (bf16[38,128,128]{2,1,0:T(8,128)(2,1)}, f32[36,64,128]{2,1,0:T(8,128)}, bf16[72,32,128]{2,1,0:T(8,128)(2,1)}, bf16[72,32,128]{2,1,0:T(8,128)(2,1)}...) custom-call(s32[8]{0:T(128)} %stack.66.refs_0_, f32[128,4,128]{2,1,0:T(4,128)} %copy-done.6, ...), custom_call_target="tpu_custom_call" | custom-call | flops 2000000000 | bytes 6000000 | tf_op jit(solution)/shard_map/conv_two/pallas_call | solution.py:602
  72.8 4.6 %all-to-all-start.1 = ((f32[128,1,128]{2,1,0:T(1,128)}), f32[128,1,128]{2,1,0:T(1,128)S(1)}, u32[]{:S(2)}, u32[]{:S(2)}) async-start(f32[128,1,128]{2,1,0:T(1,128)} %bitcast.56), calls=%async_computation.1 | async-start | bytes 131072 | tf_op jit(solution)/shard_map/all_to_all | solution.py:635
  77.5 3.3 %collective-permute-start.6 = (bf16[72,32,128]{2,1,0:T(8,128)(2,1)}, bf16[72,32,128]{2,1,0:T(8,128)(2,1)S(1)}, u32[]{:S(2)}, u32[]{:S(2)}) collective-permute-start(bf16[72,32,128]{2,1,0:T(8,128)(2,1)} %get-tuple-element.52), channel_id=1, source_target_pairs={{0,8},{8,16},{16,24},{24,32},{32,40},{40,48},{48,56},{56,64},{64,7... | collective-permute-start | bytes 1769480 | tf_op jit(solution)/shard_map/ppermute | solution.py:626
  80.8 1.5 collective-permute-start.7
  82.3 2.3 %flipped.1 = (bf16[192,384]{1,0:T(8,128)(2,1)}, bf16[192,384]{1,0:T(8,128)(2,1)}) custom-call(bf16[27,32,32]{2,1,0:T(8,128)(2,1)} %bitcast.62, bf16[27,32,32]{2,1,0:T(8,128)(2,1)} %bitcast.64, f32[36,64,128]{2,1,0:T(8,128)} %get-tuple-element.45.refs_2_.refs_4_), custom_call_target="tpu_custom_call" | custom-call | flops 2000000000 | bytes 6000000 | tf_op jit(solution)/shard_map/flipped/pallas_call | solution.py:602
  84.6 2.2 %all-to-all-done.1 = f32[128,1,128]{2,1,0:T(1,128)S(1)} async-done(((f32[128,1,128]{2,1,0:T(1,128)}), f32[128,1,128]{2,1,0:T(1,128)S(1)}, u32[]{:S(2)}, u32[]{:S(2)}) %all-to-all-start.1) | async-done | bytes 65568 | tf_op jit(solution)/shard_map/all_to_all | solution.py:635
  86.8 0.6 copy-done.9
  87.4 4.3 %slope_two.1 = (bf16[32,64,128]{2,1,0:T(8,128)(2,1)}, f32[128,4,128]{2,1,0:T(4,128)}, f32[32,128]{1,0:T(8,128)}) custom-call(s32[8]{0:T(128)} %stack.66.refs_0_, f32[128,128]{1,0:T(8,128)} %bitcast.55, f32[32,4]{1,0:T(8,128)} %copy.30.refs_2_.refs_3_, bf16[32,64,128]{2,1,0:T(8,128)(2,1)} %bitcast.42, f32[36,64,128]{2,1,0:T(8,128)} %get-tuple-element.45.refs_2_.refs_4_, ...), custom_call_target="tpu_custom_call" | custom-call | flops 2000000000 | bytes 6000000 | tf_op jit(solution)/shard_map/slope_two/pallas_call | solution.py:602
  91.7 19.9 %all_to_all.31.refs_1_ = f32[128,4,128]{2,1,0:T(4,128)} all-to-all(f32[128,4,128]{2,1,0:T(4,128)} %get-tuple-element.50), channel_id=1, replica_groups=mesh['gx_0'=4,'gx_1'=4,'gy_0'=4,'gy_1'=2] {'gx_0','gx_1','gy_0','gy_1'}, dimensions={0} | all-to-all | bytes 524288 | tf_op jit(solution)/shard_map/all_to_all | solution.py:635
  111.6 0.0 collective-permute-done.6.refs_5_
  111.6 0.0 collective-permute-done.7.refs_6_
  111.6 0.8 copy-done
  112.4 0.2 copy-done.1
  112.7 10.0 %back_two.1 = (f32[34,64,128]{2,1,0:T(8,128)}, bf16[34,32,128]{2,1,0:T(8,128)(2,1)}, bf16[34,32,128]{2,1,0:T(8,128)(2,1)}, f32[128,8,128]{2,1,0:T(8,128)}, f32[4,128]{1,0:T(4,128)}) custom-call(s32[8]{0:T(128)} %stack.66.refs_0_, f32[128,4,128]{2,1,0:T(4,128)} %all_to_all.31.refs_1_, f32[32,128]{1,0:T(8,128)} %get-tuple-element.51.refs_2_, ...), custom_call_target="tpu_custom_call" | custom-call | flops 2000000000 | bytes 6000000 | tf_op jit(solution)/shard_map/back_two/pallas_call | solution.py:602
  122.7 0.0 copy-start.4
  122.7 4.6 %all-to-all-start.3 = ((f32[128,8,128]{2,1,0:T(8,128)}), f32[128,8,128]{2,1,0:T(8,128)S(1)}, u32[]{:S(2)}, u32[]{:S(2)}) async-start(f32[128,8,128]{2,1,0:T(8,128)} %get-tuple-element.56), calls=%async_computation.3 | async-start | bytes 1048576 | tf_op jit(solution)/shard_map/all_to_all | solution.py:635
  127.3 3.3 %collective-permute-start.8 = (bf16[34,32,128]{2,1,0:T(8,128)(2,1)}, bf16[34,32,128]{2,1,0:T(8,128)(2,1)S(1)}, u32[]{:S(2)}, u32[]{:S(2)}) collective-permute-start(bf16[34,32,128]{2,1,0:T(8,128)(2,1)} %get-tuple-element.59), channel_id=1, source_target_pairs={{0,8},{8,16},{16,24},{24,32},{32,40},{40,48},{48,56},{56,64},{64,7... | collective-permute-start | bytes 835592 | tf_op jit(solution)/shard_map/ppermute | solution.py:626
  130.6 1.3 collective-permute-start.9
  131.9 0.0 copy-done.4
  131.9 1.1 copy.41
  133.0 6.9 %collective-permute-done.8.refs_6_ = bf16[34,32,128]{2,1,0:T(8,128)(2,1)S(1)} collective-permute-done((bf16[34,32,128]{2,1,0:T(8,128)(2,1)}, bf16[34,32,128]{2,1,0:T(8,128)(2,1)S(1)}, u32[]{:S(2)}, u32[]{:S(2)}) %collective-permute-start.8) | collective-permute-done | bytes 278560 | tf_op jit(solution)/shard_map/ppermute | solution.py:626
  139.9 1.8 %collective-permute-done.9.refs_7_ = bf16[34,32,128]{2,1,0:T(8,128)(2,1)S(1)} collective-permute-done((bf16[34,32,128]{2,1,0:T(8,128)(2,1)}, bf16[34,32,128]{2,1,0:T(8,128)(2,1)S(1)}, u32[]{:S(2)}, u32[]{:S(2)}) %collective-permute-start.9) | collective-permute-done | bytes 278560 | tf_op jit(solution)/shard_map/ppermute | solution.py:631
  141.8 0.0 all-to-all-done.3.refs_1_
  141.8 0.7 copy-done.17
  142.5 0.2 copy-done.5
  142.7 3.2 %own_rows.1 = (f32[128,8,128]{2,1,0:T(8,128)}, f32[4,32]{1,0:T(4,128)}, f32[8,128]{1,0:T(8,128)}) custom-call(s32[8]{0:T(128)} %stack.66.refs_0_, f32[128,8,128]{2,1,0:T(8,128)} %copy-done.5, f32[32,128]{1,0:T(8,128)} %get-tuple-element.46.refs_5_.refs_11_.refs_2_, f32[32,4]{1,0:T(8,128)} %copy.30.refs_2_.refs_3_, f32[4,128]{1,0:T(4,128)} %get-tuple-element.57.refs_4_, ...), custom_call_target="tpu_custom_call" | custom-call | flops 2000000000 | bytes 6000000 | tf_op jit(solution)/shard_map/own_rows/pallas_call | solution.py:602
  145.8 10.6 %all-to-all-start.4 = ((f32[128,8,128]{2,1,0:T(8,128)}), f32[128,8,128]{2,1,0:T(8,128)S(1)}, u32[]{:S(2)}, u32[]{:S(2)}) async-start(f32[128,8,128]{2,1,0:T(8,128)} %get-tuple-element.63), calls=%async_computation.4 | async-start | bytes 1048576 | tf_op jit(solution)/shard_map/all_to_all | solution.py:635
  156.4 5.1 %back_one.1 = bf16[32,64,128]{2,1,0:T(8,128)(2,1)} custom-call(s32[8]{0:T(128)} %stack.66.refs_0_, f32[8,128]{1,0:T(8,128)} %get-tuple-element.61.refs_1_, f32[32,128]{1,0:T(8,128)} %get-tuple-element.46.refs_5_.refs_11_.refs_2_, f32[32,4]{1,0:T(8,128)} %copy.30.refs_2_.refs_3_, f32[38,128,128]{2,1,0:T(8,128)} %get-tuple-element.40.refs_1_.refs_3_.refs_12_.refs_4_, ...), custom_call_target="tpu_custom_call" | custom-call | flops 2000000000 | bytes 6000000 | tf_op jit(solution)/shard_map/back_one/pallas_call | solution.py:602
  161.5 2.2 %copy.40 = bf16[32,2,32,128]{3,0,1,2:T(8,128)(2,1)} copy(bf16[32,2,32,128]{3,2,1,0:T(8,128)(2,1)} %bitcast.54) | data formatting | bytes 1048576 | tf_op jit(solution)/shard_map/reshape | solution.py:718
  163.7 6.4 %all-to-all-done.4.refs_0_ = f32[128,8,128]{2,1,0:T(8,128)S(1)} async-done(((f32[128,8,128]{2,1,0:T(8,128)}), f32[128,8,128]{2,1,0:T(8,128)S(1)}, u32[]{:S(2)}, u32[]{:S(2)}) %all-to-all-start.4) | async-done | bytes 524320 | tf_op jit(solution)/shard_map/all_to_all | solution.py:635
  170.1 1.2 finish.1
  (24 shorter events, 0.1 us)
Async XLA Ops:
  0.6 7.5 %copy-start.2 = (bf16[32,2,32,128]{3,2,1,0:T(8,128)(2,1)S(1)}, bf16[32,2,32,128]{3,2,1,0:T(8,128)(2,1)}, u32[]{:S(2)}) copy-start(bf16[32,2,32,128]{3,2,1,0:T(8,128)(2,1)} %param.15) | copy-start | bytes 1572868
  2.1 7.2 %copy-start.3 = (bf16[32,2,32,128]{3,2,1,0:T(8,128)(2,1)}, bf16[32,2,32,128]{3,2,1,0:T(8,128)(2,1)S(1)}, u32[]{:S(2)}) copy-start(bf16[32,2,32,128]{3,2,1,0:T(8,128)(2,1)S(1)} %copy.28) | copy-start | bytes 1572868
  2.1 30.2 %collective-permute-start.1 = (bf16[32,64,128]{2,1,0:T(8,128)(2,1)S(1)}, bf16[32,64,128]{2,1,0:T(8,128)(2,1)S(1)}, u32[]{:S(2)}, u32[]{:S(2)}) collective-permute-start(bf16[32,64,128]{2,1,0:T(8,128)(2,1)S(1)} %bitcast.46), channel_id=1, source_target_pairs={{8,0},{16,8},{24,16},{32,24},{40,32},{48,40},{56,48},{64,56},{72,6... | collective-permute-start | bytes 1572872 | tf_op jit(solution)/shard_map/ppermute | solution.py:631
  3.4 28.9 %collective-permute-start = (bf16[32,64,128]{2,1,0:T(8,128)(2,1)S(1)}, bf16[32,64,128]{2,1,0:T(8,128)(2,1)S(1)}, u32[]{:S(2)}, u32[]{:S(2)}) collective-permute-start(bf16[32,64,128]{2,1,0:T(8,128)(2,1)S(1)} %bitcast.47), channel_id=1, source_target_pairs={{0,8},{8,16},{16,24},{24,32},{32,40},{40,48},{48,56},{56,64},{64,7... | collective-permute-start | bytes 1572872 | tf_op jit(solution)/shard_map/ppermute | solution.py:626
  11.4 6.8 %collective-permute-start.2 = (bf16[6,64,128]{2,1,0:T(8,128)(2,1)}, bf16[6,64,128]{2,1,0:T(8,128)(2,1)S(1)}, u32[]{:S(2)}, u32[]{:S(2)}) collective-permute-start(bf16[6,64,128]{2,1,0:T(8,128)(2,1)} %get-tuple-element.36), channel_id=1, source_target_pairs={{0,1},{1,2},{2,3},{3,4},{4,5},{5,6},{6,7},{8,9},{9,10},{10,11},{11... | collective-permute-start | bytes 294920 | tf_op jit(solution)/shard_map/ppermute | solution.py:626
  16.2 6.1 %collective-permute-start.3 = (bf16[6,64,128]{2,1,0:T(8,128)(2,1)}, bf16[6,64,128]{2,1,0:T(8,128)(2,1)S(1)}, u32[]{:S(2)}, u32[]{:S(2)}) collective-permute-start(bf16[6,64,128]{2,1,0:T(8,128)(2,1)} %get-tuple-element.37), channel_id=1, source_target_pairs={{1,0},{2,1},{3,2},{4,3},{5,4},{6,5},{7,6},{9,8},{10,9},{11,10},{12... | collective-permute-start | bytes 294920 | tf_op jit(solution)/shard_map/ppermute | solution.py:631
  18.2 4.2 %copy-start.7 = (bf16[6,64,128]{2,1,0:T(8,128)(2,1)}, bf16[6,64,128]{2,1,0:T(8,128)(2,1)S(1)}, u32[]{:S(2)}) copy-start(bf16[6,64,128]{2,1,0:T(8,128)(2,1)S(1)} %collective-permute-done.2.refs_0_.refs_3_.refs_5_.refs_8_) | copy-start | bytes 294916
  22.3 0.6 copy-start.8
  24.7 7.5 %collective-permute-start.5 = (bf16[8,64,128]{2,1,0:T(8,128)(2,1)}, bf16[8,64,128]{2,1,0:T(8,128)(2,1)S(1)}, u32[]{:S(2)}, u32[]{:S(2)}) collective-permute-start(bf16[8,64,128]{2,1,0:T(8,128)(2,1)} %corner.1), channel_id=1, source_target_pairs={{8,0},{16,8},{24,16},{32,24},{40,32},{48,40},{56,48},{64,56},{72,6... | collective-permute-start | bytes 393224 | tf_op jit(solution)/shard_map/ppermute | solution.py:631
  26.0 6.3 %collective-permute-start.4 = (bf16[8,64,128]{2,1,0:T(8,128)(2,1)}, bf16[8,64,128]{2,1,0:T(8,128)(2,1)S(1)}, u32[]{:S(2)}, u32[]{:S(2)}) collective-permute-start(bf16[8,64,128]{2,1,0:T(8,128)(2,1)} %corner.1), channel_id=1, source_target_pairs={{0,8},{8,16},{16,24},{24,32},{32,40},{40,48},{48,56},{56,64},{64,7... | collective-permute-start | bytes 393224 | tf_op jit(solution)/shard_map/ppermute | solution.py:626
  32.2 0.7 copy-start.18
  32.2 0.7 copy-start.19
  32.3 0.9 copy-start.14
  32.3 1.0 copy-start.15
  33.3 21.3 %copy-start.10 = (f32[32]{0:T(128)S(1)}, f32[32]{0:T(128)}, u32[]{:S(2)}) copy-start(f32[32]{0:T(128)} %param.14) | copy-start | bytes 388
  33.3 21.3 %copy-start.11 = (f32[32]{0:T(128)S(1)}, f32[32]{0:T(128)}, u32[]{:S(2)}) copy-start(f32[32]{0:T(128)} %param.13) | copy-start | bytes 388
  33.3 21.3 %copy-start.12 = (f32[32]{0:T(128)S(1)}, f32[32]{0:T(128)}, u32[]{:S(2)}) copy-start(f32[32]{0:T(128)} %param.11) | copy-start | bytes 388
  33.3 21.4 %copy-start.13 = (f32[32]{0:T(128)S(1)}, f32[32]{0:T(128)}, u32[]{:S(2)}) copy-start(f32[32]{0:T(128)} %param.10) | copy-start | bytes 388
  39.3 26.3 %all-to-all-start = ((f32[128,4,128]{2,1,0:T(4,128)}), f32[128,4,128]{2,1,0:T(4,128)S(1)}, u32[]{:S(2)}, u32[]{:S(2)}) async-start(f32[128,4,128]{2,1,0:T(4,128)} %get-tuple-element.39), calls=%async_computation | async-start | bytes 524288 | tf_op jit(solution)/shard_map/all_to_all | solution.py:635
  65.5 0.7 copy-start.6
  72.8 13.9 %all-to-all-start.1 = ((f32[128,1,128]{2,1,0:T(1,128)}), f32[128,1,128]{2,1,0:T(1,128)S(1)}, u32[]{:S(2)}, u32[]{:S(2)}) async-start(f32[128,1,128]{2,1,0:T(1,128)} %bitcast.56), calls=%async_computation.1 | async-start | bytes 131072 | tf_op jit(solution)/shard_map/all_to_all | solution.py:635
  77.5 34.1 %collective-permute-start.6 = (bf16[72,32,128]{2,1,0:T(8,128)(2,1)}, bf16[72,32,128]{2,1,0:T(8,128)(2,1)S(1)}, u32[]{:S(2)}, u32[]{:S(2)}) collective-permute-start(bf16[72,32,128]{2,1,0:T(8,128)(2,1)} %get-tuple-element.52), channel_id=1, source_target_pairs={{0,8},{8,16},{16,24},{24,32},{32,40},{40,48},{48,56},{56,64},{64,7... | collective-permute-start | bytes 1769480 | tf_op jit(solution)/shard_map/ppermute | solution.py:626
  80.8 30.8 %collective-permute-start.7 = (bf16[72,32,128]{2,1,0:T(8,128)(2,1)}, bf16[72,32,128]{2,1,0:T(8,128)(2,1)S(1)}, u32[]{:S(2)}, u32[]{:S(2)}) collective-permute-start(bf16[72,32,128]{2,1,0:T(8,128)(2,1)} %get-tuple-element.53), channel_id=1, source_target_pairs={{8,0},{16,8},{24,16},{32,24},{40,32},{48,40},{56,48},{64,56},{72,6... | collective-permute-start | bytes 1769480 | tf_op jit(solution)/shard_map/ppermute | solution.py:631
  86.8 0.6 copy-start.9
  111.6 0.9 copy-start
  111.6 1.1 copy-start.1
  122.7 9.2 %copy-start.4 = (bf16[32,64,128]{2,1,0:T(8,128)(2,1)S(1)}, bf16[32,64,128]{2,1,0:T(8,128)(2,1)}, u32[]{:S(2)}) copy-start(bf16[32,64,128]{2,1,0:T(8,128)(2,1)} %get-tuple-element.49) | copy-start | bytes 1572868
  122.7 19.1 %all-to-all-start.3 = ((f32[128,8,128]{2,1,0:T(8,128)}), f32[128,8,128]{2,1,0:T(8,128)S(1)}, u32[]{:S(2)}, u32[]{:S(2)}) async-start(f32[128,8,128]{2,1,0:T(8,128)} %get-tuple-element.56), calls=%async_computation.3 | async-start | bytes 1048576 | tf_op jit(solution)/shard_map/all_to_all | solution.py:635
  127.3 12.6 %collective-permute-start.8 = (bf16[34,32,128]{2,1,0:T(8,128)(2,1)}, bf16[34,32,128]{2,1,0:T(8,128)(2,1)S(1)}, u32[]{:S(2)}, u32[]{:S(2)}) collective-permute-start(bf16[34,32,128]{2,1,0:T(8,128)(2,1)} %get-tuple-element.59), channel_id=1, source_target_pairs={{0,8},{8,16},{16,24},{24,32},{32,40},{40,48},{48,56},{56,64},{64,7... | collective-permute-start | bytes 835592 | tf_op jit(solution)/shard_map/ppermute | solution.py:626
  130.6 11.2 %collective-permute-start.9 = (bf16[34,32,128]{2,1,0:T(8,128)(2,1)}, bf16[34,32,128]{2,1,0:T(8,128)(2,1)S(1)}, u32[]{:S(2)}, u32[]{:S(2)}) collective-permute-start(bf16[34,32,128]{2,1,0:T(8,128)(2,1)} %get-tuple-element.60), channel_id=1, source_target_pairs={{8,0},{16,8},{24,16},{32,24},{40,32},{48,40},{56,48},{64,56},{72,6... | collective-permute-start | bytes 835592 | tf_op jit(solution)/shard_map/ppermute | solution.py:631
  139.9 1.9 %copy-start.16 = (bf16[34,32,128]{2,1,0:T(8,128)(2,1)}, bf16[34,32,128]{2,1,0:T(8,128)(2,1)S(1)}, u32[]{:S(2)}) copy-start(bf16[34,32,128]{2,1,0:T(8,128)(2,1)S(1)} %collective-permute-done.8.refs_6_) | copy-start | bytes 835588
  141.8 0.7 copy-start.17
  141.8 0.9 copy-start.5
  145.8 24.3 %all-to-all-start.4 = ((f32[128,8,128]{2,1,0:T(8,128)}), f32[128,8,128]{2,1,0:T(8,128)S(1)}, u32[]{:S(2)}, u32[]{:S(2)}) async-start(f32[128,8,128]{2,1,0:T(8,128)} %get-tuple-element.63), calls=%async_computation.4 | async-start | bytes 1048576 | tf_op jit(solution)/shard_map/all_to_all | solution.py:635

commit v7 on v6

--- a/solution.py
+++ b/solution.py
@@ -316,12 +316,11 @@
 
 
 def second_kernel(
-    cells, need, send, place, r1, gb, h1, cot, y_low, y_high, w, v, h, low, high, msg, st1, x1
+    cells, need, send, place, r1, gb, h1, cot, y_low, y_high, w, v, h, low, high, msg, st1
 ):
     need(gb)
     mean, inverse, _, _ = stats_of(r1[:, 0, :], place, cells, st1)
-    x1[...] = jnp.sum(r1[...], axis=0)
-    send(st1, x1)
+    send(st1)
     mean4, scale4 = fourfold(mean), fourfold(inverse * gb[:, 0:1])
     shift4 = fourfold(gb[:, 1:2])
     rows = ROWS + 6
@@ -355,6 +354,11 @@
         high[2 * y + 1] = values[C:]
         send(low, high, row=2 * y + 1)
     message((center, fold(total(spread))), msg)
+
+
+def total_kernel(need, send, parts, whole):
+    need(parts)
+    whole[...] = jnp.sum(parts[...], axis=0)
 
 
 def side_kernel(need, send, center, h1, v1, xh, g, acc):
@@ -489,17 +493,20 @@
     one = lead * one
     two = fourth[4:7] * scale
     tile = jnp.concatenate([one, two, jnp.zeros((2, 128), F32)], axis=0)
-    msg[...] = jnp.broadcast_to(tile[None], msg.shape)
+    pair = twice(tile).astype(BF16)
+    for k in range(0, msg.shape[0], 16):
+        msg[k : k + 16] = pair
     for k, row in enumerate((fourth[0:1], third[0:1])):
         norms[2 * k : 2 * k + 1] = row[:, 0:C] * scale
         norms[2 * k + 1 : 2 * k + 2] = row[:, C : 2 * C] * scale
 
 
-def finish_kernel(need, send, parts, one, two):
+def finish_kernel(need, send, parts, one, two, rows):
+    rows[...] = parts[0 : 3 * C * 8].astype(F32)
     for dz in range(3):
         for dy in range(3):
             for k, out in enumerate((one, two)):
-                tile = parts[dz * C : (dz + 1) * C, 3 * k + dy, :]
+                tile = rows[pl.ds(dz * C * 8 + 3 * k + dy, C, stride=8), :]
                 for dx in range(3):
                     out[dx * 9 + dy * 3 + dz] = tile[:, dx * C : (dx + 1) * C]
 
@@ -690,27 +697,29 @@
         cut=(h1,),
     )
 
-    v2, h2, low, high, m2, st1, x1 = call(
+    b1, b2 = call(flipped_kernel, taps, matrices, "flipped", smem_first=False, after=(center,))
+    v2, h2, low, high, m2, st1 = call(
         lambda *refs: second_kernel(cells, *refs),
         (place, r1, gb, h1, cot, y_low, y_high, w2),
         [
             sh((38, 128, 128), BF16), sh((36, 64, 128), F32), *rims(72), msg, stats,
-            sh((4, 128), F32),
         ],
         "conv_two",
         near=1,
-        after=(xh,),
+        after=(xh, b1),
     )
     h2_low, h2_high = up(high, GX), down(low, GX)
     r2 = share(m2)
-    b1, b2 = call(flipped_kernel, taps, matrices, "flipped", smem_first=False, after=(h2,))
+    (x1,) = call(
+        total_kernel, (r1,), [sh((4, 128), F32)], "total", smem_first=False, after=(st1,)
+    )
     output, m3, st2 = call(
         lambda *refs: third_kernel(cells, *refs),
         (place, r2, gb, cot, h2, st1, x1_own, xh),
         [sh((ROWS, 64, 128), BF16), four, stats],
         "slope_two",
         near=1,
-        after=(b1,),
+        after=(x1,),
     )
     r3 = share(m3)
 
@@ -738,12 +747,13 @@
     m5, norm_grads, t4 = call(
         lambda *refs: owner_kernel(cells, *refs),
         (place, r4, st1, gb, t3, x1),
-        [wide, sh((4, C), F32), sh((8, 128), F32)],
+        [sh((count * 8, 128), BF16), sh((4, C), F32), sh((8, 128), F32)],
         "own_rows",
         near=1,
+        grant=16,
         after=(s_low, s_high, output),
     )
-    r5 = share(m5)
+    r5 = share(m5.reshape(count, 8, 128)).reshape(count * 8, 128)
     (grad,) = call(
         lambda *refs: fifth_kernel(cells, *refs),
         (place, t4, st1, gb, h1, slope1, s_low, s_high, b1),
@@ -751,7 +761,16 @@
         "back_one",
         scratch=(pltpu.VMEM((34, 128, 128), BF16),),
     )
-    grads = call(finish_kernel, (r5,), [sh((27, C, C), F32)] * 2, "finish", smem_first=False, near=1, grant=16)
+    grads = call(
+        finish_kernel,
+        (r5,),
+        [sh((27, C, C), F32)] * 2,
+        "finish",
+        scratch=(pltpu.VMEM((3 * C * 8, 128), F32),),
+        smem_first=False,
+        near=1,
+        grant=16,
+    )
     one, two = [jnp.transpose(k.reshape(3, 3, 3, C, C), (3, 4, 0, 1, 2)) for k in grads]
 
     return output, back(grad), one, two, norm_grads

time: 173 us -> 168 us (0.971)
  waiting for transfers between devices: 27.3 us -> 23.6 us
    all_to_all x4, waiting for transfers between devices: 14.4 us -> 11.2 us  [share(): return lax.all_to_all(msg, ALL, 0, 0, tiled=True)]
    pallas_call x12 -> x13, Pallas kernels: 48.4 us -> 48.8 us  [call(): pl.pallas_call(body, out_shape=outs, in_specs=[SM] * lead + [pl.BlockSpec...]
    unnamed x40 -> x52, local copies, waits for them, and re-layouts: 4.93 us -> 4.69 us
  transfers between devices with their start and end apart: 14 -> 14, of which waited for: 6 -> 6; matrix products, arithmetic and copies ran while one was open for 3% -> 3% of each run, Pallas kernels for 12% -> 14%
where the time goes in v7:
time: 168 us; the launch traced here: 167 us
  starting transfers between devices  63 us (38%)
  Pallas kernels  48.8 us (29%)
  waiting for transfers between devices  23.6 us (14%)
  blocking collectives  19.3 us (11%)
  local copies, waits for them, and re-layouts  11.1 us (7%)
    pallas_call x13, Pallas kernels, call(): pl.pallas_call(body, out_shape=outs, in_specs=[SM] * lead + [pl.BlockSpec...  48.8 us
    all_to_all x4, starting transfers between devices, share(): return lax.all_to_all(msg, ALL, 0, 0, tiled=True)  35.5 us
    ppermute x5, starting transfers between devices, up(): return lax.ppermute(values, axes, [(i, i + 1) for i in range(count - 1)])  20.2 us
    all_to_all x1, blocking collectives, share(): return lax.all_to_all(msg, ALL, 0, 0, tiled=True)  19.3 us
    all_to_all x4, waiting for transfers between devices, share(): return lax.all_to_all(msg, ALL, 0, 0, tiled=True)  11.2 us
    ppermute x5, waiting for transfers between devices, up(): return lax.ppermute(values, axes, [(i, i + 1) for i in range(count - 1)])  7.69 us
    ppermute x5, starting transfers between devices, down(): return lax.ppermute(values, axes, [(i + 1, i) for i in range(count - 1)])  7.27 us
    ppermute x5, waiting for transfers between devices, down(): return lax.ppermute(values, axes, [(i + 1, i) for i in range(count - 1)])  4.72 us
  transfers between devices with their start and end apart: 14, of which 6 were waited for; matrix products, arithmetic and copies ran while one was open for 3% of the time, Pallas kernels for 14%

profile of v7, /device:TPU:1, one launch (start us, length us, event | category | flops | bytes accessed | tf_op | source)
XLA Modules:
  0.0 167.2 jit_solution(12855306319379484819)
XLA Ops:
  0.6 1.4 copy.28
  2.1 0.0 copy-start.12
  2.1 1.3 collective-permute-start.1
  3.4 4.7 %collective-permute-start = (bf16[32,64,128]{2,1,0:T(8,128)(2,1)S(1)}, bf16[32,64,128]{2,1,0:T(8,128)(2,1)S(1)}, u32[]{:S(2)}, u32[]{:S(2)}) collective-permute-start(bf16[32,64,128]{2,1,0:T(8,128)(2,1)S(1)} %bitcast.52), channel_id=1, source_target_pairs={{0,8},{8,16},{16,24},{24,32},{32,40},{40,48},{48,56},{56,64},{64,7... | collective-permute-start | bytes 1572872 | tf_op jit(solution)/shard_map/ppermute | solution.py:633
  8.1 1.1 copy.29
  9.3 0.0 copy-start.21
  9.3 2.1 %pack.1 = (bf16[6,64,128]{2,1,0:T(8,128)(2,1)}, bf16[6,64,128]{2,1,0:T(8,128)(2,1)}) custom-call(bf16[32,64,128]{2,1,0:T(8,128)(2,1)} %bitcast.53, bf16[32,64,128]{2,1,0:T(8,128)(2,1)} %bitcast.45), custom_call_target="tpu_custom_call" | custom-call | flops 2000000000 | bytes 6000000 | tf_op jit(solution)/shard_map/pack/pallas_call | solution.py:609
  11.4 4.8 %collective-permute-start.2 = (bf16[6,64,128]{2,1,0:T(8,128)(2,1)}, bf16[6,64,128]{2,1,0:T(8,128)(2,1)S(1)}, u32[]{:S(2)}, u32[]{:S(2)}) collective-permute-start(bf16[6,64,128]{2,1,0:T(8,128)(2,1)} %get-tuple-element.35), channel_id=1, source_target_pairs={{0,1},{1,2},{2,3},{3,4},{4,5},{5,6},{6,7},{8,9},{9,10},{10,11},{11... | collective-permute-start | bytes 294920 | tf_op jit(solution)/shard_map/ppermute | solution.py:633
  16.2 1.9 %collective-permute-start.3 = (bf16[6,64,128]{2,1,0:T(8,128)(2,1)}, bf16[6,64,128]{2,1,0:T(8,128)(2,1)S(1)}, u32[]{:S(2)}, u32[]{:S(2)}) collective-permute-start(bf16[6,64,128]{2,1,0:T(8,128)(2,1)} %get-tuple-element.36), channel_id=1, source_target_pairs={{1,0},{2,1},{3,2},{4,3},{5,4},{6,5},{7,6},{9,8},{10,9},{11,10},{12... | collective-permute-start | bytes 294920 | tf_op jit(solution)/shard_map/ppermute | solution.py:638
  18.2 0.7 copy.30.refs_2_.refs_3_
  18.9 0.6 stack.66.refs_0_
  19.5 0.0 collective-permute-done.2.refs_0_.refs_3_.refs_5_.refs_8_
  19.6 2.8 %collective-permute-done.3.refs_1_.refs_4_.refs_6_.refs_9_ = bf16[6,64,128]{2,1,0:T(8,128)(2,1)S(1)} collective-permute-done((bf16[6,64,128]{2,1,0:T(8,128)(2,1)}, bf16[6,64,128]{2,1,0:T(8,128)(2,1)S(1)}, u32[]{:S(2)}, u32[]{:S(2)}) %collective-permute-start.3) | collective-permute-done | bytes 98336 | tf_op jit(solution)/shard_map/ppermute | solution.py:638
  22.4 0.6 copy-done.16
  23.0 1.7 %corner.1 = bf16[8,64,128]{2,1,0:T(8,128)(2,1)} custom-call(bf16[6,64,128]{2,1,0:T(8,128)(2,1)} %copy-done.15, bf16[6,64,128]{2,1,0:T(8,128)(2,1)} %copy-done.16), custom_call_target="tpu_custom_call" | custom-call | flops 2000000000 | bytes 6000000 | tf_op jit(solution)/shard_map/corner/pallas_call | solution.py:609
  24.7 1.3 collective-permute-start.5
  26.0 4.0 %collective-permute-start.4 = (bf16[8,64,128]{2,1,0:T(8,128)(2,1)}, bf16[8,64,128]{2,1,0:T(8,128)(2,1)S(1)}, u32[]{:S(2)}, u32[]{:S(2)}) collective-permute-start(bf16[8,64,128]{2,1,0:T(8,128)(2,1)} %corner.1), channel_id=1, source_target_pairs={{0,8},{8,16},{16,24},{24,32},{32,40},{40,48},{48,56},{56,64},{64,7... | collective-permute-start | bytes 393224 | tf_op jit(solution)/shard_map/ppermute | solution.py:633
  30.0 2.2 %weights.1 = (bf16[192,384]{1,0:T(8,128)(2,1)}, bf16[192,384]{1,0:T(8,128)(2,1)}) custom-call(bf16[27,32,32]{2,1,0:T(8,128)(2,1)} %bitcast.64, bf16[27,32,32]{2,1,0:T(8,128)(2,1)} %bitcast.66), custom_call_target="tpu_custom_call" | custom-call | flops 2000000000 | bytes 6000000 | tf_op jit(solution)/shard_map/weights/pallas_call | solution.py:609
  32.3 0.0 collective-permute-done.5.refs_6_
  32.3 0.0 collective-permute-done.4.refs_5_
  32.3 0.0 collective-permute-done.1.refs_2_
  32.3 0.0 collective-permute-done.refs_1_
  32.3 0.0 copy-start.23
  32.4 0.6 copy-done.24
  32.9 0.1 copy-done.25
  33.0 0.2 copy-done.22
  33.2 0.2 copy-done.23
  33.3 5.9 %conv_one.1 = (bf16[40,128,128]{2,1,0:T(8,128)(2,1)}, f32[38,128,128]{2,1,0:T(8,128)}, f32[128,4,128]{2,1,0:T(4,128)}, f32[16,128]{1,0:T(8,128)}, f32[32,128]{1,0:T(8,128)}) custom-call(bf16[32,64,128]{2,1,0:T(8,128)(2,1)} %bitcast.54, bf16[32,64,128]{2,1,0:T(8,128)(2,1)} %copy-done.23, bf16[32,64,128]{2,1,0:T(8,128)(2,1)} %copy-done.22, ...), custom_call_target="tpu_custom_call" | custom-call | flops 2000000000 | bytes 6000000 | tf_op jit(solution)/shard_map/conv_one/pallas_call | solution.py:609
  39.3 15.3 %all-to-all-start = ((f32[128,4,128]{2,1,0:T(4,128)}), f32[128,4,128]{2,1,0:T(4,128)S(1)}, u32[]{:S(2)}, u32[]{:S(2)}) async-start(f32[128,4,128]{2,1,0:T(4,128)} %get-tuple-element.38), calls=%async_computation | async-start | bytes 524288 | tf_op jit(solution)/shard_map/all_to_all | solution.py:642
  54.6 2.3 %flipped.1 = (bf16[192,384]{1,0:T(8,128)(2,1)}, bf16[192,384]{1,0:T(8,128)(2,1)}) custom-call(bf16[27,32,32]{2,1,0:T(8,128)(2,1)} %bitcast.65, bf16[27,32,32]{2,1,0:T(8,128)(2,1)} %bitcast.67, f32[32,128]{1,0:T(8,128)} %get-tuple-element.41.refs_0_.refs_2_), custom_call_target="tpu_custom_call" | custom-call | flops 2000000000 | bytes 6000000 | tf_op jit(solution)/shard_map/flipped/pallas_call | solution.py:609
  56.9 3.8 %hidden_features.1.refs_8_.refs_7_ = f32[9,32,128]{2,1,0:T(8,128)} custom-call(f32[32,128]{1,0:T(8,128)} %get-tuple-element.41.refs_0_.refs_2_, f32[38,128,128]{2,1,0:T(8,128)} %get-tuple-element.39.refs_1_.refs_3_.refs_12_.refs_4_, bf16[40,128,128]{2,1,0:T(8,128)(2,1)} %get-tuple-element.42.refs_2_.refs_14_), custom_call_target="tpu_custom_call" | custom-call | flops 2000000000 | bytes 6000000 | tf_op jit(solution)/shard_map/hidden_features/pallas_call | solution.py:609
  60.7 4.8 %all-to-all-done.refs_1_.refs_0_ = f32[128,4,128]{2,1,0:T(4,128)S(1)} async-done(((f32[128,4,128]{2,1,0:T(4,128)}), f32[128,4,128]{2,1,0:T(4,128)S(1)}, u32[]{:S(2)}, u32[]{:S(2)}) %all-to-all-start) | async-done | bytes 262176 | tf_op jit(solution)/shard_map/all_to_all | solution.py:642
  65.5 0.7 copy-done.14
  66.2 6.5 %conv_two.1 = (bf16[38,128,128]{2,1,0:T(8,128)(2,1)}, f32[36,64,128]{2,1,0:T(8,128)}, bf16[72,32,128]{2,1,0:T(8,128)(2,1)}, bf16[72,32,128]{2,1,0:T(8,128)(2,1)}, f32[128,128]{1,0:T(8,128)}, /*index=5*/f32[32,128]{1,0:T(8,128)}) custom-call(s32[8]{0:T(128)} %stack.66.refs_0_, f32[128,4,128]{2,1,0:T(4,128)} %copy-done.14, f32[32,4]{1,0:T(8,128)} %copy.30.refs_2_.refs_3_, ...), custom_call_target="tpu_custom_call" | custom-call | flops 2000000000 | bytes 6000000 | tf_op jit(solution)/shard_map/conv_two/pallas_call | solution.py:609
  72.8 4.9 %all-to-all-start.1 = ((f32[128,1,128]{2,1,0:T(1,128)}), f32[128,1,128]{2,1,0:T(1,128)S(1)}, u32[]{:S(2)}, u32[]{:S(2)}) async-start(f32[128,1,128]{2,1,0:T(1,128)} %bitcast.59), calls=%async_computation.1 | async-start | bytes 131072 | tf_op jit(solution)/shard_map/all_to_all | solution.py:642
  77.7 3.3 %collective-permute-start.6 = (bf16[72,32,128]{2,1,0:T(8,128)(2,1)}, bf16[72,32,128]{2,1,0:T(8,128)(2,1)S(1)}, u32[]{:S(2)}, u32[]{:S(2)}) collective-permute-start(bf16[72,32,128]{2,1,0:T(8,128)(2,1)} %get-tuple-element.51), channel_id=1, source_target_pairs={{0,8},{8,16},{16,24},{24,32},{32,40},{40,48},{48,56},{56,64},{64,7... | collective-permute-start | bytes 1769480 | tf_op jit(solution)/shard_map/ppermute | solution.py:633
  81.1 1.5 collective-permute-start.7
  82.5 1.7 %total.1.refs_8_.refs_5_ = f32[4,128]{1,0:T(4,128)} custom-call(f32[128,4,128]{2,1,0:T(4,128)} %copy-done.14, f32[32,128]{1,0:T(8,128)} %get-tuple-element.46.refs_1_.refs_5_.refs_11_.refs_2_), custom_call_target="tpu_custom_call" | custom-call | flops 2000000000 | bytes 6000000 | tf_op jit(solution)/shard_map/total/pallas_call | solution.py:609
  84.3 2.7 %all-to-all-done.1 = f32[128,1,128]{2,1,0:T(1,128)S(1)} async-done(((f32[128,1,128]{2,1,0:T(1,128)}), f32[128,1,128]{2,1,0:T(1,128)S(1)}, u32[]{:S(2)}, u32[]{:S(2)}) %all-to-all-start.1) | async-done | bytes 65568 | tf_op jit(solution)/shard_map/all_to_all | solution.py:642
  87.0 0.6 copy-done.17
  87.6 4.3 %slope_two.1 = (bf16[32,64,128]{2,1,0:T(8,128)(2,1)}, f32[128,4,128]{2,1,0:T(4,128)}, f32[32,128]{1,0:T(8,128)}) custom-call(s32[8]{0:T(128)} %stack.66.refs_0_, f32[128,128]{1,0:T(8,128)} %bitcast.58, f32[32,4]{1,0:T(8,128)} %copy.30.refs_2_.refs_3_, bf16[32,64,128]{2,1,0:T(8,128)(2,1)} %bitcast.47, f32[36,64,128]{2,1,0:T(8,128)} %get-tuple-element.45.refs_4_, ...), custom_call_target="tpu_custom_call" | custom-call | flops 2000000000 | bytes 6000000 | tf_op jit(solution)/shard_map/slope_two/pallas_call | solution.py:609
  91.9 19.3 %all_to_all.31.refs_1_ = f32[128,4,128]{2,1,0:T(4,128)} all-to-all(f32[128,4,128]{2,1,0:T(4,128)} %get-tuple-element.49), channel_id=1, replica_groups=mesh['gx_0'=4,'gx_1'=4,'gy_0'=4,'gy_1'=2] {'gx_0','gx_1','gy_0','gy_1'}, dimensions={0} | all-to-all | bytes 524288 | tf_op jit(solution)/shard_map/all_to_all | solution.py:642
  111.2 0.0 collective-permute-done.6.refs_5_
  111.2 0.0 collective-permute-done.7.refs_6_
  111.3 0.8 copy-done.9
  112.1 0.2 copy-done.10
  112.3 10.0 %back_two.1 = (f32[34,64,128]{2,1,0:T(8,128)}, bf16[34,32,128]{2,1,0:T(8,128)(2,1)}, bf16[34,32,128]{2,1,0:T(8,128)(2,1)}, f32[128,8,128]{2,1,0:T(8,128)}, f32[4,128]{1,0:T(4,128)}) custom-call(s32[8]{0:T(128)} %stack.66.refs_0_, f32[128,4,128]{2,1,0:T(4,128)} %all_to_all.31.refs_1_, f32[32,128]{1,0:T(8,128)} %get-tuple-element.50.refs_2_, ...), custom_call_target="tpu_custom_call" | custom-call | flops 2000000000 | bytes 6000000 | tf_op jit(solution)/shard_map/back_two/pallas_call | solution.py:609
  122.3 0.0 copy-start.13
  122.4 0.0 copy-start.8
  122.4 4.6 %all-to-all-start.3 = ((f32[128,8,128]{2,1,0:T(8,128)}), f32[128,8,128]{2,1,0:T(8,128)S(1)}, u32[]{:S(2)}, u32[]{:S(2)}) async-start(f32[128,8,128]{2,1,0:T(8,128)} %get-tuple-element.55), calls=%async_computation.3 | async-start | bytes 1048576 | tf_op jit(solution)/shard_map/all_to_all | solution.py:642
  127.0 3.4 %collective-permute-start.8 = (bf16[34,32,128]{2,1,0:T(8,128)(2,1)}, bf16[34,32,128]{2,1,0:T(8,128)(2,1)S(1)}, u32[]{:S(2)}, u32[]{:S(2)}) collective-permute-start(bf16[34,32,128]{2,1,0:T(8,128)(2,1)} %get-tuple-element.57), channel_id=1, source_target_pairs={{0,8},{8,16},{16,24},{24,32},{32,40},{40,48},{48,56},{56,64},{64,7... | collective-permute-start | bytes 835592 | tf_op jit(solution)/shard_map/ppermute | solution.py:633
  130.4 1.3 collective-permute-start.9
  131.7 0.3 copy.41
  132.1 0.0 copy-start
  132.1 7.7 %collective-permute-done.8.refs_6_ = bf16[34,32,128]{2,1,0:T(8,128)(2,1)S(1)} collective-permute-done((bf16[34,32,128]{2,1,0:T(8,128)(2,1)}, bf16[34,32,128]{2,1,0:T(8,128)(2,1)S(1)}, u32[]{:S(2)}, u32[]{:S(2)}) %collective-permute-start.8) | collective-permute-done | bytes 278560 | tf_op jit(solution)/shard_map/ppermute | solution.py:633
  139.8 1.9 %collective-permute-done.9.refs_7_ = bf16[34,32,128]{2,1,0:T(8,128)(2,1)S(1)} collective-permute-done((bf16[34,32,128]{2,1,0:T(8,128)(2,1)}, bf16[34,32,128]{2,1,0:T(8,128)(2,1)S(1)}, u32[]{:S(2)}, u32[]{:S(2)}) %collective-permute-start.9) | collective-permute-done | bytes 278560 | tf_op jit(solution)/shard_map/ppermute | solution.py:638
  141.7 1.9 %own_rows.1 = (bf16[1024,128]{1,0:T(8,128)(2,1)}, f32[4,32]{1,0:T(4,128)}, f32[8,128]{1,0:T(8,128)S(1)}) custom-call(s32[8]{0:T(128)S(1)} %copy-done.3, f32[128,8,128]{2,1,0:T(8,128)S(1)} %all-to-all-done.3.refs_1_, f32[32,128]{1,0:T(8,128)S(1)} %copy-done.2, f32[32,4]{1,0:T(8,128)S(1)} %copy-done.1, f32[4,128]{1,0:T(4,128)S(1)} %copy-done.6, ...), custom_call_target="tpu_custom_call" | custom-call | flops 2000000000 | bytes 6000000 | tf_op jit(solution)/shard_map/own_rows/pallas_call | solution.py:609
  143.6 0.0 copy-start.7
  143.6 0.6 copy-done.7
  144.2 10.6 %all-to-all-start.4 = ((bf16[128,8,128]{2,1,0:T(8,128)(2,1)}), bf16[128,8,128]{2,1,0:T(8,128)(2,1)S(1)}, u32[]{:S(2)}, u32[]{:S(2)}) async-start(bf16[128,8,128]{2,1,0:T(8,128)(2,1)} %bitcast.29), calls=%async_computation.4 | async-start | bytes 524288 | tf_op jit(solution)/shard_map/all_to_all | solution.py:642
  154.8 5.1 %back_one.1 = bf16[32,64,128]{2,1,0:T(8,128)(2,1)} custom-call(s32[8]{0:T(128)} %stack.66.refs_0_, f32[8,128]{1,0:T(8,128)} %copy-done.7, f32[32,128]{1,0:T(8,128)} %get-tuple-element.46.refs_1_.refs_5_.refs_11_.refs_2_, f32[32,4]{1,0:T(8,128)} %copy.30.refs_2_.refs_3_, f32[38,128,128]{2,1,0:T(8,128)} %get-tuple-element.39.refs_1_.refs_3_.refs_12_.refs_4_, ...), custom_call_target="tpu_custom_call" | custom-call | flops 2000000000 | bytes 6000000 | tf_op jit(solution)/shard_map/back_one/pallas_call | solution.py:609
  159.9 2.2 %copy.40 = bf16[32,2,32,128]{3,0,1,2:T(8,128)(2,1)} copy(bf16[32,2,32,128]{3,2,1,0:T(8,128)(2,1)} %bitcast.57) | data formatting | bytes 1048576 | tf_op jit(solution)/shard_map/reshape | solution.py:727
  162.1 3.7 %all-to-all-done.4 = bf16[128,8,128]{2,1,0:T(8,128)(2,1)S(1)} async-done(((bf16[128,8,128]{2,1,0:T(8,128)(2,1)}), bf16[128,8,128]{2,1,0:T(8,128)(2,1)S(1)}, u32[]{:S(2)}, u32[]{:S(2)}) %all-to-all-start.4) | async-done | bytes 262176 | tf_op jit(solution)/shard_map/all_to_all | solution.py:642
  165.8 1.2 finish.1
  (37 shorter events, 0.1 us)
Async XLA Ops:
  0.6 7.5 %copy-start.11 = (bf16[32,2,32,128]{3,2,1,0:T(8,128)(2,1)S(1)}, bf16[32,2,32,128]{3,2,1,0:T(8,128)(2,1)}, u32[]{:S(2)}) copy-start(bf16[32,2,32,128]{3,2,1,0:T(8,128)(2,1)} %param.15) | copy-start | bytes 1572868
  2.1 7.2 %copy-start.12 = (bf16[32,2,32,128]{3,2,1,0:T(8,128)(2,1)}, bf16[32,2,32,128]{3,2,1,0:T(8,128)(2,1)S(1)}, u32[]{:S(2)}) copy-start(bf16[32,2,32,128]{3,2,1,0:T(8,128)(2,1)S(1)} %copy.28) | copy-start | bytes 1572868
  2.1 30.2 %collective-permute-start.1 = (bf16[32,64,128]{2,1,0:T(8,128)(2,1)S(1)}, bf16[32,64,128]{2,1,0:T(8,128)(2,1)S(1)}, u32[]{:S(2)}, u32[]{:S(2)}) collective-permute-start(bf16[32,64,128]{2,1,0:T(8,128)(2,1)S(1)} %bitcast.51), channel_id=1, source_target_pairs={{8,0},{16,8},{24,16},{32,24},{40,32},{48,40},{56,48},{64,56},{72,6... | collective-permute-start | bytes 1572872 | tf_op jit(solution)/shard_map/ppermute | solution.py:638
  3.4 28.9 %collective-permute-start = (bf16[32,64,128]{2,1,0:T(8,128)(2,1)S(1)}, bf16[32,64,128]{2,1,0:T(8,128)(2,1)S(1)}, u32[]{:S(2)}, u32[]{:S(2)}) collective-permute-start(bf16[32,64,128]{2,1,0:T(8,128)(2,1)S(1)} %bitcast.52), channel_id=1, source_target_pairs={{0,8},{8,16},{16,24},{24,32},{32,40},{40,48},{48,56},{56,64},{64,7... | collective-permute-start | bytes 1572872 | tf_op jit(solution)/shard_map/ppermute | solution.py:633
  9.2 8.9 %copy-start.18 = (f32[32]{0:T(128)S(1)}, f32[32]{0:T(128)}, u32[]{:S(2)}) copy-start(f32[32]{0:T(128)} %param.14) | copy-start | bytes 388
  9.2 9.0 %copy-start.19 = (f32[32]{0:T(128)S(1)}, f32[32]{0:T(128)}, u32[]{:S(2)}) copy-start(f32[32]{0:T(128)} %param.13) | copy-start | bytes 388
  9.2 9.0 %copy-start.20 = (f32[32]{0:T(128)S(1)}, f32[32]{0:T(128)}, u32[]{:S(2)}) copy-start(f32[32]{0:T(128)} %param.11) | copy-start | bytes 388
  9.3 9.0 %copy-start.21 = (f32[32]{0:T(128)S(1)}, f32[32]{0:T(128)}, u32[]{:S(2)}) copy-start(f32[32]{0:T(128)} %param.10) | copy-start | bytes 388
  11.4 8.1 %collective-permute-start.2 = (bf16[6,64,128]{2,1,0:T(8,128)(2,1)}, bf16[6,64,128]{2,1,0:T(8,128)(2,1)S(1)}, u32[]{:S(2)}, u32[]{:S(2)}) collective-permute-start(bf16[6,64,128]{2,1,0:T(8,128)(2,1)} %get-tuple-element.35), channel_id=1, source_target_pairs={{0,1},{1,2},{2,3},{3,4},{4,5},{5,6},{6,7},{8,9},{9,10},{10,11},{11... | collective-permute-start | bytes 294920 | tf_op jit(solution)/shard_map/ppermute | solution.py:633
  16.2 6.1 %collective-permute-start.3 = (bf16[6,64,128]{2,1,0:T(8,128)(2,1)}, bf16[6,64,128]{2,1,0:T(8,128)(2,1)S(1)}, u32[]{:S(2)}, u32[]{:S(2)}) collective-permute-start(bf16[6,64,128]{2,1,0:T(8,128)(2,1)} %get-tuple-element.36), channel_id=1, source_target_pairs={{1,0},{2,1},{3,2},{4,3},{5,4},{6,5},{7,6},{9,8},{10,9},{11,10},{12... | collective-permute-start | bytes 294920 | tf_op jit(solution)/shard_map/ppermute | solution.py:638
  19.6 2.8 %copy-start.15 = (bf16[6,64,128]{2,1,0:T(8,128)(2,1)}, bf16[6,64,128]{2,1,0:T(8,128)(2,1)S(1)}, u32[]{:S(2)}) copy-start(bf16[6,64,128]{2,1,0:T(8,128)(2,1)S(1)} %collective-permute-done.2.refs_0_.refs_3_.refs_5_.refs_8_) | copy-start | bytes 294916
  22.4 0.6 copy-start.16
  24.7 7.5 %collective-permute-start.5 = (bf16[8,64,128]{2,1,0:T(8,128)(2,1)}, bf16[8,64,128]{2,1,0:T(8,128)(2,1)S(1)}, u32[]{:S(2)}, u32[]{:S(2)}) collective-permute-start(bf16[8,64,128]{2,1,0:T(8,128)(2,1)} %corner.1), channel_id=1, source_target_pairs={{8,0},{16,8},{24,16},{32,24},{40,32},{48,40},{56,48},{64,56},{72,6... | collective-permute-start | bytes 393224 | tf_op jit(solution)/shard_map/ppermute | solution.py:638
  26.0 6.3 %collective-permute-start.4 = (bf16[8,64,128]{2,1,0:T(8,128)(2,1)}, bf16[8,64,128]{2,1,0:T(8,128)(2,1)S(1)}, u32[]{:S(2)}, u32[]{:S(2)}) collective-permute-start(bf16[8,64,128]{2,1,0:T(8,128)(2,1)} %corner.1), channel_id=1, source_target_pairs={{0,8},{8,16},{16,24},{24,32},{32,40},{40,48},{48,56},{56,64},{64,7... | collective-permute-start | bytes 393224 | tf_op jit(solution)/shard_map/ppermute | solution.py:633
  32.3 0.6 copy-start.24
  32.3 0.7 copy-start.25
  32.3 0.9 copy-start.22
  32.3 1.0 copy-start.23
  39.3 26.3 %all-to-all-start = ((f32[128,4,128]{2,1,0:T(4,128)}), f32[128,4,128]{2,1,0:T(4,128)S(1)}, u32[]{:S(2)}, u32[]{:S(2)}) async-start(f32[128,4,128]{2,1,0:T(4,128)} %get-tuple-element.38), calls=%async_computation | async-start | bytes 524288 | tf_op jit(solution)/shard_map/all_to_all | solution.py:642
  65.5 0.7 copy-start.14
  72.8 14.2 %all-to-all-start.1 = ((f32[128,1,128]{2,1,0:T(1,128)}), f32[128,1,128]{2,1,0:T(1,128)S(1)}, u32[]{:S(2)}, u32[]{:S(2)}) async-start(f32[128,1,128]{2,1,0:T(1,128)} %bitcast.59), calls=%async_computation.1 | async-start | bytes 131072 | tf_op jit(solution)/shard_map/all_to_all | solution.py:642
  77.7 33.5 %collective-permute-start.6 = (bf16[72,32,128]{2,1,0:T(8,128)(2,1)}, bf16[72,32,128]{2,1,0:T(8,128)(2,1)S(1)}, u32[]{:S(2)}, u32[]{:S(2)}) collective-permute-start(bf16[72,32,128]{2,1,0:T(8,128)(2,1)} %get-tuple-element.51), channel_id=1, source_target_pairs={{0,8},{8,16},{16,24},{24,32},{32,40},{40,48},{48,56},{56,64},{64,7... | collective-permute-start | bytes 1769480 | tf_op jit(solution)/shard_map/ppermute | solution.py:633
  81.1 30.2 %collective-permute-start.7 = (bf16[72,32,128]{2,1,0:T(8,128)(2,1)}, bf16[72,32,128]{2,1,0:T(8,128)(2,1)S(1)}, u32[]{:S(2)}, u32[]{:S(2)}) collective-permute-start(bf16[72,32,128]{2,1,0:T(8,128)(2,1)} %get-tuple-element.52), channel_id=1, source_target_pairs={{8,0},{16,8},{24,16},{32,24},{40,32},{48,40},{56,48},{64,56},{72,6... | collective-permute-start | bytes 1769480 | tf_op jit(solution)/shard_map/ppermute | solution.py:638
  87.0 0.6 copy-start.17
  111.2 0.9 copy-start.9
  111.2 1.1 copy-start.10
  122.3 9.4 %copy-start.13 = (bf16[32,64,128]{2,1,0:T(8,128)(2,1)S(1)}, bf16[32,64,128]{2,1,0:T(8,128)(2,1)}, u32[]{:S(2)}) copy-start(bf16[32,64,128]{2,1,0:T(8,128)(2,1)} %get-tuple-element.48) | copy-start | bytes 1572868
  122.3 19.3 %copy-start.1 = (f32[32,4]{1,0:T(8,128)S(1)}, f32[32,4]{1,0:T(8,128)}, u32[]{:S(2)}) copy-start(f32[32,4]{1,0:T(8,128)} %copy.30.refs_2_.refs_3_) | copy-start | bytes 1540
  122.3 19.3 %copy-start.2 = (f32[32,128]{1,0:T(8,128)S(1)}, f32[32,128]{1,0:T(8,128)}, u32[]{:S(2)}) copy-start(f32[32,128]{1,0:T(8,128)} %get-tuple-element.46.refs_1_.refs_5_.refs_11_.refs_2_) | copy-start | bytes 49156
  122.3 19.3 %copy-start.3 = (s32[8]{0:T(128)S(1)}, s32[8]{0:T(128)}, u32[]{:S(2)}) copy-start(s32[8]{0:T(128)} %stack.66.refs_0_) | copy-start | bytes 100
  122.4 19.3 %copy-start.6 = (f32[4,128]{1,0:T(4,128)S(1)}, f32[4,128]{1,0:T(4,128)}, u32[]{:S(2)}) copy-start(f32[4,128]{1,0:T(4,128)} %get-tuple-element.56.refs_4_) | copy-start | bytes 6148
  122.4 19.3 %copy-start.8 = (f32[4,128]{1,0:T(4,128)S(1)}, f32[4,128]{1,0:T(4,128)}, u32[]{:S(2)}) copy-start(f32[4,128]{1,0:T(4,128)} %total.1.refs_8_.refs_5_) | copy-start | bytes 6148
  122.4 19.3 %all-to-all-start.3 = ((f32[128,8,128]{2,1,0:T(8,128)}), f32[128,8,128]{2,1,0:T(8,128)S(1)}, u32[]{:S(2)}, u32[]{:S(2)}) async-start(f32[128,8,128]{2,1,0:T(8,128)} %get-tuple-element.55), calls=%async_computation.3 | async-start | bytes 1048576 | tf_op jit(solution)/shard_map/all_to_all | solution.py:642
  127.0 12.7 %collective-permute-start.8 = (bf16[34,32,128]{2,1,0:T(8,128)(2,1)}, bf16[34,32,128]{2,1,0:T(8,128)(2,1)S(1)}, u32[]{:S(2)}, u32[]{:S(2)}) collective-permute-start(bf16[34,32,128]{2,1,0:T(8,128)(2,1)} %get-tuple-element.57), channel_id=1, source_target_pairs={{0,8},{8,16},{16,24},{24,32},{32,40},{40,48},{48,56},{56,64},{64,7... | collective-permute-start | bytes 835592 | tf_op jit(solution)/shard_map/ppermute | solution.py:633
  130.4 11.2 %collective-permute-start.9 = (bf16[34,32,128]{2,1,0:T(8,128)(2,1)}, bf16[34,32,128]{2,1,0:T(8,128)(2,1)S(1)}, u32[]{:S(2)}, u32[]{:S(2)}) collective-permute-start(bf16[34,32,128]{2,1,0:T(8,128)(2,1)} %get-tuple-element.58), channel_id=1, source_target_pairs={{8,0},{16,8},{24,16},{32,24},{40,32},{48,40},{56,48},{64,56},{72,6... | collective-permute-start | bytes 835592 | tf_op jit(solution)/shard_map/ppermute | solution.py:638
  132.1 11.5 %copy-start = (bf16[32,2,32,128]{3,0,1,2:T(8,128)(2,1)}, bf16[32,2,32,128]{3,0,1,2:T(8,128)(2,1)S(1)}, u32[]{:S(2)}) copy-start(bf16[32,2,32,128]{3,0,1,2:T(8,128)(2,1)S(1)} %copy.41) | copy-start | bytes 1572868
  139.7 3.8 %copy-start.4 = (bf16[34,32,128]{2,1,0:T(8,128)(2,1)}, bf16[34,32,128]{2,1,0:T(8,128)(2,1)S(1)}, u32[]{:S(2)}) copy-start(bf16[34,32,128]{2,1,0:T(8,128)(2,1)S(1)} %collective-permute-done.8.refs_6_) | copy-start | bytes 835588
  141.6 2.0 %copy-start.5 = (bf16[34,32,128]{2,1,0:T(8,128)(2,1)}, bf16[34,32,128]{2,1,0:T(8,128)(2,1)S(1)}, u32[]{:S(2)}) copy-start(bf16[34,32,128]{2,1,0:T(8,128)(2,1)S(1)} %collective-permute-done.9.refs_7_) | copy-start | bytes 835588
  143.6 0.6 copy-start.7
  144.2 21.5 %all-to-all-start.4 = ((bf16[128,8,128]{2,1,0:T(8,128)(2,1)}), bf16[128,8,128]{2,1,0:T(8,128)(2,1)S(1)}, u32[]{:S(2)}, u32[]{:S(2)}) async-start(bf16[128,8,128]{2,1,0:T(8,128)(2,1)} %bitcast.29), calls=%async_computation.4 | async-start | bytes 524288 | tf_op jit(solution)/shard_map/all_to_all | solution.py:642

commit v8 on v7

--- a/solution.py
+++ b/solution.py
@@ -41,13 +41,13 @@
     return lambda y: jnp.concatenate([rows(y + k) for k in range(3) for rows in refs], axis=0)
 
 
-def joined(margin, middle, below, above, first):
+def joined(k, middle, below, above):
     def row(y):
-        if y < margin:
-            return below[y]
-        if y < margin + ROWS:
-            return middle[y - margin]
-        return above[first + y - margin - ROWS]
+        if y < 4:
+            return below[3 * y + k]
+        if y < 4 + ROWS:
+            return middle[y - 4]
+        return above[3 * (y - 4 - ROWS) + k]
 
     return row
 
@@ -221,18 +221,14 @@
     g_ref[128:192, at] = from_below(values, lane).astype(BF16)
 
 
-def pack_kernel(need, send, own, cot, up_ref, down_ref):
-    need(own, cot)
-    up_ref[0:4] = own[ROWS - 4 : ROWS]
-    up_ref[4:6] = cot[ROWS - 2 : ROWS]
-    down_ref[0:4] = own[0:4]
-    down_ref[4:6] = cot[0:2]
-
-
-def corner_kernel(need, send, y_low, y_high, rows):
-    need(y_low, y_high)
-    rows[0:4] = y_low[0:4]
-    rows[4:8] = y_high[0:4]
+def pack_kernel(need, send, x_low, x_high, own, cot, up_ref, down_ref):
+    need(x_low, x_high, own, cot)
+    for y in range(4):
+        for k, part in enumerate((x_low, own, x_high)):
+            up_ref[3 * y + k] = part[ROWS - 4 + y]
+            down_ref[3 * y + k] = part[y]
+    up_ref[12:14] = cot[ROWS - 2 : ROWS]
+    down_ref[12:14] = cot[0:2]
 
 
 def weights_kernel(need, send, k1, k2, w1, w2):
@@ -281,12 +277,12 @@
 
 
 def first_kernel(
-    need, send, own, x_low, x_high, y_low, y_high, c_low, c_high, w, v, h, msg, x1, center_out
+    need, send, y_low, y_high, w, own, x_low, x_high, v, h, msg, x1, center_out
 ):
-    need(own, x_low, x_high, y_low, y_high, c_low, c_high, w)
-    low = joined(4, x_low, c_low, c_low, 4)
-    high = joined(4, x_high, c_high, c_high, 4)
-    own = joined(4, own, y_low, y_high, 0)
+    need(own, x_low, x_high, y_low, y_high, w)
+    low = joined(0, x_low, y_low, y_high)
+    own = joined(1, own, y_low, y_high)
+    high = joined(2, x_high, y_low, y_high)
     acc = [jnp.zeros((64, 128), F32), jnp.zeros((64, 128), F32)]
     for k, pair in enumerate(((low, own), (own, high))):
 
@@ -318,7 +314,7 @@
 def second_kernel(
     cells, need, send, place, r1, gb, h1, cot, y_low, y_high, w, v, h, low, high, msg, st1
 ):
-    need(gb)
+    need(r1, gb)
     mean, inverse, _, _ = stats_of(r1[:, 0, :], place, cells, st1)
     send(st1)
     mean4, scale4 = fourfold(mean), fourfold(inverse * gb[:, 0:1])
@@ -378,14 +374,14 @@
 
 def cot_row(cot, y_low, y_high, y):
     if y < 2:
-        return y_low[4 + y]
+        return y_low[12 + y]
     if y < 2 + ROWS:
         return cot[y - 2]
-    return y_high[2 + y - ROWS]
+    return y_high[10 + y - ROWS]
 
 
 def third_kernel(cells, need, send, place, r2, gb, cot, h2, st1, x1, xh, out, msg, st2):
-    need(gb)
+    need(r2, gb)
     mean, inverse, _, _ = stats_of(r2[...], place, cells, st2)
     mean2, inverse2 = twice(mean), twice(inverse)
     gain2, bias2 = twice(gb[:, 2:3]), twice(gb[:, 3:4])
@@ -416,7 +412,7 @@
 def fourth_kernel(
     cells, need, send, place, r3, st2, gb, h2, x_low, x_high, cot, y_low, y_high, w, st1, h1, v2, v1, slope1, low, high, msg, t3, v, g, acc, acc1,
 ):
-    need(st2, gb)
+    need(r3, st2, gb)
     mean, inverse, o_low, o_high = kept_stats(st2)
     t3[...] = jnp.sum(r3[...], axis=0)
     send(t3)
@@ -639,7 +635,18 @@
 
 
 def share(msg):
-    return lax.all_to_all(msg, ALL, 0, 0, tiled=True)
+    return lax.all_to_all(msg, ALL[::-1], 0, 0, tiled=True)
+
+
+def rank_of(gx, gy):
+    rank = gy % lax.axis_size(GY[1])
+    for part, axis in (
+        (gy // lax.axis_size(GY[1]), GY[0]),
+        (gx % lax.axis_size(GX[1]), GX[1]),
+        (gx // lax.axis_size(GX[1]), GX[0]),
+    ):
+        rank = rank * lax.axis_size(axis) + part
+    return rank
 
 
 def local(features, kernel_one, gain_one, bias_one, kernel_two, gain_two, bias_two, cotangent):
@@ -647,10 +654,10 @@
     count = count_x * count_y
     cells = float(count * 2 * ROWS * 128)
     gx, gy = lax.axis_index(GX), lax.axis_index(GY)
-    at = gx * count_y + gy
-    place = jnp.stack(
-        [at - count_y, at + count_y, gx > 0, gx < count_x - 1, gy > 0, gy < count_y - 1, at % C, at]
-    ).astype(jnp.int32)
+    at = rank_of(gx, gy)
+    beside = [rank_of(jnp.clip(gx + k, 0, count_x - 1), gy) for k in (-1, 1)]
+    edges = [gx > 0, gx < count_x - 1, gy > 0, gy < count_y - 1]
+    place = jnp.stack([*beside, *edges, at % C, at]).astype(jnp.int32)
     gb = jnp.stack([gain_one, bias_one, gain_two, bias_two], axis=1)
 
     own = jnp.transpose(features, (2, 1, 0, 3)).reshape(ROWS, 64, 128)
@@ -664,23 +671,25 @@
     corr = (pltpu.VMEM((192, ROWS * 128), BF16), pltpu.VMEM((192, 384), F32))
 
     x_low, x_high = up(own, GX), down(own, GX)
-    y_up, y_down = call(
-        pack_kernel, (own, cot), [sh((6, 64, 128), BF16)] * 2, "pack", smem_first=False
-    )
-    y_low, y_high = up(y_up, GY), down(y_down, GY)
-    (corner,) = call(
-        corner_kernel, (y_low, y_high), [sh((8, 64, 128), BF16)], "corner", smem_first=False
-    )
-    c_low, c_high = up(corner, GX), down(corner, GX)
     taps = [
         jnp.transpose(k, (2, 3, 4, 0, 1)).reshape(27, C, C) for k in (kernel_one, kernel_two)
     ]
     matrices = [sh((192, 384), BF16)] * 2
     w1, w2 = call(weights_kernel, taps, matrices, "weights", smem_first=False)
+    b1, b2 = call(flipped_kernel, taps, matrices, "flipped", smem_first=False)
+    y_up, y_down = call(
+        pack_kernel,
+        (x_low, x_high, own, cot),
+        [sh((14, 64, 128), BF16)] * 2,
+        "pack",
+        smem_first=False,
+        after=(w1, b1),
+    )
+    y_low, y_high = up(y_up, GY), down(y_down, GY)
 
     v1, h1, m1, x1_own, center = call(
         first_kernel,
-        (own, x_low, x_high, y_low, y_high, c_low, c_high, w1),
+        (y_low, y_high, w1, own, x_low, x_high),
         [sh((40, 128, 128), BF16), sh((38, 128, 128), F32), four, sh((16, 128), F32), stats],
         "conv_one",
         smem_first=False,
@@ -697,7 +706,6 @@
         cut=(h1,),
     )
 
-    b1, b2 = call(flipped_kernel, taps, matrices, "flipped", smem_first=False, after=(center,))
     v2, h2, low, high, m2, st1 = call(
         lambda *refs: second_kernel(cells, *refs),
         (place, r1, gb, h1, cot, y_low, y_high, w2),
@@ -705,8 +713,7 @@
             sh((38, 128, 128), BF16), sh((36, 64, 128), F32), *rims(72), msg, stats,
         ],
         "conv_two",
-        near=1,
-        after=(xh, b1),
+        after=(xh,),
     )
     h2_low, h2_high = up(high, GX), down(low, GX)
     r2 = share(m2)
@@ -718,7 +725,6 @@
         (place, r2, gb, cot, h2, st1, x1_own, xh),
         [sh((ROWS, 64, 128), BF16), four, stats],
         "slope_two",
-        near=1,
         after=(x1,),
     )
     r3 = share(m3)
@@ -736,7 +742,6 @@
         ),
         [sh((34, 64, 128), F32), *rims(34), wide, sh((4, 128), F32)],
         "back_two",
-        near=1,
         late=5,
         cut=(h1,),
         scratch=(pltpu.VMEM((36, 128, 128), BF16), *corr, corr[1]),

time: 168 us -> 166 us (0.988)
  starting transfers between devices: 63 us -> 54.6 us
  waiting for transfers between devices: 23.6 us -> 31.8 us
  Pallas kernels: 48.8 us -> 47 us
    ppermute x5 -> x4, waiting for transfers between devices: 4.72 us -> 9.77 us  [down(): return lax.ppermute(values, axes, [(i + 1, i) for i in range(count - 1)])]
    all_to_all x4, starting transfers between devices: 35.5 us -> 31.7 us  [share(): return lax.all_to_all(msg, ALL[::-1], 0, 0, tiled=True)]
    ppermute x5 -> x4, starting transfers between devices: 20.2 us -> 17 us  [up(): return lax.ppermute(values, axes, [(i, i + 1) for i in range(count - 1)])]
    ppermute x5 -> x4, waiting for transfers between devices: 7.69 us -> 9.68 us  [up(): return lax.ppermute(values, axes, [(i, i + 1) for i in range(count - 1)])]
    pallas_call x13 -> x12, Pallas kernels: 48.8 us -> 47 us  [call(): pl.pallas_call(body, out_shape=outs, in_specs=[SM] * lead + [pl.BlockSpec...]
    ppermute x5 -> x4, starting transfers between devices: 7.27 us -> 5.98 us  [down(): return lax.ppermute(values, axes, [(i + 1, i) for i in range(count - 1)])]
    unnamed x52 -> x48, local copies, waits for them, and re-layouts: 4.69 us -> 4.55 us
  transfers between devices with their start and end apart: 14 -> 12, of which waited for: 6 -> 9; matrix products, arithmetic and copies ran while one was open for 3% -> 3% of each run, Pallas kernels for 14% -> 12%
where the time goes in v8:
time: 166 us; the launch traced here: 165 us
  starting transfers between devices  54.6 us (33%)
  Pallas kernels  47 us (28%)
  waiting for transfers between devices  31.8 us (19%)
  blocking collectives  19.1 us (12%)
  local copies, waits for them, and re-layouts  11 us (7%)
    pallas_call x12, Pallas kernels, call(): pl.pallas_call(body, out_shape=outs, in_specs=[SM] * lead + [pl.BlockSpec...  47 us
    all_to_all x4, starting transfers between devices, share(): return lax.all_to_all(msg, ALL[::-1], 0, 0, tiled=True)  31.7 us
    all_to_all x1, blocking collectives, share(): return lax.all_to_all(msg, ALL[::-1], 0, 0, tiled=True)  19.1 us
    ppermute x4, starting transfers between devices, up(): return lax.ppermute(values, axes, [(i, i + 1) for i in range(count - 1)])  17 us
    all_to_all x4, waiting for transfers between devices, share(): return lax.all_to_all(msg, ALL[::-1], 0, 0, tiled=True)  12.4 us
    ppermute x4, waiting for transfers between devices, down(): return lax.ppermute(values, axes, [(i + 1, i) for i in range(count - 1)])  9.77 us
    ppermute x4, waiting for transfers between devices, up(): return lax.ppermute(values, axes, [(i, i + 1) for i in range(count - 1)])  9.68 us
    ppermute x4, starting transfers between devices, down(): return lax.ppermute(values, axes, [(i + 1, i) for i in range(count - 1)])  5.98 us
  transfers between devices with their start and end apart: 12, of which 9 were waited for; matrix products, arithmetic and copies ran while one was open for 3% of the time, Pallas kernels for 12%

profile of v8, /device:TPU:1, one launch (start us, length us, event | category | flops | bytes accessed | tf_op | source)
XLA Modules:
  0.0 165.0 jit_solution(9270523485220005146)
XLA Ops:
  0.6 0.0 copy-start.11
  0.6 1.4 copy.28
  2.1 1.3 collective-permute-start.1
  3.4 4.7 %collective-permute-start = (bf16[32,64,128]{2,1,0:T(8,128)(2,1)S(1)}, bf16[32,64,128]{2,1,0:T(8,128)(2,1)S(1)}, u32[]{:S(2)}, u32[]{:S(2)}) collective-permute-start(bf16[32,64,128]{2,1,0:T(8,128)(2,1)S(1)} %bitcast.52), channel_id=1, source_target_pairs={{0,8},{8,16},{16,24},{24,32},{32,40},{40,48},{48,56},{56,64},{64,7... | collective-permute-start | bytes 1572872 | tf_op jit(solution)/shard_map/ppermute | solution.py:629
  8.1 1.1 copy.29
  9.2 2.3 %flipped.1 = (bf16[192,384]{1,0:T(8,128)(2,1)}, bf16[192,384]{1,0:T(8,128)(2,1)}) custom-call(bf16[27,32,32]{2,1,0:T(8,128)(2,1)} %bitcast.64, bf16[27,32,32]{2,1,0:T(8,128)(2,1)} %bitcast.66), custom_call_target="tpu_custom_call" | custom-call | flops 2000000000 | bytes 6000000 | tf_op jit(solution)/shard_map/flipped/pallas_call | solution.py:605
  11.6 2.2 %weights.1 = (bf16[192,384]{1,0:T(8,128)(2,1)}, bf16[192,384]{1,0:T(8,128)(2,1)}) custom-call(bf16[27,32,32]{2,1,0:T(8,128)(2,1)} %bitcast.65, bf16[27,32,32]{2,1,0:T(8,128)(2,1)} %bitcast.67), custom_call_target="tpu_custom_call" | custom-call | flops 2000000000 | bytes 6000000 | tf_op jit(solution)/shard_map/weights/pallas_call | solution.py:605
  13.8 3.6 %collective-permute-done.1.refs_1_.refs_5_ = bf16[32,64,128]{2,1,0:T(8,128)(2,1)S(1)} collective-permute-done((bf16[32,64,128]{2,1,0:T(8,128)(2,1)S(1)}, bf16[32,64,128]{2,1,0:T(8,128)(2,1)S(1)}, u32[]{:S(2)}, u32[]{:S(2)}) %collective-permute-start.1) | collective-permute-done | bytes 524320 | tf_op jit(solution)/shard_map/ppermute | solution.py:634
  17.4 0.9 collective-permute-done.refs_0_.refs_4_
  18.2 0.0 copy-done.22
  18.2 0.8 copy-done.23
  19.0 2.6 %pack.1 = (bf16[14,64,128]{2,1,0:T(8,128)(2,1)}, bf16[14,64,128]{2,1,0:T(8,128)(2,1)}) custom-call(bf16[32,64,128]{2,1,0:T(8,128)(2,1)} %copy-done.23, bf16[32,64,128]{2,1,0:T(8,128)(2,1)} %copy-done.22, bf16[32,64,128]{2,1,0:T(8,128)(2,1)} %bitcast.53, bf16[32,64,128]{2,1,0:T(8,128)(2,1)} %bitcast.45, bf16[192,384]{1,0:T(8,128)(2,1)} %get-tuple-element.35.refs_4_.refs_2_, ...), custom_call_target="tpu_custom_call" | custom-call | flops 2000000000 | bytes 6000000 | tf_op jit(solution)/shard_map/pack/pallas_call | solution.py:605
  21.6 5.5 %collective-permute-start.2 = (bf16[14,64,128]{2,1,0:T(8,128)(2,1)}, bf16[14,64,128]{2,1,0:T(8,128)(2,1)S(1)}, u32[]{:S(2)}, u32[]{:S(2)}) collective-permute-start(bf16[14,64,128]{2,1,0:T(8,128)(2,1)} %get-tuple-element.37), channel_id=1, source_target_pairs={{0,1},{1,2},{2,3},{3,4},{4,5},{5,6},{6,7},{8,9},{9,10},{10,11},{11... | collective-permute-start | bytes 688136 | tf_op jit(solution)/shard_map/ppermute | solution.py:629
  27.2 1.9 %collective-permute-start.3 = (bf16[14,64,128]{2,1,0:T(8,128)(2,1)}, bf16[14,64,128]{2,1,0:T(8,128)(2,1)S(1)}, u32[]{:S(2)}, u32[]{:S(2)}) collective-permute-start(bf16[14,64,128]{2,1,0:T(8,128)(2,1)} %get-tuple-element.38), channel_id=1, source_target_pairs={{1,0},{2,1},{3,2},{4,3},{5,4},{6,5},{7,6},{9,8},{10,9},{11,10},{12... | collective-permute-start | bytes 688136 | tf_op jit(solution)/shard_map/ppermute | solution.py:634
  29.2 0.0 copy-start.18
  29.2 0.0 copy-start.19
  29.2 0.0 copy-start.20
  29.2 0.0 copy-start.21
  29.2 1.2 collective-permute-done.2.refs_0_.refs_5_.refs_8_
  30.4 4.3 %collective-permute-done.3.refs_1_.refs_6_.refs_9_ = bf16[14,64,128]{2,1,0:T(8,128)(2,1)S(1)} collective-permute-done((bf16[14,64,128]{2,1,0:T(8,128)(2,1)}, bf16[14,64,128]{2,1,0:T(8,128)(2,1)S(1)}, u32[]{:S(2)}, u32[]{:S(2)}) %collective-permute-start.3) | collective-permute-done | bytes 229408 | tf_op jit(solution)/shard_map/ppermute | solution.py:634
  34.7 0.7 copy-done.16
  35.4 5.9 %conv_one.1 = (bf16[40,128,128]{2,1,0:T(8,128)(2,1)}, f32[38,128,128]{2,1,0:T(8,128)}, f32[128,4,128]{2,1,0:T(4,128)}, f32[16,128]{1,0:T(8,128)}, f32[32,128]{1,0:T(8,128)}) custom-call(bf16[14,64,128]{2,1,0:T(8,128)(2,1)} %copy-done.15, bf16[14,64,128]{2,1,0:T(8,128)(2,1)} %copy-done.16, bf16[192,384]{1,0:T(8,128)(2,1)} %get-tuple-element.35.refs_4_.refs_2_, ...), custom_call_target="tpu_custom_call" | custom-call | flops 2000000000 | bytes 6000000 | tf_op jit(solution)/shard_map/conv_one/pallas_call | solution.py:605
  41.3 12.6 %all-to-all-start = ((f32[128,4,128]{2,1,0:T(4,128)}), f32[128,4,128]{2,1,0:T(4,128)S(1)}, u32[]{:S(2)}, u32[]{:S(2)}) async-start(f32[128,4,128]{2,1,0:T(4,128)} %get-tuple-element.39), calls=%async_computation | async-start | bytes 524288 | tf_op jit(solution)/shard_map/all_to_all | solution.py:638
  53.9 0.0 copy-done.18
  53.9 0.0 copy-done.19
  53.9 0.0 copy-done.20
  53.9 0.0 copy-done.21
  53.9 0.7 copy.30.refs_2_.refs_3_
  54.6 0.6 stack.66.refs_0_
  55.3 3.7 %hidden_features.1.refs_8_.refs_7_ = f32[9,32,128]{2,1,0:T(8,128)} custom-call(f32[32,128]{1,0:T(8,128)} %get-tuple-element.42.refs_0_, f32[38,128,128]{2,1,0:T(8,128)} %get-tuple-element.40.refs_1_.refs_3_.refs_12_.refs_4_, bf16[40,128,128]{2,1,0:T(8,128)(2,1)} %get-tuple-element.43.refs_2_.refs_14_), custom_call_target="tpu_custom_call" | custom-call | flops 2000000000 | bytes 6000000 | tf_op jit(solution)/shard_map/hidden_features/pallas_call | solution.py:605
  59.0 5.8 %all-to-all-done.refs_1_.refs_0_ = f32[128,4,128]{2,1,0:T(4,128)S(1)} async-done(((f32[128,4,128]{2,1,0:T(4,128)}), f32[128,4,128]{2,1,0:T(4,128)S(1)}, u32[]{:S(2)}, u32[]{:S(2)}) %all-to-all-start) | async-done | bytes 262176 | tf_op jit(solution)/shard_map/all_to_all | solution.py:638
  64.8 0.7 copy-done.14
  65.5 6.4 %conv_two.1 = (bf16[38,128,128]{2,1,0:T(8,128)(2,1)}, f32[36,64,128]{2,1,0:T(8,128)}, bf16[72,32,128]{2,1,0:T(8,128)(2,1)}, bf16[72,32,128]{2,1,0:T(8,128)(2,1)}, f32[128,128]{1,0:T(8,128)}, /*index=5*/f32[32,128]{1,0:T(8,128)}) custom-call(s32[8]{0:T(128)} %stack.66.refs_0_, f32[128,4,128]{2,1,0:T(4,128)} %copy-done.14, f32[32,4]{1,0:T(8,128)} %copy.30.refs_2_.refs_3_, ...), custom_call_target="tpu_custom_call" | custom-call | flops 2000000000 | bytes 6000000 | tf_op jit(solution)/shard_map/conv_two/pallas_call | solution.py:605
  71.9 4.1 %all-to-all-start.1 = ((f32[128,1,128]{2,1,0:T(1,128)}), f32[128,1,128]{2,1,0:T(1,128)S(1)}, u32[]{:S(2)}, u32[]{:S(2)}) async-start(f32[128,1,128]{2,1,0:T(1,128)} %bitcast.59), calls=%async_computation.1 | async-start | bytes 131072 | tf_op jit(solution)/shard_map/all_to_all | solution.py:638
  76.1 3.4 %collective-permute-start.4 = (bf16[72,32,128]{2,1,0:T(8,128)(2,1)}, bf16[72,32,128]{2,1,0:T(8,128)(2,1)S(1)}, u32[]{:S(2)}, u32[]{:S(2)}) collective-permute-start(bf16[72,32,128]{2,1,0:T(8,128)(2,1)} %get-tuple-element.51), channel_id=1, source_target_pairs={{0,8},{8,16},{16,24},{24,32},{32,40},{40,48},{48,56},{56,64},{64,7... | collective-permute-start | bytes 1769480 | tf_op jit(solution)/shard_map/ppermute | solution.py:629
  79.5 1.5 collective-permute-start.5
  80.9 1.7 %total.1.refs_8_.refs_5_ = f32[4,128]{1,0:T(4,128)} custom-call(f32[128,4,128]{2,1,0:T(4,128)} %copy-done.14, f32[32,128]{1,0:T(8,128)} %get-tuple-element.46.refs_1_.refs_5_.refs_11_.refs_2_), custom_call_target="tpu_custom_call" | custom-call | flops 2000000000 | bytes 6000000 | tf_op jit(solution)/shard_map/total/pallas_call | solution.py:605
  82.7 3.0 %all-to-all-done.1 = f32[128,1,128]{2,1,0:T(1,128)S(1)} async-done(((f32[128,1,128]{2,1,0:T(1,128)}), f32[128,1,128]{2,1,0:T(1,128)S(1)}, u32[]{:S(2)}, u32[]{:S(2)}) %all-to-all-start.1) | async-done | bytes 65568 | tf_op jit(solution)/shard_map/all_to_all | solution.py:638
  85.6 0.6 copy-done.17
  86.3 4.2 %slope_two.1 = (bf16[32,64,128]{2,1,0:T(8,128)(2,1)}, f32[128,4,128]{2,1,0:T(4,128)}, f32[32,128]{1,0:T(8,128)}) custom-call(s32[8]{0:T(128)} %stack.66.refs_0_, f32[128,128]{1,0:T(8,128)} %bitcast.58, f32[32,4]{1,0:T(8,128)} %copy.30.refs_2_.refs_3_, bf16[32,64,128]{2,1,0:T(8,128)(2,1)} %bitcast.47, f32[36,64,128]{2,1,0:T(8,128)} %get-tuple-element.45.refs_4_, ...), custom_call_target="tpu_custom_call" | custom-call | flops 2000000000 | bytes 6000000 | tf_op jit(solution)/shard_map/slope_two/pallas_call | solution.py:605
  90.4 19.1 %all_to_all.31.refs_1_ = f32[128,4,128]{2,1,0:T(4,128)} all-to-all(f32[128,4,128]{2,1,0:T(4,128)} %get-tuple-element.49), channel_id=1, replica_groups=mesh['gx_0'=4,'gx_1'=4,'gy_0'=4,'gy_1'=2] {'gy_1','gy_0','gx_1','gx_0'}, dimensions={0} | all-to-all | bytes 524288 | tf_op jit(solution)/shard_map/all_to_all | solution.py:638
  109.6 0.0 collective-permute-done.4.refs_5_
  109.6 0.0 collective-permute-done.5.refs_6_
  109.6 0.8 copy-done.9
  110.5 0.2 copy-done.10
  110.7 9.8 %back_two.1 = (f32[34,64,128]{2,1,0:T(8,128)}, bf16[34,32,128]{2,1,0:T(8,128)(2,1)}, bf16[34,32,128]{2,1,0:T(8,128)(2,1)}, f32[128,8,128]{2,1,0:T(8,128)}, f32[4,128]{1,0:T(4,128)}) custom-call(s32[8]{0:T(128)} %stack.66.refs_0_, f32[128,4,128]{2,1,0:T(4,128)} %all_to_all.31.refs_1_, f32[32,128]{1,0:T(8,128)} %get-tuple-element.50.refs_2_, ...), custom_call_target="tpu_custom_call" | custom-call | flops 2000000000 | bytes 6000000 | tf_op jit(solution)/shard_map/back_two/pallas_call | solution.py:605
  120.5 0.0 copy-start.13
  120.6 0.0 copy-start.8
  120.6 4.3 %all-to-all-start.3 = ((f32[128,8,128]{2,1,0:T(8,128)}), f32[128,8,128]{2,1,0:T(8,128)S(1)}, u32[]{:S(2)}, u32[]{:S(2)}) async-start(f32[128,8,128]{2,1,0:T(8,128)} %get-tuple-element.55), calls=%async_computation.3 | async-start | bytes 1048576 | tf_op jit(solution)/shard_map/all_to_all | solution.py:638
  124.9 3.4 %collective-permute-start.6 = (bf16[34,32,128]{2,1,0:T(8,128)(2,1)}, bf16[34,32,128]{2,1,0:T(8,128)(2,1)S(1)}, u32[]{:S(2)}, u32[]{:S(2)}) collective-permute-start(bf16[34,32,128]{2,1,0:T(8,128)(2,1)} %get-tuple-element.57), channel_id=1, source_target_pairs={{0,8},{8,16},{16,24},{24,32},{32,40},{40,48},{48,56},{56,64},{64,7... | collective-permute-start | bytes 835592 | tf_op jit(solution)/shard_map/ppermute | solution.py:629
  128.3 1.3 collective-permute-start.7
  129.6 0.3 copy.41
  129.9 0.0 copy-start
  129.9 7.6 %collective-permute-done.6.refs_6_ = bf16[34,32,128]{2,1,0:T(8,128)(2,1)S(1)} collective-permute-done((bf16[34,32,128]{2,1,0:T(8,128)(2,1)}, bf16[34,32,128]{2,1,0:T(8,128)(2,1)S(1)}, u32[]{:S(2)}, u32[]{:S(2)}) %collective-permute-start.6) | collective-permute-done | bytes 278560 | tf_op jit(solution)/shard_map/ppermute | solution.py:629
  137.6 1.9 %collective-permute-done.7.refs_7_ = bf16[34,32,128]{2,1,0:T(8,128)(2,1)S(1)} collective-permute-done((bf16[34,32,128]{2,1,0:T(8,128)(2,1)}, bf16[34,32,128]{2,1,0:T(8,128)(2,1)S(1)}, u32[]{:S(2)}, u32[]{:S(2)}) %collective-permute-start.7) | collective-permute-done | bytes 278560 | tf_op jit(solution)/shard_map/ppermute | solution.py:634
  139.5 0.0 all-to-all-done.3.refs_1_
  139.5 1.9 %own_rows.1 = (bf16[1024,128]{1,0:T(8,128)(2,1)}, f32[4,32]{1,0:T(4,128)}, f32[8,128]{1,0:T(8,128)S(1)}) custom-call(s32[8]{0:T(128)S(1)} %copy-done.3, f32[128,8,128]{2,1,0:T(8,128)S(1)} %all-to-all-done.3.refs_1_, f32[32,128]{1,0:T(8,128)S(1)} %copy-done.2, f32[32,4]{1,0:T(8,128)S(1)} %copy-done.1, f32[4,128]{1,0:T(4,128)S(1)} %copy-done.6, ...), custom_call_target="tpu_custom_call" | custom-call | flops 2000000000 | bytes 6000000 | tf_op jit(solution)/shard_map/own_rows/pallas_call | solution.py:605
  141.4 0.0 copy-start.7
  141.4 0.6 copy-done.7
  142.0 10.6 %all-to-all-start.4 = ((bf16[128,8,128]{2,1,0:T(8,128)(2,1)}), bf16[128,8,128]{2,1,0:T(8,128)(2,1)S(1)}, u32[]{:S(2)}, u32[]{:S(2)}) async-start(bf16[128,8,128]{2,1,0:T(8,128)(2,1)} %bitcast.29), calls=%async_computation.4 | async-start | bytes 524288 | tf_op jit(solution)/shard_map/all_to_all | solution.py:638
  152.7 5.1 %back_one.1 = bf16[32,64,128]{2,1,0:T(8,128)(2,1)} custom-call(s32[8]{0:T(128)} %stack.66.refs_0_, f32[8,128]{1,0:T(8,128)} %copy-done.7, f32[32,128]{1,0:T(8,128)} %get-tuple-element.46.refs_1_.refs_5_.refs_11_.refs_2_, f32[32,4]{1,0:T(8,128)} %copy.30.refs_2_.refs_3_, f32[38,128,128]{2,1,0:T(8,128)} %get-tuple-element.40.refs_1_.refs_3_.refs_12_.refs_4_, ...), custom_call_target="tpu_custom_call" | custom-call | flops 2000000000 | bytes 6000000 | tf_op jit(solution)/shard_map/back_one/pallas_call | solution.py:605
  157.7 2.2 %copy.40 = bf16[32,2,32,128]{3,0,1,2:T(8,128)(2,1)} copy(bf16[32,2,32,128]{3,2,1,0:T(8,128)(2,1)} %bitcast.57) | data formatting | bytes 1048576 | tf_op jit(solution)/shard_map/reshape | solution.py:733
  159.9 3.6 %all-to-all-done.4 = bf16[128,8,128]{2,1,0:T(8,128)(2,1)S(1)} async-done(((bf16[128,8,128]{2,1,0:T(8,128)(2,1)}), bf16[128,8,128]{2,1,0:T(8,128)(2,1)S(1)}, u32[]{:S(2)}, u32[]{:S(2)}) %all-to-all-start.4) | async-done | bytes 262176 | tf_op jit(solution)/shard_map/all_to_all | solution.py:638
  163.6 1.2 finish.1
  (28 shorter events, 0.1 us)
Async XLA Ops:
  0.6 7.5 %copy-start.11 = (bf16[32,2,32,128]{3,2,1,0:T(8,128)(2,1)S(1)}, bf16[32,2,32,128]{3,2,1,0:T(8,128)(2,1)}, u32[]{:S(2)}) copy-start(bf16[32,2,32,128]{3,2,1,0:T(8,128)(2,1)} %param.15) | copy-start | bytes 1572868
  2.1 9.5 %copy-start.12 = (bf16[32,2,32,128]{3,2,1,0:T(8,128)(2,1)}, bf16[32,2,32,128]{3,2,1,0:T(8,128)(2,1)S(1)}, u32[]{:S(2)}) copy-start(bf16[32,2,32,128]{3,2,1,0:T(8,128)(2,1)S(1)} %copy.28) | copy-start | bytes 1572868
  2.1 15.3 %collective-permute-start.1 = (bf16[32,64,128]{2,1,0:T(8,128)(2,1)S(1)}, bf16[32,64,128]{2,1,0:T(8,128)(2,1)S(1)}, u32[]{:S(2)}, u32[]{:S(2)}) collective-permute-start(bf16[32,64,128]{2,1,0:T(8,128)(2,1)S(1)} %bitcast.51), channel_id=1, source_target_pairs={{8,0},{16,8},{24,16},{32,24},{40,32},{48,40},{56,48},{64,56},{72,6... | collective-permute-start | bytes 1572872 | tf_op jit(solution)/shard_map/ppermute | solution.py:634
  3.4 14.8 %collective-permute-start = (bf16[32,64,128]{2,1,0:T(8,128)(2,1)S(1)}, bf16[32,64,128]{2,1,0:T(8,128)(2,1)S(1)}, u32[]{:S(2)}, u32[]{:S(2)}) collective-permute-start(bf16[32,64,128]{2,1,0:T(8,128)(2,1)S(1)} %bitcast.52), channel_id=1, source_target_pairs={{0,8},{8,16},{16,24},{24,32},{32,40},{40,48},{48,56},{56,64},{64,7... | collective-permute-start | bytes 1572872 | tf_op jit(solution)/shard_map/ppermute | solution.py:629
  17.4 0.9 copy-start.22
  18.2 0.8 copy-start.23
  21.6 8.8 %collective-permute-start.2 = (bf16[14,64,128]{2,1,0:T(8,128)(2,1)}, bf16[14,64,128]{2,1,0:T(8,128)(2,1)S(1)}, u32[]{:S(2)}, u32[]{:S(2)}) collective-permute-start(bf16[14,64,128]{2,1,0:T(8,128)(2,1)} %get-tuple-element.37), channel_id=1, source_target_pairs={{0,1},{1,2},{2,3},{3,4},{4,5},{5,6},{6,7},{8,9},{9,10},{10,11},{11... | collective-permute-start | bytes 688136 | tf_op jit(solution)/shard_map/ppermute | solution.py:629
  27.2 7.5 %collective-permute-start.3 = (bf16[14,64,128]{2,1,0:T(8,128)(2,1)}, bf16[14,64,128]{2,1,0:T(8,128)(2,1)S(1)}, u32[]{:S(2)}, u32[]{:S(2)}) collective-permute-start(bf16[14,64,128]{2,1,0:T(8,128)(2,1)} %get-tuple-element.38), channel_id=1, source_target_pairs={{1,0},{2,1},{3,2},{4,3},{5,4},{6,5},{7,6},{9,8},{10,9},{11,10},{12... | collective-permute-start | bytes 688136 | tf_op jit(solution)/shard_map/ppermute | solution.py:634
  29.2 24.7 %copy-start.18 = (f32[32]{0:T(128)S(1)}, f32[32]{0:T(128)}, u32[]{:S(2)}) copy-start(f32[32]{0:T(128)} %param.14) | copy-start | bytes 388
  29.2 24.7 %copy-start.19 = (f32[32]{0:T(128)S(1)}, f32[32]{0:T(128)}, u32[]{:S(2)}) copy-start(f32[32]{0:T(128)} %param.13) | copy-start | bytes 388
  29.2 24.7 %copy-start.20 = (f32[32]{0:T(128)S(1)}, f32[32]{0:T(128)}, u32[]{:S(2)}) copy-start(f32[32]{0:T(128)} %param.11) | copy-start | bytes 388
  29.2 24.7 %copy-start.21 = (f32[32]{0:T(128)S(1)}, f32[32]{0:T(128)}, u32[]{:S(2)}) copy-start(f32[32]{0:T(128)} %param.10) | copy-start | bytes 388
  30.4 4.3 %copy-start.15 = (bf16[14,64,128]{2,1,0:T(8,128)(2,1)}, bf16[14,64,128]{2,1,0:T(8,128)(2,1)S(1)}, u32[]{:S(2)}) copy-start(bf16[14,64,128]{2,1,0:T(8,128)(2,1)S(1)} %collective-permute-done.2.refs_0_.refs_5_.refs_8_) | copy-start | bytes 688132
  34.7 0.7 copy-start.16
  41.3 23.5 %all-to-all-start = ((f32[128,4,128]{2,1,0:T(4,128)}), f32[128,4,128]{2,1,0:T(4,128)S(1)}, u32[]{:S(2)}, u32[]{:S(2)}) async-start(f32[128,4,128]{2,1,0:T(4,128)} %get-tuple-element.39), calls=%async_computation | async-start | bytes 524288 | tf_op jit(solution)/shard_map/all_to_all | solution.py:638
  64.8 0.7 copy-start.14
  71.9 13.7 %all-to-all-start.1 = ((f32[128,1,128]{2,1,0:T(1,128)}), f32[128,1,128]{2,1,0:T(1,128)S(1)}, u32[]{:S(2)}, u32[]{:S(2)}) async-start(f32[128,1,128]{2,1,0:T(1,128)} %bitcast.59), calls=%async_computation.1 | async-start | bytes 131072 | tf_op jit(solution)/shard_map/all_to_all | solution.py:638
  76.1 33.5 %collective-permute-start.4 = (bf16[72,32,128]{2,1,0:T(8,128)(2,1)}, bf16[72,32,128]{2,1,0:T(8,128)(2,1)S(1)}, u32[]{:S(2)}, u32[]{:S(2)}) collective-permute-start(bf16[72,32,128]{2,1,0:T(8,128)(2,1)} %get-tuple-element.51), channel_id=1, source_target_pairs={{0,8},{8,16},{16,24},{24,32},{32,40},{40,48},{48,56},{56,64},{64,7... | collective-permute-start | bytes 1769480 | tf_op jit(solution)/shard_map/ppermute | solution.py:629
  79.5 30.1 %collective-permute-start.5 = (bf16[72,32,128]{2,1,0:T(8,128)(2,1)}, bf16[72,32,128]{2,1,0:T(8,128)(2,1)S(1)}, u32[]{:S(2)}, u32[]{:S(2)}) collective-permute-start(bf16[72,32,128]{2,1,0:T(8,128)(2,1)} %get-tuple-element.52), channel_id=1, source_target_pairs={{8,0},{16,8},{24,16},{32,24},{40,32},{48,40},{56,48},{64,56},{72,6... | collective-permute-start | bytes 1769480 | tf_op jit(solution)/shard_map/ppermute | solution.py:634
  85.6 0.6 copy-start.17
  109.6 0.9 copy-start.9
  109.6 1.1 copy-start.10
  120.5 9.0 %copy-start.13 = (bf16[32,64,128]{2,1,0:T(8,128)(2,1)S(1)}, bf16[32,64,128]{2,1,0:T(8,128)(2,1)}, u32[]{:S(2)}) copy-start(bf16[32,64,128]{2,1,0:T(8,128)(2,1)} %get-tuple-element.48) | copy-start | bytes 1572868
  120.5 18.9 %copy-start.1 = (f32[32,4]{1,0:T(8,128)S(1)}, f32[32,4]{1,0:T(8,128)}, u32[]{:S(2)}) copy-start(f32[32,4]{1,0:T(8,128)} %copy.30.refs_2_.refs_3_) | copy-start | bytes 1540
  120.6 18.9 %copy-start.2 = (f32[32,128]{1,0:T(8,128)S(1)}, f32[32,128]{1,0:T(8,128)}, u32[]{:S(2)}) copy-start(f32[32,128]{1,0:T(8,128)} %get-tuple-element.46.refs_1_.refs_5_.refs_11_.refs_2_) | copy-start | bytes 49156
  120.6 18.9 %copy-start.3 = (s32[8]{0:T(128)S(1)}, s32[8]{0:T(128)}, u32[]{:S(2)}) copy-start(s32[8]{0:T(128)} %stack.66.refs_0_) | copy-start | bytes 100
  120.6 18.9 %copy-start.6 = (f32[4,128]{1,0:T(4,128)S(1)}, f32[4,128]{1,0:T(4,128)}, u32[]{:S(2)}) copy-start(f32[4,128]{1,0:T(4,128)} %get-tuple-element.56.refs_4_) | copy-start | bytes 6148
  120.6 18.9 %copy-start.8 = (f32[4,128]{1,0:T(4,128)S(1)}, f32[4,128]{1,0:T(4,128)}, u32[]{:S(2)}) copy-start(f32[4,128]{1,0:T(4,128)} %total.1.refs_8_.refs_5_) | copy-start | bytes 6148
  120.6 18.9 %all-to-all-start.3 = ((f32[128,8,128]{2,1,0:T(8,128)}), f32[128,8,128]{2,1,0:T(8,128)S(1)}, u32[]{:S(2)}, u32[]{:S(2)}) async-start(f32[128,8,128]{2,1,0:T(8,128)} %get-tuple-element.55), calls=%async_computation.3 | async-start | bytes 1048576 | tf_op jit(solution)/shard_map/all_to_all | solution.py:638
  124.9 12.7 %collective-permute-start.6 = (bf16[34,32,128]{2,1,0:T(8,128)(2,1)}, bf16[34,32,128]{2,1,0:T(8,128)(2,1)S(1)}, u32[]{:S(2)}, u32[]{:S(2)}) collective-permute-start(bf16[34,32,128]{2,1,0:T(8,128)(2,1)} %get-tuple-element.57), channel_id=1, source_target_pairs={{0,8},{8,16},{16,24},{24,32},{32,40},{40,48},{48,56},{56,64},{64,7... | collective-permute-start | bytes 835592 | tf_op jit(solution)/shard_map/ppermute | solution.py:629
  128.3 11.2 %collective-permute-start.7 = (bf16[34,32,128]{2,1,0:T(8,128)(2,1)}, bf16[34,32,128]{2,1,0:T(8,128)(2,1)S(1)}, u32[]{:S(2)}, u32[]{:S(2)}) collective-permute-start(bf16[34,32,128]{2,1,0:T(8,128)(2,1)} %get-tuple-element.58), channel_id=1, source_target_pairs={{8,0},{16,8},{24,16},{32,24},{40,32},{48,40},{56,48},{64,56},{72,6... | collective-permute-start | bytes 835592 | tf_op jit(solution)/shard_map/ppermute | solution.py:634
  129.9 11.5 %copy-start = (bf16[32,2,32,128]{3,0,1,2:T(8,128)(2,1)}, bf16[32,2,32,128]{3,0,1,2:T(8,128)(2,1)S(1)}, u32[]{:S(2)}) copy-start(bf16[32,2,32,128]{3,0,1,2:T(8,128)(2,1)S(1)} %copy.41) | copy-start | bytes 1572868
  137.6 3.8 %copy-start.4 = (bf16[34,32,128]{2,1,0:T(8,128)(2,1)}, bf16[34,32,128]{2,1,0:T(8,128)(2,1)S(1)}, u32[]{:S(2)}) copy-start(bf16[34,32,128]{2,1,0:T(8,128)(2,1)S(1)} %collective-permute-done.6.refs_6_) | copy-start | bytes 835588
  139.5 1.9 %copy-start.5 = (bf16[34,32,128]{2,1,0:T(8,128)(2,1)}, bf16[34,32,128]{2,1,0:T(8,128)(2,1)S(1)}, u32[]{:S(2)}) copy-start(bf16[34,32,128]{2,1,0:T(8,128)(2,1)S(1)} %collective-permute-done.7.refs_7_) | copy-start | bytes 835588
  141.4 0.6 copy-start.7
  142.0 21.6 %all-to-all-start.4 = ((bf16[128,8,128]{2,1,0:T(8,128)(2,1)}), bf16[128,8,128]{2,1,0:T(8,128)(2,1)S(1)}, u32[]{:S(2)}, u32[]{:S(2)}) async-start(bf16[128,8,128]{2,1,0:T(8,128)(2,1)} %bitcast.29), calls=%async_computation.4 | async-start | bytes 524288 | tf_op jit(solution)/shard_map/all_to_all | solution.py:638

commit v9 on v8

--- a/solution.py
+++ b/solution.py
@@ -193,12 +193,14 @@
 def weight_sums(g_ref, v_ref, first, acc_ref):
     step = 4
     for y in range(0, ROWS, step):
-        right = jnp.concatenate(
+        window = jnp.concatenate(
             [v_ref[first + y + k : first + y + k + 3].reshape(384, 128) for k in range(step)], axis=1
         )
-        left = g_ref[:, y * 128 : (y + step) * 128]
         product = lax.dot_general(
-            left, right, (((1,), (1,)), ((), ())), preferred_element_type=F32
+            window,
+            g_ref[:, y * 128 : (y + step) * 128],
+            (((1,), (1,)), ((), ())),
+            preferred_element_type=F32,
         )
         if y == 0:
             acc_ref[...] = product
@@ -207,8 +209,10 @@
 
 
 def folded(acc_ref):
+    turned = [jnp.transpose(acc_ref[dy * 128 : dy * 128 + 128]) for dy in range(3)]
+
     def tile(dz, dy):
-        both = acc_ref[dz * 64 : dz * 64 + 64, dy * 128 : dy * 128 + 128]
+        both = turned[dy][dz * 64 : dz * 64 + 64]
         return both[0:C] + pltpu.roll(both[C:], 96, 1)
 
     return tile
@@ -222,7 +226,7 @@
 
 
 def pack_kernel(need, send, x_low, x_high, own, cot, up_ref, down_ref):
-    need(x_low, x_high, own, cot)
+    need(own, cot)
     for y in range(4):
         for k, part in enumerate((x_low, own, x_high)):
             up_ref[3 * y + k] = part[ROWS - 4 + y]
@@ -380,7 +384,7 @@
     return y_high[10 + y - ROWS]
 
 
-def third_kernel(cells, need, send, place, r2, gb, cot, h2, st1, x1, xh, out, msg, st2):
+def third_kernel(cells, need, send, place, r2, gb, cot, h2, st1, x1, xh, msg, st2):
     need(r2, gb)
     mean, inverse, _, _ = stats_of(r2[...], place, cells, st2)
     mean2, inverse2 = twice(mean), twice(inverse)
@@ -392,12 +396,9 @@
         need(cot, row=y)
         normed = (h2[y + 2] - mean2) * inverse2
         z = normed * gain2 + bias2
-        out[y] = act(z).astype(BF16)
-        send(out, row=y)
         slope = cot[y].astype(F32) * act_slope(z)
         plain = plain + slope
         both = both + slope * normed
-    send(out)
     need(st1, x1, xh)
     inverse1, own1 = st1[:, 1:2], st1[:, 4:5]
     ones = ones_of(x1)
@@ -407,6 +408,17 @@
 
 
     rows_message((fold(total(both)), fold(total(plain))), (xn,), msg)
+
+
+def output_kernel(need, send, st2, gb, h2, out):
+    need(st2, gb)
+    mean, inverse, _, _ = kept_stats(st2)
+    mean2, scale2 = twice(mean), twice(inverse * gb[:, 2:3])
+    shift2 = twice(gb[:, 3:4])
+    for y in range(ROWS):
+        need(h2, row=y + 2)
+        out[y] = act((h2[y + 2] - mean2) * scale2 + shift2).astype(BF16)
+        send(out, row=y)
 
 
 def fourth_kernel(
@@ -668,7 +680,7 @@
 
     msg, four, wide = (sh((count, *tile), F32) for tile in ((128,), (4, 128), (8, 128)))
     stats = sh((C, 128), F32)
-    corr = (pltpu.VMEM((192, ROWS * 128), BF16), pltpu.VMEM((192, 384), F32))
+    corr = (pltpu.VMEM((192, ROWS * 128), BF16), pltpu.VMEM((384, 192), F32))
 
     x_low, x_high = up(own, GX), down(own, GX)
     taps = [
@@ -684,6 +696,8 @@
         "pack",
         smem_first=False,
         after=(w1, b1),
+        near=2,
+        grant=16,
     )
     y_low, y_high = up(y_up, GY), down(y_down, GY)
 
@@ -720,19 +734,19 @@
     (x1,) = call(
         total_kernel, (r1,), [sh((4, 128), F32)], "total", smem_first=False, after=(st1,)
     )
-    output, m3, st2 = call(
+    m3, st2 = call(
         lambda *refs: third_kernel(cells, *refs),
         (place, r2, gb, cot, h2, st1, x1_own, xh),
-        [sh((ROWS, 64, 128), BF16), four, stats],
+        [four, stats],
         "slope_two",
         after=(x1,),
     )
     r3 = share(m3)
-
-    def back(rows):
-        return jnp.transpose(rows.reshape(ROWS, 2, C, 128), (2, 1, 0, 3))
-
-    output = back(output)
+    (output,) = call(
+        output_kernel, (st2, gb, h2), [sh((ROWS, 64, 128), BF16)], "output", smem_first=False
+    )
+
+    rows_out = output
 
     slope1, low, high, m4, t3 = call(
         lambda *refs: fourth_kernel(cells, *refs),
@@ -742,12 +756,18 @@
         ),
         [sh((34, 64, 128), F32), *rims(34), wide, sh((4, 128), F32)],
         "back_two",
+        after=(rows_out,),
         late=5,
         cut=(h1,),
         scratch=(pltpu.VMEM((36, 128, 128), BF16), *corr, corr[1]),
     )
     s_low, s_high = up(high, GX), down(low, GX)
     r4 = share(m4)
+
+    def back(rows):
+        return jnp.transpose(rows.reshape(ROWS, 2, C, 128), (2, 1, 0, 3))
+
+    output = back(rows_out)
 
     m5, norm_grads, t4 = call(
         lambda *refs: owner_kernel(cells, *refs),

time: 166 us -> 165 us (level)
  blocking collectives: 19.1 us -> 0 us
  waiting for transfers between devices: 31.8 us -> 43.7 us
  starting transfers between devices: 54.6 us -> 59.7 us
    all_to_all x1 -> x0, blocking collectives: 19.1 us -> none  [share(): return lax.all_to_all(msg, ALL[::-1], 0, 0, tiled=True)]
    all_to_all x4 -> x5, waiting for transfers between devices: 12.4 us -> 21 us  [share(): return lax.all_to_all(msg, ALL[::-1], 0, 0, tiled=True)]
    all_to_all x4 -> x5, starting transfers between devices: 31.7 us -> 37.8 us  [share(): return lax.all_to_all(msg, ALL[::-1], 0, 0, tiled=True)]
    ppermute x4, waiting for transfers between devices: 9.68 us -> 12.6 us  [up(): return lax.ppermute(values, axes, [(i, i + 1) for i in range(count - 1)])]
    pallas_call x12 -> x13, Pallas kernels: 47 us -> 48.6 us  [call(): pl.pallas_call(body, out_shape=outs, in_specs=[SM] * lead + [pl.BlockSpec...]
    unnamed x48 -> x56, local copies, waits for them, and re-layouts: 4.55 us -> 4.96 us
  transfers between devices with their start and end apart: 12 -> 13, of which waited for: 9 -> 10; matrix products, arithmetic and copies ran while one was open for 3% -> 3% of each run, Pallas kernels for 12% -> 13%
where the time goes in v9:
time: 165 us; the launch traced here: 164 us
  starting transfers between devices  59.7 us (36%)
  Pallas kernels  48.6 us (29%)
  waiting for transfers between devices  43.7 us (26%)
  local copies, waits for them, and re-layouts  10.6 us (6%)
    pallas_call x13, Pallas kernels, call(): pl.pallas_call(body, out_shape=outs, in_specs=[SM] * lead + [pl.BlockSpec...  48.6 us
    all_to_all x5, starting transfers between devices, share(): return lax.all_to_all(msg, ALL[::-1], 0, 0, tiled=True)  37.8 us
    all_to_all x5, waiting for transfers between devices, share(): return lax.all_to_all(msg, ALL[::-1], 0, 0, tiled=True)  21 us
    ppermute x4, starting transfers between devices, up(): return lax.ppermute(values, axes, [(i, i + 1) for i in range(count - 1)])  16.1 us
    ppermute x4, waiting for transfers between devices, up(): return lax.ppermute(values, axes, [(i, i + 1) for i in range(count - 1)])  12.6 us
    ppermute x4, waiting for transfers between devices, down(): return lax.ppermute(values, axes, [(i + 1, i) for i in range(count - 1)])  10.1 us
    ppermute x4, starting transfers between devices, down(): return lax.ppermute(values, axes, [(i + 1, i) for i in range(count - 1)])  5.8 us
    unnamed x56, local copies, waits for them, and re-layouts  4.96 us
  transfers between devices with their start and end apart: 13, of which 10 were waited for; matrix products, arithmetic and copies ran while one was open for 3% of the time, Pallas kernels for 13%

profile of v9, /device:TPU:1, one launch (start us, length us, event | category | flops | bytes accessed | tf_op | source)
XLA Modules:
  0.0 164.0 jit_solution(1190984822183387087)
XLA Ops:
  0.6 1.4 copy.28
  2.1 0.0 copy-start.1
  2.1 4.1 %collective-permute-start = (bf16[32,64,128]{2,1,0:T(8,128)(2,1)S(1)}, bf16[32,64,128]{2,1,0:T(8,128)(2,1)S(1)}, u32[]{:S(2)}, u32[]{:S(2)}) collective-permute-start(bf16[32,64,128]{2,1,0:T(8,128)(2,1)S(1)} %bitcast.46), channel_id=1, source_target_pairs={{0,8},{8,16},{16,24},{24,32},{32,40},{40,48},{48,56},{56,64},{64,7... | collective-permute-start | bytes 1572872 | tf_op jit(solution)/shard_map/ppermute | solution.py:641
  6.2 1.3 collective-permute-start.1
  7.5 0.3 copy.29
  7.8 2.4 %weights.1 = (bf16[192,384]{1,0:T(8,128)(2,1)}, bf16[192,384]{1,0:T(8,128)(2,1)}) custom-call(bf16[27,32,32]{2,1,0:T(8,128)(2,1)} %bitcast.64, bf16[27,32,32]{2,1,0:T(8,128)(2,1)} %bitcast.66), custom_call_target="tpu_custom_call" | custom-call | flops 2000000000 | bytes 6000000 | tf_op jit(solution)/shard_map/weights/pallas_call | solution.py:617
  10.2 0.0 copy-start.12
  10.3 2.4 %flipped.1 = (bf16[192,384]{1,0:T(8,128)(2,1)}, bf16[192,384]{1,0:T(8,128)(2,1)}) custom-call(bf16[27,32,32]{2,1,0:T(8,128)(2,1)} %bitcast.65, bf16[27,32,32]{2,1,0:T(8,128)(2,1)} %bitcast.67), custom_call_target="tpu_custom_call" | custom-call | flops 2000000000 | bytes 6000000 | tf_op jit(solution)/shard_map/flipped/pallas_call | solution.py:617
  12.6 4.1 %collective-permute-done.refs_0_.refs_4_ = bf16[32,64,128]{2,1,0:T(8,128)(2,1)S(1)} collective-permute-done((bf16[32,64,128]{2,1,0:T(8,128)(2,1)S(1)}, bf16[32,64,128]{2,1,0:T(8,128)(2,1)S(1)}, u32[]{:S(2)}, u32[]{:S(2)}) %collective-permute-start) | collective-permute-done | bytes 524320 | tf_op jit(solution)/shard_map/ppermute | solution.py:641
  16.7 3.8 %collective-permute-done.1.refs_1_.refs_5_ = bf16[32,64,128]{2,1,0:T(8,128)(2,1)S(1)} collective-permute-done((bf16[32,64,128]{2,1,0:T(8,128)(2,1)S(1)}, bf16[32,64,128]{2,1,0:T(8,128)(2,1)S(1)}, u32[]{:S(2)}, u32[]{:S(2)}) %collective-permute-start.1) | collective-permute-done | bytes 524320 | tf_op jit(solution)/shard_map/ppermute | solution.py:646
  20.5 0.0 copy-done
  20.6 1.1 copy-done.11
  21.6 2.1 %pack.1 = (bf16[14,64,128]{2,1,0:T(8,128)(2,1)S(1)}, bf16[14,64,128]{2,1,0:T(8,128)(2,1)S(1)}) custom-call(bf16[32,64,128]{2,1,0:T(8,128)(2,1)S(1)} %collective-permute-done.refs_0_.refs_4_, bf16[32,64,128]{2,1,0:T(8,128)(2,1)S(1)} %collective-permute-done.1.refs_1_.refs_5_, bf16[32,64,128]{2,1,0:T(8,128)(2,1)S(1)} %bitcast.48, ...), custom_call_target="tpu_custom_call" | custom-call | flops 2000000000 | bytes 6000000 | tf_op jit(solution)/shard_map/pack/pallas_call | solution.py:617
  23.7 5.3 %collective-permute-start.2 = (bf16[14,64,128]{2,1,0:T(8,128)(2,1)S(1)}, bf16[14,64,128]{2,1,0:T(8,128)(2,1)S(1)}, u32[]{:S(2)}, u32[]{:S(2)}) collective-permute-start(bf16[14,64,128]{2,1,0:T(8,128)(2,1)S(1)} %get-tuple-element.36), channel_id=1, source_target_pairs={{0,1},{1,2},{2,3},{3,4},{4,5},{5,6},{6,7},{8,9},{9,10},{10,11},{11... | collective-permute-start | bytes 688136 | tf_op jit(solution)/shard_map/ppermute | solution.py:641
  29.0 1.9 %collective-permute-start.3 = (bf16[14,64,128]{2,1,0:T(8,128)(2,1)S(1)}, bf16[14,64,128]{2,1,0:T(8,128)(2,1)S(1)}, u32[]{:S(2)}, u32[]{:S(2)}) collective-permute-start(bf16[14,64,128]{2,1,0:T(8,128)(2,1)S(1)} %get-tuple-element.37), channel_id=1, source_target_pairs={{1,0},{2,1},{3,2},{4,3},{5,4},{6,5},{7,6},{9,8},{10,9},{11,10},{12... | collective-permute-start | bytes 688136 | tf_op jit(solution)/shard_map/ppermute | solution.py:646
  31.1 0.0 copy-start.24
  31.1 0.0 copy-start.25
  31.1 0.0 copy-start.26
  31.1 0.0 copy-start.27
  31.1 0.9 collective-permute-done.2.refs_0_.refs_5_.refs_8_
  32.0 4.4 %collective-permute-done.3.refs_1_.refs_6_.refs_9_ = bf16[14,64,128]{2,1,0:T(8,128)(2,1)S(1)} collective-permute-done((bf16[14,64,128]{2,1,0:T(8,128)(2,1)S(1)}, bf16[14,64,128]{2,1,0:T(8,128)(2,1)S(1)}, u32[]{:S(2)}, u32[]{:S(2)}) %collective-permute-start.3) | collective-permute-done | bytes 229408 | tf_op jit(solution)/shard_map/ppermute | solution.py:646
  36.4 0.7 copy-done.22
  37.1 5.9 %conv_one.1 = (bf16[40,128,128]{2,1,0:T(8,128)(2,1)}, f32[38,128,128]{2,1,0:T(8,128)}, f32[128,4,128]{2,1,0:T(4,128)}, f32[16,128]{1,0:T(8,128)}, f32[32,128]{1,0:T(8,128)}) custom-call(bf16[14,64,128]{2,1,0:T(8,128)(2,1)} %copy-done.21, bf16[14,64,128]{2,1,0:T(8,128)(2,1)} %copy-done.22, bf16[192,384]{1,0:T(8,128)(2,1)} %get-tuple-element.34.refs_4_.refs_2_, ...), custom_call_target="tpu_custom_call" | custom-call | flops 2000000000 | bytes 6000000 | tf_op jit(solution)/shard_map/conv_one/pallas_call | solution.py:617
  43.0 10.8 %all-to-all-start = ((f32[128,4,128]{2,1,0:T(4,128)}), f32[128,4,128]{2,1,0:T(4,128)S(1)}, u32[]{:S(2)}, u32[]{:S(2)}) async-start(f32[128,4,128]{2,1,0:T(4,128)} %get-tuple-element.38), calls=%async_computation | async-start | bytes 524288 | tf_op jit(solution)/shard_map/all_to_all | solution.py:650
  53.9 0.7 copy.30.refs_2_.refs_1_.refs_3_
  54.5 0.7 stack.66.refs_0_
  55.2 3.8 %hidden_features.1.refs_8_.refs_7_ = f32[9,32,128]{2,1,0:T(8,128)} custom-call(f32[32,128]{1,0:T(8,128)} %get-tuple-element.41.refs_0_, f32[38,128,128]{2,1,0:T(8,128)} %get-tuple-element.39.refs_1_.refs_3_.refs_12_.refs_4_, bf16[40,128,128]{2,1,0:T(8,128)(2,1)} %get-tuple-element.42.refs_2_.refs_14_), custom_call_target="tpu_custom_call" | custom-call | flops 2000000000 | bytes 6000000 | tf_op jit(solution)/shard_map/hidden_features/pallas_call | solution.py:617
  59.1 5.7 %all-to-all-done.refs_1_.refs_0_ = f32[128,4,128]{2,1,0:T(4,128)S(1)} async-done(((f32[128,4,128]{2,1,0:T(4,128)}), f32[128,4,128]{2,1,0:T(4,128)S(1)}, u32[]{:S(2)}, u32[]{:S(2)}) %all-to-all-start) | async-done | bytes 262176 | tf_op jit(solution)/shard_map/all_to_all | solution.py:650
  64.7 0.7 copy-done.20
  65.4 6.4 %conv_two.1 = (bf16[38,128,128]{2,1,0:T(8,128)(2,1)}, f32[36,64,128]{2,1,0:T(8,128)}, bf16[72,32,128]{2,1,0:T(8,128)(2,1)}, bf16[72,32,128]{2,1,0:T(8,128)(2,1)}, f32[128,128]{1,0:T(8,128)}, /*index=5*/f32[32,128]{1,0:T(8,128)}) custom-call(s32[8]{0:T(128)} %stack.66.refs_0_, f32[128,4,128]{2,1,0:T(4,128)} %copy-done.20, ...), custom_call_target="tpu_custom_call" | custom-call | flops 2000000000 | bytes 6000000 | tf_op jit(solution)/shard_map/conv_two/pallas_call | solution.py:617
  71.8 4.1 %all-to-all-start.1 = ((f32[128,1,128]{2,1,0:T(1,128)}), f32[128,1,128]{2,1,0:T(1,128)S(1)}, u32[]{:S(2)}, u32[]{:S(2)}) async-start(f32[128,1,128]{2,1,0:T(1,128)} %bitcast.59), calls=%async_computation.1 | async-start | bytes 131072 | tf_op jit(solution)/shard_map/all_to_all | solution.py:650
  76.0 3.4 %collective-permute-start.4 = (bf16[72,32,128]{2,1,0:T(8,128)(2,1)}, bf16[72,32,128]{2,1,0:T(8,128)(2,1)S(1)}, u32[]{:S(2)}, u32[]{:S(2)}) collective-permute-start(bf16[72,32,128]{2,1,0:T(8,128)(2,1)} %get-tuple-element.49), channel_id=1, source_target_pairs={{0,8},{8,16},{16,24},{24,32},{32,40},{40,48},{48,56},{56,64},{64,7... | collective-permute-start | bytes 1769480 | tf_op jit(solution)/shard_map/ppermute | solution.py:641
  79.4 1.3 collective-permute-start.5
  80.7 1.7 %total.1.refs_8_.refs_5_ = f32[4,128]{1,0:T(4,128)} custom-call(f32[128,4,128]{2,1,0:T(4,128)} %copy-done.20, f32[32,128]{1,0:T(8,128)} %get-tuple-element.45.refs_1_.refs_5_.refs_11_.refs_2_), custom_call_target="tpu_custom_call" | custom-call | flops 2000000000 | bytes 6000000 | tf_op jit(solution)/shard_map/total/pallas_call | solution.py:617
  82.4 3.1 %all-to-all-done.1 = f32[128,1,128]{2,1,0:T(1,128)S(1)} async-done(((f32[128,1,128]{2,1,0:T(1,128)}), f32[128,1,128]{2,1,0:T(1,128)S(1)}, u32[]{:S(2)}, u32[]{:S(2)}) %all-to-all-start.1) | async-done | bytes 65568 | tf_op jit(solution)/shard_map/all_to_all | solution.py:650
  85.6 0.6 copy-done.23
  86.2 3.7 %slope_two.1 = (f32[128,4,128]{2,1,0:T(4,128)}, f32[32,128]{1,0:T(8,128)}) custom-call(s32[8]{0:T(128)} %stack.66.refs_0_, f32[128,128]{1,0:T(8,128)} %bitcast.58, f32[32,4]{1,0:T(8,128)} %copy.30.refs_2_.refs_1_.refs_3_, bf16[32,64,128]{2,1,0:T(8,128)(2,1)} %bitcast.44, f32[36,64,128]{2,1,0:T(8,128)} %get-tuple-element.44.refs_4_.refs_2_, ...), custom_call_target="tpu_custom_call" | custom-call | flops 2000000000 | bytes 6000000 | tf_op jit(solution)/shard_map/slope_two/pallas_call | solution.py:617
  89.9 7.9 %all-to-all-start.2 = ((f32[128,4,128]{2,1,0:T(4,128)}), f32[128,4,128]{2,1,0:T(4,128)S(1)}, u32[]{:S(2)}, u32[]{:S(2)}) async-start(f32[128,4,128]{2,1,0:T(4,128)} %get-tuple-element.48), calls=%async_computation.2 | async-start | bytes 524288 | tf_op jit(solution)/shard_map/all_to_all | solution.py:650
  97.9 2.4 %output.1.refs_15_ = bf16[32,64,128]{2,1,0:T(8,128)(2,1)} custom-call(f32[32,128]{1,0:T(8,128)} %get-tuple-element.47.refs_0_.refs_2_, f32[32,4]{1,0:T(8,128)} %copy.30.refs_2_.refs_1_.refs_3_, f32[36,64,128]{2,1,0:T(8,128)} %get-tuple-element.44.refs_4_.refs_2_), custom_call_target="tpu_custom_call" | custom-call | flops 2000000000 | bytes 6000000 | tf_op jit(solution)/shard_map/output/pallas_call | solution.py:617
  100.3 8.5 %all-to-all-done.2.refs_1_ = f32[128,4,128]{2,1,0:T(4,128)S(1)} async-done(((f32[128,4,128]{2,1,0:T(4,128)}), f32[128,4,128]{2,1,0:T(4,128)S(1)}, u32[]{:S(2)}, u32[]{:S(2)}) %all-to-all-start.2) | async-done | bytes 262176 | tf_op jit(solution)/shard_map/all_to_all | solution.py:650
  108.8 0.0 collective-permute-done.4.refs_5_
  108.8 0.0 collective-permute-done.5.refs_6_
  108.8 0.7 copy-done.16
  109.5 0.3 copy-done.17
  109.8 0.2 copy-done.18
  110.0 9.5 %back_two.1 = (f32[34,64,128]{2,1,0:T(8,128)}, bf16[34,32,128]{2,1,0:T(8,128)(2,1)}, bf16[34,32,128]{2,1,0:T(8,128)(2,1)}, f32[128,8,128]{2,1,0:T(8,128)}, f32[4,128]{1,0:T(4,128)}) custom-call(s32[8]{0:T(128)} %stack.66.refs_0_, f32[128,4,128]{2,1,0:T(4,128)} %copy-done.16, f32[32,128]{1,0:T(8,128)} %get-tuple-element.47.refs_0_.refs_2_, ...), custom_call_target="tpu_custom_call" | custom-call | flops 2000000000 | bytes 6000000 | tf_op jit(solution)/shard_map/back_two/pallas_call | solution.py:617
  119.5 0.0 copy-start.15
  119.6 0.0 copy-start.14
  119.6 4.3 %all-to-all-start.3 = ((f32[128,8,128]{2,1,0:T(8,128)}), f32[128,8,128]{2,1,0:T(8,128)S(1)}, u32[]{:S(2)}, u32[]{:S(2)}) async-start(f32[128,8,128]{2,1,0:T(8,128)} %get-tuple-element.53), calls=%async_computation.3 | async-start | bytes 1048576 | tf_op jit(solution)/shard_map/all_to_all | solution.py:650
  123.9 3.4 %collective-permute-start.6 = (bf16[34,32,128]{2,1,0:T(8,128)(2,1)}, bf16[34,32,128]{2,1,0:T(8,128)(2,1)S(1)}, u32[]{:S(2)}, u32[]{:S(2)}) collective-permute-start(bf16[34,32,128]{2,1,0:T(8,128)(2,1)} %get-tuple-element.55), channel_id=1, source_target_pairs={{0,8},{8,16},{16,24},{24,32},{32,40},{40,48},{48,56},{56,64},{64,7... | collective-permute-start | bytes 835592 | tf_op jit(solution)/shard_map/ppermute | solution.py:641
  127.3 1.3 collective-permute-start.7
  128.6 0.3 copy.42
  128.9 0.0 copy-start.2
  128.9 7.6 %collective-permute-done.6.refs_6_ = bf16[34,32,128]{2,1,0:T(8,128)(2,1)S(1)} collective-permute-done((bf16[34,32,128]{2,1,0:T(8,128)(2,1)}, bf16[34,32,128]{2,1,0:T(8,128)(2,1)S(1)}, u32[]{:S(2)}, u32[]{:S(2)}) %collective-permute-start.6) | collective-permute-done | bytes 278560 | tf_op jit(solution)/shard_map/ppermute | solution.py:641
  136.6 1.9 %collective-permute-done.7.refs_7_ = bf16[34,32,128]{2,1,0:T(8,128)(2,1)S(1)} collective-permute-done((bf16[34,32,128]{2,1,0:T(8,128)(2,1)}, bf16[34,32,128]{2,1,0:T(8,128)(2,1)S(1)}, u32[]{:S(2)}, u32[]{:S(2)}) %collective-permute-start.7) | collective-permute-done | bytes 278560 | tf_op jit(solution)/shard_map/ppermute | solution.py:646
  138.5 0.0 all-to-all-done.3.refs_1_
  138.5 1.9 %own_rows.1 = (bf16[1024,128]{1,0:T(8,128)(2,1)}, f32[4,32]{1,0:T(4,128)}, f32[8,128]{1,0:T(8,128)S(1)}) custom-call(s32[8]{0:T(128)S(1)} %copy-done.5, f32[128,8,128]{2,1,0:T(8,128)S(1)} %all-to-all-done.3.refs_1_, f32[32,128]{1,0:T(8,128)S(1)} %copy-done.4, f32[32,4]{1,0:T(8,128)S(1)} %copy-done.3, f32[4,128]{1,0:T(4,128)S(1)} %copy-done.10, ...), custom_call_target="tpu_custom_call" | custom-call | flops 2000000000 | bytes 6000000 | tf_op jit(solution)/shard_map/own_rows/pallas_call | solution.py:617
  140.5 0.0 copy-start.13
  140.5 0.6 copy-done.13
  141.1 10.6 %all-to-all-start.4 = ((bf16[128,8,128]{2,1,0:T(8,128)(2,1)}), bf16[128,8,128]{2,1,0:T(8,128)(2,1)S(1)}, u32[]{:S(2)}, u32[]{:S(2)}) async-start(bf16[128,8,128]{2,1,0:T(8,128)(2,1)} %bitcast.29), calls=%async_computation.4 | async-start | bytes 524288 | tf_op jit(solution)/shard_map/all_to_all | solution.py:650
  151.7 5.1 %back_one.1 = bf16[32,64,128]{2,1,0:T(8,128)(2,1)} custom-call(s32[8]{0:T(128)} %stack.66.refs_0_, f32[8,128]{1,0:T(8,128)} %copy-done.13, f32[32,128]{1,0:T(8,128)} %get-tuple-element.45.refs_1_.refs_5_.refs_11_.refs_2_, f32[32,4]{1,0:T(8,128)} %copy.30.refs_2_.refs_1_.refs_3_, f32[38,128,128]{2,1,0:T(8,128)} %get-tuple-element.39.refs_1_.refs_3_.refs_12_.refs_4_, ...), custom_call_target="tpu_custom_call" | custom-call | flops 2000000000 | bytes 6000000 | tf_op jit(solution)/shard_map/back_one/pallas_call | solution.py:617
  156.8 2.2 %copy.41 = bf16[32,2,32,128]{3,0,1,2:T(8,128)(2,1)} copy(bf16[32,2,32,128]{3,2,1,0:T(8,128)(2,1)} %bitcast.57) | data formatting | bytes 1048576 | tf_op jit(solution)/shard_map/reshape | solution.py:768
  159.0 3.7 %all-to-all-done.4 = bf16[128,8,128]{2,1,0:T(8,128)(2,1)S(1)} async-done(((bf16[128,8,128]{2,1,0:T(8,128)(2,1)}), bf16[128,8,128]{2,1,0:T(8,128)(2,1)S(1)}, u32[]{:S(2)}, u32[]{:S(2)}) %all-to-all-start.4) | async-done | bytes 262176 | tf_op jit(solution)/shard_map/all_to_all | solution.py:650
  162.6 1.2 finish.1
  (38 shorter events, 0.1 us)
Async XLA Ops:
  0.6 6.8 %copy-start.19 = (bf16[32,2,32,128]{3,2,1,0:T(8,128)(2,1)S(1)}, bf16[32,2,32,128]{3,2,1,0:T(8,128)(2,1)}, u32[]{:S(2)}) copy-start(bf16[32,2,32,128]{3,2,1,0:T(8,128)(2,1)} %param.15) | copy-start | bytes 1572868
  2.1 18.5 %copy-start.1 = (bf16[32,2,32,128]{3,2,1,0:T(8,128)(2,1)}, bf16[32,2,32,128]{3,2,1,0:T(8,128)(2,1)S(1)}, u32[]{:S(2)}) copy-start(bf16[32,2,32,128]{3,2,1,0:T(8,128)(2,1)S(1)} %copy.28) | copy-start | bytes 1572868
  2.1 14.6 %collective-permute-start = (bf16[32,64,128]{2,1,0:T(8,128)(2,1)S(1)}, bf16[32,64,128]{2,1,0:T(8,128)(2,1)S(1)}, u32[]{:S(2)}, u32[]{:S(2)}) collective-permute-start(bf16[32,64,128]{2,1,0:T(8,128)(2,1)S(1)} %bitcast.46), channel_id=1, source_target_pairs={{0,8},{8,16},{16,24},{24,32},{32,40},{40,48},{48,56},{56,64},{64,7... | collective-permute-start | bytes 1572872 | tf_op jit(solution)/shard_map/ppermute | solution.py:641
  6.2 14.4 %collective-permute-start.1 = (bf16[32,64,128]{2,1,0:T(8,128)(2,1)S(1)}, bf16[32,64,128]{2,1,0:T(8,128)(2,1)S(1)}, u32[]{:S(2)}, u32[]{:S(2)}) collective-permute-start(bf16[32,64,128]{2,1,0:T(8,128)(2,1)S(1)} %bitcast.47), channel_id=1, source_target_pairs={{8,0},{16,8},{24,16},{32,24},{40,32},{48,40},{56,48},{64,56},{72,6... | collective-permute-start | bytes 1572872 | tf_op jit(solution)/shard_map/ppermute | solution.py:646
  7.8 12.7 %copy-start = (bf16[32,2,32,128]{3,2,1,0:T(8,128)(2,1)}, bf16[32,2,32,128]{3,2,1,0:T(8,128)(2,1)S(1)}, u32[]{:S(2)}) copy-start(bf16[32,2,32,128]{3,2,1,0:T(8,128)(2,1)S(1)} %copy.29) | copy-start | bytes 1572868
  10.2 10.3 %copy-start.12 = (bf16[192,384]{1,0:T(8,128)(2,1)S(1)}, bf16[192,384]{1,0:T(8,128)(2,1)}, u32[]{:S(2)}) copy-start(bf16[192,384]{1,0:T(8,128)(2,1)} %get-tuple-element.34.refs_4_.refs_2_) | copy-start | bytes 442372
  16.7 7.0 %copy-start.6 = (bf16[32,64,128]{2,1,0:T(8,128)(2,1)}, bf16[32,64,128]{2,1,0:T(8,128)(2,1)S(1)}, u32[]{:S(2)}) copy-start(bf16[32,64,128]{2,1,0:T(8,128)(2,1)S(1)} %collective-permute-done.refs_0_.refs_4_) | copy-start | bytes 1572868
  20.5 3.2 %copy-start.7 = (bf16[32,64,128]{2,1,0:T(8,128)(2,1)}, bf16[32,64,128]{2,1,0:T(8,128)(2,1)S(1)}, u32[]{:S(2)}) copy-start(bf16[32,64,128]{2,1,0:T(8,128)(2,1)S(1)} %collective-permute-done.1.refs_1_.refs_5_) | copy-start | bytes 1572868
  20.5 1.1 copy-start.11
  23.7 8.2 %collective-permute-start.2 = (bf16[14,64,128]{2,1,0:T(8,128)(2,1)S(1)}, bf16[14,64,128]{2,1,0:T(8,128)(2,1)S(1)}, u32[]{:S(2)}, u32[]{:S(2)}) collective-permute-start(bf16[14,64,128]{2,1,0:T(8,128)(2,1)S(1)} %get-tuple-element.36), channel_id=1, source_target_pairs={{0,1},{1,2},{2,3},{3,4},{4,5},{5,6},{6,7},{8,9},{9,10},{10,11},{11... | collective-permute-start | bytes 688136 | tf_op jit(solution)/shard_map/ppermute | solution.py:641
  29.0 7.3 %collective-permute-start.3 = (bf16[14,64,128]{2,1,0:T(8,128)(2,1)S(1)}, bf16[14,64,128]{2,1,0:T(8,128)(2,1)S(1)}, u32[]{:S(2)}, u32[]{:S(2)}) collective-permute-start(bf16[14,64,128]{2,1,0:T(8,128)(2,1)S(1)} %get-tuple-element.37), channel_id=1, source_target_pairs={{1,0},{2,1},{3,2},{4,3},{5,4},{6,5},{7,6},{9,8},{10,9},{11,10},{12... | collective-permute-start | bytes 688136 | tf_op jit(solution)/shard_map/ppermute | solution.py:646
  31.1 22.8 %copy-start.24 = (f32[32]{0:T(128)S(1)}, f32[32]{0:T(128)}, u32[]{:S(2)}) copy-start(f32[32]{0:T(128)} %param.14) | copy-start | bytes 388
  31.1 22.7 %copy-start.25 = (f32[32]{0:T(128)S(1)}, f32[32]{0:T(128)}, u32[]{:S(2)}) copy-start(f32[32]{0:T(128)} %param.13) | copy-start | bytes 388
  31.1 22.7 %copy-start.26 = (f32[32]{0:T(128)S(1)}, f32[32]{0:T(128)}, u32[]{:S(2)}) copy-start(f32[32]{0:T(128)} %param.11) | copy-start | bytes 388
  31.1 22.7 %copy-start.27 = (f32[32]{0:T(128)S(1)}, f32[32]{0:T(128)}, u32[]{:S(2)}) copy-start(f32[32]{0:T(128)} %param.10) | copy-start | bytes 388
  32.0 4.4 %copy-start.21 = (bf16[14,64,128]{2,1,0:T(8,128)(2,1)}, bf16[14,64,128]{2,1,0:T(8,128)(2,1)S(1)}, u32[]{:S(2)}) copy-start(bf16[14,64,128]{2,1,0:T(8,128)(2,1)S(1)} %collective-permute-done.2.refs_0_.refs_5_.refs_8_) | copy-start | bytes 688132
  36.4 0.7 copy-start.22
  43.0 21.8 %all-to-all-start = ((f32[128,4,128]{2,1,0:T(4,128)}), f32[128,4,128]{2,1,0:T(4,128)S(1)}, u32[]{:S(2)}, u32[]{:S(2)}) async-start(f32[128,4,128]{2,1,0:T(4,128)} %get-tuple-element.38), calls=%async_computation | async-start | bytes 524288 | tf_op jit(solution)/shard_map/all_to_all | solution.py:650
  64.7 0.7 copy-start.20
  71.8 13.7 %all-to-all-start.1 = ((f32[128,1,128]{2,1,0:T(1,128)}), f32[128,1,128]{2,1,0:T(1,128)S(1)}, u32[]{:S(2)}, u32[]{:S(2)}) async-start(f32[128,1,128]{2,1,0:T(1,128)} %bitcast.59), calls=%async_computation.1 | async-start | bytes 131072 | tf_op jit(solution)/shard_map/all_to_all | solution.py:650
  76.0 32.8 %collective-permute-start.4 = (bf16[72,32,128]{2,1,0:T(8,128)(2,1)}, bf16[72,32,128]{2,1,0:T(8,128)(2,1)S(1)}, u32[]{:S(2)}, u32[]{:S(2)}) collective-permute-start(bf16[72,32,128]{2,1,0:T(8,128)(2,1)} %get-tuple-element.49), channel_id=1, source_target_pairs={{0,8},{8,16},{16,24},{24,32},{32,40},{40,48},{48,56},{56,64},{64,7... | collective-permute-start | bytes 1769480 | tf_op jit(solution)/shard_map/ppermute | solution.py:641
  79.4 29.4 %collective-permute-start.5 = (bf16[72,32,128]{2,1,0:T(8,128)(2,1)}, bf16[72,32,128]{2,1,0:T(8,128)(2,1)S(1)}, u32[]{:S(2)}, u32[]{:S(2)}) collective-permute-start(bf16[72,32,128]{2,1,0:T(8,128)(2,1)} %get-tuple-element.50), channel_id=1, source_target_pairs={{8,0},{16,8},{24,16},{32,24},{40,32},{48,40},{56,48},{64,56},{72,6... | collective-permute-start | bytes 1769480 | tf_op jit(solution)/shard_map/ppermute | solution.py:646
  85.6 0.6 copy-start.23
  89.9 18.9 %all-to-all-start.2 = ((f32[128,4,128]{2,1,0:T(4,128)}), f32[128,4,128]{2,1,0:T(4,128)S(1)}, u32[]{:S(2)}, u32[]{:S(2)}) async-start(f32[128,4,128]{2,1,0:T(4,128)} %get-tuple-element.48), calls=%async_computation.2 | async-start | bytes 524288 | tf_op jit(solution)/shard_map/all_to_all | solution.py:650
  108.8 0.7 copy-start.16
  108.8 1.0 copy-start.17
  108.8 1.2 copy-start.18
  119.5 9.0 %copy-start.15 = (bf16[32,64,128]{2,1,0:T(8,128)(2,1)S(1)}, bf16[32,64,128]{2,1,0:T(8,128)(2,1)}, u32[]{:S(2)}) copy-start(bf16[32,64,128]{2,1,0:T(8,128)(2,1)} %output.1.refs_15_) | copy-start | bytes 1572868
  119.5 18.9 %copy-start.3 = (f32[32,4]{1,0:T(8,128)S(1)}, f32[32,4]{1,0:T(8,128)}, u32[]{:S(2)}) copy-start(f32[32,4]{1,0:T(8,128)} %copy.30.refs_2_.refs_1_.refs_3_) | copy-start | bytes 1540
  119.6 18.9 %copy-start.4 = (f32[32,128]{1,0:T(8,128)S(1)}, f32[32,128]{1,0:T(8,128)}, u32[]{:S(2)}) copy-start(f32[32,128]{1,0:T(8,128)} %get-tuple-element.45.refs_1_.refs_5_.refs_11_.refs_2_) | copy-start | bytes 49156
  119.6 18.9 %copy-start.5 = (s32[8]{0:T(128)S(1)}, s32[8]{0:T(128)}, u32[]{:S(2)}) copy-start(s32[8]{0:T(128)} %stack.66.refs_0_) | copy-start | bytes 100
  119.6 18.9 %copy-start.10 = (f32[4,128]{1,0:T(4,128)S(1)}, f32[4,128]{1,0:T(4,128)}, u32[]{:S(2)}) copy-start(f32[4,128]{1,0:T(4,128)} %get-tuple-element.54.refs_4_) | copy-start | bytes 6148
  119.6 18.9 %copy-start.14 = (f32[4,128]{1,0:T(4,128)S(1)}, f32[4,128]{1,0:T(4,128)}, u32[]{:S(2)}) copy-start(f32[4,128]{1,0:T(4,128)} %total.1.refs_8_.refs_5_) | copy-start | bytes 6148
  119.6 18.9 %all-to-all-start.3 = ((f32[128,8,128]{2,1,0:T(8,128)}), f32[128,8,128]{2,1,0:T(8,128)S(1)}, u32[]{:S(2)}, u32[]{:S(2)}) async-start(f32[128,8,128]{2,1,0:T(8,128)} %get-tuple-element.53), calls=%async_computation.3 | async-start | bytes 1048576 | tf_op jit(solution)/shard_map/all_to_all | solution.py:650
  123.9 12.7 %collective-permute-start.6 = (bf16[34,32,128]{2,1,0:T(8,128)(2,1)}, bf16[34,32,128]{2,1,0:T(8,128)(2,1)S(1)}, u32[]{:S(2)}, u32[]{:S(2)}) collective-permute-start(bf16[34,32,128]{2,1,0:T(8,128)(2,1)} %get-tuple-element.55), channel_id=1, source_target_pairs={{0,8},{8,16},{16,24},{24,32},{32,40},{40,48},{48,56},{56,64},{64,7... | collective-permute-start | bytes 835592 | tf_op jit(solution)/shard_map/ppermute | solution.py:641
  127.3 11.2 %collective-permute-start.7 = (bf16[34,32,128]{2,1,0:T(8,128)(2,1)}, bf16[34,32,128]{2,1,0:T(8,128)(2,1)S(1)}, u32[]{:S(2)}, u32[]{:S(2)}) collective-permute-start(bf16[34,32,128]{2,1,0:T(8,128)(2,1)} %get-tuple-element.56), channel_id=1, source_target_pairs={{8,0},{16,8},{24,16},{32,24},{40,32},{48,40},{56,48},{64,56},{72,6... | collective-permute-start | bytes 835592 | tf_op jit(solution)/shard_map/ppermute | solution.py:646
  128.9 11.5 %copy-start.2 = (bf16[32,2,32,128]{3,0,1,2:T(8,128)(2,1)}, bf16[32,2,32,128]{3,0,1,2:T(8,128)(2,1)S(1)}, u32[]{:S(2)}) copy-start(bf16[32,2,32,128]{3,0,1,2:T(8,128)(2,1)S(1)} %copy.42) | copy-start | bytes 1572868
  136.6 3.9 %copy-start.8 = (bf16[34,32,128]{2,1,0:T(8,128)(2,1)}, bf16[34,32,128]{2,1,0:T(8,128)(2,1)S(1)}, u32[]{:S(2)}) copy-start(bf16[34,32,128]{2,1,0:T(8,128)(2,1)S(1)} %collective-permute-done.6.refs_6_) | copy-start | bytes 835588
  138.5 2.0 %copy-start.9 = (bf16[34,32,128]{2,1,0:T(8,128)(2,1)}, bf16[34,32,128]{2,1,0:T(8,128)(2,1)S(1)}, u32[]{:S(2)}) copy-start(bf16[34,32,128]{2,1,0:T(8,128)(2,1)S(1)} %collective-permute-done.7.refs_7_) | copy-start | bytes 835588
  140.5 0.6 copy-start.13
  141.1 21.6 %all-to-all-start.4 = ((bf16[128,8,128]{2,1,0:T(8,128)(2,1)}), bf16[128,8,128]{2,1,0:T(8,128)(2,1)S(1)}, u32[]{:S(2)}, u32[]{:S(2)}) async-start(bf16[128,8,128]{2,1,0:T(8,128)(2,1)} %bitcast.29), calls=%async_computation.4 | async-start | bytes 524288 | tf_op jit(solution)/shard_map/all_to_all | solution.py:650

commit v10 on v9

--- a/solution.py
+++ b/solution.py
@@ -519,7 +519,7 @@
                     out[dx * 9 + dy * 3 + dz] = tile[:, dx * C : (dx + 1) * C]
 
 
-def fifth_kernel(cells, need, send, place, t4, st1, gb, h1, slope1, s_low, s_high, w, out, v):
+def fifth_kernel(cells, need, send, place, t4, st1, gb, h1, slope1, s_low, s_high, w, out, v, turned):
     need(t4, st1, gb)
     mean, inverse, _, _ = kept_stats(st1)
     nsum, plain = sums_of(t4[0:1])
@@ -538,10 +538,13 @@
     need(w)
 
     def emit(y, values):
-        out[y] = values.astype(BF16)
-        send(out, row=y)
+        turned[:, y, :] = values
 
     conv_rows(windows_of(v), w, ROWS, emit)
+    for i in range(C):
+        for x in range(2):
+            out[i, x] = turned[x * C + i].astype(BF16)
+        send(out, row=i)
 
 
 def pieces_of(shape):
@@ -782,9 +785,9 @@
     (grad,) = call(
         lambda *refs: fifth_kernel(cells, *refs),
         (place, t4, st1, gb, h1, slope1, s_low, s_high, b1),
-        [sh((ROWS, 64, 128), BF16)],
+        [sh((C, 2, ROWS, 128), BF16)],
         "back_one",
-        scratch=(pltpu.VMEM((34, 128, 128), BF16),),
+        scratch=(pltpu.VMEM((34, 128, 128), BF16), pltpu.VMEM((64, ROWS, 128), F32)),
     )
     grads = call(
         finish_kernel,
@@ -798,7 +801,7 @@
     )
     one, two = [jnp.transpose(k.reshape(3, 3, 3, C, C), (3, 4, 0, 1, 2)) for k in grads]
 
-    return output, back(grad), one, two, norm_grads
+    return output, grad, one, two, norm_grads
 
 
 def solution(mesh):

time: 165 us -> 165 us (level)
  local copies, waits for them, and re-layouts: 10.6 us -> 8.42 us
    reshape x2 -> x1, local copies, waits for them, and re-layouts: 2.52 us -> 0.34 us  [back(): return jnp.transpose(rows.reshape(ROWS, 2, C, 128), (2, 1, 0, 3))]
  transfers between devices with their start and end apart: 13 -> 13, of which waited for: 10 -> 10; matrix products, arithmetic and copies ran while one was open for 3% -> 1% of each run, Pallas kernels for 13% -> 13%
where the time goes in v10:
time: 165 us; the launch traced here: 164 us
  starting transfers between devices  59.7 us (36%)
  Pallas kernels  49.1 us (30%)
  waiting for transfers between devices  45.2 us (27%)
  local copies, waits for them, and re-layouts  8.42 us (5%)
    pallas_call x13, Pallas kernels, call(): pl.pallas_call(body, out_shape=outs, in_specs=[SM] * lead + [pl.BlockSpec...  49.1 us
    all_to_all x5, starting transfers between devices, share(): return lax.all_to_all(msg, ALL[::-1], 0, 0, tiled=True)  37.8 us
    all_to_all x5, waiting for transfers between devices, share(): return lax.all_to_all(msg, ALL[::-1], 0, 0, tiled=True)  22.5 us
    ppermute x4, starting transfers between devices, up(): return lax.ppermute(values, axes, [(i, i + 1) for i in range(count - 1)])  16.1 us
    ppermute x4, waiting for transfers between devices, up(): return lax.ppermute(values, axes, [(i, i + 1) for i in range(count - 1)])  12.6 us
    ppermute x4, waiting for transfers between devices, down(): return lax.ppermute(values, axes, [(i + 1, i) for i in range(count - 1)])  10.1 us
    ppermute x4, starting transfers between devices, down(): return lax.ppermute(values, axes, [(i + 1, i) for i in range(count - 1)])  5.8 us
    unnamed x56, local copies, waits for them, and re-layouts  4.94 us
  transfers between devices with their start and end apart: 13, of which 10 were waited for; matrix products, arithmetic and copies ran while one was open for 1% of the time, Pallas kernels for 13%

profile of v10, /device:TPU:1, one launch (start us, length us, event | category | flops | bytes accessed | tf_op | source)
XLA Modules:
  0.0 164.0 jit_solution(15109262867505699970)
XLA Ops:
  0.6 0.0 copy-start.19
  0.6 1.4 copy.26
  2.1 0.0 copy-start.1
  2.1 4.1 %collective-permute-start = (bf16[32,64,128]{2,1,0:T(8,128)(2,1)S(1)}, bf16[32,64,128]{2,1,0:T(8,128)(2,1)S(1)}, u32[]{:S(2)}, u32[]{:S(2)}) collective-permute-start(bf16[32,64,128]{2,1,0:T(8,128)(2,1)S(1)} %bitcast.42), channel_id=1, source_target_pairs={{0,8},{8,16},{16,24},{24,32},{32,40},{40,48},{48,56},{56,64},{64,7... | collective-permute-start | bytes 1572872 | tf_op jit(solution)/shard_map/ppermute | solution.py:644
  6.2 1.3 collective-permute-start.1
  7.5 0.3 copy.27
  7.8 0.0 copy-start
  7.8 2.4 %weights.1 = (bf16[192,384]{1,0:T(8,128)(2,1)}, bf16[192,384]{1,0:T(8,128)(2,1)}) custom-call(bf16[27,32,32]{2,1,0:T(8,128)(2,1)} %bitcast.58, bf16[27,32,32]{2,1,0:T(8,128)(2,1)} %bitcast.60), custom_call_target="tpu_custom_call" | custom-call | flops 2000000000 | bytes 6000000 | tf_op jit(solution)/shard_map/weights/pallas_call | solution.py:620
  10.2 0.0 copy-start.12
  10.3 2.4 %flipped.1 = (bf16[192,384]{1,0:T(8,128)(2,1)}, bf16[192,384]{1,0:T(8,128)(2,1)}) custom-call(bf16[27,32,32]{2,1,0:T(8,128)(2,1)} %bitcast.59, bf16[27,32,32]{2,1,0:T(8,128)(2,1)} %bitcast.61), custom_call_target="tpu_custom_call" | custom-call | flops 2000000000 | bytes 6000000 | tf_op jit(solution)/shard_map/flipped/pallas_call | solution.py:620
  12.6 4.1 %collective-permute-done.refs_0_.refs_4_ = bf16[32,64,128]{2,1,0:T(8,128)(2,1)S(1)} collective-permute-done((bf16[32,64,128]{2,1,0:T(8,128)(2,1)S(1)}, bf16[32,64,128]{2,1,0:T(8,128)(2,1)S(1)}, u32[]{:S(2)}, u32[]{:S(2)}) %collective-permute-start) | collective-permute-done | bytes 524320 | tf_op jit(solution)/shard_map/ppermute | solution.py:644
  16.7 3.8 %collective-permute-done.1.refs_1_.refs_5_ = bf16[32,64,128]{2,1,0:T(8,128)(2,1)S(1)} collective-permute-done((bf16[32,64,128]{2,1,0:T(8,128)(2,1)S(1)}, bf16[32,64,128]{2,1,0:T(8,128)(2,1)S(1)}, u32[]{:S(2)}, u32[]{:S(2)}) %collective-permute-start.1) | collective-permute-done | bytes 524320 | tf_op jit(solution)/shard_map/ppermute | solution.py:649
  20.6 1.1 copy-done.11
  21.6 2.1 %pack.1 = (bf16[14,64,128]{2,1,0:T(8,128)(2,1)S(1)}, bf16[14,64,128]{2,1,0:T(8,128)(2,1)S(1)}) custom-call(bf16[32,64,128]{2,1,0:T(8,128)(2,1)S(1)} %collective-permute-done.refs_0_.refs_4_, bf16[32,64,128]{2,1,0:T(8,128)(2,1)S(1)} %collective-permute-done.1.refs_1_.refs_5_, bf16[32,64,128]{2,1,0:T(8,128)(2,1)S(1)} %bitcast.44, ...), custom_call_target="tpu_custom_call" | custom-call | flops 2000000000 | bytes 6000000 | tf_op jit(solution)/shard_map/pack/pallas_call | solution.py:620
  23.7 5.3 %collective-permute-start.2 = (bf16[14,64,128]{2,1,0:T(8,128)(2,1)S(1)}, bf16[14,64,128]{2,1,0:T(8,128)(2,1)S(1)}, u32[]{:S(2)}, u32[]{:S(2)}) collective-permute-start(bf16[14,64,128]{2,1,0:T(8,128)(2,1)S(1)} %get-tuple-element.36), channel_id=1, source_target_pairs={{0,1},{1,2},{2,3},{3,4},{4,5},{5,6},{6,7},{8,9},{9,10},{10,11},{11... | collective-permute-start | bytes 688136 | tf_op jit(solution)/shard_map/ppermute | solution.py:644
  29.0 1.9 %collective-permute-start.3 = (bf16[14,64,128]{2,1,0:T(8,128)(2,1)S(1)}, bf16[14,64,128]{2,1,0:T(8,128)(2,1)S(1)}, u32[]{:S(2)}, u32[]{:S(2)}) collective-permute-start(bf16[14,64,128]{2,1,0:T(8,128)(2,1)S(1)} %get-tuple-element.37), channel_id=1, source_target_pairs={{1,0},{2,1},{3,2},{4,3},{5,4},{6,5},{7,6},{9,8},{10,9},{11,10},{12... | collective-permute-start | bytes 688136 | tf_op jit(solution)/shard_map/ppermute | solution.py:649
  31.1 0.0 copy-start.24
  31.1 0.0 copy-start.25
  31.1 0.0 copy-start.26
  31.1 0.0 copy-start.27
  31.1 0.9 collective-permute-done.2.refs_0_.refs_5_.refs_8_
  32.0 4.4 %collective-permute-done.3.refs_1_.refs_6_.refs_9_ = bf16[14,64,128]{2,1,0:T(8,128)(2,1)S(1)} collective-permute-done((bf16[14,64,128]{2,1,0:T(8,128)(2,1)S(1)}, bf16[14,64,128]{2,1,0:T(8,128)(2,1)S(1)}, u32[]{:S(2)}, u32[]{:S(2)}) %collective-permute-start.3) | collective-permute-done | bytes 229408 | tf_op jit(solution)/shard_map/ppermute | solution.py:649
  36.4 0.7 copy-done.22
  37.1 5.9 %conv_one.1 = (bf16[40,128,128]{2,1,0:T(8,128)(2,1)}, f32[38,128,128]{2,1,0:T(8,128)}, f32[128,4,128]{2,1,0:T(4,128)}, f32[16,128]{1,0:T(8,128)}, f32[32,128]{1,0:T(8,128)}) custom-call(bf16[14,64,128]{2,1,0:T(8,128)(2,1)} %copy-done.21, bf16[14,64,128]{2,1,0:T(8,128)(2,1)} %copy-done.22, bf16[192,384]{1,0:T(8,128)(2,1)} %get-tuple-element.34.refs_4_.refs_2_, ...), custom_call_target="tpu_custom_call" | custom-call | flops 2000000000 | bytes 6000000 | tf_op jit(solution)/shard_map/conv_one/pallas_call | solution.py:620
  43.0 10.8 %all-to-all-start = ((f32[128,4,128]{2,1,0:T(4,128)}), f32[128,4,128]{2,1,0:T(4,128)S(1)}, u32[]{:S(2)}, u32[]{:S(2)}) async-start(f32[128,4,128]{2,1,0:T(4,128)} %get-tuple-element.38), calls=%async_computation | async-start | bytes 524288 | tf_op jit(solution)/shard_map/all_to_all | solution.py:653
  53.9 0.7 copy.28.refs_2_.refs_1_.refs_3_
  54.5 0.7 stack.66.refs_0_
  55.2 3.8 %hidden_features.1.refs_8_.refs_7_ = f32[9,32,128]{2,1,0:T(8,128)} custom-call(f32[32,128]{1,0:T(8,128)} %get-tuple-element.41.refs_0_, f32[38,128,128]{2,1,0:T(8,128)} %get-tuple-element.39.refs_1_.refs_3_.refs_12_.refs_4_, bf16[40,128,128]{2,1,0:T(8,128)(2,1)} %get-tuple-element.42.refs_2_.refs_14_), custom_call_target="tpu_custom_call" | custom-call | flops 2000000000 | bytes 6000000 | tf_op jit(solution)/shard_map/hidden_features/pallas_call | solution.py:620
  59.1 5.7 %all-to-all-done.refs_1_.refs_0_ = f32[128,4,128]{2,1,0:T(4,128)S(1)} async-done(((f32[128,4,128]{2,1,0:T(4,128)}), f32[128,4,128]{2,1,0:T(4,128)S(1)}, u32[]{:S(2)}, u32[]{:S(2)}) %all-to-all-start) | async-done | bytes 262176 | tf_op jit(solution)/shard_map/all_to_all | solution.py:653
  64.7 0.7 copy-done.20
  65.4 6.4 %conv_two.1 = (bf16[38,128,128]{2,1,0:T(8,128)(2,1)}, f32[36,64,128]{2,1,0:T(8,128)}, bf16[72,32,128]{2,1,0:T(8,128)(2,1)}, bf16[72,32,128]{2,1,0:T(8,128)(2,1)}, f32[128,128]{1,0:T(8,128)}, /*index=5*/f32[32,128]{1,0:T(8,128)}) custom-call(s32[8]{0:T(128)} %stack.66.refs_0_, f32[128,4,128]{2,1,0:T(4,128)} %copy-done.20, ...), custom_call_target="tpu_custom_call" | custom-call | flops 2000000000 | bytes 6000000 | tf_op jit(solution)/shard_map/conv_two/pallas_call | solution.py:620
  71.8 4.1 %all-to-all-start.1 = ((f32[128,1,128]{2,1,0:T(1,128)}), f32[128,1,128]{2,1,0:T(1,128)S(1)}, u32[]{:S(2)}, u32[]{:S(2)}) async-start(f32[128,1,128]{2,1,0:T(1,128)} %bitcast.53), calls=%async_computation.1 | async-start | bytes 131072 | tf_op jit(solution)/shard_map/all_to_all | solution.py:653
  76.0 3.4 %collective-permute-start.4 = (bf16[72,32,128]{2,1,0:T(8,128)(2,1)}, bf16[72,32,128]{2,1,0:T(8,128)(2,1)S(1)}, u32[]{:S(2)}, u32[]{:S(2)}) collective-permute-start(bf16[72,32,128]{2,1,0:T(8,128)(2,1)} %get-tuple-element.49), channel_id=1, source_target_pairs={{0,8},{8,16},{16,24},{24,32},{32,40},{40,48},{48,56},{56,64},{64,7... | collective-permute-start | bytes 1769480 | tf_op jit(solution)/shard_map/ppermute | solution.py:644
  79.4 1.3 collective-permute-start.5
  80.7 1.7 %total.1.refs_8_.refs_5_ = f32[4,128]{1,0:T(4,128)} custom-call(f32[128,4,128]{2,1,0:T(4,128)} %copy-done.20, f32[32,128]{1,0:T(8,128)} %get-tuple-element.45.refs_1_.refs_5_.refs_11_.refs_2_), custom_call_target="tpu_custom_call" | custom-call | flops 2000000000 | bytes 6000000 | tf_op jit(solution)/shard_map/total/pallas_call | solution.py:620
  82.4 3.1 %all-to-all-done.1 = f32[128,1,128]{2,1,0:T(1,128)S(1)} async-done(((f32[128,1,128]{2,1,0:T(1,128)}), f32[128,1,128]{2,1,0:T(1,128)S(1)}, u32[]{:S(2)}, u32[]{:S(2)}) %all-to-all-start.1) | async-done | bytes 65568 | tf_op jit(solution)/shard_map/all_to_all | solution.py:653
  85.6 0.6 copy-done.23
  86.2 3.7 %slope_two.1 = (f32[128,4,128]{2,1,0:T(4,128)}, f32[32,128]{1,0:T(8,128)}) custom-call(s32[8]{0:T(128)} %stack.66.refs_0_, f32[128,128]{1,0:T(8,128)} %bitcast.52, f32[32,4]{1,0:T(8,128)} %copy.28.refs_2_.refs_1_.refs_3_, bf16[32,64,128]{2,1,0:T(8,128)(2,1)} %bitcast.40, f32[36,64,128]{2,1,0:T(8,128)} %get-tuple-element.44.refs_4_.refs_2_, ...), custom_call_target="tpu_custom_call" | custom-call | flops 2000000000 | bytes 6000000 | tf_op jit(solution)/shard_map/slope_two/pallas_call | solution.py:620
  89.9 7.9 %all-to-all-start.2 = ((f32[128,4,128]{2,1,0:T(4,128)}), f32[128,4,128]{2,1,0:T(4,128)S(1)}, u32[]{:S(2)}, u32[]{:S(2)}) async-start(f32[128,4,128]{2,1,0:T(4,128)} %get-tuple-element.48), calls=%async_computation.2 | async-start | bytes 524288 | tf_op jit(solution)/shard_map/all_to_all | solution.py:653
  97.9 2.4 %output.1.refs_15_ = bf16[32,64,128]{2,1,0:T(8,128)(2,1)} custom-call(f32[32,128]{1,0:T(8,128)} %get-tuple-element.47.refs_0_.refs_2_, f32[32,4]{1,0:T(8,128)} %copy.28.refs_2_.refs_1_.refs_3_, f32[36,64,128]{2,1,0:T(8,128)} %get-tuple-element.44.refs_4_.refs_2_), custom_call_target="tpu_custom_call" | custom-call | flops 2000000000 | bytes 6000000 | tf_op jit(solution)/shard_map/output/pallas_call | solution.py:620
  100.3 8.5 %all-to-all-done.2.refs_1_ = f32[128,4,128]{2,1,0:T(4,128)S(1)} async-done(((f32[128,4,128]{2,1,0:T(4,128)}), f32[128,4,128]{2,1,0:T(4,128)S(1)}, u32[]{:S(2)}, u32[]{:S(2)}) %all-to-all-start.2) | async-done | bytes 262176 | tf_op jit(solution)/shard_map/all_to_all | solution.py:653
  108.8 0.0 collective-permute-done.4.refs_5_
  108.8 0.0 collective-permute-done.5.refs_6_
  108.8 0.0 copy-start.18
  108.8 0.7 copy-done.16
  109.5 0.3 copy-done.17
  109.8 0.2 copy-done.18
  110.0 9.5 %back_two.1 = (f32[34,64,128]{2,1,0:T(8,128)}, bf16[34,32,128]{2,1,0:T(8,128)(2,1)}, bf16[34,32,128]{2,1,0:T(8,128)(2,1)}, f32[128,8,128]{2,1,0:T(8,128)}, f32[4,128]{1,0:T(4,128)}) custom-call(s32[8]{0:T(128)} %stack.66.refs_0_, f32[128,4,128]{2,1,0:T(4,128)} %copy-done.16, f32[32,128]{1,0:T(8,128)} %get-tuple-element.47.refs_0_.refs_2_, ...), custom_call_target="tpu_custom_call" | custom-call | flops 2000000000 | bytes 6000000 | tf_op jit(solution)/shard_map/back_two/pallas_call | solution.py:620
  119.5 0.0 copy-start.15
  119.6 0.0 copy-start.14
  119.6 4.3 %all-to-all-start.3 = ((f32[128,8,128]{2,1,0:T(8,128)}), f32[128,8,128]{2,1,0:T(8,128)S(1)}, u32[]{:S(2)}, u32[]{:S(2)}) async-start(f32[128,8,128]{2,1,0:T(8,128)} %get-tuple-element.53), calls=%async_computation.3 | async-start | bytes 1048576 | tf_op jit(solution)/shard_map/all_to_all | solution.py:653
  123.9 3.4 %collective-permute-start.6 = (bf16[34,32,128]{2,1,0:T(8,128)(2,1)}, bf16[34,32,128]{2,1,0:T(8,128)(2,1)S(1)}, u32[]{:S(2)}, u32[]{:S(2)}) collective-permute-start(bf16[34,32,128]{2,1,0:T(8,128)(2,1)} %get-tuple-element.55), channel_id=1, source_target_pairs={{0,8},{8,16},{16,24},{24,32},{32,40},{40,48},{48,56},{56,64},{64,7... | collective-permute-start | bytes 835592 | tf_op jit(solution)/shard_map/ppermute | solution.py:644
  127.3 1.3 collective-permute-start.7
  128.6 0.3 copy.37
  128.9 0.0 copy-start.2
  128.9 7.6 %collective-permute-done.6.refs_6_ = bf16[34,32,128]{2,1,0:T(8,128)(2,1)S(1)} collective-permute-done((bf16[34,32,128]{2,1,0:T(8,128)(2,1)}, bf16[34,32,128]{2,1,0:T(8,128)(2,1)S(1)}, u32[]{:S(2)}, u32[]{:S(2)}) %collective-permute-start.6) | collective-permute-done | bytes 278560 | tf_op jit(solution)/shard_map/ppermute | solution.py:644
  136.6 1.9 %collective-permute-done.7.refs_7_ = bf16[34,32,128]{2,1,0:T(8,128)(2,1)S(1)} collective-permute-done((bf16[34,32,128]{2,1,0:T(8,128)(2,1)}, bf16[34,32,128]{2,1,0:T(8,128)(2,1)S(1)}, u32[]{:S(2)}, u32[]{:S(2)}) %collective-permute-start.7) | collective-permute-done | bytes 278560 | tf_op jit(solution)/shard_map/ppermute | solution.py:649
  138.5 0.0 all-to-all-done.3.refs_1_
  138.5 1.9 %own_rows.1 = (bf16[1024,128]{1,0:T(8,128)(2,1)}, f32[4,32]{1,0:T(4,128)}, f32[8,128]{1,0:T(8,128)S(1)}) custom-call(s32[8]{0:T(128)S(1)} %copy-done.5, f32[128,8,128]{2,1,0:T(8,128)S(1)} %all-to-all-done.3.refs_1_, f32[32,128]{1,0:T(8,128)S(1)} %copy-done.4, f32[32,4]{1,0:T(8,128)S(1)} %copy-done.3, f32[4,128]{1,0:T(4,128)S(1)} %copy-done.10, ...), custom_call_target="tpu_custom_call" | custom-call | flops 2000000000 | bytes 6000000 | tf_op jit(solution)/shard_map/own_rows/pallas_call | solution.py:620
  140.4 0.6 copy-done.13
  141.0 10.6 %all-to-all-start.4 = ((bf16[128,8,128]{2,1,0:T(8,128)(2,1)}), bf16[128,8,128]{2,1,0:T(8,128)(2,1)S(1)}, u32[]{:S(2)}, u32[]{:S(2)}) async-start(bf16[128,8,128]{2,1,0:T(8,128)(2,1)} %bitcast.27), calls=%async_computation.4 | async-start | bytes 524288 | tf_op jit(solution)/shard_map/all_to_all | solution.py:653
  151.6 5.7 %back_one.1 = bf16[32,2,32,128]{3,2,1,0:T(8,128)(2,1)} custom-call(s32[8]{0:T(128)} %stack.66.refs_0_, f32[8,128]{1,0:T(8,128)} %copy-done.13, f32[32,128]{1,0:T(8,128)} %get-tuple-element.45.refs_1_.refs_5_.refs_11_.refs_2_, f32[32,4]{1,0:T(8,128)} %copy.28.refs_2_.refs_1_.refs_3_, f32[38,128,128]{2,1,0:T(8,128)} %get-tuple-element.39.refs_1_.refs_3_.refs_12_.refs_4_, ...), custom_call_target="tpu_custom_call" | custom-call | flops 2000000000 | bytes 6000000 | tf_op jit(solution)/shard_map/back_one/pallas_call | solution.py:620
  157.3 5.2 %all-to-all-done.4 = bf16[128,8,128]{2,1,0:T(8,128)(2,1)S(1)} async-done(((bf16[128,8,128]{2,1,0:T(8,128)(2,1)}), bf16[128,8,128]{2,1,0:T(8,128)(2,1)S(1)}, u32[]{:S(2)}, u32[]{:S(2)}) %all-to-all-start.4) | async-done | bytes 262176 | tf_op jit(solution)/shard_map/all_to_all | solution.py:653
  162.6 1.2 finish.1
  (37 shorter events, 0.1 us)
Async XLA Ops:
  0.6 6.8 %copy-start.19 = (bf16[32,2,32,128]{3,2,1,0:T(8,128)(2,1)S(1)}, bf16[32,2,32,128]{3,2,1,0:T(8,128)(2,1)}, u32[]{:S(2)}) copy-start(bf16[32,2,32,128]{3,2,1,0:T(8,128)(2,1)} %param.15) | copy-start | bytes 1572868
  2.1 18.5 %copy-start.1 = (bf16[32,2,32,128]{3,2,1,0:T(8,128)(2,1)}, bf16[32,2,32,128]{3,2,1,0:T(8,128)(2,1)S(1)}, u32[]{:S(2)}) copy-start(bf16[32,2,32,128]{3,2,1,0:T(8,128)(2,1)S(1)} %copy.26) | copy-start | bytes 1572868
  2.1 14.6 %collective-permute-start = (bf16[32,64,128]{2,1,0:T(8,128)(2,1)S(1)}, bf16[32,64,128]{2,1,0:T(8,128)(2,1)S(1)}, u32[]{:S(2)}, u32[]{:S(2)}) collective-permute-start(bf16[32,64,128]{2,1,0:T(8,128)(2,1)S(1)} %bitcast.42), channel_id=1, source_target_pairs={{0,8},{8,16},{16,24},{24,32},{32,40},{40,48},{48,56},{56,64},{64,7... | collective-permute-start | bytes 1572872 | tf_op jit(solution)/shard_map/ppermute | solution.py:644
  6.2 14.4 %collective-permute-start.1 = (bf16[32,64,128]{2,1,0:T(8,128)(2,1)S(1)}, bf16[32,64,128]{2,1,0:T(8,128)(2,1)S(1)}, u32[]{:S(2)}, u32[]{:S(2)}) collective-permute-start(bf16[32,64,128]{2,1,0:T(8,128)(2,1)S(1)} %bitcast.43), channel_id=1, source_target_pairs={{8,0},{16,8},{24,16},{32,24},{40,32},{48,40},{56,48},{64,56},{72,6... | collective-permute-start | bytes 1572872 | tf_op jit(solution)/shard_map/ppermute | solution.py:649
  7.8 12.7 %copy-start = (bf16[32,2,32,128]{3,2,1,0:T(8,128)(2,1)}, bf16[32,2,32,128]{3,2,1,0:T(8,128)(2,1)S(1)}, u32[]{:S(2)}) copy-start(bf16[32,2,32,128]{3,2,1,0:T(8,128)(2,1)S(1)} %copy.27) | copy-start | bytes 1572868
  10.2 10.3 %copy-start.12 = (bf16[192,384]{1,0:T(8,128)(2,1)S(1)}, bf16[192,384]{1,0:T(8,128)(2,1)}, u32[]{:S(2)}) copy-start(bf16[192,384]{1,0:T(8,128)(2,1)} %get-tuple-element.34.refs_4_.refs_2_) | copy-start | bytes 442372
  16.7 7.0 %copy-start.6 = (bf16[32,64,128]{2,1,0:T(8,128)(2,1)}, bf16[32,64,128]{2,1,0:T(8,128)(2,1)S(1)}, u32[]{:S(2)}) copy-start(bf16[32,64,128]{2,1,0:T(8,128)(2,1)S(1)} %collective-permute-done.refs_0_.refs_4_) | copy-start | bytes 1572868
  20.5 3.2 %copy-start.7 = (bf16[32,64,128]{2,1,0:T(8,128)(2,1)}, bf16[32,64,128]{2,1,0:T(8,128)(2,1)S(1)}, u32[]{:S(2)}) copy-start(bf16[32,64,128]{2,1,0:T(8,128)(2,1)S(1)} %collective-permute-done.1.refs_1_.refs_5_) | copy-start | bytes 1572868
  20.5 1.1 copy-start.11
  23.7 8.2 %collective-permute-start.2 = (bf16[14,64,128]{2,1,0:T(8,128)(2,1)S(1)}, bf16[14,64,128]{2,1,0:T(8,128)(2,1)S(1)}, u32[]{:S(2)}, u32[]{:S(2)}) collective-permute-start(bf16[14,64,128]{2,1,0:T(8,128)(2,1)S(1)} %get-tuple-element.36), channel_id=1, source_target_pairs={{0,1},{1,2},{2,3},{3,4},{4,5},{5,6},{6,7},{8,9},{9,10},{10,11},{11... | collective-permute-start | bytes 688136 | tf_op jit(solution)/shard_map/ppermute | solution.py:644
  29.0 7.3 %collective-permute-start.3 = (bf16[14,64,128]{2,1,0:T(8,128)(2,1)S(1)}, bf16[14,64,128]{2,1,0:T(8,128)(2,1)S(1)}, u32[]{:S(2)}, u32[]{:S(2)}) collective-permute-start(bf16[14,64,128]{2,1,0:T(8,128)(2,1)S(1)} %get-tuple-element.37), channel_id=1, source_target_pairs={{1,0},{2,1},{3,2},{4,3},{5,4},{6,5},{7,6},{9,8},{10,9},{11,10},{12... | collective-permute-start | bytes 688136 | tf_op jit(solution)/shard_map/ppermute | solution.py:649
  31.1 22.8 %copy-start.24 = (f32[32]{0:T(128)S(1)}, f32[32]{0:T(128)}, u32[]{:S(2)}) copy-start(f32[32]{0:T(128)} %param.14) | copy-start | bytes 388
  31.1 22.7 %copy-start.25 = (f32[32]{0:T(128)S(1)}, f32[32]{0:T(128)}, u32[]{:S(2)}) copy-start(f32[32]{0:T(128)} %param.13) | copy-start | bytes 388
  31.1 22.7 %copy-start.26 = (f32[32]{0:T(128)S(1)}, f32[32]{0:T(128)}, u32[]{:S(2)}) copy-start(f32[32]{0:T(128)} %param.11) | copy-start | bytes 388
  31.1 22.7 %copy-start.27 = (f32[32]{0:T(128)S(1)}, f32[32]{0:T(128)}, u32[]{:S(2)}) copy-start(f32[32]{0:T(128)} %param.10) | copy-start | bytes 388
  32.0 4.4 %copy-start.21 = (bf16[14,64,128]{2,1,0:T(8,128)(2,1)}, bf16[14,64,128]{2,1,0:T(8,128)(2,1)S(1)}, u32[]{:S(2)}) copy-start(bf16[14,64,128]{2,1,0:T(8,128)(2,1)S(1)} %collective-permute-done.2.refs_0_.refs_5_.refs_8_) | copy-start | bytes 688132
  36.4 0.7 copy-start.22
  43.0 21.8 %all-to-all-start = ((f32[128,4,128]{2,1,0:T(4,128)}), f32[128,4,128]{2,1,0:T(4,128)S(1)}, u32[]{:S(2)}, u32[]{:S(2)}) async-start(f32[128,4,128]{2,1,0:T(4,128)} %get-tuple-element.38), calls=%async_computation | async-start | bytes 524288 | tf_op jit(solution)/shard_map/all_to_all | solution.py:653
  64.7 0.7 copy-start.20
  71.8 13.7 %all-to-all-start.1 = ((f32[128,1,128]{2,1,0:T(1,128)}), f32[128,1,128]{2,1,0:T(1,128)S(1)}, u32[]{:S(2)}, u32[]{:S(2)}) async-start(f32[128,1,128]{2,1,0:T(1,128)} %bitcast.53), calls=%async_computation.1 | async-start | bytes 131072 | tf_op jit(solution)/shard_map/all_to_all | solution.py:653
  76.0 32.8 %collective-permute-start.4 = (bf16[72,32,128]{2,1,0:T(8,128)(2,1)}, bf16[72,32,128]{2,1,0:T(8,128)(2,1)S(1)}, u32[]{:S(2)}, u32[]{:S(2)}) collective-permute-start(bf16[72,32,128]{2,1,0:T(8,128)(2,1)} %get-tuple-element.49), channel_id=1, source_target_pairs={{0,8},{8,16},{16,24},{24,32},{32,40},{40,48},{48,56},{56,64},{64,7... | collective-permute-start | bytes 1769480 | tf_op jit(solution)/shard_map/ppermute | solution.py:644
  79.4 29.4 %collective-permute-start.5 = (bf16[72,32,128]{2,1,0:T(8,128)(2,1)}, bf16[72,32,128]{2,1,0:T(8,128)(2,1)S(1)}, u32[]{:S(2)}, u32[]{:S(2)}) collective-permute-start(bf16[72,32,128]{2,1,0:T(8,128)(2,1)} %get-tuple-element.50), channel_id=1, source_target_pairs={{8,0},{16,8},{24,16},{32,24},{40,32},{48,40},{56,48},{64,56},{72,6... | collective-permute-start | bytes 1769480 | tf_op jit(solution)/shard_map/ppermute | solution.py:649
  85.6 0.6 copy-start.23
  89.9 18.9 %all-to-all-start.2 = ((f32[128,4,128]{2,1,0:T(4,128)}), f32[128,4,128]{2,1,0:T(4,128)S(1)}, u32[]{:S(2)}, u32[]{:S(2)}) async-start(f32[128,4,128]{2,1,0:T(4,128)} %get-tuple-element.48), calls=%async_computation.2 | async-start | bytes 524288 | tf_op jit(solution)/shard_map/all_to_all | solution.py:653
  108.8 0.7 copy-start.16
  108.8 1.0 copy-start.17
  108.8 1.2 copy-start.18
  119.5 9.0 %copy-start.15 = (bf16[32,64,128]{2,1,0:T(8,128)(2,1)S(1)}, bf16[32,64,128]{2,1,0:T(8,128)(2,1)}, u32[]{:S(2)}) copy-start(bf16[32,64,128]{2,1,0:T(8,128)(2,1)} %output.1.refs_15_) | copy-start | bytes 1572868
  119.5 18.9 %copy-start.3 = (f32[32,4]{1,0:T(8,128)S(1)}, f32[32,4]{1,0:T(8,128)}, u32[]{:S(2)}) copy-start(f32[32,4]{1,0:T(8,128)} %copy.28.refs_2_.refs_1_.refs_3_) | copy-start | bytes 1540
  119.6 18.9 %copy-start.4 = (f32[32,128]{1,0:T(8,128)S(1)}, f32[32,128]{1,0:T(8,128)}, u32[]{:S(2)}) copy-start(f32[32,128]{1,0:T(8,128)} %get-tuple-element.45.refs_1_.refs_5_.refs_11_.refs_2_) | copy-start | bytes 49156
  119.6 18.9 %copy-start.5 = (s32[8]{0:T(128)S(1)}, s32[8]{0:T(128)}, u32[]{:S(2)}) copy-start(s32[8]{0:T(128)} %stack.66.refs_0_) | copy-start | bytes 100
  119.6 18.9 %copy-start.10 = (f32[4,128]{1,0:T(4,128)S(1)}, f32[4,128]{1,0:T(4,128)}, u32[]{:S(2)}) copy-start(f32[4,128]{1,0:T(4,128)} %get-tuple-element.54.refs_4_) | copy-start | bytes 6148
  119.6 18.9 %copy-start.14 = (f32[4,128]{1,0:T(4,128)S(1)}, f32[4,128]{1,0:T(4,128)}, u32[]{:S(2)}) copy-start(f32[4,128]{1,0:T(4,128)} %total.1.refs_8_.refs_5_) | copy-start | bytes 6148
  119.6 18.9 %all-to-all-start.3 = ((f32[128,8,128]{2,1,0:T(8,128)}), f32[128,8,128]{2,1,0:T(8,128)S(1)}, u32[]{:S(2)}, u32[]{:S(2)}) async-start(f32[128,8,128]{2,1,0:T(8,128)} %get-tuple-element.53), calls=%async_computation.3 | async-start | bytes 1048576 | tf_op jit(solution)/shard_map/all_to_all | solution.py:653
  123.9 12.7 %collective-permute-start.6 = (bf16[34,32,128]{2,1,0:T(8,128)(2,1)}, bf16[34,32,128]{2,1,0:T(8,128)(2,1)S(1)}, u32[]{:S(2)}, u32[]{:S(2)}) collective-permute-start(bf16[34,32,128]{2,1,0:T(8,128)(2,1)} %get-tuple-element.55), channel_id=1, source_target_pairs={{0,8},{8,16},{16,24},{24,32},{32,40},{40,48},{48,56},{56,64},{64,7... | collective-permute-start | bytes 835592 | tf_op jit(solution)/shard_map/ppermute | solution.py:644
  127.3 11.2 %collective-permute-start.7 = (bf16[34,32,128]{2,1,0:T(8,128)(2,1)}, bf16[34,32,128]{2,1,0:T(8,128)(2,1)S(1)}, u32[]{:S(2)}, u32[]{:S(2)}) collective-permute-start(bf16[34,32,128]{2,1,0:T(8,128)(2,1)} %get-tuple-element.56), channel_id=1, source_target_pairs={{8,0},{16,8},{24,16},{32,24},{40,32},{48,40},{56,48},{64,56},{72,6... | collective-permute-start | bytes 835592 | tf_op jit(solution)/shard_map/ppermute | solution.py:649
  128.9 11.5 %copy-start.2 = (bf16[32,2,32,128]{3,0,1,2:T(8,128)(2,1)}, bf16[32,2,32,128]{3,0,1,2:T(8,128)(2,1)S(1)}, u32[]{:S(2)}) copy-start(bf16[32,2,32,128]{3,0,1,2:T(8,128)(2,1)S(1)} %copy.37) | copy-start | bytes 1572868
  136.6 3.8 %copy-start.8 = (bf16[34,32,128]{2,1,0:T(8,128)(2,1)}, bf16[34,32,128]{2,1,0:T(8,128)(2,1)S(1)}, u32[]{:S(2)}) copy-start(bf16[34,32,128]{2,1,0:T(8,128)(2,1)S(1)} %collective-permute-done.6.refs_6_) | copy-start | bytes 835588
  138.5 1.9 %copy-start.9 = (bf16[34,32,128]{2,1,0:T(8,128)(2,1)}, bf16[34,32,128]{2,1,0:T(8,128)(2,1)S(1)}, u32[]{:S(2)}) copy-start(bf16[34,32,128]{2,1,0:T(8,128)(2,1)S(1)} %collective-permute-done.7.refs_7_) | copy-start | bytes 835588
  140.4 0.6 copy-start.13
  141.0 21.6 %all-to-all-start.4 = ((bf16[128,8,128]{2,1,0:T(8,128)(2,1)}), bf16[128,8,128]{2,1,0:T(8,128)(2,1)S(1)}, u32[]{:S(2)}, u32[]{:S(2)}) async-start(bf16[128,8,128]{2,1,0:T(8,128)(2,1)} %bitcast.27), calls=%async_computation.4 | async-start | bytes 524288 | tf_op jit(solution)/shard_map/all_to_all | solution.py:653

commit v11 on v10

--- a/solution.py
+++ b/solution.py
@@ -698,7 +698,7 @@
         [sh((14, 64, 128), BF16)] * 2,
         "pack",
         smem_first=False,
-        after=(w1, b1),
+        after=(w1,),
         near=2,
         grant=16,
     )

time: 165 us -> 165 us (level)
    ppermute x4, waiting for transfers between devices: 12.6 us -> 15 us  [up(): return lax.ppermute(values, axes, [(i, i + 1) for i in range(count - 1)])]
    all_to_all x5, waiting for transfers between devices: 22.5 us -> 20.2 us  [share(): return lax.all_to_all(msg, ALL[::-1], 0, 0, tiled=True)]
    unnamed x56 -> x54, local copies, waits for them, and re-layouts: 4.94 us -> 4.93 us
where the time goes in v11:
time: 165 us; the launch traced here: 164 us
  starting transfers between devices  59.7 us (36%)
  Pallas kernels  49.1 us (30%)
  waiting for transfers between devices  45.3 us (27%)
  local copies, waits for them, and re-layouts  8.37 us (5%)
    pallas_call x13, Pallas kernels, call(): pl.pallas_call(body, out_shape=outs, in_specs=[SM] * lead + [pl.BlockSpec...  49.1 us
    all_to_all x5, starting transfers between devices, share(): return lax.all_to_all(msg, ALL[::-1], 0, 0, tiled=True)  37.8 us
    all_to_all x5, waiting for transfers between devices, share(): return lax.all_to_all(msg, ALL[::-1], 0, 0, tiled=True)  20.2 us
    ppermute x4, starting transfers between devices, up(): return lax.ppermute(values, axes, [(i, i + 1) for i in range(count - 1)])  16.1 us
    ppermute x4, waiting for transfers between devices, up(): return lax.ppermute(values, axes, [(i, i + 1) for i in range(count - 1)])  15 us
    ppermute x4, waiting for transfers between devices, down(): return lax.ppermute(values, axes, [(i + 1, i) for i in range(count - 1)])  10.1 us
    ppermute x4, starting transfers between devices, down(): return lax.ppermute(values, axes, [(i + 1, i) for i in range(count - 1)])  5.8 us
    unnamed x54, local copies, waits for them, and re-layouts  4.93 us
  transfers between devices with their start and end apart: 13, of which 10 were waited for; matrix products, arithmetic and copies ran while one was open for 1% of the time, Pallas kernels for 13%

profile of v11, /device:TPU:1, one launch (start us, length us, event | category | flops | bytes accessed | tf_op | source)
XLA Modules:
  0.0 163.9 jit_solution(11420520651646523762)
XLA Ops:
  0.6 1.4 copy.26
  2.1 0.0 copy-start.1
  2.1 4.1 %collective-permute-start = (bf16[32,64,128]{2,1,0:T(8,128)(2,1)S(1)}, bf16[32,64,128]{2,1,0:T(8,128)(2,1)S(1)}, u32[]{:S(2)}, u32[]{:S(2)}) collective-permute-start(bf16[32,64,128]{2,1,0:T(8,128)(2,1)S(1)} %bitcast.42), channel_id=1, source_target_pairs={{0,8},{8,16},{16,24},{24,32},{32,40},{40,48},{48,56},{56,64},{64,7... | collective-permute-start | bytes 1572872 | tf_op jit(solution)/shard_map/ppermute | solution.py:644
  6.2 1.3 collective-permute-start.1
  7.5 0.3 copy.27
  7.8 0.0 copy-start
  7.8 2.4 %weights.1 = (bf16[192,384]{1,0:T(8,128)(2,1)}, bf16[192,384]{1,0:T(8,128)(2,1)}) custom-call(bf16[27,32,32]{2,1,0:T(8,128)(2,1)} %bitcast.58, bf16[27,32,32]{2,1,0:T(8,128)(2,1)} %bitcast.60), custom_call_target="tpu_custom_call" | custom-call | flops 2000000000 | bytes 6000000 | tf_op jit(solution)/shard_map/weights/pallas_call | solution.py:620
  10.2 6.5 %collective-permute-done.refs_0_.refs_4_ = bf16[32,64,128]{2,1,0:T(8,128)(2,1)S(1)} collective-permute-done((bf16[32,64,128]{2,1,0:T(8,128)(2,1)S(1)}, bf16[32,64,128]{2,1,0:T(8,128)(2,1)S(1)}, u32[]{:S(2)}, u32[]{:S(2)}) %collective-permute-start) | collective-permute-done | bytes 524320 | tf_op jit(solution)/shard_map/ppermute | solution.py:644
  16.7 3.8 %collective-permute-done.1.refs_1_.refs_5_ = bf16[32,64,128]{2,1,0:T(8,128)(2,1)S(1)} collective-permute-done((bf16[32,64,128]{2,1,0:T(8,128)(2,1)S(1)}, bf16[32,64,128]{2,1,0:T(8,128)(2,1)S(1)}, u32[]{:S(2)}, u32[]{:S(2)}) %collective-permute-start.1) | collective-permute-done | bytes 524320 | tf_op jit(solution)/shard_map/ppermute | solution.py:649
  20.5 1.1 copy-done.11
  21.6 2.1 %pack.1 = (bf16[14,64,128]{2,1,0:T(8,128)(2,1)S(1)}, bf16[14,64,128]{2,1,0:T(8,128)(2,1)S(1)}) custom-call(bf16[32,64,128]{2,1,0:T(8,128)(2,1)S(1)} %collective-permute-done.refs_0_.refs_4_, bf16[32,64,128]{2,1,0:T(8,128)(2,1)S(1)} %collective-permute-done.1.refs_1_.refs_5_, bf16[32,64,128]{2,1,0:T(8,128)(2,1)S(1)} %bitcast.44, ...), custom_call_target="tpu_custom_call" | custom-call | flops 2000000000 | bytes 6000000 | tf_op jit(solution)/shard_map/pack/pallas_call | solution.py:620
  23.7 5.3 %collective-permute-start.2 = (bf16[14,64,128]{2,1,0:T(8,128)(2,1)S(1)}, bf16[14,64,128]{2,1,0:T(8,128)(2,1)S(1)}, u32[]{:S(2)}, u32[]{:S(2)}) collective-permute-start(bf16[14,64,128]{2,1,0:T(8,128)(2,1)S(1)} %get-tuple-element.35), channel_id=1, source_target_pairs={{0,1},{1,2},{2,3},{3,4},{4,5},{5,6},{6,7},{8,9},{9,10},{10,11},{11... | collective-permute-start | bytes 688136 | tf_op jit(solution)/shard_map/ppermute | solution.py:644
  29.0 1.9 %collective-permute-start.3 = (bf16[14,64,128]{2,1,0:T(8,128)(2,1)S(1)}, bf16[14,64,128]{2,1,0:T(8,128)(2,1)S(1)}, u32[]{:S(2)}, u32[]{:S(2)}) collective-permute-start(bf16[14,64,128]{2,1,0:T(8,128)(2,1)S(1)} %get-tuple-element.36), channel_id=1, source_target_pairs={{1,0},{2,1},{3,2},{4,3},{5,4},{6,5},{7,6},{9,8},{10,9},{11,10},{12... | collective-permute-start | bytes 688136 | tf_op jit(solution)/shard_map/ppermute | solution.py:649
  31.1 0.0 copy-start.23
  31.1 0.0 copy-start.24
  31.1 0.0 copy-start.25
  31.1 0.0 copy-start.26
  31.1 0.9 collective-permute-done.2.refs_0_.refs_5_.refs_8_
  32.0 4.4 %collective-permute-done.3.refs_1_.refs_6_.refs_9_ = bf16[14,64,128]{2,1,0:T(8,128)(2,1)S(1)} collective-permute-done((bf16[14,64,128]{2,1,0:T(8,128)(2,1)S(1)}, bf16[14,64,128]{2,1,0:T(8,128)(2,1)S(1)}, u32[]{:S(2)}, u32[]{:S(2)}) %collective-permute-start.3) | collective-permute-done | bytes 229408 | tf_op jit(solution)/shard_map/ppermute | solution.py:649
  36.4 0.7 copy-done.21
  37.1 5.9 %conv_one.1 = (bf16[40,128,128]{2,1,0:T(8,128)(2,1)}, f32[38,128,128]{2,1,0:T(8,128)}, f32[128,4,128]{2,1,0:T(4,128)}, f32[16,128]{1,0:T(8,128)}, f32[32,128]{1,0:T(8,128)}) custom-call(bf16[14,64,128]{2,1,0:T(8,128)(2,1)} %copy-done.20, bf16[14,64,128]{2,1,0:T(8,128)(2,1)} %copy-done.21, bf16[192,384]{1,0:T(8,128)(2,1)} %get-tuple-element.34.refs_4_.refs_2_, ...), custom_call_target="tpu_custom_call" | custom-call | flops 2000000000 | bytes 6000000 | tf_op jit(solution)/shard_map/conv_one/pallas_call | solution.py:620
  43.0 10.8 %all-to-all-start = ((f32[128,4,128]{2,1,0:T(4,128)}), f32[128,4,128]{2,1,0:T(4,128)S(1)}, u32[]{:S(2)}, u32[]{:S(2)}) async-start(f32[128,4,128]{2,1,0:T(4,128)} %get-tuple-element.37), calls=%async_computation | async-start | bytes 524288 | tf_op jit(solution)/shard_map/all_to_all | solution.py:653
  53.8 0.0 copy-done.23
  53.8 0.0 copy-done.24
  53.8 0.0 copy-done.25
  53.9 0.7 copy.28.refs_2_.refs_1_.refs_3_
  54.5 0.6 stack.66.refs_0_
  55.2 3.8 %hidden_features.1.refs_8_.refs_7_ = f32[9,32,128]{2,1,0:T(8,128)} custom-call(f32[32,128]{1,0:T(8,128)} %get-tuple-element.40.refs_0_, f32[38,128,128]{2,1,0:T(8,128)} %get-tuple-element.38.refs_1_.refs_3_.refs_12_.refs_4_, bf16[40,128,128]{2,1,0:T(8,128)(2,1)} %get-tuple-element.41.refs_2_.refs_14_), custom_call_target="tpu_custom_call" | custom-call | flops 2000000000 | bytes 6000000 | tf_op jit(solution)/shard_map/hidden_features/pallas_call | solution.py:620
  59.0 5.7 %all-to-all-done.refs_1_.refs_0_ = f32[128,4,128]{2,1,0:T(4,128)S(1)} async-done(((f32[128,4,128]{2,1,0:T(4,128)}), f32[128,4,128]{2,1,0:T(4,128)S(1)}, u32[]{:S(2)}, u32[]{:S(2)}) %all-to-all-start) | async-done | bytes 262176 | tf_op jit(solution)/shard_map/all_to_all | solution.py:653
  64.7 0.7 copy-done.19
  65.4 6.4 %conv_two.1 = (bf16[38,128,128]{2,1,0:T(8,128)(2,1)}, f32[36,64,128]{2,1,0:T(8,128)}, bf16[72,32,128]{2,1,0:T(8,128)(2,1)}, bf16[72,32,128]{2,1,0:T(8,128)(2,1)}, f32[128,128]{1,0:T(8,128)}, /*index=5*/f32[32,128]{1,0:T(8,128)}) custom-call(s32[8]{0:T(128)} %stack.66.refs_0_, f32[128,4,128]{2,1,0:T(4,128)} %copy-done.19, ...), custom_call_target="tpu_custom_call" | custom-call | flops 2000000000 | bytes 6000000 | tf_op jit(solution)/shard_map/conv_two/pallas_call | solution.py:620
  71.8 4.1 %all-to-all-start.1 = ((f32[128,1,128]{2,1,0:T(1,128)}), f32[128,1,128]{2,1,0:T(1,128)S(1)}, u32[]{:S(2)}, u32[]{:S(2)}) async-start(f32[128,1,128]{2,1,0:T(1,128)} %bitcast.53), calls=%async_computation.1 | async-start | bytes 131072 | tf_op jit(solution)/shard_map/all_to_all | solution.py:653
  76.0 3.4 %collective-permute-start.4 = (bf16[72,32,128]{2,1,0:T(8,128)(2,1)}, bf16[72,32,128]{2,1,0:T(8,128)(2,1)S(1)}, u32[]{:S(2)}, u32[]{:S(2)}) collective-permute-start(bf16[72,32,128]{2,1,0:T(8,128)(2,1)} %get-tuple-element.48), channel_id=1, source_target_pairs={{0,8},{8,16},{16,24},{24,32},{32,40},{40,48},{48,56},{56,64},{64,7... | collective-permute-start | bytes 1769480 | tf_op jit(solution)/shard_map/ppermute | solution.py:644
  79.4 1.3 collective-permute-start.5
  80.7 1.7 %total.1.refs_8_.refs_5_ = f32[4,128]{1,0:T(4,128)} custom-call(f32[128,4,128]{2,1,0:T(4,128)} %copy-done.19, f32[32,128]{1,0:T(8,128)} %get-tuple-element.44.refs_1_.refs_5_.refs_11_.refs_2_), custom_call_target="tpu_custom_call" | custom-call | flops 2000000000 | bytes 6000000 | tf_op jit(solution)/shard_map/total/pallas_call | solution.py:620
  82.4 3.1 %all-to-all-done.1 = f32[128,1,128]{2,1,0:T(1,128)S(1)} async-done(((f32[128,1,128]{2,1,0:T(1,128)}), f32[128,1,128]{2,1,0:T(1,128)S(1)}, u32[]{:S(2)}, u32[]{:S(2)}) %all-to-all-start.1) | async-done | bytes 65568 | tf_op jit(solution)/shard_map/all_to_all | solution.py:653
  85.6 0.6 copy-done.22
  86.2 3.7 %slope_two.1 = (f32[128,4,128]{2,1,0:T(4,128)}, f32[32,128]{1,0:T(8,128)}) custom-call(s32[8]{0:T(128)} %stack.66.refs_0_, f32[128,128]{1,0:T(8,128)} %bitcast.52, f32[32,4]{1,0:T(8,128)} %copy.28.refs_2_.refs_1_.refs_3_, bf16[32,64,128]{2,1,0:T(8,128)(2,1)} %bitcast.40, f32[36,64,128]{2,1,0:T(8,128)} %get-tuple-element.43.refs_4_.refs_2_, ...), custom_call_target="tpu_custom_call" | custom-call | flops 2000000000 | bytes 6000000 | tf_op jit(solution)/shard_map/slope_two/pallas_call | solution.py:620
  89.9 7.9 %all-to-all-start.2 = ((f32[128,4,128]{2,1,0:T(4,128)}), f32[128,4,128]{2,1,0:T(4,128)S(1)}, u32[]{:S(2)}, u32[]{:S(2)}) async-start(f32[128,4,128]{2,1,0:T(4,128)} %get-tuple-element.47), calls=%async_computation.2 | async-start | bytes 524288 | tf_op jit(solution)/shard_map/all_to_all | solution.py:653
  97.9 2.3 %flipped.1 = (bf16[192,384]{1,0:T(8,128)(2,1)}, bf16[192,384]{1,0:T(8,128)(2,1)}) custom-call(bf16[27,32,32]{2,1,0:T(8,128)(2,1)} %bitcast.59, bf16[27,32,32]{2,1,0:T(8,128)(2,1)} %bitcast.61), custom_call_target="tpu_custom_call" | custom-call | flops 2000000000 | bytes 6000000 | tf_op jit(solution)/shard_map/flipped/pallas_call | solution.py:620
  100.2 2.4 %output.1.refs_15_ = bf16[32,64,128]{2,1,0:T(8,128)(2,1)} custom-call(f32[32,128]{1,0:T(8,128)} %get-tuple-element.46.refs_0_.refs_2_, f32[32,4]{1,0:T(8,128)} %copy.28.refs_2_.refs_1_.refs_3_, f32[36,64,128]{2,1,0:T(8,128)} %get-tuple-element.43.refs_4_.refs_2_), custom_call_target="tpu_custom_call" | custom-call | flops 2000000000 | bytes 6000000 | tf_op jit(solution)/shard_map/output/pallas_call | solution.py:620
  102.6 6.2 %all-to-all-done.2.refs_1_ = f32[128,4,128]{2,1,0:T(4,128)S(1)} async-done(((f32[128,4,128]{2,1,0:T(4,128)}), f32[128,4,128]{2,1,0:T(4,128)S(1)}, u32[]{:S(2)}, u32[]{:S(2)}) %all-to-all-start.2) | async-done | bytes 262176 | tf_op jit(solution)/shard_map/all_to_all | solution.py:653
  108.8 0.0 collective-permute-done.4.refs_5_
  108.8 0.0 collective-permute-done.5.refs_6_
  108.8 0.7 copy-done.15
  109.5 0.3 copy-done.16
  109.7 0.2 copy-done.17
  110.0 9.5 %back_two.1 = (f32[34,64,128]{2,1,0:T(8,128)}, bf16[34,32,128]{2,1,0:T(8,128)(2,1)}, bf16[34,32,128]{2,1,0:T(8,128)(2,1)}, f32[128,8,128]{2,1,0:T(8,128)}, f32[4,128]{1,0:T(4,128)}) custom-call(s32[8]{0:T(128)} %stack.66.refs_0_, f32[128,4,128]{2,1,0:T(4,128)} %copy-done.15, f32[32,128]{1,0:T(8,128)} %get-tuple-element.46.refs_0_.refs_2_, ...), custom_call_target="tpu_custom_call" | custom-call | flops 2000000000 | bytes 6000000 | tf_op jit(solution)/shard_map/back_two/pallas_call | solution.py:620
  119.5 0.0 copy-start.14
  119.6 0.0 copy-start.13
  119.6 4.3 %all-to-all-start.3 = ((f32[128,8,128]{2,1,0:T(8,128)}), f32[128,8,128]{2,1,0:T(8,128)S(1)}, u32[]{:S(2)}, u32[]{:S(2)}) async-start(f32[128,8,128]{2,1,0:T(8,128)} %get-tuple-element.52), calls=%async_computation.3 | async-start | bytes 1048576 | tf_op jit(solution)/shard_map/all_to_all | solution.py:653
  123.8 3.4 %collective-permute-start.6 = (bf16[34,32,128]{2,1,0:T(8,128)(2,1)}, bf16[34,32,128]{2,1,0:T(8,128)(2,1)S(1)}, u32[]{:S(2)}, u32[]{:S(2)}) collective-permute-start(bf16[34,32,128]{2,1,0:T(8,128)(2,1)} %get-tuple-element.54), channel_id=1, source_target_pairs={{0,8},{8,16},{16,24},{24,32},{32,40},{40,48},{48,56},{56,64},{64,7... | collective-permute-start | bytes 835592 | tf_op jit(solution)/shard_map/ppermute | solution.py:644
  127.2 1.3 collective-permute-start.7
  128.5 0.3 copy.37
  128.9 0.0 copy-start.2
  128.9 7.6 %collective-permute-done.6.refs_6_ = bf16[34,32,128]{2,1,0:T(8,128)(2,1)S(1)} collective-permute-done((bf16[34,32,128]{2,1,0:T(8,128)(2,1)}, bf16[34,32,128]{2,1,0:T(8,128)(2,1)S(1)}, u32[]{:S(2)}, u32[]{:S(2)}) %collective-permute-start.6) | collective-permute-done | bytes 278560 | tf_op jit(solution)/shard_map/ppermute | solution.py:644
  136.5 1.9 %collective-permute-done.7.refs_7_ = bf16[34,32,128]{2,1,0:T(8,128)(2,1)S(1)} collective-permute-done((bf16[34,32,128]{2,1,0:T(8,128)(2,1)}, bf16[34,32,128]{2,1,0:T(8,128)(2,1)S(1)}, u32[]{:S(2)}, u32[]{:S(2)}) %collective-permute-start.7) | collective-permute-done | bytes 278560 | tf_op jit(solution)/shard_map/ppermute | solution.py:649
  138.4 0.0 all-to-all-done.3.refs_1_
  138.5 1.9 %own_rows.1 = (bf16[1024,128]{1,0:T(8,128)(2,1)}, f32[4,32]{1,0:T(4,128)}, f32[8,128]{1,0:T(8,128)S(1)}) custom-call(s32[8]{0:T(128)S(1)} %copy-done.5, f32[128,8,128]{2,1,0:T(8,128)S(1)} %all-to-all-done.3.refs_1_, f32[32,128]{1,0:T(8,128)S(1)} %copy-done.4, f32[32,4]{1,0:T(8,128)S(1)} %copy-done.3, f32[4,128]{1,0:T(4,128)S(1)} %copy-done.10, ...), custom_call_target="tpu_custom_call" | custom-call | flops 2000000000 | bytes 6000000 | tf_op jit(solution)/shard_map/own_rows/pallas_call | solution.py:620
  140.4 0.6 copy-done.12
  141.0 10.6 %all-to-all-start.4 = ((bf16[128,8,128]{2,1,0:T(8,128)(2,1)}), bf16[128,8,128]{2,1,0:T(8,128)(2,1)S(1)}, u32[]{:S(2)}, u32[]{:S(2)}) async-start(bf16[128,8,128]{2,1,0:T(8,128)(2,1)} %bitcast.27), calls=%async_computation.4 | async-start | bytes 524288 | tf_op jit(solution)/shard_map/all_to_all | solution.py:653
  151.6 5.7 %back_one.1 = bf16[32,2,32,128]{3,2,1,0:T(8,128)(2,1)} custom-call(s32[8]{0:T(128)} %stack.66.refs_0_, f32[8,128]{1,0:T(8,128)} %copy-done.12, f32[32,128]{1,0:T(8,128)} %get-tuple-element.44.refs_1_.refs_5_.refs_11_.refs_2_, f32[32,4]{1,0:T(8,128)} %copy.28.refs_2_.refs_1_.refs_3_, f32[38,128,128]{2,1,0:T(8,128)} %get-tuple-element.38.refs_1_.refs_3_.refs_12_.refs_4_, ...), custom_call_target="tpu_custom_call" | custom-call | flops 2000000000 | bytes 6000000 | tf_op jit(solution)/shard_map/back_one/pallas_call | solution.py:620
  157.3 5.2 %all-to-all-done.4 = bf16[128,8,128]{2,1,0:T(8,128)(2,1)S(1)} async-done(((bf16[128,8,128]{2,1,0:T(8,128)(2,1)}), bf16[128,8,128]{2,1,0:T(8,128)(2,1)S(1)}, u32[]{:S(2)}, u32[]{:S(2)}) %all-to-all-start.4) | async-done | bytes 262176 | tf_op jit(solution)/shard_map/all_to_all | solution.py:653
  162.5 1.2 finish.1
  (35 shorter events, 0.1 us)
Async XLA Ops:
  0.6 6.8 %copy-start.18 = (bf16[32,2,32,128]{3,2,1,0:T(8,128)(2,1)S(1)}, bf16[32,2,32,128]{3,2,1,0:T(8,128)(2,1)}, u32[]{:S(2)}) copy-start(bf16[32,2,32,128]{3,2,1,0:T(8,128)(2,1)} %param.15) | copy-start | bytes 1572868
  2.1 18.5 %copy-start.1 = (bf16[32,2,32,128]{3,2,1,0:T(8,128)(2,1)}, bf16[32,2,32,128]{3,2,1,0:T(8,128)(2,1)S(1)}, u32[]{:S(2)}) copy-start(bf16[32,2,32,128]{3,2,1,0:T(8,128)(2,1)S(1)} %copy.26) | copy-start | bytes 1572868
  2.1 14.6 %collective-permute-start = (bf16[32,64,128]{2,1,0:T(8,128)(2,1)S(1)}, bf16[32,64,128]{2,1,0:T(8,128)(2,1)S(1)}, u32[]{:S(2)}, u32[]{:S(2)}) collective-permute-start(bf16[32,64,128]{2,1,0:T(8,128)(2,1)S(1)} %bitcast.42), channel_id=1, source_target_pairs={{0,8},{8,16},{16,24},{24,32},{32,40},{40,48},{48,56},{56,64},{64,7... | collective-permute-start | bytes 1572872 | tf_op jit(solution)/shard_map/ppermute | solution.py:644
  6.2 14.4 %collective-permute-start.1 = (bf16[32,64,128]{2,1,0:T(8,128)(2,1)S(1)}, bf16[32,64,128]{2,1,0:T(8,128)(2,1)S(1)}, u32[]{:S(2)}, u32[]{:S(2)}) collective-permute-start(bf16[32,64,128]{2,1,0:T(8,128)(2,1)S(1)} %bitcast.43), channel_id=1, source_target_pairs={{8,0},{16,8},{24,16},{32,24},{40,32},{48,40},{56,48},{64,56},{72,6... | collective-permute-start | bytes 1572872 | tf_op jit(solution)/shard_map/ppermute | solution.py:649
  7.8 12.7 %copy-start = (bf16[32,2,32,128]{3,2,1,0:T(8,128)(2,1)}, bf16[32,2,32,128]{3,2,1,0:T(8,128)(2,1)S(1)}, u32[]{:S(2)}) copy-start(bf16[32,2,32,128]{3,2,1,0:T(8,128)(2,1)S(1)} %copy.27) | copy-start | bytes 1572868
  16.7 7.0 %copy-start.6 = (bf16[32,64,128]{2,1,0:T(8,128)(2,1)}, bf16[32,64,128]{2,1,0:T(8,128)(2,1)S(1)}, u32[]{:S(2)}) copy-start(bf16[32,64,128]{2,1,0:T(8,128)(2,1)S(1)} %collective-permute-done.refs_0_.refs_4_) | copy-start | bytes 1572868
  20.5 3.2 %copy-start.7 = (bf16[32,64,128]{2,1,0:T(8,128)(2,1)}, bf16[32,64,128]{2,1,0:T(8,128)(2,1)S(1)}, u32[]{:S(2)}) copy-start(bf16[32,64,128]{2,1,0:T(8,128)(2,1)S(1)} %collective-permute-done.1.refs_1_.refs_5_) | copy-start | bytes 1572868
  20.5 1.1 copy-start.11
  23.7 8.2 %collective-permute-start.2 = (bf16[14,64,128]{2,1,0:T(8,128)(2,1)S(1)}, bf16[14,64,128]{2,1,0:T(8,128)(2,1)S(1)}, u32[]{:S(2)}, u32[]{:S(2)}) collective-permute-start(bf16[14,64,128]{2,1,0:T(8,128)(2,1)S(1)} %get-tuple-element.35), channel_id=1, source_target_pairs={{0,1},{1,2},{2,3},{3,4},{4,5},{5,6},{6,7},{8,9},{9,10},{10,11},{11... | collective-permute-start | bytes 688136 | tf_op jit(solution)/shard_map/ppermute | solution.py:644
  29.0 7.3 %collective-permute-start.3 = (bf16[14,64,128]{2,1,0:T(8,128)(2,1)S(1)}, bf16[14,64,128]{2,1,0:T(8,128)(2,1)S(1)}, u32[]{:S(2)}, u32[]{:S(2)}) collective-permute-start(bf16[14,64,128]{2,1,0:T(8,128)(2,1)S(1)} %get-tuple-element.36), channel_id=1, source_target_pairs={{1,0},{2,1},{3,2},{4,3},{5,4},{6,5},{7,6},{9,8},{10,9},{11,10},{12... | collective-permute-start | bytes 688136 | tf_op jit(solution)/shard_map/ppermute | solution.py:649
  31.1 22.7 %copy-start.23 = (f32[32]{0:T(128)S(1)}, f32[32]{0:T(128)}, u32[]{:S(2)}) copy-start(f32[32]{0:T(128)} %param.14) | copy-start | bytes 388
  31.1 22.7 %copy-start.24 = (f32[32]{0:T(128)S(1)}, f32[32]{0:T(128)}, u32[]{:S(2)}) copy-start(f32[32]{0:T(128)} %param.13) | copy-start | bytes 388
  31.1 22.7 %copy-start.25 = (f32[32]{0:T(128)S(1)}, f32[32]{0:T(128)}, u32[]{:S(2)}) copy-start(f32[32]{0:T(128)} %param.11) | copy-start | bytes 388
  31.1 22.7 %copy-start.26 = (f32[32]{0:T(128)S(1)}, f32[32]{0:T(128)}, u32[]{:S(2)}) copy-start(f32[32]{0:T(128)} %param.10) | copy-start | bytes 388
  32.0 4.4 %copy-start.20 = (bf16[14,64,128]{2,1,0:T(8,128)(2,1)}, bf16[14,64,128]{2,1,0:T(8,128)(2,1)S(1)}, u32[]{:S(2)}) copy-start(bf16[14,64,128]{2,1,0:T(8,128)(2,1)S(1)} %collective-permute-done.2.refs_0_.refs_5_.refs_8_) | copy-start | bytes 688132
  36.4 0.7 copy-start.21
  43.0 21.8 %all-to-all-start = ((f32[128,4,128]{2,1,0:T(4,128)}), f32[128,4,128]{2,1,0:T(4,128)S(1)}, u32[]{:S(2)}, u32[]{:S(2)}) async-start(f32[128,4,128]{2,1,0:T(4,128)} %get-tuple-element.37), calls=%async_computation | async-start | bytes 524288 | tf_op jit(solution)/shard_map/all_to_all | solution.py:653
  64.7 0.7 copy-start.19
  71.8 13.7 %all-to-all-start.1 = ((f32[128,1,128]{2,1,0:T(1,128)}), f32[128,1,128]{2,1,0:T(1,128)S(1)}, u32[]{:S(2)}, u32[]{:S(2)}) async-start(f32[128,1,128]{2,1,0:T(1,128)} %bitcast.53), calls=%async_computation.1 | async-start | bytes 131072 | tf_op jit(solution)/shard_map/all_to_all | solution.py:653
  76.0 32.8 %collective-permute-start.4 = (bf16[72,32,128]{2,1,0:T(8,128)(2,1)}, bf16[72,32,128]{2,1,0:T(8,128)(2,1)S(1)}, u32[]{:S(2)}, u32[]{:S(2)}) collective-permute-start(bf16[72,32,128]{2,1,0:T(8,128)(2,1)} %get-tuple-element.48), channel_id=1, source_target_pairs={{0,8},{8,16},{16,24},{24,32},{32,40},{40,48},{48,56},{56,64},{64,7... | collective-permute-start | bytes 1769480 | tf_op jit(solution)/shard_map/ppermute | solution.py:644
  79.4 29.4 %collective-permute-start.5 = (bf16[72,32,128]{2,1,0:T(8,128)(2,1)}, bf16[72,32,128]{2,1,0:T(8,128)(2,1)S(1)}, u32[]{:S(2)}, u32[]{:S(2)}) collective-permute-start(bf16[72,32,128]{2,1,0:T(8,128)(2,1)} %get-tuple-element.49), channel_id=1, source_target_pairs={{8,0},{16,8},{24,16},{32,24},{40,32},{48,40},{56,48},{64,56},{72,6... | collective-permute-start | bytes 1769480 | tf_op jit(solution)/shard_map/ppermute | solution.py:649
  85.6 0.6 copy-start.22
  89.9 18.9 %all-to-all-start.2 = ((f32[128,4,128]{2,1,0:T(4,128)}), f32[128,4,128]{2,1,0:T(4,128)S(1)}, u32[]{:S(2)}, u32[]{:S(2)}) async-start(f32[128,4,128]{2,1,0:T(4,128)} %get-tuple-element.47), calls=%async_computation.2 | async-start | bytes 524288 | tf_op jit(solution)/shard_map/all_to_all | solution.py:653
  108.8 0.7 copy-start.15
  108.8 1.0 copy-start.16
  108.8 1.2 copy-start.17
  119.5 9.0 %copy-start.14 = (bf16[32,64,128]{2,1,0:T(8,128)(2,1)S(1)}, bf16[32,64,128]{2,1,0:T(8,128)(2,1)}, u32[]{:S(2)}) copy-start(bf16[32,64,128]{2,1,0:T(8,128)(2,1)} %output.1.refs_15_) | copy-start | bytes 1572868
  119.5 18.9 %copy-start.3 = (f32[32,4]{1,0:T(8,128)S(1)}, f32[32,4]{1,0:T(8,128)}, u32[]{:S(2)}) copy-start(f32[32,4]{1,0:T(8,128)} %copy.28.refs_2_.refs_1_.refs_3_) | copy-start | bytes 1540
  119.5 18.9 %copy-start.4 = (f32[32,128]{1,0:T(8,128)S(1)}, f32[32,128]{1,0:T(8,128)}, u32[]{:S(2)}) copy-start(f32[32,128]{1,0:T(8,128)} %get-tuple-element.44.refs_1_.refs_5_.refs_11_.refs_2_) | copy-start | bytes 49156
  119.5 18.9 %copy-start.5 = (s32[8]{0:T(128)S(1)}, s32[8]{0:T(128)}, u32[]{:S(2)}) copy-start(s32[8]{0:T(128)} %stack.66.refs_0_) | copy-start | bytes 100
  119.5 18.9 %copy-start.10 = (f32[4,128]{1,0:T(4,128)S(1)}, f32[4,128]{1,0:T(4,128)}, u32[]{:S(2)}) copy-start(f32[4,128]{1,0:T(4,128)} %get-tuple-element.53.refs_4_) | copy-start | bytes 6148
  119.6 18.9 %copy-start.13 = (f32[4,128]{1,0:T(4,128)S(1)}, f32[4,128]{1,0:T(4,128)}, u32[]{:S(2)}) copy-start(f32[4,128]{1,0:T(4,128)} %total.1.refs_8_.refs_5_) | copy-start | bytes 6148
  119.6 18.9 %all-to-all-start.3 = ((f32[128,8,128]{2,1,0:T(8,128)}), f32[128,8,128]{2,1,0:T(8,128)S(1)}, u32[]{:S(2)}, u32[]{:S(2)}) async-start(f32[128,8,128]{2,1,0:T(8,128)} %get-tuple-element.52), calls=%async_computation.3 | async-start | bytes 1048576 | tf_op jit(solution)/shard_map/all_to_all | solution.py:653
  123.8 12.7 %collective-permute-start.6 = (bf16[34,32,128]{2,1,0:T(8,128)(2,1)}, bf16[34,32,128]{2,1,0:T(8,128)(2,1)S(1)}, u32[]{:S(2)}, u32[]{:S(2)}) collective-permute-start(bf16[34,32,128]{2,1,0:T(8,128)(2,1)} %get-tuple-element.54), channel_id=1, source_target_pairs={{0,8},{8,16},{16,24},{24,32},{32,40},{40,48},{48,56},{56,64},{64,7... | collective-permute-start | bytes 835592 | tf_op jit(solution)/shard_map/ppermute | solution.py:644
  127.2 11.2 %collective-permute-start.7 = (bf16[34,32,128]{2,1,0:T(8,128)(2,1)}, bf16[34,32,128]{2,1,0:T(8,128)(2,1)S(1)}, u32[]{:S(2)}, u32[]{:S(2)}) collective-permute-start(bf16[34,32,128]{2,1,0:T(8,128)(2,1)} %get-tuple-element.55), channel_id=1, source_target_pairs={{8,0},{16,8},{24,16},{32,24},{40,32},{48,40},{56,48},{64,56},{72,6... | collective-permute-start | bytes 835592 | tf_op jit(solution)/shard_map/ppermute | solution.py:649
  128.9 11.5 %copy-start.2 = (bf16[32,2,32,128]{3,0,1,2:T(8,128)(2,1)}, bf16[32,2,32,128]{3,0,1,2:T(8,128)(2,1)S(1)}, u32[]{:S(2)}) copy-start(bf16[32,2,32,128]{3,0,1,2:T(8,128)(2,1)S(1)} %copy.37) | copy-start | bytes 1572868
  136.5 3.9 %copy-start.8 = (bf16[34,32,128]{2,1,0:T(8,128)(2,1)}, bf16[34,32,128]{2,1,0:T(8,128)(2,1)S(1)}, u32[]{:S(2)}) copy-start(bf16[34,32,128]{2,1,0:T(8,128)(2,1)S(1)} %collective-permute-done.6.refs_6_) | copy-start | bytes 835588
  138.4 2.0 %copy-start.9 = (bf16[34,32,128]{2,1,0:T(8,128)(2,1)}, bf16[34,32,128]{2,1,0:T(8,128)(2,1)S(1)}, u32[]{:S(2)}) copy-start(bf16[34,32,128]{2,1,0:T(8,128)(2,1)S(1)} %collective-permute-done.7.refs_7_) | copy-start | bytes 835588
  140.4 0.6 copy-start.12
  141.0 21.6 %all-to-all-start.4 = ((bf16[128,8,128]{2,1,0:T(8,128)(2,1)}), bf16[128,8,128]{2,1,0:T(8,128)(2,1)S(1)}, u32[]{:S(2)}, u32[]{:S(2)}) async-start(bf16[128,8,128]{2,1,0:T(8,128)(2,1)} %bitcast.27), calls=%async_computation.4 | async-start | bytes 524288 | tf_op jit(solution)/shard_map/all_to_all | solution.py:653

commit v12 on v10

--- a/solution.py
+++ b/solution.py
@@ -135,12 +135,12 @@
     return parts[0:C], parts[C : 2 * C]
 
 
-def feature_sums(v):
+def feature_sums(v, first):
     lane = lanes(128)
-    inner = v[5].astype(F32)
-    for y in range(6, 3 + ROWS):
+    inner = v[first + 2].astype(F32)
+    for y in range(first + 3, first + ROWS):
         inner = inner + v[y].astype(F32)
-    ends = [v[y].astype(F32) for y in (3, 4, 3 + ROWS, 4 + ROWS)]
+    ends = [v[first + y].astype(F32) for y in (0, 1, ROWS, ROWS + 1)]
     windows = (inner + ends[0] + ends[1], inner + ends[1] + ends[2], inner + ends[2] + ends[3])
     columns = []
     for dz in range(3):
@@ -310,7 +310,7 @@
         off = h[y, C : 3 * C] - both
         spread = spread + off * off
     center_out[...] = jnp.broadcast_to(center, (C, 128))
-    x1[...] = feature_sums(v)
+    x1[...] = feature_sums(v, 3)
     send(center_out, x1)
     rows_message((center, fold(total(spread))), (ones_of(x1),), msg)
 
@@ -410,6 +410,34 @@
     rows_message((fold(total(both)), fold(total(plain))), (xn,), msg)
 
 
+def active_kernel(need, send, st2, gb, h2, cot, v2, s2, n2, a1, g, acc):
+    need(st2, gb)
+    mean, inverse, _, _ = kept_stats(st2)
+    mean2, inverse2 = twice(mean), twice(inverse)
+    gain2, bias2 = twice(gb[:, 2:3]), twice(gb[:, 3:4])
+    lane = lanes(64)
+
+    def sums_to(out):
+        weight_sums(g, v2, 2, acc)
+        tile = folded(acc)
+        for dz in range(3):
+            for dy in range(3):
+                out[dz * 3 + dy] = tile(dz, dy)
+        send(out)
+
+    for y in range(ROWS):
+        need(h2, row=y + 2)
+        put_shifted(g, y, (h2[y + 2] - mean2) * inverse2, lane)
+    need(v2)
+    sums_to(n2)
+    for y in range(ROWS):
+        need(cot, row=y)
+        normed = (h2[y + 2] - mean2) * inverse2
+        put_shifted(g, y, cot[y].astype(F32) * act_slope(normed * gain2 + bias2), lane)
+    sums_to(s2)
+    a1[...] = feature_sums(v2, 2)
+
+
 def output_kernel(need, send, st2, gb, h2, out):
     need(st2, gb)
     mean, inverse, _, _ = kept_stats(st2)
@@ -422,7 +450,8 @@
 
 
 def fourth_kernel(
-    cells, need, send, place, r3, st2, gb, h2, x_low, x_high, cot, y_low, y_high, w, st1, h1, v2, v1, slope1, low, high, msg, t3, v, g, acc, acc1,
+    cells, need, send, place, r3, st2, gb, h2, x_low, x_high, cot, y_low, y_high, w, st1, h1, v1, s2, n2, a1,
+    slope1, low, high, msg, t3, v, g, acc,
 ):
     need(r3, st2, gb)
     mean, inverse, o_low, o_high = kept_stats(st2)
@@ -439,7 +468,7 @@
         return lead * (slope - p_mean - normed * n_mean)
 
     one = (gain, bias, lead, p_mean, n_mean)
-    two = tuple(twice(a) for a in one)
+    both = tuple(twice(a) for a in one)
     mean2, inverse2 = twice(mean), twice(inverse)
     lane = lanes(64)
     rows = ROWS + 4
@@ -448,15 +477,10 @@
         need(x_low, x_high, row=2 * y + 1)
         need(cot, row=min(max(y - 2, 0), ROWS - 1))
         g_low = grad((x_low[2 * y].astype(F32) + o_low) * inverse, x_low[2 * y + 1], *one)
-        g_own = grad((h2[y] - mean2) * inverse2, cot_row(cot, y_low, y_high, y), *two)
+        g_own = grad((h2[y] - mean2) * inverse2, cot_row(cot, y_low, y_high, y), *both)
         g_high = grad((x_high[2 * y].astype(F32) + o_high) * inverse, x_high[2 * y + 1], *one)
-        both = jnp.concatenate([g_low, g_own, g_high], axis=0)
-        v[y] = masked(both, kept(place, y, rows, 2))
-        if 2 <= y < 2 + ROWS:
-            put_shifted(g, y - 2, g_own, lane)
-    need(v2)
-    weight_sums(g, v2, 2, acc)
-
+        planes = jnp.concatenate([g_low, g_own, g_high], axis=0)
+        v[y] = masked(planes, kept(place, y, rows, 2))
     need(h1, st1, w)
     mean, inverse, _, _ = kept_stats(st1)
     mean2, inverse2 = twice(mean), twice(inverse)
@@ -478,9 +502,16 @@
     conv_rows(windows_of(v), w, ROWS + 2, emit)
     send(slope1, low, high)
     need(v1)
-    weight_sums(g, v1, 3, acc1)
+    weight_sums(g, v1, 3, acc)
+    need(s2, n2, a1)
+    ones = ones_of(a1)
+
+    def two(dz, dy):
+        k = dz * 3 + dy
+        return lead * (s2[k] - p_mean * ones(dz, dy) - n_mean * n2[k])
+
     rows_message(
-        (fold(total(sums[0])), fold(total(sums[1]))), (folded(acc1), folded(acc)), msg
+        (fold(total(sums[0])), fold(total(sums[1]))), (folded(acc), two), msg
     )
 
 
@@ -745,27 +776,38 @@
         after=(x1,),
     )
     r3 = share(m3)
-    (output,) = call(
-        output_kernel, (st2, gb, h2), [sh((ROWS, 64, 128), BF16)], "output", smem_first=False
-    )
-
-    rows_out = output
+    s2, n2, a1 = call(
+        active_kernel,
+        (st2, gb, h2, cot, v2),
+        [sh((9, C, 128), F32), sh((9, C, 128), F32), sh((16, 128), F32)],
+        "active_sums",
+        scratch=corr,
+        smem_first=False,
+    )
 
     slope1, low, high, m4, t3 = call(
         lambda *refs: fourth_kernel(cells, *refs),
         (
             place, r3, st2, gb, h2, h2_low, h2_high, cot, y_low, y_high,
-            b2, st1, h1, v2, v1,
+            b2, st1, h1, v1, s2, n2, a1,
         ),
         [sh((34, 64, 128), F32), *rims(34), wide, sh((4, 128), F32)],
         "back_two",
-        after=(rows_out,),
-        late=5,
+        late=7,
         cut=(h1,),
-        scratch=(pltpu.VMEM((36, 128, 128), BF16), *corr, corr[1]),
+        scratch=(pltpu.VMEM((36, 128, 128), BF16), *corr),
     )
     s_low, s_high = up(high, GX), down(low, GX)
     r4 = share(m4)
+
+    (rows_out,) = call(
+        output_kernel,
+        (st2, gb, h2),
+        [sh((ROWS, 64, 128), BF16)],
+        "output",
+        smem_first=False,
+        after=(slope1,),
+    )
 
     def back(rows):
         return jnp.transpose(rows.reshape(ROWS, 2, C, 128), (2, 1, 0, 3))

time: 165 us -> 164 us (level)
  waiting for transfers between devices: 45.2 us -> 35 us
  Pallas kernels: 49.1 us -> 54.1 us
  starting transfers between devices: 59.7 us -> 63.1 us
    ppermute x4, waiting for transfers between devices: 12.6 us -> 5.9 us  [up(): return lax.ppermute(values, axes, [(i, i + 1) for i in range(count - 1)])]
    pallas_call x13 -> x14, Pallas kernels: 49.1 us -> 54.1 us  [call(): pl.pallas_call(body, out_shape=outs, in_specs=[SM] * lead + [pl.BlockSpec...]
    all_to_all x5, waiting for transfers between devices: 22.5 us -> 18.7 us  [share(): return lax.all_to_all(msg, ALL[::-1], 0, 0, tiled=True)]
    all_to_all x5, starting transfers between devices: 37.8 us -> 40.4 us  [share(): return lax.all_to_all(msg, ALL[::-1], 0, 0, tiled=True)]
    unnamed x56 -> x54, local copies, waits for them, and re-layouts: 4.94 us -> 4.88 us
  transfers between devices with their start and end apart: 13 -> 13, of which waited for: 10 -> 10; matrix products, arithmetic and copies ran while one was open for 1% -> 2% of each run, Pallas kernels for 13% -> 17%
where the time goes in v12:
time: 164 us; the launch traced here: 163 us
  starting transfers between devices  63.1 us (38%)
  Pallas kernels  54.1 us (33%)
  waiting for transfers between devices  35 us (21%)
  local copies, waits for them, and re-layouts  9.37 us (6%)
    pallas_call x14, Pallas kernels, call(): pl.pallas_call(body, out_shape=outs, in_specs=[SM] * lead + [pl.BlockSpec...  54.1 us
    all_to_all x5, starting transfers between devices, share(): return lax.all_to_all(msg, ALL[::-1], 0, 0, tiled=True)  40.4 us
    all_to_all x5, waiting for transfers between devices, share(): return lax.all_to_all(msg, ALL[::-1], 0, 0, tiled=True)  18.7 us
    ppermute x4, starting transfers between devices, up(): return lax.ppermute(values, axes, [(i, i + 1) for i in range(count - 1)])  16.9 us
    ppermute x4, waiting for transfers between devices, down(): return lax.ppermute(values, axes, [(i + 1, i) for i in range(count - 1)])  10.3 us
    ppermute x4, waiting for transfers between devices, up(): return lax.ppermute(values, axes, [(i, i + 1) for i in range(count - 1)])  5.9 us
    ppermute x4, starting transfers between devices, down(): return lax.ppermute(values, axes, [(i + 1, i) for i in range(count - 1)])  5.8 us
    unnamed x54, local copies, waits for them, and re-layouts  4.88 us
  transfers between devices with their start and end apart: 13, of which 10 were waited for; matrix products, arithmetic and copies ran while one was open for 2% of the time, Pallas kernels for 17%

profile of v12, /device:TPU:1, one launch (start us, length us, event | category | flops | bytes accessed | tf_op | source)
XLA Modules:
  0.0 163.0 jit_solution(7731984108799800526)
XLA Ops:
  0.6 1.4 copy.26
  2.1 0.0 copy-start.1
  2.1 1.3 collective-permute-start.1
  3.4 4.7 %collective-permute-start = (bf16[32,64,128]{2,1,0:T(8,128)(2,1)S(1)}, bf16[32,64,128]{2,1,0:T(8,128)(2,1)S(1)}, u32[]{:S(2)}, u32[]{:S(2)}) collective-permute-start(bf16[32,64,128]{2,1,0:T(8,128)(2,1)S(1)} %bitcast.44), channel_id=1, source_target_pairs={{0,8},{8,16},{16,24},{24,32},{32,40},{40,48},{48,56},{56,64},{64,7... | collective-permute-start | bytes 1572872 | tf_op jit(solution)/shard_map/ppermute | solution.py:675
  8.1 0.3 copy.27
  8.5 0.0 copy-start
  8.5 2.5 %flipped.1 = (bf16[192,384]{1,0:T(8,128)(2,1)}, bf16[192,384]{1,0:T(8,128)(2,1)}) custom-call(bf16[27,32,32]{2,1,0:T(8,128)(2,1)} %bitcast.59, bf16[27,32,32]{2,1,0:T(8,128)(2,1)} %bitcast.61), custom_call_target="tpu_custom_call" | custom-call | flops 2000000000 | bytes 6000000 | tf_op jit(solution)/shard_map/flipped/pallas_call | solution.py:651
  11.0 2.3 %weights.1 = (bf16[192,384]{1,0:T(8,128)(2,1)}, bf16[192,384]{1,0:T(8,128)(2,1)}) custom-call(bf16[27,32,32]{2,1,0:T(8,128)(2,1)} %bitcast.60, bf16[27,32,32]{2,1,0:T(8,128)(2,1)} %bitcast.62), custom_call_target="tpu_custom_call" | custom-call | flops 2000000000 | bytes 6000000 | tf_op jit(solution)/shard_map/weights/pallas_call | solution.py:651
  13.3 4.1 %collective-permute-done.1.refs_1_.refs_5_ = bf16[32,64,128]{2,1,0:T(8,128)(2,1)S(1)} collective-permute-done((bf16[32,64,128]{2,1,0:T(8,128)(2,1)S(1)}, bf16[32,64,128]{2,1,0:T(8,128)(2,1)S(1)}, u32[]{:S(2)}, u32[]{:S(2)}) %collective-permute-start.1) | collective-permute-done | bytes 524320 | tf_op jit(solution)/shard_map/ppermute | solution.py:680
  17.4 0.9 collective-permute-done.refs_0_.refs_4_
  18.2 0.0 copy-done.1
  18.2 0.0 copy-start.12
  18.3 1.1 copy-done.12
  19.3 2.1 %pack.1 = (bf16[14,64,128]{2,1,0:T(8,128)(2,1)S(1)}, bf16[14,64,128]{2,1,0:T(8,128)(2,1)S(1)}) custom-call(bf16[32,64,128]{2,1,0:T(8,128)(2,1)S(1)} %collective-permute-done.refs_0_.refs_4_, bf16[32,64,128]{2,1,0:T(8,128)(2,1)S(1)} %collective-permute-done.1.refs_1_.refs_5_, bf16[32,64,128]{2,1,0:T(8,128)(2,1)S(1)} %bitcast.45, ...), custom_call_target="tpu_custom_call" | custom-call | flops 2000000000 | bytes 6000000 | tf_op jit(solution)/shard_map/pack/pallas_call | solution.py:651
  21.4 5.5 %collective-permute-start.2 = (bf16[14,64,128]{2,1,0:T(8,128)(2,1)S(1)}, bf16[14,64,128]{2,1,0:T(8,128)(2,1)S(1)}, u32[]{:S(2)}, u32[]{:S(2)}) collective-permute-start(bf16[14,64,128]{2,1,0:T(8,128)(2,1)S(1)} %get-tuple-element.39), channel_id=1, source_target_pairs={{0,1},{1,2},{2,3},{3,4},{4,5},{5,6},{6,7},{8,9},{9,10},{10,11},{11... | collective-permute-start | bytes 688136 | tf_op jit(solution)/shard_map/ppermute | solution.py:675
  27.0 1.9 %collective-permute-start.3 = (bf16[14,64,128]{2,1,0:T(8,128)(2,1)S(1)}, bf16[14,64,128]{2,1,0:T(8,128)(2,1)S(1)}, u32[]{:S(2)}, u32[]{:S(2)}) collective-permute-start(bf16[14,64,128]{2,1,0:T(8,128)(2,1)S(1)} %get-tuple-element.40), channel_id=1, source_target_pairs={{1,0},{2,1},{3,2},{4,3},{5,4},{6,5},{7,6},{9,8},{10,9},{11,10},{12... | collective-permute-start | bytes 688136 | tf_op jit(solution)/shard_map/ppermute | solution.py:680
  29.0 0.0 copy-start.23
  29.0 0.0 copy-start.24
  29.0 0.0 copy-start.25
  29.0 0.0 copy-start.26
  29.0 0.9 collective-permute-done.2.refs_0_.refs_5_.refs_8_
  29.9 4.4 %collective-permute-done.3.refs_1_.refs_6_.refs_9_ = bf16[14,64,128]{2,1,0:T(8,128)(2,1)S(1)} collective-permute-done((bf16[14,64,128]{2,1,0:T(8,128)(2,1)S(1)}, bf16[14,64,128]{2,1,0:T(8,128)(2,1)S(1)}, u32[]{:S(2)}, u32[]{:S(2)}) %collective-permute-start.3) | collective-permute-done | bytes 229408 | tf_op jit(solution)/shard_map/ppermute | solution.py:680
  34.3 0.7 copy-done.21
  35.0 5.9 %conv_one.1 = (bf16[40,128,128]{2,1,0:T(8,128)(2,1)}, f32[38,128,128]{2,1,0:T(8,128)}, f32[128,4,128]{2,1,0:T(4,128)}, f32[16,128]{1,0:T(8,128)}, f32[32,128]{1,0:T(8,128)}) custom-call(bf16[14,64,128]{2,1,0:T(8,128)(2,1)} %copy-done.20, bf16[14,64,128]{2,1,0:T(8,128)(2,1)} %copy-done.21, bf16[192,384]{1,0:T(8,128)(2,1)} %get-tuple-element.37.refs_4_.refs_2_, ...), custom_call_target="tpu_custom_call" | custom-call | flops 2000000000 | bytes 6000000 | tf_op jit(solution)/shard_map/conv_one/pallas_call | solution.py:651
  40.9 12.6 %all-to-all-start = ((f32[128,4,128]{2,1,0:T(4,128)}), f32[128,4,128]{2,1,0:T(4,128)S(1)}, u32[]{:S(2)}, u32[]{:S(2)}) async-start(f32[128,4,128]{2,1,0:T(4,128)} %get-tuple-element.41), calls=%async_computation | async-start | bytes 524288 | tf_op jit(solution)/shard_map/all_to_all | solution.py:684
  53.6 0.7 copy.28.refs_2_.refs_1_.refs_3_
  54.3 0.6 stack.66.refs_0_
  54.9 3.8 %hidden_features.1.refs_8_.refs_7_ = f32[9,32,128]{2,1,0:T(8,128)} custom-call(f32[32,128]{1,0:T(8,128)} %get-tuple-element.44.refs_0_, f32[38,128,128]{2,1,0:T(8,128)} %get-tuple-element.42.refs_1_.refs_3_.refs_12_.refs_4_, bf16[40,128,128]{2,1,0:T(8,128)(2,1)} %get-tuple-element.45.refs_2_.refs_13_), custom_call_target="tpu_custom_call" | custom-call | flops 2000000000 | bytes 6000000 | tf_op jit(solution)/shard_map/hidden_features/pallas_call | solution.py:651
  58.8 5.7 %all-to-all-done.refs_1_.refs_0_ = f32[128,4,128]{2,1,0:T(4,128)S(1)} async-done(((f32[128,4,128]{2,1,0:T(4,128)}), f32[128,4,128]{2,1,0:T(4,128)S(1)}, u32[]{:S(2)}, u32[]{:S(2)}) %all-to-all-start) | async-done | bytes 262176 | tf_op jit(solution)/shard_map/all_to_all | solution.py:684
  64.4 0.7 copy-done.19
  65.1 6.4 %conv_two.1 = (bf16[38,128,128]{2,1,0:T(8,128)(2,1)}, f32[36,64,128]{2,1,0:T(8,128)}, bf16[72,32,128]{2,1,0:T(8,128)(2,1)}, bf16[72,32,128]{2,1,0:T(8,128)(2,1)}, f32[128,128]{1,0:T(8,128)}, /*index=5*/f32[32,128]{1,0:T(8,128)}) custom-call(s32[8]{0:T(128)} %stack.66.refs_0_, f32[128,4,128]{2,1,0:T(4,128)} %copy-done.19, ...), custom_call_target="tpu_custom_call" | custom-call | flops 2000000000 | bytes 6000000 | tf_op jit(solution)/shard_map/conv_two/pallas_call | solution.py:651
  71.6 4.1 %all-to-all-start.1 = ((f32[128,1,128]{2,1,0:T(1,128)}), f32[128,1,128]{2,1,0:T(1,128)S(1)}, u32[]{:S(2)}, u32[]{:S(2)}) async-start(f32[128,1,128]{2,1,0:T(1,128)} %bitcast.54), calls=%async_computation.1 | async-start | bytes 131072 | tf_op jit(solution)/shard_map/all_to_all | solution.py:684
  75.7 3.4 %collective-permute-start.4 = (bf16[72,32,128]{2,1,0:T(8,128)(2,1)}, bf16[72,32,128]{2,1,0:T(8,128)(2,1)S(1)}, u32[]{:S(2)}, u32[]{:S(2)}) collective-permute-start(bf16[72,32,128]{2,1,0:T(8,128)(2,1)} %get-tuple-element.52), channel_id=1, source_target_pairs={{0,8},{8,16},{16,24},{24,32},{32,40},{40,48},{48,56},{56,64},{64,7... | collective-permute-start | bytes 1769480 | tf_op jit(solution)/shard_map/ppermute | solution.py:675
  79.1 1.3 collective-permute-start.5
  80.4 1.7 %total.1.refs_8_.refs_5_ = f32[4,128]{1,0:T(4,128)} custom-call(f32[128,4,128]{2,1,0:T(4,128)} %copy-done.19, f32[32,128]{1,0:T(8,128)} %get-tuple-element.48.refs_1_.refs_5_.refs_11_.refs_2_), custom_call_target="tpu_custom_call" | custom-call | flops 2000000000 | bytes 6000000 | tf_op jit(solution)/shard_map/total/pallas_call | solution.py:651
  82.2 3.1 %all-to-all-done.1 = f32[128,1,128]{2,1,0:T(1,128)S(1)} async-done(((f32[128,1,128]{2,1,0:T(1,128)}), f32[128,1,128]{2,1,0:T(1,128)S(1)}, u32[]{:S(2)}, u32[]{:S(2)}) %all-to-all-start.1) | async-done | bytes 65568 | tf_op jit(solution)/shard_map/all_to_all | solution.py:684
  85.3 0.6 copy-done.22
  85.9 3.7 %slope_two.1 = (f32[128,4,128]{2,1,0:T(4,128)}, f32[32,128]{1,0:T(8,128)}) custom-call(s32[8]{0:T(128)} %stack.66.refs_0_, f32[128,128]{1,0:T(8,128)} %bitcast.53, f32[32,4]{1,0:T(8,128)} %copy.28.refs_2_.refs_1_.refs_3_, bf16[32,64,128]{2,1,0:T(8,128)(2,1)} %bitcast.40, f32[36,64,128]{2,1,0:T(8,128)} %get-tuple-element.47.refs_4_.refs_2_, ...), custom_call_target="tpu_custom_call" | custom-call | flops 2000000000 | bytes 6000000 | tf_op jit(solution)/shard_map/slope_two/pallas_call | solution.py:651
  89.7 7.9 %all-to-all-start.2 = ((f32[128,4,128]{2,1,0:T(4,128)}), f32[128,4,128]{2,1,0:T(4,128)S(1)}, u32[]{:S(2)}, u32[]{:S(2)}) async-start(f32[128,4,128]{2,1,0:T(4,128)} %get-tuple-element.51), calls=%async_computation.2 | async-start | bytes 524288 | tf_op jit(solution)/shard_map/all_to_all | solution.py:684
  97.6 6.2 %active_sums.1 = (f32[9,32,128]{2,1,0:T(8,128)}, f32[9,32,128]{2,1,0:T(8,128)}, f32[16,128]{1,0:T(8,128)}) custom-call(f32[32,128]{1,0:T(8,128)} %get-tuple-element.50.refs_0_.refs_2_, f32[32,4]{1,0:T(8,128)} %copy.28.refs_2_.refs_1_.refs_3_, f32[36,64,128]{2,1,0:T(8,128)} %get-tuple-element.47.refs_4_.refs_2_, bf16[32,64,128]{2,1,0:T(8,128)(2,1)} %bitcast.41, ...), custom_call_target="tpu_custom_call" | custom-call | flops 2000000000 | bytes 6000000 | tf_op jit(solution)/shard_map/active_sums/pallas_call | solution.py:651
  103.9 4.7 %all-to-all-done.2.refs_1_ = f32[128,4,128]{2,1,0:T(4,128)S(1)} async-done(((f32[128,4,128]{2,1,0:T(4,128)}), f32[128,4,128]{2,1,0:T(4,128)S(1)}, u32[]{:S(2)}, u32[]{:S(2)}) %all-to-all-start.2) | async-done | bytes 262176 | tf_op jit(solution)/shard_map/all_to_all | solution.py:684
  108.5 0.0 collective-permute-done.4.refs_5_
  108.5 0.0 collective-permute-done.5.refs_6_
  108.6 0.7 copy-done.15
  109.2 0.2 copy-done.16
  109.4 0.2 copy-done.17
  109.6 8.3 %back_two.1 = (f32[34,64,128]{2,1,0:T(8,128)}, bf16[34,32,128]{2,1,0:T(8,128)(2,1)}, bf16[34,32,128]{2,1,0:T(8,128)(2,1)}, f32[128,8,128]{2,1,0:T(8,128)}, f32[4,128]{1,0:T(4,128)}) custom-call(s32[8]{0:T(128)} %stack.66.refs_0_, f32[128,4,128]{2,1,0:T(4,128)} %copy-done.15, f32[32,128]{1,0:T(8,128)} %get-tuple-element.50.refs_0_.refs_2_, ...), custom_call_target="tpu_custom_call" | custom-call | flops 2000000000 | bytes 6000000 | tf_op jit(solution)/shard_map/back_two/pallas_call | solution.py:651
  117.9 5.1 %all-to-all-start.3 = ((f32[128,8,128]{2,1,0:T(8,128)}), f32[128,8,128]{2,1,0:T(8,128)S(1)}, u32[]{:S(2)}, u32[]{:S(2)}) async-start(f32[128,8,128]{2,1,0:T(8,128)} %get-tuple-element.60), calls=%async_computation.3 | async-start | bytes 1048576 | tf_op jit(solution)/shard_map/all_to_all | solution.py:684
  123.0 3.3 %collective-permute-start.6 = (bf16[34,32,128]{2,1,0:T(8,128)(2,1)}, bf16[34,32,128]{2,1,0:T(8,128)(2,1)S(1)}, u32[]{:S(2)}, u32[]{:S(2)}) collective-permute-start(bf16[34,32,128]{2,1,0:T(8,128)(2,1)} %get-tuple-element.62), channel_id=1, source_target_pairs={{0,8},{8,16},{16,24},{24,32},{32,40},{40,48},{48,56},{56,64},{64,7... | collective-permute-start | bytes 835592 | tf_op jit(solution)/shard_map/ppermute | solution.py:675
  126.3 1.3 collective-permute-start.7
  127.7 0.0 copy-start.14
  127.7 2.4 %output.1 = bf16[32,64,128]{2,1,0:T(8,128)(2,1)} custom-call(f32[32,128]{1,0:T(8,128)} %get-tuple-element.50.refs_0_.refs_2_, f32[32,4]{1,0:T(8,128)} %copy.28.refs_2_.refs_1_.refs_3_, f32[36,64,128]{2,1,0:T(8,128)} %get-tuple-element.47.refs_4_.refs_2_, f32[34,64,128]{2,1,0:T(8,128)} %get-tuple-element.59.refs_3_.refs_5_), custom_call_target="tpu_custom_call" | custom-call | flops 2000000000 | bytes 6000000 | tf_op jit(solution)/shard_map/output/pallas_call | solution.py:651
  130.1 1.4 copy.38
  131.5 0.0 copy-start.2
  131.5 4.2 %collective-permute-done.6.refs_6_ = bf16[34,32,128]{2,1,0:T(8,128)(2,1)S(1)} collective-permute-done((bf16[34,32,128]{2,1,0:T(8,128)(2,1)}, bf16[34,32,128]{2,1,0:T(8,128)(2,1)S(1)}, u32[]{:S(2)}, u32[]{:S(2)}) %collective-permute-start.6) | collective-permute-done | bytes 278560 | tf_op jit(solution)/shard_map/ppermute | solution.py:675
  135.7 1.8 %collective-permute-done.7.refs_7_ = bf16[34,32,128]{2,1,0:T(8,128)(2,1)S(1)} collective-permute-done((bf16[34,32,128]{2,1,0:T(8,128)(2,1)}, bf16[34,32,128]{2,1,0:T(8,128)(2,1)S(1)}, u32[]{:S(2)}, u32[]{:S(2)}) %collective-permute-start.7) | collective-permute-done | bytes 278560 | tf_op jit(solution)/shard_map/ppermute | solution.py:680
  137.5 0.0 all-to-all-done.3.refs_1_
  137.6 1.9 %own_rows.1 = (bf16[1024,128]{1,0:T(8,128)(2,1)}, f32[4,32]{1,0:T(4,128)}, f32[8,128]{1,0:T(8,128)S(1)}) custom-call(s32[8]{0:T(128)S(1)} %copy-done.5, f32[128,8,128]{2,1,0:T(8,128)S(1)} %all-to-all-done.3.refs_1_, f32[32,128]{1,0:T(8,128)S(1)} %copy-done.4, f32[32,4]{1,0:T(8,128)S(1)} %copy-done.3, f32[4,128]{1,0:T(4,128)S(1)} %copy-done.10, ...), custom_call_target="tpu_custom_call" | custom-call | flops 2000000000 | bytes 6000000 | tf_op jit(solution)/shard_map/own_rows/pallas_call | solution.py:651
  139.4 0.0 copy-done.2
  139.5 0.6 copy-done.13
  140.1 10.6 %all-to-all-start.4 = ((bf16[128,8,128]{2,1,0:T(8,128)(2,1)}), bf16[128,8,128]{2,1,0:T(8,128)(2,1)S(1)}, u32[]{:S(2)}, u32[]{:S(2)}) async-start(bf16[128,8,128]{2,1,0:T(8,128)(2,1)} %bitcast.27), calls=%async_computation.4 | async-start | bytes 524288 | tf_op jit(solution)/shard_map/all_to_all | solution.py:684
  150.7 5.7 %back_one.1 = bf16[32,2,32,128]{3,2,1,0:T(8,128)(2,1)} custom-call(s32[8]{0:T(128)} %stack.66.refs_0_, f32[8,128]{1,0:T(8,128)} %copy-done.13, f32[32,128]{1,0:T(8,128)} %get-tuple-element.48.refs_1_.refs_5_.refs_11_.refs_2_, f32[32,4]{1,0:T(8,128)} %copy.28.refs_2_.refs_1_.refs_3_, f32[38,128,128]{2,1,0:T(8,128)} %get-tuple-element.42.refs_1_.refs_3_.refs_12_.refs_4_, ...), custom_call_target="tpu_custom_call" | custom-call | flops 2000000000 | bytes 6000000 | tf_op jit(solution)/shard_map/back_one/pallas_call | solution.py:651
  156.3 5.2 %all-to-all-done.4 = bf16[128,8,128]{2,1,0:T(8,128)(2,1)S(1)} async-done(((bf16[128,8,128]{2,1,0:T(8,128)(2,1)}), bf16[128,8,128]{2,1,0:T(8,128)(2,1)S(1)}, u32[]{:S(2)}, u32[]{:S(2)}) %all-to-all-start.4) | async-done | bytes 262176 | tf_op jit(solution)/shard_map/all_to_all | solution.py:684
  161.6 1.2 finish.1
  (36 shorter events, 0.1 us)
Async XLA Ops:
  0.6 7.5 %copy-start.18 = (bf16[32,2,32,128]{3,2,1,0:T(8,128)(2,1)S(1)}, bf16[32,2,32,128]{3,2,1,0:T(8,128)(2,1)}, u32[]{:S(2)}) copy-start(bf16[32,2,32,128]{3,2,1,0:T(8,128)(2,1)} %param.15) | copy-start | bytes 1572868
  2.1 16.2 %copy-start.1 = (bf16[32,2,32,128]{3,2,1,0:T(8,128)(2,1)}, bf16[32,2,32,128]{3,2,1,0:T(8,128)(2,1)S(1)}, u32[]{:S(2)}) copy-start(bf16[32,2,32,128]{3,2,1,0:T(8,128)(2,1)S(1)} %copy.26) | copy-start | bytes 1572868
  2.1 15.3 %collective-permute-start.1 = (bf16[32,64,128]{2,1,0:T(8,128)(2,1)S(1)}, bf16[32,64,128]{2,1,0:T(8,128)(2,1)S(1)}, u32[]{:S(2)}, u32[]{:S(2)}) collective-permute-start(bf16[32,64,128]{2,1,0:T(8,128)(2,1)S(1)} %bitcast.43), channel_id=1, source_target_pairs={{8,0},{16,8},{24,16},{32,24},{40,32},{48,40},{56,48},{64,56},{72,6... | collective-permute-start | bytes 1572872 | tf_op jit(solution)/shard_map/ppermute | solution.py:680
  3.4 14.8 %collective-permute-start = (bf16[32,64,128]{2,1,0:T(8,128)(2,1)S(1)}, bf16[32,64,128]{2,1,0:T(8,128)(2,1)S(1)}, u32[]{:S(2)}, u32[]{:S(2)}) collective-permute-start(bf16[32,64,128]{2,1,0:T(8,128)(2,1)S(1)} %bitcast.44), channel_id=1, source_target_pairs={{0,8},{8,16},{16,24},{24,32},{32,40},{40,48},{48,56},{56,64},{64,7... | collective-permute-start | bytes 1572872 | tf_op jit(solution)/shard_map/ppermute | solution.py:675
  8.5 9.8 %copy-start = (bf16[32,2,32,128]{3,2,1,0:T(8,128)(2,1)}, bf16[32,2,32,128]{3,2,1,0:T(8,128)(2,1)S(1)}, u32[]{:S(2)}) copy-start(bf16[32,2,32,128]{3,2,1,0:T(8,128)(2,1)S(1)} %copy.27) | copy-start | bytes 1572868
  11.0 7.3 %copy-start.11 = (bf16[192,384]{1,0:T(8,128)(2,1)S(1)}, bf16[192,384]{1,0:T(8,128)(2,1)}, u32[]{:S(2)}) copy-start(bf16[192,384]{1,0:T(8,128)(2,1)} %get-tuple-element.38.refs_5_.refs_8_) | copy-start | bytes 442372
  17.4 4.1 %copy-start.6 = (bf16[32,64,128]{2,1,0:T(8,128)(2,1)}, bf16[32,64,128]{2,1,0:T(8,128)(2,1)S(1)}, u32[]{:S(2)}) copy-start(bf16[32,64,128]{2,1,0:T(8,128)(2,1)S(1)} %collective-permute-done.1.refs_1_.refs_5_) | copy-start | bytes 1572868
  18.2 3.2 %copy-start.7 = (bf16[32,64,128]{2,1,0:T(8,128)(2,1)}, bf16[32,64,128]{2,1,0:T(8,128)(2,1)S(1)}, u32[]{:S(2)}) copy-start(bf16[32,64,128]{2,1,0:T(8,128)(2,1)S(1)} %collective-permute-done.refs_0_.refs_4_) | copy-start | bytes 1572868
  18.2 1.1 copy-start.12
  21.4 8.5 %collective-permute-start.2 = (bf16[14,64,128]{2,1,0:T(8,128)(2,1)S(1)}, bf16[14,64,128]{2,1,0:T(8,128)(2,1)S(1)}, u32[]{:S(2)}, u32[]{:S(2)}) collective-permute-start(bf16[14,64,128]{2,1,0:T(8,128)(2,1)S(1)} %get-tuple-element.39), channel_id=1, source_target_pairs={{0,1},{1,2},{2,3},{3,4},{4,5},{5,6},{6,7},{8,9},{9,10},{10,11},{11... | collective-permute-start | bytes 688136 | tf_op jit(solution)/shard_map/ppermute | solution.py:675
  27.0 7.3 %collective-permute-start.3 = (bf16[14,64,128]{2,1,0:T(8,128)(2,1)S(1)}, bf16[14,64,128]{2,1,0:T(8,128)(2,1)S(1)}, u32[]{:S(2)}, u32[]{:S(2)}) collective-permute-start(bf16[14,64,128]{2,1,0:T(8,128)(2,1)S(1)} %get-tuple-element.40), channel_id=1, source_target_pairs={{1,0},{2,1},{3,2},{4,3},{5,4},{6,5},{7,6},{9,8},{10,9},{11,10},{12... | collective-permute-start | bytes 688136 | tf_op jit(solution)/shard_map/ppermute | solution.py:680
  29.0 24.5 %copy-start.23 = (f32[32]{0:T(128)S(1)}, f32[32]{0:T(128)}, u32[]{:S(2)}) copy-start(f32[32]{0:T(128)} %param.14) | copy-start | bytes 388
  29.0 24.5 %copy-start.24 = (f32[32]{0:T(128)S(1)}, f32[32]{0:T(128)}, u32[]{:S(2)}) copy-start(f32[32]{0:T(128)} %param.13) | copy-start | bytes 388
  29.0 24.5 %copy-start.25 = (f32[32]{0:T(128)S(1)}, f32[32]{0:T(128)}, u32[]{:S(2)}) copy-start(f32[32]{0:T(128)} %param.11) | copy-start | bytes 388
  29.0 24.5 %copy-start.26 = (f32[32]{0:T(128)S(1)}, f32[32]{0:T(128)}, u32[]{:S(2)}) copy-start(f32[32]{0:T(128)} %param.10) | copy-start | bytes 388
  29.9 4.4 %copy-start.20 = (bf16[14,64,128]{2,1,0:T(8,128)(2,1)}, bf16[14,64,128]{2,1,0:T(8,128)(2,1)S(1)}, u32[]{:S(2)}) copy-start(bf16[14,64,128]{2,1,0:T(8,128)(2,1)S(1)} %collective-permute-done.2.refs_0_.refs_5_.refs_8_) | copy-start | bytes 688132
  34.3 0.7 copy-start.21
  40.9 23.5 %all-to-all-start = ((f32[128,4,128]{2,1,0:T(4,128)}), f32[128,4,128]{2,1,0:T(4,128)S(1)}, u32[]{:S(2)}, u32[]{:S(2)}) async-start(f32[128,4,128]{2,1,0:T(4,128)} %get-tuple-element.41), calls=%async_computation | async-start | bytes 524288 | tf_op jit(solution)/shard_map/all_to_all | solution.py:684
  64.4 0.7 copy-start.19
  71.6 13.7 %all-to-all-start.1 = ((f32[128,1,128]{2,1,0:T(1,128)}), f32[128,1,128]{2,1,0:T(1,128)S(1)}, u32[]{:S(2)}, u32[]{:S(2)}) async-start(f32[128,1,128]{2,1,0:T(1,128)} %bitcast.54), calls=%async_computation.1 | async-start | bytes 131072 | tf_op jit(solution)/shard_map/all_to_all | solution.py:684
  75.7 32.8 %collective-permute-start.4 = (bf16[72,32,128]{2,1,0:T(8,128)(2,1)}, bf16[72,32,128]{2,1,0:T(8,128)(2,1)S(1)}, u32[]{:S(2)}, u32[]{:S(2)}) collective-permute-start(bf16[72,32,128]{2,1,0:T(8,128)(2,1)} %get-tuple-element.52), channel_id=1, source_target_pairs={{0,8},{8,16},{16,24},{24,32},{32,40},{40,48},{48,56},{56,64},{64,7... | collective-permute-start | bytes 1769480 | tf_op jit(solution)/shard_map/ppermute | solution.py:675
  79.1 29.4 %collective-permute-start.5 = (bf16[72,32,128]{2,1,0:T(8,128)(2,1)}, bf16[72,32,128]{2,1,0:T(8,128)(2,1)S(1)}, u32[]{:S(2)}, u32[]{:S(2)}) collective-permute-start(bf16[72,32,128]{2,1,0:T(8,128)(2,1)} %get-tuple-element.53), channel_id=1, source_target_pairs={{8,0},{16,8},{24,16},{32,24},{40,32},{48,40},{56,48},{64,56},{72,6... | collective-permute-start | bytes 1769480 | tf_op jit(solution)/shard_map/ppermute | solution.py:680
  85.3 0.6 copy-start.22
  89.7 18.9 %all-to-all-start.2 = ((f32[128,4,128]{2,1,0:T(4,128)}), f32[128,4,128]{2,1,0:T(4,128)S(1)}, u32[]{:S(2)}, u32[]{:S(2)}) async-start(f32[128,4,128]{2,1,0:T(4,128)} %get-tuple-element.51), calls=%async_computation.2 | async-start | bytes 524288 | tf_op jit(solution)/shard_map/all_to_all | solution.py:684
  108.5 0.7 copy-start.15
  108.5 0.9 copy-start.16
  108.5 1.1 copy-start.17
  117.9 19.6 %all-to-all-start.3 = ((f32[128,8,128]{2,1,0:T(8,128)}), f32[128,8,128]{2,1,0:T(8,128)S(1)}, u32[]{:S(2)}, u32[]{:S(2)}) async-start(f32[128,8,128]{2,1,0:T(8,128)} %get-tuple-element.60), calls=%async_computation.3 | async-start | bytes 1048576 | tf_op jit(solution)/shard_map/all_to_all | solution.py:684
  123.0 12.6 %collective-permute-start.6 = (bf16[34,32,128]{2,1,0:T(8,128)(2,1)}, bf16[34,32,128]{2,1,0:T(8,128)(2,1)S(1)}, u32[]{:S(2)}, u32[]{:S(2)}) collective-permute-start(bf16[34,32,128]{2,1,0:T(8,128)(2,1)} %get-tuple-element.62), channel_id=1, source_target_pairs={{0,8},{8,16},{16,24},{24,32},{32,40},{40,48},{48,56},{56,64},{64,7... | collective-permute-start | bytes 835592 | tf_op jit(solution)/shard_map/ppermute | solution.py:675
  126.3 11.2 %collective-permute-start.7 = (bf16[34,32,128]{2,1,0:T(8,128)(2,1)}, bf16[34,32,128]{2,1,0:T(8,128)(2,1)S(1)}, u32[]{:S(2)}, u32[]{:S(2)}) collective-permute-start(bf16[34,32,128]{2,1,0:T(8,128)(2,1)} %get-tuple-element.63), channel_id=1, source_target_pairs={{8,0},{16,8},{24,16},{32,24},{40,32},{48,40},{56,48},{64,56},{72,6... | collective-permute-start | bytes 835592 | tf_op jit(solution)/shard_map/ppermute | solution.py:680
  127.6 9.9 %copy-start.3 = (f32[32,4]{1,0:T(8,128)S(1)}, f32[32,4]{1,0:T(8,128)}, u32[]{:S(2)}) copy-start(f32[32,4]{1,0:T(8,128)} %copy.28.refs_2_.refs_1_.refs_3_) | copy-start | bytes 1540
  127.7 9.9 %copy-start.4 = (f32[32,128]{1,0:T(8,128)S(1)}, f32[32,128]{1,0:T(8,128)}, u32[]{:S(2)}) copy-start(f32[32,128]{1,0:T(8,128)} %get-tuple-element.48.refs_1_.refs_5_.refs_11_.refs_2_) | copy-start | bytes 49156
  127.7 9.9 %copy-start.5 = (s32[8]{0:T(128)S(1)}, s32[8]{0:T(128)}, u32[]{:S(2)}) copy-start(s32[8]{0:T(128)} %stack.66.refs_0_) | copy-start | bytes 100
  127.7 9.9 %copy-start.10 = (f32[4,128]{1,0:T(4,128)S(1)}, f32[4,128]{1,0:T(4,128)}, u32[]{:S(2)}) copy-start(f32[4,128]{1,0:T(4,128)} %get-tuple-element.61.refs_4_) | copy-start | bytes 6148
  127.7 9.9 %copy-start.14 = (f32[4,128]{1,0:T(4,128)S(1)}, f32[4,128]{1,0:T(4,128)}, u32[]{:S(2)}) copy-start(f32[4,128]{1,0:T(4,128)} %total.1.refs_8_.refs_5_) | copy-start | bytes 6148
  131.5 7.9 %copy-start.2 = (bf16[32,2,32,128]{3,0,1,2:T(8,128)(2,1)}, bf16[32,2,32,128]{3,0,1,2:T(8,128)(2,1)S(1)}, u32[]{:S(2)}) copy-start(bf16[32,2,32,128]{3,0,1,2:T(8,128)(2,1)S(1)} %copy.38) | copy-start | bytes 1572868
  135.7 3.8 %copy-start.8 = (bf16[34,32,128]{2,1,0:T(8,128)(2,1)}, bf16[34,32,128]{2,1,0:T(8,128)(2,1)S(1)}, u32[]{:S(2)}) copy-start(bf16[34,32,128]{2,1,0:T(8,128)(2,1)S(1)} %collective-permute-done.6.refs_6_) | copy-start | bytes 835588
  137.5 1.9 %copy-start.9 = (bf16[34,32,128]{2,1,0:T(8,128)(2,1)}, bf16[34,32,128]{2,1,0:T(8,128)(2,1)S(1)}, u32[]{:S(2)}) copy-start(bf16[34,32,128]{2,1,0:T(8,128)(2,1)S(1)} %collective-permute-done.7.refs_7_) | copy-start | bytes 835588
  139.5 0.6 copy-start.13
  140.1 21.5 %all-to-all-start.4 = ((bf16[128,8,128]{2,1,0:T(8,128)(2,1)}), bf16[128,8,128]{2,1,0:T(8,128)(2,1)S(1)}, u32[]{:S(2)}, u32[]{:S(2)}) async-start(bf16[128,8,128]{2,1,0:T(8,128)(2,1)} %bitcast.27), calls=%async_computation.4 | async-start | bytes 524288 | tf_op jit(solution)/shard_map/all_to_all | solution.py:684

commit v13 on v12

--- a/solution.py
+++ b/solution.py
@@ -252,26 +252,25 @@
                 put_tile(w_ref, dz, dy, lined[t * C : t * C + C])
 
 
-def flipped_kernel(need, send, k1, k2, b1, b2):
-    need(k1, k2)
+def flipped_kernel(need, send, k_ref, b_ref):
+    need(k_ref)
     row = lax.broadcasted_iota(jnp.int32, (C, 128), 0)
     col = lax.broadcasted_iota(jnp.int32, (C, 128), 1)
     eye = jnp.where(row == col, 1.0, 0.0)[:, 0:C].astype(BF16)
     zero = jnp.zeros((C, C), BF16)
-    for k_ref, b_ref in ((k1, b1), (k2, b2)):
-        stack = []
-        for t in range(9):
-            stack += [k_ref[18 + t], k_ref[9 + t], k_ref[t], zero]
-        turned = lax.dot_general(
-            eye,
-            jnp.concatenate(stack, axis=0),
-            (((1,), (1,)), ((), ())),
-            preferred_element_type=F32,
-        )
-        for dy in range(3):
-            for dz in range(3):
-                t = 8 - dy * 3 - dz
-                put_tile(b_ref, dz, dy, turned[:, t * 128 : t * 128 + 128])
+    stack = []
+    for t in range(9):
+        stack += [k_ref[18 + t], k_ref[9 + t], k_ref[t], zero]
+    turned = lax.dot_general(
+        eye,
+        jnp.concatenate(stack, axis=0),
+        (((1,), (1,)), ((), ())),
+        preferred_element_type=F32,
+    )
+    for dy in range(3):
+        for dz in range(3):
+            t = 8 - dy * 3 - dz
+            put_tile(b_ref, dz, dy, turned[:, t * 128 : t * 128 + 128])
 
 
 def put_tile(ref, dz, dy, tile):
@@ -722,14 +721,13 @@
     ]
     matrices = [sh((192, 384), BF16)] * 2
     w1, w2 = call(weights_kernel, taps, matrices, "weights", smem_first=False)
-    b1, b2 = call(flipped_kernel, taps, matrices, "flipped", smem_first=False)
     y_up, y_down = call(
         pack_kernel,
         (x_low, x_high, own, cot),
         [sh((14, 64, 128), BF16)] * 2,
         "pack",
         smem_first=False,
-        after=(w1, b1),
+        after=(w1,),
         near=2,
         grant=16,
     )
@@ -765,15 +763,15 @@
     )
     h2_low, h2_high = up(high, GX), down(low, GX)
     r2 = share(m2)
-    (x1,) = call(
-        total_kernel, (r1,), [sh((4, 128), F32)], "total", smem_first=False, after=(st1,)
+    (b2,) = call(
+        flipped_kernel, taps[1:], matrices[1:], "flipped_two", smem_first=False, after=(st1,)
     )
     m3, st2 = call(
         lambda *refs: third_kernel(cells, *refs),
         (place, r2, gb, cot, h2, st1, x1_own, xh),
         [four, stats],
         "slope_two",
-        after=(x1,),
+        after=(b2,),
     )
     r3 = share(m3)
     s2, n2, a1 = call(
@@ -800,6 +798,10 @@
     s_low, s_high = up(high, GX), down(low, GX)
     r4 = share(m4)
 
+    (b1,) = call(
+        flipped_kernel, taps[:1], matrices[1:], "flipped_one", smem_first=False, after=(slope1,)
+    )
+    (x1,) = call(total_kernel, (r1,), [sh((4, 128), F32)], "total", smem_first=False, after=(b1,))
     (rows_out,) = call(
         output_kernel,
         (st2, gb, h2),

time: 164 us -> 165 us (level)
  Pallas kernels: 54.1 us -> 56 us
    ppermute x4, waiting for transfers between devices: 5.9 us -> 2.97 us  [up(): return lax.ppermute(values, axes, [(i, i + 1) for i in range(count - 1)])]
    ppermute x4, waiting for transfers between devices: 10.3 us -> 12.7 us  [down(): return lax.ppermute(values, axes, [(i + 1, i) for i in range(count - 1)])]
    pallas_call x14 -> x15, Pallas kernels: 54.1 us -> 56 us  [call(): pl.pallas_call(body, out_shape=outs, in_specs=[SM] * lead + [pl.BlockSpec...]
  transfers between devices with their start and end apart: 13 -> 13, of which waited for: 10 -> 10; matrix products, arithmetic and copies ran while one was open for 2% -> 1% of each run, Pallas kernels for 17% -> 18%
where the time goes in v13:
time: 165 us; the launch traced here: 164 us
  starting transfers between devices  63.4 us (38%)
  Pallas kernels  56 us (34%)
  waiting for transfers between devices  34.1 us (21%)
  local copies, waits for them, and re-layouts  9 us (5%)
    pallas_call x15, Pallas kernels, call(): pl.pallas_call(body, out_shape=outs, in_specs=[SM] * lead + [pl.BlockSpec...  56 us
    all_to_all x5, starting transfers between devices, share(): return lax.all_to_all(msg, ALL[::-1], 0, 0, tiled=True)  40.7 us
    all_to_all x5, waiting for transfers between devices, share(): return lax.all_to_all(msg, ALL[::-1], 0, 0, tiled=True)  18.4 us
    ppermute x4, starting transfers between devices, up(): return lax.ppermute(values, axes, [(i, i + 1) for i in range(count - 1)])  16.9 us
    ppermute x4, waiting for transfers between devices, down(): return lax.ppermute(values, axes, [(i + 1, i) for i in range(count - 1)])  12.7 us
    ppermute x4, starting transfers between devices, down(): return lax.ppermute(values, axes, [(i + 1, i) for i in range(count - 1)])  5.8 us
    unnamed x54, local copies, waits for them, and re-layouts  5.52 us
  transfers between devices with their start and end apart: 13, of which 10 were waited for; matrix products, arithmetic and copies ran while one was open for 1% of the time, Pallas kernels for 18%

profile of v13, /device:TPU:1, one launch (start us, length us, event | category | flops | bytes accessed | tf_op | source)
XLA Modules:
  0.0 163.9 jit_solution(126768786006758906)
XLA Ops:
  0.6 1.4 copy.26
  2.1 0.0 copy-start.1
  2.1 1.3 collective-permute-start.1
  3.4 4.7 %collective-permute-start = (bf16[32,64,128]{2,1,0:T(8,128)(2,1)S(1)}, bf16[32,64,128]{2,1,0:T(8,128)(2,1)S(1)}, u32[]{:S(2)}, u32[]{:S(2)}) collective-permute-start(bf16[32,64,128]{2,1,0:T(8,128)(2,1)S(1)} %bitcast.44), channel_id=1, source_target_pairs={{0,8},{8,16},{16,24},{24,32},{32,40},{40,48},{48,56},{56,64},{64,7... | collective-permute-start | bytes 1572872 | tf_op jit(solution)/shard_map/ppermute | solution.py:674
  8.1 0.3 copy.27
  8.5 0.0 copy-start
  8.5 2.4 %weights.1 = (bf16[192,384]{1,0:T(8,128)(2,1)}, bf16[192,384]{1,0:T(8,128)(2,1)}) custom-call(bf16[27,32,32]{2,1,0:T(8,128)(2,1)} %bitcast.61, bf16[27,32,32]{2,1,0:T(8,128)(2,1)} %bitcast.59), custom_call_target="tpu_custom_call" | custom-call | flops 2000000000 | bytes 6000000 | tf_op jit(solution)/shard_map/weights/pallas_call | solution.py:650
  10.9 6.5 %collective-permute-done.1.refs_1_.refs_5_ = bf16[32,64,128]{2,1,0:T(8,128)(2,1)S(1)} collective-permute-done((bf16[32,64,128]{2,1,0:T(8,128)(2,1)S(1)}, bf16[32,64,128]{2,1,0:T(8,128)(2,1)S(1)}, u32[]{:S(2)}, u32[]{:S(2)}) %collective-permute-start.1) | collective-permute-done | bytes 524320 | tf_op jit(solution)/shard_map/ppermute | solution.py:679
  17.4 0.9 collective-permute-done.refs_0_.refs_4_
  18.2 1.1 copy-done.11
  19.3 2.1 %pack.1 = (bf16[14,64,128]{2,1,0:T(8,128)(2,1)S(1)}, bf16[14,64,128]{2,1,0:T(8,128)(2,1)S(1)}) custom-call(bf16[32,64,128]{2,1,0:T(8,128)(2,1)S(1)} %collective-permute-done.refs_0_.refs_4_, bf16[32,64,128]{2,1,0:T(8,128)(2,1)S(1)} %collective-permute-done.1.refs_1_.refs_5_, bf16[32,64,128]{2,1,0:T(8,128)(2,1)S(1)} %bitcast.45, ...), custom_call_target="tpu_custom_call" | custom-call | flops 2000000000 | bytes 6000000 | tf_op jit(solution)/shard_map/pack/pallas_call | solution.py:650
  21.4 5.5 %collective-permute-start.2 = (bf16[14,64,128]{2,1,0:T(8,128)(2,1)S(1)}, bf16[14,64,128]{2,1,0:T(8,128)(2,1)S(1)}, u32[]{:S(2)}, u32[]{:S(2)}) collective-permute-start(bf16[14,64,128]{2,1,0:T(8,128)(2,1)S(1)} %get-tuple-element.36), channel_id=1, source_target_pairs={{0,1},{1,2},{2,3},{3,4},{4,5},{5,6},{6,7},{8,9},{9,10},{10,11},{11... | collective-permute-start | bytes 688136 | tf_op jit(solution)/shard_map/ppermute | solution.py:674
  27.0 1.9 %collective-permute-start.3 = (bf16[14,64,128]{2,1,0:T(8,128)(2,1)S(1)}, bf16[14,64,128]{2,1,0:T(8,128)(2,1)S(1)}, u32[]{:S(2)}, u32[]{:S(2)}) collective-permute-start(bf16[14,64,128]{2,1,0:T(8,128)(2,1)S(1)} %get-tuple-element.37), channel_id=1, source_target_pairs={{1,0},{2,1},{3,2},{4,3},{5,4},{6,5},{7,6},{9,8},{10,9},{11,10},{12... | collective-permute-start | bytes 688136 | tf_op jit(solution)/shard_map/ppermute | solution.py:679
  29.0 0.0 copy-start.23
  29.0 0.0 copy-start.24
  29.0 0.0 copy-start.25
  29.0 0.0 copy-start.26
  29.0 0.9 collective-permute-done.2.refs_0_.refs_5_.refs_8_
  29.9 4.4 %collective-permute-done.3.refs_1_.refs_6_.refs_9_ = bf16[14,64,128]{2,1,0:T(8,128)(2,1)S(1)} collective-permute-done((bf16[14,64,128]{2,1,0:T(8,128)(2,1)S(1)}, bf16[14,64,128]{2,1,0:T(8,128)(2,1)S(1)}, u32[]{:S(2)}, u32[]{:S(2)}) %collective-permute-start.3) | collective-permute-done | bytes 229408 | tf_op jit(solution)/shard_map/ppermute | solution.py:679
  34.3 0.7 copy-done.21
  35.0 5.9 %conv_one.1 = (bf16[40,128,128]{2,1,0:T(8,128)(2,1)}, f32[38,128,128]{2,1,0:T(8,128)}, f32[128,4,128]{2,1,0:T(4,128)}, f32[16,128]{1,0:T(8,128)}, f32[32,128]{1,0:T(8,128)}) custom-call(bf16[14,64,128]{2,1,0:T(8,128)(2,1)} %copy-done.20, bf16[14,64,128]{2,1,0:T(8,128)(2,1)} %copy-done.21, bf16[192,384]{1,0:T(8,128)(2,1)} %get-tuple-element.35.refs_4_.refs_2_, ...), custom_call_target="tpu_custom_call" | custom-call | flops 2000000000 | bytes 6000000 | tf_op jit(solution)/shard_map/conv_one/pallas_call | solution.py:650
  40.9 12.6 %all-to-all-start = ((f32[128,4,128]{2,1,0:T(4,128)}), f32[128,4,128]{2,1,0:T(4,128)S(1)}, u32[]{:S(2)}, u32[]{:S(2)}) async-start(f32[128,4,128]{2,1,0:T(4,128)} %get-tuple-element.38), calls=%async_computation | async-start | bytes 524288 | tf_op jit(solution)/shard_map/all_to_all | solution.py:683
  53.6 0.7 copy.28.refs_2_.refs_1_.refs_3_
  54.3 0.7 stack.66.refs_0_
  54.9 3.8 %hidden_features.1.refs_8_.refs_7_ = f32[9,32,128]{2,1,0:T(8,128)} custom-call(f32[32,128]{1,0:T(8,128)} %get-tuple-element.41.refs_0_, f32[38,128,128]{2,1,0:T(8,128)} %get-tuple-element.39.refs_1_.refs_3_.refs_12_.refs_4_, bf16[40,128,128]{2,1,0:T(8,128)(2,1)} %get-tuple-element.42.refs_2_.refs_13_), custom_call_target="tpu_custom_call" | custom-call | flops 2000000000 | bytes 6000000 | tf_op jit(solution)/shard_map/hidden_features/pallas_call | solution.py:650
  58.8 5.7 %all-to-all-done.refs_1_.refs_0_ = f32[128,4,128]{2,1,0:T(4,128)S(1)} async-done(((f32[128,4,128]{2,1,0:T(4,128)}), f32[128,4,128]{2,1,0:T(4,128)S(1)}, u32[]{:S(2)}, u32[]{:S(2)}) %all-to-all-start) | async-done | bytes 262176 | tf_op jit(solution)/shard_map/all_to_all | solution.py:683
  64.4 0.7 copy-done.19
  65.1 6.4 %conv_two.1 = (bf16[38,128,128]{2,1,0:T(8,128)(2,1)}, f32[36,64,128]{2,1,0:T(8,128)}, bf16[72,32,128]{2,1,0:T(8,128)(2,1)}, bf16[72,32,128]{2,1,0:T(8,128)(2,1)}, f32[128,128]{1,0:T(8,128)}, /*index=5*/f32[32,128]{1,0:T(8,128)}) custom-call(s32[8]{0:T(128)} %stack.66.refs_0_, f32[128,4,128]{2,1,0:T(4,128)} %copy-done.19, ...), custom_call_target="tpu_custom_call" | custom-call | flops 2000000000 | bytes 6000000 | tf_op jit(solution)/shard_map/conv_two/pallas_call | solution.py:650
  71.6 4.1 %all-to-all-start.1 = ((f32[128,1,128]{2,1,0:T(1,128)}), f32[128,1,128]{2,1,0:T(1,128)S(1)}, u32[]{:S(2)}, u32[]{:S(2)}) async-start(f32[128,1,128]{2,1,0:T(1,128)} %bitcast.54), calls=%async_computation.1 | async-start | bytes 131072 | tf_op jit(solution)/shard_map/all_to_all | solution.py:683
  75.7 3.4 %collective-permute-start.4 = (bf16[72,32,128]{2,1,0:T(8,128)(2,1)}, bf16[72,32,128]{2,1,0:T(8,128)(2,1)S(1)}, u32[]{:S(2)}, u32[]{:S(2)}) collective-permute-start(bf16[72,32,128]{2,1,0:T(8,128)(2,1)} %get-tuple-element.49), channel_id=1, source_target_pairs={{0,8},{8,16},{16,24},{24,32},{32,40},{40,48},{48,56},{56,64},{64,7... | collective-permute-start | bytes 1769480 | tf_op jit(solution)/shard_map/ppermute | solution.py:674
  79.1 1.3 collective-permute-start.5
  80.4 2.0 %flipped_two.1.refs_8_.refs_10_ = bf16[192,384]{1,0:T(8,128)(2,1)} custom-call(bf16[27,32,32]{2,1,0:T(8,128)(2,1)} %bitcast.60, f32[32,128]{1,0:T(8,128)} %get-tuple-element.45.refs_1_.refs_5_.refs_11_.refs_2_), custom_call_target="tpu_custom_call" | custom-call | flops 2000000000 | bytes 6000000 | tf_op jit(solution)/shard_map/flipped_two/pallas_call | solution.py:650
  82.4 2.9 %all-to-all-done.1 = f32[128,1,128]{2,1,0:T(1,128)S(1)} async-done(((f32[128,1,128]{2,1,0:T(1,128)}), f32[128,1,128]{2,1,0:T(1,128)S(1)}, u32[]{:S(2)}, u32[]{:S(2)}) %all-to-all-start.1) | async-done | bytes 65568 | tf_op jit(solution)/shard_map/all_to_all | solution.py:683
  85.3 0.6 copy-done.22
  85.9 3.7 %slope_two.1 = (f32[128,4,128]{2,1,0:T(4,128)}, f32[32,128]{1,0:T(8,128)}) custom-call(s32[8]{0:T(128)} %stack.66.refs_0_, f32[128,128]{1,0:T(8,128)} %bitcast.53, f32[32,4]{1,0:T(8,128)} %copy.28.refs_2_.refs_1_.refs_3_, bf16[32,64,128]{2,1,0:T(8,128)(2,1)} %bitcast.40, f32[36,64,128]{2,1,0:T(8,128)} %get-tuple-element.44.refs_4_.refs_2_, ...), custom_call_target="tpu_custom_call" | custom-call | flops 2000000000 | bytes 6000000 | tf_op jit(solution)/shard_map/slope_two/pallas_call | solution.py:650
  89.7 8.2 %all-to-all-start.2 = ((f32[128,4,128]{2,1,0:T(4,128)}), f32[128,4,128]{2,1,0:T(4,128)S(1)}, u32[]{:S(2)}, u32[]{:S(2)}) async-start(f32[128,4,128]{2,1,0:T(4,128)} %get-tuple-element.48), calls=%async_computation.2 | async-start | bytes 524288 | tf_op jit(solution)/shard_map/all_to_all | solution.py:683
  97.9 6.2 %active_sums.1 = (f32[9,32,128]{2,1,0:T(8,128)}, f32[9,32,128]{2,1,0:T(8,128)}, f32[16,128]{1,0:T(8,128)}) custom-call(f32[32,128]{1,0:T(8,128)} %get-tuple-element.47.refs_0_.refs_2_, f32[32,4]{1,0:T(8,128)} %copy.28.refs_2_.refs_1_.refs_3_, f32[36,64,128]{2,1,0:T(8,128)} %get-tuple-element.44.refs_4_.refs_2_, bf16[32,64,128]{2,1,0:T(8,128)(2,1)} %bitcast.41, ...), custom_call_target="tpu_custom_call" | custom-call | flops 2000000000 | bytes 6000000 | tf_op jit(solution)/shard_map/active_sums/pallas_call | solution.py:650
  104.1 4.7 %all-to-all-done.2.refs_1_ = f32[128,4,128]{2,1,0:T(4,128)S(1)} async-done(((f32[128,4,128]{2,1,0:T(4,128)}), f32[128,4,128]{2,1,0:T(4,128)S(1)}, u32[]{:S(2)}, u32[]{:S(2)}) %all-to-all-start.2) | async-done | bytes 262176 | tf_op jit(solution)/shard_map/all_to_all | solution.py:683
  108.8 0.0 collective-permute-done.4.refs_5_
  108.8 0.0 collective-permute-done.5.refs_6_
  108.8 0.7 copy-done.14
  109.5 0.2 copy-done.15
  109.7 0.2 copy-done.16
  109.9 8.3 %back_two.1 = (f32[34,64,128]{2,1,0:T(8,128)}, bf16[34,32,128]{2,1,0:T(8,128)(2,1)}, bf16[34,32,128]{2,1,0:T(8,128)(2,1)}, f32[128,8,128]{2,1,0:T(8,128)}, f32[4,128]{1,0:T(4,128)}) custom-call(s32[8]{0:T(128)} %stack.66.refs_0_, f32[128,4,128]{2,1,0:T(4,128)} %copy-done.14, f32[32,128]{1,0:T(8,128)} %get-tuple-element.47.refs_0_.refs_2_, ...), custom_call_target="tpu_custom_call" | custom-call | flops 2000000000 | bytes 6000000 | tf_op jit(solution)/shard_map/back_two/pallas_call | solution.py:650
  118.2 5.1 %all-to-all-start.3 = ((f32[128,8,128]{2,1,0:T(8,128)}), f32[128,8,128]{2,1,0:T(8,128)S(1)}, u32[]{:S(2)}, u32[]{:S(2)}) async-start(f32[128,8,128]{2,1,0:T(8,128)} %get-tuple-element.56), calls=%async_computation.3 | async-start | bytes 1048576 | tf_op jit(solution)/shard_map/all_to_all | solution.py:683
  123.3 3.3 %collective-permute-start.6 = (bf16[34,32,128]{2,1,0:T(8,128)(2,1)}, bf16[34,32,128]{2,1,0:T(8,128)(2,1)S(1)}, u32[]{:S(2)}, u32[]{:S(2)}) collective-permute-start(bf16[34,32,128]{2,1,0:T(8,128)(2,1)} %get-tuple-element.58), channel_id=1, source_target_pairs={{0,8},{8,16},{16,24},{24,32},{32,40},{40,48},{48,56},{56,64},{64,7... | collective-permute-start | bytes 835592 | tf_op jit(solution)/shard_map/ppermute | solution.py:674
  126.6 1.3 collective-permute-start.7
  127.9 2.4 %output.1 = bf16[32,64,128]{2,1,0:T(8,128)(2,1)} custom-call(f32[32,128]{1,0:T(8,128)} %get-tuple-element.47.refs_0_.refs_2_, f32[32,4]{1,0:T(8,128)} %copy.28.refs_2_.refs_1_.refs_3_, f32[36,64,128]{2,1,0:T(8,128)} %get-tuple-element.44.refs_4_.refs_2_, f32[34,64,128]{2,1,0:T(8,128)} %get-tuple-element.55.refs_3_.refs_1_.refs_5_), custom_call_target="tpu_custom_call" | custom-call | flops 2000000000 | bytes 6000000 | tf_op jit(solution)/shard_map/output/pallas_call | solution.py:650
  130.3 0.0 copy-start.18
  130.3 2.1 %flipped_one.1.refs_1_.refs_8_ = bf16[192,384]{1,0:T(8,128)(2,1)} custom-call(bf16[27,32,32]{2,1,0:T(8,128)(2,1)} %bitcast.62, f32[34,64,128]{2,1,0:T(8,128)} %get-tuple-element.55.refs_3_.refs_1_.refs_5_), custom_call_target="tpu_custom_call" | custom-call | flops 2000000000 | bytes 6000000 | tf_op jit(solution)/shard_map/flipped_one/pallas_call | solution.py:650
  132.4 0.3 copy.38
  132.8 0.0 copy-start.2
  132.8 0.0 copy-start.10
  132.8 1.9 %total.1.refs_5_ = f32[4,128]{1,0:T(4,128)} custom-call(f32[128,4,128]{2,1,0:T(4,128)} %copy-done.19, bf16[192,384]{1,0:T(8,128)(2,1)} %flipped_one.1.refs_1_.refs_8_), custom_call_target="tpu_custom_call" | custom-call | flops 2000000000 | bytes 6000000 | tf_op jit(solution)/shard_map/total/pallas_call | solution.py:650
  134.7 1.2 collective-permute-done.6.refs_6_
  135.9 1.8 %collective-permute-done.7.refs_7_ = bf16[34,32,128]{2,1,0:T(8,128)(2,1)S(1)} collective-permute-done((bf16[34,32,128]{2,1,0:T(8,128)(2,1)}, bf16[34,32,128]{2,1,0:T(8,128)(2,1)S(1)}, u32[]{:S(2)}, u32[]{:S(2)}) %collective-permute-start.7) | collective-permute-done | bytes 278560 | tf_op jit(solution)/shard_map/ppermute | solution.py:679
  137.8 0.0 all-to-all-done.3.refs_1_
  137.8 0.6 copy-done.13
  138.5 1.9 %own_rows.1 = (bf16[1024,128]{1,0:T(8,128)(2,1)}, f32[4,32]{1,0:T(4,128)}, f32[8,128]{1,0:T(8,128)S(1)}) custom-call(s32[8]{0:T(128)S(1)} %copy-done.5, f32[128,8,128]{2,1,0:T(8,128)S(1)} %all-to-all-done.3.refs_1_, f32[32,128]{1,0:T(8,128)S(1)} %copy-done.4, f32[32,4]{1,0:T(8,128)S(1)} %copy-done.3, f32[4,128]{1,0:T(4,128)S(1)} %copy-done.10, ...), custom_call_target="tpu_custom_call" | custom-call | flops 2000000000 | bytes 6000000 | tf_op jit(solution)/shard_map/own_rows/pallas_call | solution.py:650
  140.4 0.6 copy-done.12
  141.0 10.6 %all-to-all-start.4 = ((bf16[128,8,128]{2,1,0:T(8,128)(2,1)}), bf16[128,8,128]{2,1,0:T(8,128)(2,1)S(1)}, u32[]{:S(2)}, u32[]{:S(2)}) async-start(bf16[128,8,128]{2,1,0:T(8,128)(2,1)} %bitcast.27), calls=%async_computation.4 | async-start | bytes 524288 | tf_op jit(solution)/shard_map/all_to_all | solution.py:683
  151.6 5.7 %back_one.1 = bf16[32,2,32,128]{3,2,1,0:T(8,128)(2,1)} custom-call(s32[8]{0:T(128)} %stack.66.refs_0_, f32[8,128]{1,0:T(8,128)} %copy-done.12, f32[32,128]{1,0:T(8,128)} %get-tuple-element.45.refs_1_.refs_5_.refs_11_.refs_2_, f32[32,4]{1,0:T(8,128)} %copy.28.refs_2_.refs_1_.refs_3_, f32[38,128,128]{2,1,0:T(8,128)} %get-tuple-element.39.refs_1_.refs_3_.refs_12_.refs_4_, ...), custom_call_target="tpu_custom_call" | custom-call | flops 2000000000 | bytes 6000000 | tf_op jit(solution)/shard_map/back_one/pallas_call | solution.py:650
  157.2 5.2 %all-to-all-done.4 = bf16[128,8,128]{2,1,0:T(8,128)(2,1)S(1)} async-done(((bf16[128,8,128]{2,1,0:T(8,128)(2,1)}), bf16[128,8,128]{2,1,0:T(8,128)(2,1)S(1)}, u32[]{:S(2)}, u32[]{:S(2)}) %all-to-all-start.4) | async-done | bytes 262176 | tf_op jit(solution)/shard_map/all_to_all | solution.py:683
  162.5 1.2 finish.1
  (37 shorter events, 0.1 us)
Async XLA Ops:
  0.6 7.5 %copy-start.17 = (bf16[32,2,32,128]{3,2,1,0:T(8,128)(2,1)S(1)}, bf16[32,2,32,128]{3,2,1,0:T(8,128)(2,1)}, u32[]{:S(2)}) copy-start(bf16[32,2,32,128]{3,2,1,0:T(8,128)(2,1)} %param.15) | copy-start | bytes 1572868
  2.1 16.2 %copy-start.1 = (bf16[32,2,32,128]{3,2,1,0:T(8,128)(2,1)}, bf16[32,2,32,128]{3,2,1,0:T(8,128)(2,1)S(1)}, u32[]{:S(2)}) copy-start(bf16[32,2,32,128]{3,2,1,0:T(8,128)(2,1)S(1)} %copy.26) | copy-start | bytes 1572868
  2.1 15.3 %collective-permute-start.1 = (bf16[32,64,128]{2,1,0:T(8,128)(2,1)S(1)}, bf16[32,64,128]{2,1,0:T(8,128)(2,1)S(1)}, u32[]{:S(2)}, u32[]{:S(2)}) collective-permute-start(bf16[32,64,128]{2,1,0:T(8,128)(2,1)S(1)} %bitcast.43), channel_id=1, source_target_pairs={{8,0},{16,8},{24,16},{32,24},{40,32},{48,40},{56,48},{64,56},{72,6... | collective-permute-start | bytes 1572872 | tf_op jit(solution)/shard_map/ppermute | solution.py:679
  3.4 14.8 %collective-permute-start = (bf16[32,64,128]{2,1,0:T(8,128)(2,1)S(1)}, bf16[32,64,128]{2,1,0:T(8,128)(2,1)S(1)}, u32[]{:S(2)}, u32[]{:S(2)}) collective-permute-start(bf16[32,64,128]{2,1,0:T(8,128)(2,1)S(1)} %bitcast.44), channel_id=1, source_target_pairs={{0,8},{8,16},{16,24},{24,32},{32,40},{40,48},{48,56},{56,64},{64,7... | collective-permute-start | bytes 1572872 | tf_op jit(solution)/shard_map/ppermute | solution.py:674
  8.5 9.8 %copy-start = (bf16[32,2,32,128]{3,2,1,0:T(8,128)(2,1)}, bf16[32,2,32,128]{3,2,1,0:T(8,128)(2,1)S(1)}, u32[]{:S(2)}) copy-start(bf16[32,2,32,128]{3,2,1,0:T(8,128)(2,1)S(1)} %copy.27) | copy-start | bytes 1572868
  17.4 4.0 %copy-start.6 = (bf16[32,64,128]{2,1,0:T(8,128)(2,1)}, bf16[32,64,128]{2,1,0:T(8,128)(2,1)S(1)}, u32[]{:S(2)}) copy-start(bf16[32,64,128]{2,1,0:T(8,128)(2,1)S(1)} %collective-permute-done.1.refs_1_.refs_5_) | copy-start | bytes 1572868
  18.2 3.2 %copy-start.7 = (bf16[32,64,128]{2,1,0:T(8,128)(2,1)}, bf16[32,64,128]{2,1,0:T(8,128)(2,1)S(1)}, u32[]{:S(2)}) copy-start(bf16[32,64,128]{2,1,0:T(8,128)(2,1)S(1)} %collective-permute-done.refs_0_.refs_4_) | copy-start | bytes 1572868
  18.2 1.1 copy-start.11
  21.4 8.5 %collective-permute-start.2 = (bf16[14,64,128]{2,1,0:T(8,128)(2,1)S(1)}, bf16[14,64,128]{2,1,0:T(8,128)(2,1)S(1)}, u32[]{:S(2)}, u32[]{:S(2)}) collective-permute-start(bf16[14,64,128]{2,1,0:T(8,128)(2,1)S(1)} %get-tuple-element.36), channel_id=1, source_target_pairs={{0,1},{1,2},{2,3},{3,4},{4,5},{5,6},{6,7},{8,9},{9,10},{10,11},{11... | collective-permute-start | bytes 688136 | tf_op jit(solution)/shard_map/ppermute | solution.py:674
  27.0 7.3 %collective-permute-start.3 = (bf16[14,64,128]{2,1,0:T(8,128)(2,1)S(1)}, bf16[14,64,128]{2,1,0:T(8,128)(2,1)S(1)}, u32[]{:S(2)}, u32[]{:S(2)}) collective-permute-start(bf16[14,64,128]{2,1,0:T(8,128)(2,1)S(1)} %get-tuple-element.37), channel_id=1, source_target_pairs={{1,0},{2,1},{3,2},{4,3},{5,4},{6,5},{7,6},{9,8},{10,9},{11,10},{12... | collective-permute-start | bytes 688136 | tf_op jit(solution)/shard_map/ppermute | solution.py:679
  29.0 24.5 %copy-start.23 = (f32[32]{0:T(128)S(1)}, f32[32]{0:T(128)}, u32[]{:S(2)}) copy-start(f32[32]{0:T(128)} %param.14) | copy-start | bytes 388
  29.0 24.5 %copy-start.24 = (f32[32]{0:T(128)S(1)}, f32[32]{0:T(128)}, u32[]{:S(2)}) copy-start(f32[32]{0:T(128)} %param.13) | copy-start | bytes 388
  29.0 24.5 %copy-start.25 = (f32[32]{0:T(128)S(1)}, f32[32]{0:T(128)}, u32[]{:S(2)}) copy-start(f32[32]{0:T(128)} %param.11) | copy-start | bytes 388
  29.0 24.5 %copy-start.26 = (f32[32]{0:T(128)S(1)}, f32[32]{0:T(128)}, u32[]{:S(2)}) copy-start(f32[32]{0:T(128)} %param.10) | copy-start | bytes 388
  29.9 4.4 %copy-start.20 = (bf16[14,64,128]{2,1,0:T(8,128)(2,1)}, bf16[14,64,128]{2,1,0:T(8,128)(2,1)S(1)}, u32[]{:S(2)}) copy-start(bf16[14,64,128]{2,1,0:T(8,128)(2,1)S(1)} %collective-permute-done.2.refs_0_.refs_5_.refs_8_) | copy-start | bytes 688132
  34.3 0.7 copy-start.21
  40.9 23.5 %all-to-all-start = ((f32[128,4,128]{2,1,0:T(4,128)}), f32[128,4,128]{2,1,0:T(4,128)S(1)}, u32[]{:S(2)}, u32[]{:S(2)}) async-start(f32[128,4,128]{2,1,0:T(4,128)} %get-tuple-element.38), calls=%async_computation | async-start | bytes 524288 | tf_op jit(solution)/shard_map/all_to_all | solution.py:683
  64.4 0.7 copy-start.19
  71.6 13.7 %all-to-all-start.1 = ((f32[128,1,128]{2,1,0:T(1,128)}), f32[128,1,128]{2,1,0:T(1,128)S(1)}, u32[]{:S(2)}, u32[]{:S(2)}) async-start(f32[128,1,128]{2,1,0:T(1,128)} %bitcast.54), calls=%async_computation.1 | async-start | bytes 131072 | tf_op jit(solution)/shard_map/all_to_all | solution.py:683
  75.7 33.1 %collective-permute-start.4 = (bf16[72,32,128]{2,1,0:T(8,128)(2,1)}, bf16[72,32,128]{2,1,0:T(8,128)(2,1)S(1)}, u32[]{:S(2)}, u32[]{:S(2)}) collective-permute-start(bf16[72,32,128]{2,1,0:T(8,128)(2,1)} %get-tuple-element.49), channel_id=1, source_target_pairs={{0,8},{8,16},{16,24},{24,32},{32,40},{40,48},{48,56},{56,64},{64,7... | collective-permute-start | bytes 1769480 | tf_op jit(solution)/shard_map/ppermute | solution.py:674
  79.1 29.7 %collective-permute-start.5 = (bf16[72,32,128]{2,1,0:T(8,128)(2,1)}, bf16[72,32,128]{2,1,0:T(8,128)(2,1)S(1)}, u32[]{:S(2)}, u32[]{:S(2)}) collective-permute-start(bf16[72,32,128]{2,1,0:T(8,128)(2,1)} %get-tuple-element.50), channel_id=1, source_target_pairs={{8,0},{16,8},{24,16},{32,24},{40,32},{48,40},{56,48},{64,56},{72,6... | collective-permute-start | bytes 1769480 | tf_op jit(solution)/shard_map/ppermute | solution.py:679
  85.3 0.6 copy-start.22
  89.7 19.1 %all-to-all-start.2 = ((f32[128,4,128]{2,1,0:T(4,128)}), f32[128,4,128]{2,1,0:T(4,128)S(1)}, u32[]{:S(2)}, u32[]{:S(2)}) async-start(f32[128,4,128]{2,1,0:T(4,128)} %get-tuple-element.48), calls=%async_computation.2 | async-start | bytes 524288 | tf_op jit(solution)/shard_map/all_to_all | solution.py:683
  108.8 0.7 copy-start.14
  108.8 0.9 copy-start.15
  108.8 1.1 copy-start.16
  118.2 19.6 %all-to-all-start.3 = ((f32[128,8,128]{2,1,0:T(8,128)}), f32[128,8,128]{2,1,0:T(8,128)S(1)}, u32[]{:S(2)}, u32[]{:S(2)}) async-start(f32[128,8,128]{2,1,0:T(8,128)} %get-tuple-element.56), calls=%async_computation.3 | async-start | bytes 1048576 | tf_op jit(solution)/shard_map/all_to_all | solution.py:683
  123.3 12.6 %collective-permute-start.6 = (bf16[34,32,128]{2,1,0:T(8,128)(2,1)}, bf16[34,32,128]{2,1,0:T(8,128)(2,1)S(1)}, u32[]{:S(2)}, u32[]{:S(2)}) collective-permute-start(bf16[34,32,128]{2,1,0:T(8,128)(2,1)} %get-tuple-element.58), channel_id=1, source_target_pairs={{0,8},{8,16},{16,24},{24,32},{32,40},{40,48},{48,56},{56,64},{64,7... | collective-permute-start | bytes 835592 | tf_op jit(solution)/shard_map/ppermute | solution.py:674
  126.6 11.2 %collective-permute-start.7 = (bf16[34,32,128]{2,1,0:T(8,128)(2,1)}, bf16[34,32,128]{2,1,0:T(8,128)(2,1)S(1)}, u32[]{:S(2)}, u32[]{:S(2)}) collective-permute-start(bf16[34,32,128]{2,1,0:T(8,128)(2,1)} %get-tuple-element.59), channel_id=1, source_target_pairs={{8,0},{16,8},{24,16},{32,24},{40,32},{48,40},{56,48},{64,56},{72,6... | collective-permute-start | bytes 835592 | tf_op jit(solution)/shard_map/ppermute | solution.py:679
  130.3 2.1 %copy-start.18 = (bf16[32,64,128]{2,1,0:T(8,128)(2,1)S(1)}, bf16[32,64,128]{2,1,0:T(8,128)(2,1)}, u32[]{:S(2)}) copy-start(bf16[32,64,128]{2,1,0:T(8,128)(2,1)} %output.1) | copy-start | bytes 1572868
  132.8 5.0 %copy-start.2 = (bf16[32,2,32,128]{3,0,1,2:T(8,128)(2,1)}, bf16[32,2,32,128]{3,0,1,2:T(8,128)(2,1)S(1)}, u32[]{:S(2)}) copy-start(bf16[32,2,32,128]{3,0,1,2:T(8,128)(2,1)S(1)} %copy.38) | copy-start | bytes 1572868
  132.8 5.0 %copy-start.3 = (f32[32,4]{1,0:T(8,128)S(1)}, f32[32,4]{1,0:T(8,128)}, u32[]{:S(2)}) copy-start(f32[32,4]{1,0:T(8,128)} %copy.28.refs_2_.refs_1_.refs_3_) | copy-start | bytes 1540
  132.8 5.0 %copy-start.4 = (f32[32,128]{1,0:T(8,128)S(1)}, f32[32,128]{1,0:T(8,128)}, u32[]{:S(2)}) copy-start(f32[32,128]{1,0:T(8,128)} %get-tuple-element.45.refs_1_.refs_5_.refs_11_.refs_2_) | copy-start | bytes 49156
  132.8 5.0 %copy-start.5 = (s32[8]{0:T(128)S(1)}, s32[8]{0:T(128)}, u32[]{:S(2)}) copy-start(s32[8]{0:T(128)} %stack.66.refs_0_) | copy-start | bytes 100
  132.8 5.0 %copy-start.10 = (f32[4,128]{1,0:T(4,128)S(1)}, f32[4,128]{1,0:T(4,128)}, u32[]{:S(2)}) copy-start(f32[4,128]{1,0:T(4,128)} %get-tuple-element.57.refs_4_) | copy-start | bytes 6148
  135.9 4.4 %copy-start.8 = (bf16[34,32,128]{2,1,0:T(8,128)(2,1)}, bf16[34,32,128]{2,1,0:T(8,128)(2,1)S(1)}, u32[]{:S(2)}) copy-start(bf16[34,32,128]{2,1,0:T(8,128)(2,1)S(1)} %collective-permute-done.6.refs_6_) | copy-start | bytes 835588
  137.8 2.6 %copy-start.9 = (bf16[34,32,128]{2,1,0:T(8,128)(2,1)}, bf16[34,32,128]{2,1,0:T(8,128)(2,1)S(1)}, u32[]{:S(2)}) copy-start(bf16[34,32,128]{2,1,0:T(8,128)(2,1)S(1)} %collective-permute-done.7.refs_7_) | copy-start | bytes 835588
  137.8 0.7 copy-start.13
  140.4 0.6 copy-start.12
  141.0 21.5 %all-to-all-start.4 = ((bf16[128,8,128]{2,1,0:T(8,128)(2,1)}), bf16[128,8,128]{2,1,0:T(8,128)(2,1)S(1)}, u32[]{:S(2)}, u32[]{:S(2)}) async-start(bf16[128,8,128]{2,1,0:T(8,128)(2,1)} %bitcast.27), calls=%async_computation.4 | async-start | bytes 524288 | tf_op jit(solution)/shard_map/all_to_all | solution.py:683

commit v14 on v13

--- a/solution.py
+++ b/solution.py
@@ -727,7 +727,6 @@
         [sh((14, 64, 128), BF16)] * 2,
         "pack",
         smem_first=False,
-        after=(w1,),
         near=2,
         grant=16,
     )

time: 165 us -> 164 us (level)
    unnamed x54 -> x52, local copies, waits for them, and re-layouts: 5.52 us -> 4.44 us
  transfers between devices with their start and end apart: 13 -> 13, of which waited for: 10 -> 9; matrix products, arithmetic and copies ran while one was open for 1% -> 1% of each run, Pallas kernels for 18% -> 18%
where the time goes in v14:
time: 164 us; the launch traced here: 163 us
  starting transfers between devices  63.4 us (39%)
  Pallas kernels  55.9 us (34%)
  waiting for transfers between devices  34.3 us (21%)
  local copies, waits for them, and re-layouts  7.92 us (5%)
    pallas_call x15, Pallas kernels, call(): pl.pallas_call(body, out_shape=outs, in_specs=[SM] * lead + [pl.BlockSpec...  55.9 us
    all_to_all x5, starting transfers between devices, share(): return lax.all_to_all(msg, ALL[::-1], 0, 0, tiled=True)  40.7 us
    all_to_all x5, waiting for transfers between devices, share(): return lax.all_to_all(msg, ALL[::-1], 0, 0, tiled=True)  18.4 us
    ppermute x4, starting transfers between devices, up(): return lax.ppermute(values, axes, [(i, i + 1) for i in range(count - 1)])  16.9 us
    ppermute x4, waiting for transfers between devices, down(): return lax.ppermute(values, axes, [(i + 1, i) for i in range(count - 1)])  13.8 us
    ppermute x4, starting transfers between devices, down(): return lax.ppermute(values, axes, [(i + 1, i) for i in range(count - 1)])  5.8 us
    unnamed x52, local copies, waits for them, and re-layouts  4.44 us
  transfers between devices with their start and end apart: 13, of which 9 were waited for; matrix products, arithmetic and copies ran while one was open for 1% of the time, Pallas kernels for 18%

profile of v14, /device:TPU:1, one launch (start us, length us, event | category | flops | bytes accessed | tf_op | source)
XLA Modules:
  0.0 162.9 jit_solution(17654757528992019008)
XLA Ops:
  0.6 0.0 copy-start.16
  0.6 1.4 copy.26
  2.1 0.0 copy-start.1
  2.1 1.3 collective-permute-start.1
  3.4 4.7 %collective-permute-start = (bf16[32,64,128]{2,1,0:T(8,128)(2,1)S(1)}, bf16[32,64,128]{2,1,0:T(8,128)(2,1)S(1)}, u32[]{:S(2)}, u32[]{:S(2)}) collective-permute-start(bf16[32,64,128]{2,1,0:T(8,128)(2,1)S(1)} %bitcast.44), channel_id=1, source_target_pairs={{0,8},{8,16},{16,24},{24,32},{32,40},{40,48},{48,56},{56,64},{64,7... | collective-permute-start | bytes 1572872 | tf_op jit(solution)/shard_map/ppermute | solution.py:674
  8.1 0.3 copy.27
  8.5 0.0 copy-start
  8.5 8.9 %collective-permute-done.1.refs_1_.refs_5_ = bf16[32,64,128]{2,1,0:T(8,128)(2,1)S(1)} collective-permute-done((bf16[32,64,128]{2,1,0:T(8,128)(2,1)S(1)}, bf16[32,64,128]{2,1,0:T(8,128)(2,1)S(1)}, u32[]{:S(2)}, u32[]{:S(2)}) %collective-permute-start.1) | collective-permute-done | bytes 524320 | tf_op jit(solution)/shard_map/ppermute | solution.py:679
  17.4 0.9 collective-permute-done.refs_0_.refs_4_
  18.2 2.1 %pack.1 = (bf16[14,64,128]{2,1,0:T(8,128)(2,1)S(1)}, bf16[14,64,128]{2,1,0:T(8,128)(2,1)S(1)}) custom-call(bf16[32,64,128]{2,1,0:T(8,128)(2,1)S(1)} %collective-permute-done.refs_0_.refs_4_, bf16[32,64,128]{2,1,0:T(8,128)(2,1)S(1)} %collective-permute-done.1.refs_1_.refs_5_, bf16[32,64,128]{2,1,0:T(8,128)(2,1)S(1)} %bitcast.45, bf16[32,64,128]{2,1,0:T(8,128)(2,1)S(1)} %bitcast.38), custom_call_target="tpu_custom_call" | custom-call | flops 2000000000 | bytes 6000000 | tf_op jit(solution)/shard_map/pack/pallas_call | solution.py:650
  20.4 5.5 %collective-permute-start.2 = (bf16[14,64,128]{2,1,0:T(8,128)(2,1)S(1)}, bf16[14,64,128]{2,1,0:T(8,128)(2,1)S(1)}, u32[]{:S(2)}, u32[]{:S(2)}) collective-permute-start(bf16[14,64,128]{2,1,0:T(8,128)(2,1)S(1)} %get-tuple-element.35), channel_id=1, source_target_pairs={{0,1},{1,2},{2,3},{3,4},{4,5},{5,6},{6,7},{8,9},{9,10},{10,11},{11... | collective-permute-start | bytes 688136 | tf_op jit(solution)/shard_map/ppermute | solution.py:674
  25.9 1.9 %collective-permute-start.3 = (bf16[14,64,128]{2,1,0:T(8,128)(2,1)S(1)}, bf16[14,64,128]{2,1,0:T(8,128)(2,1)S(1)}, u32[]{:S(2)}, u32[]{:S(2)}) collective-permute-start(bf16[14,64,128]{2,1,0:T(8,128)(2,1)S(1)} %get-tuple-element.36), channel_id=1, source_target_pairs={{1,0},{2,1},{3,2},{4,3},{5,4},{6,5},{7,6},{9,8},{10,9},{11,10},{12... | collective-permute-start | bytes 688136 | tf_op jit(solution)/shard_map/ppermute | solution.py:679
  27.9 2.2 %weights.1 = (bf16[192,384]{1,0:T(8,128)(2,1)}, bf16[192,384]{1,0:T(8,128)(2,1)}) custom-call(bf16[27,32,32]{2,1,0:T(8,128)(2,1)} %bitcast.61, bf16[27,32,32]{2,1,0:T(8,128)(2,1)} %bitcast.59), custom_call_target="tpu_custom_call" | custom-call | flops 2000000000 | bytes 6000000 | tf_op jit(solution)/shard_map/weights/pallas_call | solution.py:650
  30.2 0.0 collective-permute-done.2.refs_0_.refs_5_.refs_8_
  30.2 3.1 %collective-permute-done.3.refs_1_.refs_6_.refs_9_ = bf16[14,64,128]{2,1,0:T(8,128)(2,1)S(1)} collective-permute-done((bf16[14,64,128]{2,1,0:T(8,128)(2,1)S(1)}, bf16[14,64,128]{2,1,0:T(8,128)(2,1)S(1)}, u32[]{:S(2)}, u32[]{:S(2)}) %collective-permute-start.3) | collective-permute-done | bytes 229408 | tf_op jit(solution)/shard_map/ppermute | solution.py:679
  33.3 0.0 copy-done.19
  33.3 0.7 copy-done.20
  34.0 5.9 %conv_one.1 = (bf16[40,128,128]{2,1,0:T(8,128)(2,1)}, f32[38,128,128]{2,1,0:T(8,128)}, f32[128,4,128]{2,1,0:T(4,128)}, f32[16,128]{1,0:T(8,128)}, f32[32,128]{1,0:T(8,128)}) custom-call(bf16[14,64,128]{2,1,0:T(8,128)(2,1)} %copy-done.19, bf16[14,64,128]{2,1,0:T(8,128)(2,1)} %copy-done.20, bf16[192,384]{1,0:T(8,128)(2,1)} %get-tuple-element.37.refs_2_, ...), custom_call_target="tpu_custom_call" | custom-call | flops 2000000000 | bytes 6000000 | tf_op jit(solution)/shard_map/conv_one/pallas_call | solution.py:650
  39.9 12.6 %all-to-all-start = ((f32[128,4,128]{2,1,0:T(4,128)}), f32[128,4,128]{2,1,0:T(4,128)S(1)}, u32[]{:S(2)}, u32[]{:S(2)}) async-start(f32[128,4,128]{2,1,0:T(4,128)} %get-tuple-element.38), calls=%async_computation | async-start | bytes 524288 | tf_op jit(solution)/shard_map/all_to_all | solution.py:683
  52.6 0.7 copy.28.refs_2_.refs_1_.refs_3_
  53.2 0.7 stack.66.refs_0_
  53.9 3.8 %hidden_features.1.refs_8_.refs_7_ = f32[9,32,128]{2,1,0:T(8,128)} custom-call(f32[32,128]{1,0:T(8,128)} %get-tuple-element.41.refs_0_, f32[38,128,128]{2,1,0:T(8,128)} %get-tuple-element.39.refs_1_.refs_3_.refs_12_.refs_4_, bf16[40,128,128]{2,1,0:T(8,128)(2,1)} %get-tuple-element.42.refs_2_.refs_13_), custom_call_target="tpu_custom_call" | custom-call | flops 2000000000 | bytes 6000000 | tf_op jit(solution)/shard_map/hidden_features/pallas_call | solution.py:650
  57.7 5.7 %all-to-all-done.refs_1_.refs_0_ = f32[128,4,128]{2,1,0:T(4,128)S(1)} async-done(((f32[128,4,128]{2,1,0:T(4,128)}), f32[128,4,128]{2,1,0:T(4,128)S(1)}, u32[]{:S(2)}, u32[]{:S(2)}) %all-to-all-start) | async-done | bytes 262176 | tf_op jit(solution)/shard_map/all_to_all | solution.py:683
  63.4 0.7 copy-done.18
  64.1 6.4 %conv_two.1 = (bf16[38,128,128]{2,1,0:T(8,128)(2,1)}, f32[36,64,128]{2,1,0:T(8,128)}, bf16[72,32,128]{2,1,0:T(8,128)(2,1)}, bf16[72,32,128]{2,1,0:T(8,128)(2,1)}, f32[128,128]{1,0:T(8,128)}, /*index=5*/f32[32,128]{1,0:T(8,128)}) custom-call(s32[8]{0:T(128)} %stack.66.refs_0_, f32[128,4,128]{2,1,0:T(4,128)} %copy-done.18, ...), custom_call_target="tpu_custom_call" | custom-call | flops 2000000000 | bytes 6000000 | tf_op jit(solution)/shard_map/conv_two/pallas_call | solution.py:650
  70.5 4.1 %all-to-all-start.1 = ((f32[128,1,128]{2,1,0:T(1,128)}), f32[128,1,128]{2,1,0:T(1,128)S(1)}, u32[]{:S(2)}, u32[]{:S(2)}) async-start(f32[128,1,128]{2,1,0:T(1,128)} %bitcast.54), calls=%async_computation.1 | async-start | bytes 131072 | tf_op jit(solution)/shard_map/all_to_all | solution.py:683
  74.7 3.4 %collective-permute-start.4 = (bf16[72,32,128]{2,1,0:T(8,128)(2,1)}, bf16[72,32,128]{2,1,0:T(8,128)(2,1)S(1)}, u32[]{:S(2)}, u32[]{:S(2)}) collective-permute-start(bf16[72,32,128]{2,1,0:T(8,128)(2,1)} %get-tuple-element.49), channel_id=1, source_target_pairs={{0,8},{8,16},{16,24},{24,32},{32,40},{40,48},{48,56},{56,64},{64,7... | collective-permute-start | bytes 1769480 | tf_op jit(solution)/shard_map/ppermute | solution.py:674
  78.1 1.3 collective-permute-start.5
  79.4 2.0 %flipped_two.1.refs_8_.refs_10_ = bf16[192,384]{1,0:T(8,128)(2,1)} custom-call(bf16[27,32,32]{2,1,0:T(8,128)(2,1)} %bitcast.60, f32[32,128]{1,0:T(8,128)} %get-tuple-element.45.refs_1_.refs_5_.refs_11_.refs_2_), custom_call_target="tpu_custom_call" | custom-call | flops 2000000000 | bytes 6000000 | tf_op jit(solution)/shard_map/flipped_two/pallas_call | solution.py:650
  81.4 2.9 %all-to-all-done.1 = f32[128,1,128]{2,1,0:T(1,128)S(1)} async-done(((f32[128,1,128]{2,1,0:T(1,128)}), f32[128,1,128]{2,1,0:T(1,128)S(1)}, u32[]{:S(2)}, u32[]{:S(2)}) %all-to-all-start.1) | async-done | bytes 65568 | tf_op jit(solution)/shard_map/all_to_all | solution.py:683
  84.3 0.6 copy-done.21
  84.9 3.7 %slope_two.1 = (f32[128,4,128]{2,1,0:T(4,128)}, f32[32,128]{1,0:T(8,128)}) custom-call(s32[8]{0:T(128)} %stack.66.refs_0_, f32[128,128]{1,0:T(8,128)} %bitcast.53, f32[32,4]{1,0:T(8,128)} %copy.28.refs_2_.refs_1_.refs_3_, bf16[32,64,128]{2,1,0:T(8,128)(2,1)} %bitcast.40, f32[36,64,128]{2,1,0:T(8,128)} %get-tuple-element.44.refs_4_.refs_2_, ...), custom_call_target="tpu_custom_call" | custom-call | flops 2000000000 | bytes 6000000 | tf_op jit(solution)/shard_map/slope_two/pallas_call | solution.py:650
  88.6 8.2 %all-to-all-start.2 = ((f32[128,4,128]{2,1,0:T(4,128)}), f32[128,4,128]{2,1,0:T(4,128)S(1)}, u32[]{:S(2)}, u32[]{:S(2)}) async-start(f32[128,4,128]{2,1,0:T(4,128)} %get-tuple-element.48), calls=%async_computation.2 | async-start | bytes 524288 | tf_op jit(solution)/shard_map/all_to_all | solution.py:683
  96.9 6.2 %active_sums.1 = (f32[9,32,128]{2,1,0:T(8,128)}, f32[9,32,128]{2,1,0:T(8,128)}, f32[16,128]{1,0:T(8,128)}) custom-call(f32[32,128]{1,0:T(8,128)} %get-tuple-element.47.refs_0_.refs_2_, f32[32,4]{1,0:T(8,128)} %copy.28.refs_2_.refs_1_.refs_3_, f32[36,64,128]{2,1,0:T(8,128)} %get-tuple-element.44.refs_4_.refs_2_, bf16[32,64,128]{2,1,0:T(8,128)(2,1)} %bitcast.41, ...), custom_call_target="tpu_custom_call" | custom-call | flops 2000000000 | bytes 6000000 | tf_op jit(solution)/shard_map/active_sums/pallas_call | solution.py:650
  103.1 4.7 %all-to-all-done.2.refs_1_ = f32[128,4,128]{2,1,0:T(4,128)S(1)} async-done(((f32[128,4,128]{2,1,0:T(4,128)}), f32[128,4,128]{2,1,0:T(4,128)S(1)}, u32[]{:S(2)}, u32[]{:S(2)}) %all-to-all-start.2) | async-done | bytes 262176 | tf_op jit(solution)/shard_map/all_to_all | solution.py:683
  107.8 0.0 collective-permute-done.4.refs_5_
  107.8 0.0 collective-permute-done.5.refs_6_
  107.8 0.7 copy-done.13
  108.5 0.2 copy-done.14
  108.7 0.2 copy-done.15
  108.9 8.3 %back_two.1 = (f32[34,64,128]{2,1,0:T(8,128)}, bf16[34,32,128]{2,1,0:T(8,128)(2,1)}, bf16[34,32,128]{2,1,0:T(8,128)(2,1)}, f32[128,8,128]{2,1,0:T(8,128)}, f32[4,128]{1,0:T(4,128)}) custom-call(s32[8]{0:T(128)} %stack.66.refs_0_, f32[128,4,128]{2,1,0:T(4,128)} %copy-done.13, f32[32,128]{1,0:T(8,128)} %get-tuple-element.47.refs_0_.refs_2_, ...), custom_call_target="tpu_custom_call" | custom-call | flops 2000000000 | bytes 6000000 | tf_op jit(solution)/shard_map/back_two/pallas_call | solution.py:650
  117.2 5.1 %all-to-all-start.3 = ((f32[128,8,128]{2,1,0:T(8,128)}), f32[128,8,128]{2,1,0:T(8,128)S(1)}, u32[]{:S(2)}, u32[]{:S(2)}) async-start(f32[128,8,128]{2,1,0:T(8,128)} %get-tuple-element.56), calls=%async_computation.3 | async-start | bytes 1048576 | tf_op jit(solution)/shard_map/all_to_all | solution.py:683
  122.3 3.3 %collective-permute-start.6 = (bf16[34,32,128]{2,1,0:T(8,128)(2,1)}, bf16[34,32,128]{2,1,0:T(8,128)(2,1)S(1)}, u32[]{:S(2)}, u32[]{:S(2)}) collective-permute-start(bf16[34,32,128]{2,1,0:T(8,128)(2,1)} %get-tuple-element.58), channel_id=1, source_target_pairs={{0,8},{8,16},{16,24},{24,32},{32,40},{40,48},{48,56},{56,64},{64,7... | collective-permute-start | bytes 835592 | tf_op jit(solution)/shard_map/ppermute | solution.py:674
  125.6 1.3 collective-permute-start.7
  126.9 2.4 %output.1 = bf16[32,64,128]{2,1,0:T(8,128)(2,1)} custom-call(f32[32,128]{1,0:T(8,128)} %get-tuple-element.47.refs_0_.refs_2_, f32[32,4]{1,0:T(8,128)} %copy.28.refs_2_.refs_1_.refs_3_, f32[36,64,128]{2,1,0:T(8,128)} %get-tuple-element.44.refs_4_.refs_2_, f32[34,64,128]{2,1,0:T(8,128)} %get-tuple-element.55.refs_3_.refs_1_.refs_5_), custom_call_target="tpu_custom_call" | custom-call | flops 2000000000 | bytes 6000000 | tf_op jit(solution)/shard_map/output/pallas_call | solution.py:650
  129.3 0.0 copy-start.17
  129.3 2.1 %flipped_one.1.refs_1_.refs_8_ = bf16[192,384]{1,0:T(8,128)(2,1)} custom-call(bf16[27,32,32]{2,1,0:T(8,128)(2,1)} %bitcast.62, f32[34,64,128]{2,1,0:T(8,128)} %get-tuple-element.55.refs_3_.refs_1_.refs_5_), custom_call_target="tpu_custom_call" | custom-call | flops 2000000000 | bytes 6000000 | tf_op jit(solution)/shard_map/flipped_one/pallas_call | solution.py:650
  131.4 0.3 copy.38
  131.7 0.0 copy-start.2
  131.8 0.0 copy-start.10
  131.8 1.9 %total.1.refs_5_ = f32[4,128]{1,0:T(4,128)} custom-call(f32[128,4,128]{2,1,0:T(4,128)} %copy-done.18, bf16[192,384]{1,0:T(8,128)(2,1)} %flipped_one.1.refs_1_.refs_8_), custom_call_target="tpu_custom_call" | custom-call | flops 2000000000 | bytes 6000000 | tf_op jit(solution)/shard_map/total/pallas_call | solution.py:650
  133.7 1.2 collective-permute-done.6.refs_6_
  134.9 1.8 %collective-permute-done.7.refs_7_ = bf16[34,32,128]{2,1,0:T(8,128)(2,1)S(1)} collective-permute-done((bf16[34,32,128]{2,1,0:T(8,128)(2,1)}, bf16[34,32,128]{2,1,0:T(8,128)(2,1)S(1)}, u32[]{:S(2)}, u32[]{:S(2)}) %collective-permute-start.7) | collective-permute-done | bytes 278560 | tf_op jit(solution)/shard_map/ppermute | solution.py:679
  136.7 0.0 all-to-all-done.3.refs_1_
  136.8 0.7 copy-done.12
  137.5 1.9 %own_rows.1 = (bf16[1024,128]{1,0:T(8,128)(2,1)}, f32[4,32]{1,0:T(4,128)}, f32[8,128]{1,0:T(8,128)S(1)}) custom-call(s32[8]{0:T(128)S(1)} %copy-done.5, f32[128,8,128]{2,1,0:T(8,128)S(1)} %all-to-all-done.3.refs_1_, f32[32,128]{1,0:T(8,128)S(1)} %copy-done.4, f32[32,4]{1,0:T(8,128)S(1)} %copy-done.3, f32[4,128]{1,0:T(4,128)S(1)} %copy-done.10, ...), custom_call_target="tpu_custom_call" | custom-call | flops 2000000000 | bytes 6000000 | tf_op jit(solution)/shard_map/own_rows/pallas_call | solution.py:650
  139.4 0.0 copy-done.8
  139.4 0.0 copy-done.9
  139.4 0.0 copy-start.11
  139.4 0.6 copy-done.11
  140.0 10.6 %all-to-all-start.4 = ((bf16[128,8,128]{2,1,0:T(8,128)(2,1)}), bf16[128,8,128]{2,1,0:T(8,128)(2,1)S(1)}, u32[]{:S(2)}, u32[]{:S(2)}) async-start(bf16[128,8,128]{2,1,0:T(8,128)(2,1)} %bitcast.27), calls=%async_computation.4 | async-start | bytes 524288 | tf_op jit(solution)/shard_map/all_to_all | solution.py:683
  150.6 5.7 %back_one.1 = bf16[32,2,32,128]{3,2,1,0:T(8,128)(2,1)} custom-call(s32[8]{0:T(128)} %stack.66.refs_0_, f32[8,128]{1,0:T(8,128)} %copy-done.11, f32[32,128]{1,0:T(8,128)} %get-tuple-element.45.refs_1_.refs_5_.refs_11_.refs_2_, f32[32,4]{1,0:T(8,128)} %copy.28.refs_2_.refs_1_.refs_3_, f32[38,128,128]{2,1,0:T(8,128)} %get-tuple-element.39.refs_1_.refs_3_.refs_12_.refs_4_, ...), custom_call_target="tpu_custom_call" | custom-call | flops 2000000000 | bytes 6000000 | tf_op jit(solution)/shard_map/back_one/pallas_call | solution.py:650
  156.3 5.2 %all-to-all-done.4 = bf16[128,8,128]{2,1,0:T(8,128)(2,1)S(1)} async-done(((bf16[128,8,128]{2,1,0:T(8,128)(2,1)}), bf16[128,8,128]{2,1,0:T(8,128)(2,1)S(1)}, u32[]{:S(2)}, u32[]{:S(2)}) %all-to-all-start.4) | async-done | bytes 262176 | tf_op jit(solution)/shard_map/all_to_all | solution.py:683
  161.5 1.2 finish.1
  (35 shorter events, 0.1 us)
Async XLA Ops:
  0.6 7.5 %copy-start.16 = (bf16[32,2,32,128]{3,2,1,0:T(8,128)(2,1)S(1)}, bf16[32,2,32,128]{3,2,1,0:T(8,128)(2,1)}, u32[]{:S(2)}) copy-start(bf16[32,2,32,128]{3,2,1,0:T(8,128)(2,1)} %param.15) | copy-start | bytes 1572868
  2.1 18.3 %copy-start.1 = (bf16[32,2,32,128]{3,2,1,0:T(8,128)(2,1)}, bf16[32,2,32,128]{3,2,1,0:T(8,128)(2,1)S(1)}, u32[]{:S(2)}) copy-start(bf16[32,2,32,128]{3,2,1,0:T(8,128)(2,1)S(1)} %copy.26) | copy-start | bytes 1572868
  2.1 15.3 %collective-permute-start.1 = (bf16[32,64,128]{2,1,0:T(8,128)(2,1)S(1)}, bf16[32,64,128]{2,1,0:T(8,128)(2,1)S(1)}, u32[]{:S(2)}, u32[]{:S(2)}) collective-permute-start(bf16[32,64,128]{2,1,0:T(8,128)(2,1)S(1)} %bitcast.43), channel_id=1, source_target_pairs={{8,0},{16,8},{24,16},{32,24},{40,32},{48,40},{56,48},{64,56},{72,6... | collective-permute-start | bytes 1572872 | tf_op jit(solution)/shard_map/ppermute | solution.py:679
  3.4 14.8 %collective-permute-start = (bf16[32,64,128]{2,1,0:T(8,128)(2,1)S(1)}, bf16[32,64,128]{2,1,0:T(8,128)(2,1)S(1)}, u32[]{:S(2)}, u32[]{:S(2)}) collective-permute-start(bf16[32,64,128]{2,1,0:T(8,128)(2,1)S(1)} %bitcast.44), channel_id=1, source_target_pairs={{0,8},{8,16},{16,24},{24,32},{32,40},{40,48},{48,56},{56,64},{64,7... | collective-permute-start | bytes 1572872 | tf_op jit(solution)/shard_map/ppermute | solution.py:674
  8.5 11.9 %copy-start = (bf16[32,2,32,128]{3,2,1,0:T(8,128)(2,1)}, bf16[32,2,32,128]{3,2,1,0:T(8,128)(2,1)S(1)}, u32[]{:S(2)}) copy-start(bf16[32,2,32,128]{3,2,1,0:T(8,128)(2,1)S(1)} %copy.27) | copy-start | bytes 1572868
  17.4 3.0 %copy-start.6 = (bf16[32,64,128]{2,1,0:T(8,128)(2,1)}, bf16[32,64,128]{2,1,0:T(8,128)(2,1)S(1)}, u32[]{:S(2)}) copy-start(bf16[32,64,128]{2,1,0:T(8,128)(2,1)S(1)} %collective-permute-done.1.refs_1_.refs_5_) | copy-start | bytes 1572868
  18.2 2.1 %copy-start.7 = (bf16[32,64,128]{2,1,0:T(8,128)(2,1)}, bf16[32,64,128]{2,1,0:T(8,128)(2,1)S(1)}, u32[]{:S(2)}) copy-start(bf16[32,64,128]{2,1,0:T(8,128)(2,1)S(1)} %collective-permute-done.refs_0_.refs_4_) | copy-start | bytes 1572868
  20.4 9.8 %collective-permute-start.2 = (bf16[14,64,128]{2,1,0:T(8,128)(2,1)S(1)}, bf16[14,64,128]{2,1,0:T(8,128)(2,1)S(1)}, u32[]{:S(2)}, u32[]{:S(2)}) collective-permute-start(bf16[14,64,128]{2,1,0:T(8,128)(2,1)S(1)} %get-tuple-element.35), channel_id=1, source_target_pairs={{0,1},{1,2},{2,3},{3,4},{4,5},{5,6},{6,7},{8,9},{9,10},{10,11},{11... | collective-permute-start | bytes 688136 | tf_op jit(solution)/shard_map/ppermute | solution.py:674
  25.9 7.3 %collective-permute-start.3 = (bf16[14,64,128]{2,1,0:T(8,128)(2,1)S(1)}, bf16[14,64,128]{2,1,0:T(8,128)(2,1)S(1)}, u32[]{:S(2)}, u32[]{:S(2)}) collective-permute-start(bf16[14,64,128]{2,1,0:T(8,128)(2,1)S(1)} %get-tuple-element.36), channel_id=1, source_target_pairs={{1,0},{2,1},{3,2},{4,3},{5,4},{6,5},{7,6},{9,8},{10,9},{11,10},{12... | collective-permute-start | bytes 688136 | tf_op jit(solution)/shard_map/ppermute | solution.py:679
  30.2 3.1 %copy-start.19 = (bf16[14,64,128]{2,1,0:T(8,128)(2,1)}, bf16[14,64,128]{2,1,0:T(8,128)(2,1)S(1)}, u32[]{:S(2)}) copy-start(bf16[14,64,128]{2,1,0:T(8,128)(2,1)S(1)} %collective-permute-done.2.refs_0_.refs_5_.refs_8_) | copy-start | bytes 688132
  33.3 0.7 copy-start.20
  34.0 18.5 %copy-start.22 = (f32[32]{0:T(128)S(1)}, f32[32]{0:T(128)}, u32[]{:S(2)}) copy-start(f32[32]{0:T(128)} %param.14) | copy-start | bytes 388
  34.0 18.6 %copy-start.23 = (f32[32]{0:T(128)S(1)}, f32[32]{0:T(128)}, u32[]{:S(2)}) copy-start(f32[32]{0:T(128)} %param.13) | copy-start | bytes 388
  34.0 18.6 %copy-start.24 = (f32[32]{0:T(128)S(1)}, f32[32]{0:T(128)}, u32[]{:S(2)}) copy-start(f32[32]{0:T(128)} %param.11) | copy-start | bytes 388
  34.0 18.6 %copy-start.25 = (f32[32]{0:T(128)S(1)}, f32[32]{0:T(128)}, u32[]{:S(2)}) copy-start(f32[32]{0:T(128)} %param.10) | copy-start | bytes 388
  39.9 23.5 %all-to-all-start = ((f32[128,4,128]{2,1,0:T(4,128)}), f32[128,4,128]{2,1,0:T(4,128)S(1)}, u32[]{:S(2)}, u32[]{:S(2)}) async-start(f32[128,4,128]{2,1,0:T(4,128)} %get-tuple-element.38), calls=%async_computation | async-start | bytes 524288 | tf_op jit(solution)/shard_map/all_to_all | solution.py:683
  63.4 0.7 copy-start.18
  70.5 13.7 %all-to-all-start.1 = ((f32[128,1,128]{2,1,0:T(1,128)}), f32[128,1,128]{2,1,0:T(1,128)S(1)}, u32[]{:S(2)}, u32[]{:S(2)}) async-start(f32[128,1,128]{2,1,0:T(1,128)} %bitcast.54), calls=%async_computation.1 | async-start | bytes 131072 | tf_op jit(solution)/shard_map/all_to_all | solution.py:683
  74.7 33.1 %collective-permute-start.4 = (bf16[72,32,128]{2,1,0:T(8,128)(2,1)}, bf16[72,32,128]{2,1,0:T(8,128)(2,1)S(1)}, u32[]{:S(2)}, u32[]{:S(2)}) collective-permute-start(bf16[72,32,128]{2,1,0:T(8,128)(2,1)} %get-tuple-element.49), channel_id=1, source_target_pairs={{0,8},{8,16},{16,24},{24,32},{32,40},{40,48},{48,56},{56,64},{64,7... | collective-permute-start | bytes 1769480 | tf_op jit(solution)/shard_map/ppermute | solution.py:674
  78.1 29.7 %collective-permute-start.5 = (bf16[72,32,128]{2,1,0:T(8,128)(2,1)}, bf16[72,32,128]{2,1,0:T(8,128)(2,1)S(1)}, u32[]{:S(2)}, u32[]{:S(2)}) collective-permute-start(bf16[72,32,128]{2,1,0:T(8,128)(2,1)} %get-tuple-element.50), channel_id=1, source_target_pairs={{8,0},{16,8},{24,16},{32,24},{40,32},{48,40},{56,48},{64,56},{72,6... | collective-permute-start | bytes 1769480 | tf_op jit(solution)/shard_map/ppermute | solution.py:679
  84.3 0.6 copy-start.21
  88.6 19.1 %all-to-all-start.2 = ((f32[128,4,128]{2,1,0:T(4,128)}), f32[128,4,128]{2,1,0:T(4,128)S(1)}, u32[]{:S(2)}, u32[]{:S(2)}) async-start(f32[128,4,128]{2,1,0:T(4,128)} %get-tuple-element.48), calls=%async_computation.2 | async-start | bytes 524288 | tf_op jit(solution)/shard_map/all_to_all | solution.py:683
  107.8 0.7 copy-start.13
  107.8 0.9 copy-start.14
  107.8 1.1 copy-start.15
  117.2 19.6 %all-to-all-start.3 = ((f32[128,8,128]{2,1,0:T(8,128)}), f32[128,8,128]{2,1,0:T(8,128)S(1)}, u32[]{:S(2)}, u32[]{:S(2)}) async-start(f32[128,8,128]{2,1,0:T(8,128)} %get-tuple-element.56), calls=%async_computation.3 | async-start | bytes 1048576 | tf_op jit(solution)/shard_map/all_to_all | solution.py:683
  122.3 12.6 %collective-permute-start.6 = (bf16[34,32,128]{2,1,0:T(8,128)(2,1)}, bf16[34,32,128]{2,1,0:T(8,128)(2,1)S(1)}, u32[]{:S(2)}, u32[]{:S(2)}) collective-permute-start(bf16[34,32,128]{2,1,0:T(8,128)(2,1)} %get-tuple-element.58), channel_id=1, source_target_pairs={{0,8},{8,16},{16,24},{24,32},{32,40},{40,48},{48,56},{56,64},{64,7... | collective-permute-start | bytes 835592 | tf_op jit(solution)/shard_map/ppermute | solution.py:674
  125.6 11.2 %collective-permute-start.7 = (bf16[34,32,128]{2,1,0:T(8,128)(2,1)}, bf16[34,32,128]{2,1,0:T(8,128)(2,1)S(1)}, u32[]{:S(2)}, u32[]{:S(2)}) collective-permute-start(bf16[34,32,128]{2,1,0:T(8,128)(2,1)} %get-tuple-element.59), channel_id=1, source_target_pairs={{8,0},{16,8},{24,16},{32,24},{40,32},{48,40},{56,48},{64,56},{72,6... | collective-permute-start | bytes 835592 | tf_op jit(solution)/shard_map/ppermute | solution.py:679
  129.3 2.1 %copy-start.17 = (bf16[32,64,128]{2,1,0:T(8,128)(2,1)S(1)}, bf16[32,64,128]{2,1,0:T(8,128)(2,1)}, u32[]{:S(2)}) copy-start(bf16[32,64,128]{2,1,0:T(8,128)(2,1)} %output.1) | copy-start | bytes 1572868
  131.7 5.0 %copy-start.2 = (bf16[32,2,32,128]{3,0,1,2:T(8,128)(2,1)}, bf16[32,2,32,128]{3,0,1,2:T(8,128)(2,1)S(1)}, u32[]{:S(2)}) copy-start(bf16[32,2,32,128]{3,0,1,2:T(8,128)(2,1)S(1)} %copy.38) | copy-start | bytes 1572868
  131.7 5.0 %copy-start.3 = (f32[32,4]{1,0:T(8,128)S(1)}, f32[32,4]{1,0:T(8,128)}, u32[]{:S(2)}) copy-start(f32[32,4]{1,0:T(8,128)} %copy.28.refs_2_.refs_1_.refs_3_) | copy-start | bytes 1540
  131.8 5.0 %copy-start.4 = (f32[32,128]{1,0:T(8,128)S(1)}, f32[32,128]{1,0:T(8,128)}, u32[]{:S(2)}) copy-start(f32[32,128]{1,0:T(8,128)} %get-tuple-element.45.refs_1_.refs_5_.refs_11_.refs_2_) | copy-start | bytes 49156
  131.8 5.0 %copy-start.5 = (s32[8]{0:T(128)S(1)}, s32[8]{0:T(128)}, u32[]{:S(2)}) copy-start(s32[8]{0:T(128)} %stack.66.refs_0_) | copy-start | bytes 100
  131.8 5.0 %copy-start.10 = (f32[4,128]{1,0:T(4,128)S(1)}, f32[4,128]{1,0:T(4,128)}, u32[]{:S(2)}) copy-start(f32[4,128]{1,0:T(4,128)} %get-tuple-element.57.refs_4_) | copy-start | bytes 6148
  134.9 4.5 %copy-start.8 = (bf16[34,32,128]{2,1,0:T(8,128)(2,1)}, bf16[34,32,128]{2,1,0:T(8,128)(2,1)S(1)}, u32[]{:S(2)}) copy-start(bf16[34,32,128]{2,1,0:T(8,128)(2,1)S(1)} %collective-permute-done.6.refs_6_) | copy-start | bytes 835588
  136.7 2.6 %copy-start.9 = (bf16[34,32,128]{2,1,0:T(8,128)(2,1)}, bf16[34,32,128]{2,1,0:T(8,128)(2,1)S(1)}, u32[]{:S(2)}) copy-start(bf16[34,32,128]{2,1,0:T(8,128)(2,1)S(1)} %collective-permute-done.7.refs_7_) | copy-start | bytes 835588
  136.8 0.7 copy-start.12
  139.4 0.6 copy-start.11
  140.0 21.5 %all-to-all-start.4 = ((bf16[128,8,128]{2,1,0:T(8,128)(2,1)}), bf16[128,8,128]{2,1,0:T(8,128)(2,1)S(1)}, u32[]{:S(2)}, u32[]{:S(2)}) async-start(bf16[128,8,128]{2,1,0:T(8,128)(2,1)} %bitcast.27), calls=%async_computation.4 | async-start | bytes 524288 | tf_op jit(solution)/shard_map/all_to_all | solution.py:683
